TPU v7x, 32 devices: a whole 2x2x4 slice. The times are simulated.
32 devices in a mesh: rows: 8 (over z, y), hid: 4 (over x, core).
Axes of the slice: x: 2, y: 2, z: 4, core: 2. Of those that a mesh axis runs over, the one named last changes fastest.
Arguments:
- features: bfloat16 [32768, 256], P(('rows', 'hid')), may hold values from -6 to 6
- w_expand: float32 [256, 16, 256], P('rows', None, 'hid'), may hold values from -0.375 to 0.375
- w_reduce: float32 [16, 256, 256], P(None, 'hid', 'rows'), may hold values from -1.5 to 1.5
- biases: float32 [2, 16, 256], P(None, None, 'hid'), may hold values from -1.8 to 1.8
- w_select: float32 [256, 60], P('rows'), may hold values from -0.1875 to 0.1875
- grad_mix: bfloat16 [32768, 3, 256], P(('rows', 'hid')), may hold values from -6 to 6
- m_expand: float32 [256, 16, 256], P('rows', None, 'hid'), may hold values from -271.529 to 271.529
- v_expand: float32 [256, 16, 256], P('rows', None, 'hid'), may hold values from 2048 to 8192
- m_reduce: float32 [16, 256, 256], P(None, 'hid', 'rows'), may hold values from -70.59754 to 70.59754
- v_reduce: float32 [16, 256, 256], P(None, 'hid', 'rows'), may hold values from 140.8 to 563.2
- m_biases: float32 [2, 16, 256], P(None, None, 'hid'), may hold values from -203.64676 to 203.64676
- v_biases: float32 [2, 16, 256], P(None, None, 'hid'), may hold values from 768 to 3072
- m_select: float32 [256, 60], P('rows'), may hold values from -4344.464 to 4344.464
- v_select: float32 [256, 60], P('rows'), may hold values from 524288 to 2097152
Outputs:
- mixed: bfloat16 [32768, 3, 256], P(('rows', 'hid'))
- grad_features: bfloat16 [32768, 256], P(('rows', 'hid'))
- mean_expand: float32 [256, 16, 256], P('rows', None, 'hid')
- square_expand: float32 [256, 16, 256], P('rows', None, 'hid')
- updated_expand: float32 [256, 16, 256], P('rows', None, 'hid')
- mean_reduce: float32 [16, 256, 256], P(None, 'hid', 'rows')
- square_reduce: float32 [16, 256, 256], P(None, 'hid', 'rows')
- updated_reduce: float32 [16, 256, 256], P(None, 'hid', 'rows')
- mean_biases: float32 [2, 16, 256], P(None, None, 'hid')
- square_biases: float32 [2, 16, 256], P(None, None, 'hid')
- updated_biases: float32 [2, 16, 256], P(None, None, 'hid')
- mean_select: float32 [256, 60], P('rows')
- square_select: float32 [256, 60], P('rows')
- updated_select: float32 [256, 60], P('rows')
All inputs are finite; a program needn't handle non-finite values.
Results may differ from a plain program's by a relative error of at most 0.012.
Values may be sent and summed in bfloat16 or wider, within the bound.
No kernel may reach another device: no remote copies, remote signals or barrier semaphores. Data moves between devices by JAX's collectives and lax.ppermute only.
A program may use at most 256 MiB of HBM per device.

v0:
```python
import jax
import jax.numpy as jnp
from jax import lax
from jax.sharding import PartitionSpec as P

TASKS = 3
SELECT = 4
BITS = 4
STEP = 5


GAMMA = 2.0
RATE = 0.05
DECAY = 0.01
EPSILON = 1e-08
BETA_ONE = 0.5
BETA_TWO = 0.5


def selector_gate(logits_t, tasks, selectors, digits):
    count_rows = logits_t.shape[1]
    cut = tasks * selectors * digits
    zvals = logits_t[:cut].reshape(tasks, selectors, digits, count_rows)
    avals = logits_t[cut:].reshape(tasks, selectors, count_rows)
    clipped = jnp.clip(zvals, -0.5 * GAMMA, 0.5 * GAMMA)
    smooth = clipped * (1.5 / GAMMA - 2.0 / GAMMA**3 * clipped * clipped) + 0.5
    experts_n = 2**digits
    route = jnp.ones((tasks, selectors, experts_n, count_rows), jnp.float32)
    for digit in range(digits):
        code = (jnp.arange(experts_n) // 2**digit % 2).astype(jnp.float32)[:, None]
        chosen = smooth[:, :, digit, None, :]
        route = route * (code * chosen + (1.0 - code) * (1.0 - chosen))
    alpha = jax.nn.softmax(avals, axis=1)
    return jnp.sum(alpha[:, :, None, :] * route, axis=1)


def adamw(weight, grad, first, second):
    first = BETA_ONE * first + (1.0 - BETA_ONE) * grad
    second = BETA_TWO * second + (1.0 - BETA_TWO) * grad * grad
    mhat = first / (1.0 - BETA_ONE**STEP)
    vhat = second / (1.0 - BETA_TWO**STEP)
    weight = weight - RATE * (mhat / (jnp.sqrt(vhat) + EPSILON) + DECAY * weight)
    return (first, second, weight)


def per_device(
    features,
    w_expand,
    w_reduce,
    biases,
    w_select,
    grad_mix,
    m_expand,
    v_expand,
    m_reduce,
    v_reduce,
    m_biases,
    v_biases,
    m_select,
    v_select,
):
    rows_local = features.shape[0]
    tasks = grad_mix.shape[1]
    expand_full, reduce_full, select_full = (
        lax.all_gather(w_expand.astype(jnp.bfloat16), "rows", axis=0, tiled=True),
        lax.all_gather(w_reduce.astype(jnp.bfloat16), "rows", axis=2, tiled=True),
        lax.all_gather(w_select.astype(jnp.bfloat16), "rows", axis=0, tiled=True),
    )
    expand_all, reduce_all = (
        lax.all_gather(expand_full, "hid", axis=2, tiled=True),
        lax.all_gather(reduce_full, "hid", axis=1, tiled=True),
    )
    bias_all = lax.all_gather(biases, "hid", axis=2, tiled=True)
    width, experts_n, hidden_n = expand_all.shape
    expand_flat = expand_all.reshape(width, experts_n * hidden_n)
    reduce_flat = reduce_all.reshape(experts_n * hidden_n, width)
    output_bias = bias_all[1]
    pre = jnp.dot(features, expand_flat, preferred_element_type=jnp.float32) + bias_all[0].reshape(
        -1
    )
    hidden = jax.nn.silu(pre).astype(jnp.bfloat16)
    logits_t = lax.dot_general(
        select_full, features, (((0,), (1,)), ((), ())), preferred_element_type=jnp.float32
    )
    gates, gate_pull = jax.vjp(lambda values: selector_gate(values, TASKS, SELECT, BITS), logits_t)
    gate_rows = jnp.transpose(gates, (2, 0, 1))
    weighted = (
        hidden.reshape(rows_local, 1, experts_n, hidden_n) * gate_rows[:, :, :, None]
    ).astype(jnp.bfloat16)
    weighted = weighted.reshape(rows_local * tasks, experts_n * hidden_n)
    bias_term = jnp.einsum("nte,ed->ntd", gate_rows, output_bias, precision=lax.Precision.HIGHEST)
    mix_local = (
        jnp.dot(weighted, reduce_flat, preferred_element_type=jnp.float32).reshape(
            rows_local, tasks, width
        )
        + bias_term
    )
    mixed = mix_local.astype(jnp.bfloat16)
    cot_flat = grad_mix.reshape(rows_local * tasks, width)
    cot_wide = grad_mix.astype(jnp.float32)
    back = lax.dot_general(
        cot_flat, reduce_flat, (((1,), (1,)), ((), ())), preferred_element_type=jnp.float32
    )
    back = back.reshape(rows_local, tasks, experts_n, hidden_n)
    grad_gates = jnp.sum(hidden.reshape(rows_local, 1, experts_n, hidden_n) * back, axis=3)
    grad_gates = grad_gates + jnp.einsum(
        "ntd,ed->nte", cot_wide, output_bias, precision=lax.Precision.HIGHEST
    )
    grad_hidden = jnp.sum(gate_rows[:, :, :, None] * back, axis=1).reshape(
        rows_local, experts_n * hidden_n
    )
    sigma = jax.nn.sigmoid(pre)
    grad_pre = (grad_hidden * sigma * (1.0 + pre * (1.0 - sigma))).astype(jnp.bfloat16)
    grad_logits = gate_pull(jnp.transpose(grad_gates, (1, 2, 0)))[0].astype(jnp.bfloat16)
    input_part = lax.dot_general(
        grad_pre, expand_flat, (((1,), (1,)), ((), ())), preferred_element_type=jnp.float32
    )
    gate_input = lax.dot_general(
        grad_logits, select_full, (((0,), (1,)), ((), ())), preferred_element_type=jnp.float32
    )
    grad_features = (input_part + gate_input).astype(jnp.bfloat16)
    grad_expand = lax.dot_general(
        features, grad_pre, (((0,), (0,)), ((), ())), preferred_element_type=jnp.float32
    )
    grad_hbias = jnp.sum(grad_pre, axis=0, dtype=jnp.float32)
    grad_reduce = lax.dot_general(
        weighted, cot_flat, (((0,), (0,)), ((), ())), preferred_element_type=jnp.float32
    )
    grad_obias = jnp.einsum("nte,ntd->ed", gate_rows, cot_wide, precision=lax.Precision.HIGHEST)
    grad_select = lax.dot_general(
        features, grad_logits, (((0,), (1,)), ((), ())), preferred_element_type=jnp.float32
    )
    total_expand, total_reduce, total_select = (
        lax.psum_scatter(
            grad_expand.reshape(width, experts_n, hidden_n), "rows", scatter_dimension=0, tiled=True
        ),
        lax.psum_scatter(
            grad_reduce.reshape(experts_n, hidden_n, width), "rows", scatter_dimension=2, tiled=True
        ),
        lax.psum_scatter(grad_select, "rows", scatter_dimension=0, tiled=True),
    )
    total_biases = lax.psum(
        jnp.stack([grad_hbias.reshape(experts_n, hidden_n), grad_obias]), "rows"
    )
    total_expand, total_reduce, total_biases = (
        lax.psum_scatter(total_expand, "hid", scatter_dimension=2, tiled=True),
        lax.psum_scatter(total_reduce, "hid", scatter_dimension=1, tiled=True),
        lax.psum_scatter(total_biases, "hid", scatter_dimension=2, tiled=True),
    )
    total_select = lax.psum(total_select, "hid")
    mean_e, square_e, new_e = adamw(w_expand, total_expand, m_expand, v_expand)
    mean_r, square_r, new_r = adamw(w_reduce, total_reduce, m_reduce, v_reduce)
    mean_b, square_b, new_b = adamw(biases, total_biases, m_biases, v_biases)
    mean_s, square_s, new_s = adamw(w_select, total_select, m_select, v_select)
    return (
        mixed,
        grad_features,
        mean_e,
        square_e,
        new_e,
        mean_r,
        square_r,
        new_r,
        mean_b,
        square_b,
        new_b,
        mean_s,
        square_s,
        new_s,
    )


def solution(mesh):
    return jax.shard_map(
        per_device,
        mesh=mesh,
        in_specs=(
            P(("rows", "hid"), None),
            P("rows", None, "hid"),
            P(None, "hid", "rows"),
            P(None, None, "hid"),
            P("rows", None),
            P(("rows", "hid"), None, None),
            P("rows", None, "hid"),
            P("rows", None, "hid"),
            P(None, "hid", "rows"),
            P(None, "hid", "rows"),
            P(None, None, "hid"),
            P(None, None, "hid"),
            P("rows", None),
            P("rows", None),
        ),
        out_specs=(
            P(("rows", "hid"), None, None),
            P(("rows", "hid"), None),
            P("rows", None, "hid"),
            P("rows", None, "hid"),
            P("rows", None, "hid"),
            P(None, "hid", "rows"),
            P(None, "hid", "rows"),
            P(None, "hid", "rows"),
            P(None, None, "hid"),
            P(None, None, "hid"),
            P(None, None, "hid"),
            P("rows", None),
            P("rows", None),
            P("rows", None),
        ),
        check_vma=False,
    )
```

profile of v0, /device:TPU:0, one launch (start us, length us, event | category | flops | bytes accessed | tf_op | source)
XLA Modules:
  0.0 569.8 jit_solution(521983255542336841)
XLA Ops:
  7.2 1.0 convert_element_type.117
  8.3 34.6 %all_gather.18 = bf16[256,16,64]{2,1,0:T(8,128)(2,1)S(1)} all-gather(bf16[32,16,64]{2,1,0:T(8,128)(2,1)S(1)} %convert_element_type.117), channel_id=1, replica_groups=mesh['rows'=8,'hid'=4] {'rows'}, dimensions={0}, use_global_device_ids=true | all-gather | bytes 589824 | tf_op jit(solution)/shard_map/all_gather | solution.py:65
  42.8 2.2 copy.126
  45.0 1.1 copy.174
  46.2 33.1 %all_gather.22 = bf16[16,64,256]{1,0,2:T(8,128)(2,1)S(1)} all-gather(bf16[16,64,32]{1,0,2:T(8,128)(2,1)S(1)} %copy.174), channel_id=1, replica_groups=mesh['rows'=8,'hid'=4] {'rows'}, dimensions={2}, use_global_device_ids=true | all-gather | bytes 589824 | tf_op jit(solution)/shard_map/all_gather | solution.py:66
  79.3 1.6 copy.135
  81.1 0.7 convert_element_type.121
  81.9 30.5 %all_gather.21 = bf16[256,60]{1,0:T(8,128)(2,1)S(1)} all-gather(bf16[32,60]{1,0:T(8,128)(2,1)S(1)} %convert_element_type.121), channel_id=1, replica_groups=mesh['rows'=8,'hid'=4] {'rows'}, dimensions={0}, use_global_device_ids=true | all-gather | bytes 34560 | tf_op jit(solution)/shard_map/all_gather | solution.py:67
  112.4 0.3 fusion.48
  112.7 0.8 select_select_fusion.1
  113.7 0.8 copy.128
  114.6 5.8 %all_gather.20 = f32[2,16,256]{1,0,2:T(2,128)S(1)} all-gather(f32[2,16,64]{1,0,2:T(2,128)S(1)} %copy.128), channel_id=1, replica_groups=mesh['rows'=8,'hid'=4] {'hid'}, dimensions={2}, use_global_device_ids=true | all-gather | bytes 40960 | tf_op jit(solution)/shard_map/all_gather | solution.py:73
  120.3 0.9 fusion.47
  121.7 0.5 multiply_reduce_fusion.11
  122.3 2.3 copy.127
  124.6 13.3 %fusion = (f32[1024,4096]{1,0:T(8,128)}, f32[1024,4096]{1,0:T(8,128)}) fusion(f32[4096]{0:T(1024)S(1)} %bitcast.118, bf16[1024,256]{1,0:T(8,128)(2,1)S(1)} %copy-done, bf16[256,4096]{0,1:T(8,128)(2,1)S(1)} %bitcast.112), kind=kOutput, calls=%fused_computation.7 | convolution fusion | flops 2176843776 | bytes 36192256 | tf_op jit(solution)/shard_map/dot_general | solution.py:78
  138.1 17.6 %copy.154 = f32[1024,4096]{0,1:T(8,128)} copy(f32[1024,4096]{1,0:T(8,128)} %get-tuple-element.129) | data formatting | bytes 33554432 | tf_op jit(solution)/shard_map/convert_element_type | solution.py:88
  155.7 23.9 %multiply_reduce_fusion = (f32[1024,3,16]{0,2,1:T(8,128)S(1)}, f32[1024,16,256]{0,2,1:T(8,128)}, bf16[1024,3,16,256]{0,3,2,1:T(8,128)(2,1)}) fusion(f32[1024,16,256]{0,2,1:T(8,128)} %bitcast.99, f32[1024,3,16]{0,2,1:T(8,128)S(1)} %bitcast.106, bf16[16,256,256]{2,1,0:T(8,128)(2,1)} %all-gather.5.cloned.1.call-done, bf16[1024,3,256]{2,0,1:T(8,128)(2,1)S(1)} %copy-done.1), kind=kOutput, calls=%fused_computation | convolution fusion | flops 6513704960 | bytes 62783488 | tf_op jit(solution)/shard_map/dot_general | solution.py:101
  179.6 17.5 %copy.155 = f32[1024,4096]{1,0:T(8,128)} copy(f32[1024,4096]{0,1:T(8,128)} %bitcast.103) | data formatting | bytes 33554432 | tf_op jit(solution)/shard_map/reshape | solution.py:109
  197.0 13.5 %convert_reduce_fusion = (f32[4096]{0:T(1024)}, bf16[1024,4096]{1,0:T(8,128)(2,1)S(1)}) fusion(f32[1024,4096]{1,0:T(8,128)} %copy.155, f32[1024,4096]{1,0:T(8,128)} %get-tuple-element.130, f32[4096]{0:T(1024)S(1)} %bitcast.119), kind=kLoop, calls=%fused_computation.3 | loop fusion | flops 50327552 | bytes 41975808 | tf_op jit(solution)/shard_map/reduce_sum | solution.py:125
  210.5 3.2 copy-done.2
  213.7 4.6 fusion.50
  218.4 5.8 %copy.144 = f32[256,16,256]{2,1,0:T(8,128)} copy(f32[256,16,256]{0,2,1:T(8,128)} %bitcast.110) | data formatting | bytes 8388608 | tf_op jit(solution)/shard_map/reshape | solution.py:135
  224.3 2.7 copy.146
  227.0 5.0 reshape.346
  232.0 35.0 %copy.145 = bf16[1024,3,16,256]{3,2,1,0:T(8,128)(2,1)} copy(bf16[1024,3,16,256]{0,3,2,1:T(8,128)(2,1)} %get-tuple-element.115) | data formatting | bytes 50331648 | tf_op jit(solution)/shard_map/convert_element_type | solution.py:89
  267.0 23.6 %copy.168 = bf16[384,8,16,256]{3,1,2,0:T(8,128)(2,1)} copy(bf16[384,8,16,256]{3,2,1,0:T(8,128)(2,1)} %bitcast.101) | data formatting | bytes 50331648
  290.6 29.6 %copy.156 = bf16[4096,3072]{1,0:T(8,128)(2,1)} copy(bf16[4096,3072]{0,1:T(8,128)(2,1)} %bitcast.102) | data formatting | bytes 50331648 | tf_op jit(solution)/shard_map/dot_general | solution.py:126
  320.2 13.5 %fusion.7 = f32[16,256,256]{1,2,0:T(8,128)} fusion(bf16[16,256,3072]{2,1,0:T(8,128)(2,1)} %bitcast.104, bf16[3072,256]{1,0:T(8,128)(2,1)} %reshape.346), kind=kOutput, calls=%fused_computation.15 | convolution fusion | flops 6442450944 | bytes 30932992 | tf_op jit(solution)/shard_map/dot_general | solution.py:126
  333.9 0.7 sub.123
  334.6 0.7 multiply_divide_fusion
  335.4 0.7 convolution_bitcast_fusion.1
  336.1 1.3 fusion.10
  337.5 3.3 multiply_reduce_fusion.3
  340.9 0.5 fusion.27
  341.5 0.8 multiply_reduce_fusion.12
  342.4 0.7 divide_add_fusion
  343.1 0.7 stack_reshape.3
  344.0 0.8 reshape.360
  344.9 0.9 exponential_multiply_fusion
  346.0 0.8 copy.162
  346.9 5.3 copy.158
  352.2 5.1 reshape.354
  357.5 12.8 %fusion.4 = f32[1024,3,256,1]{2,0,3,1:T(8,128)} fusion(bf16[16,256,256]{2,1,0:T(8,128)(2,1)} %all-gather.5.cloned.1.call-done, f32[1024,3,16]{0,2,1:T(8,128)S(1)} %bitcast.107, f32[1024,16,256]{0,2,1:T(8,128)} %bitcast.100), kind=kOutput, calls=%fused_computation.12 | convolution fusion | flops 6467616768 | bytes 22216704 | tf_op jit(solution)/shard_map/dot_general | solution.py:93
  370.4 5.9 %fusion.49 = f32[1024,256]{1,0:T(8,128)S(1)} fusion(bf16[1024,4096]{1,0:T(8,128)(2,1)} %copy-done.2, bf16[256,4096]{0,1:T(8,128)(2,1)S(1)} %bitcast.113), kind=kOutput, calls=%fused_computation.133 | convolution fusion | flops 2147483648 | bytes 11534336 | tf_op jit(solution)/shard_map/dot_general | solution.py:115
  376.4 47.2 %reduce-scatter.17.cloned.1.call-done = f32[16,256,32]{1,2,0:T(8,128)} async-done(((f32[16,256,256]{1,2,0:T(8,128)}), f32[16,256,32]{1,2,0:T(8,128)}) %reduce-scatter.17.cloned.1.call-update) | async-done | bytes 524304 | tf_op jit(solution)/shard_map/reduce_scatter | solution.py:137
  423.6 3.5 copy.160
  427.1 2.9 reshape.356
  430.1 1.1 fusion.9
  431.2 5.2 fusion.1
  436.4 9.4 %reduce-scatter.25.cloned.1.call-done = f32[64,32]{1,0:T(8,128)} async-done(((f32[256,32]{1,0:T(8,128)}), f32[64,32]{1,0:T(8,128)}) %reduce-scatter.25.cloned.1.call-update) | async-done | bytes 8208
  445.8 0.9 reshape.361
  446.8 37.1 %psum.16 = f32[2,16,64]{2,1,0:T(8,128)S(1)} all-reduce(f32[2,16,64]{2,1,0:T(8,128)S(1)} %copy.165), channel_id=1, replica_groups=mesh['rows'=8,'hid'=4] {'rows'}, use_global_device_ids=true, to_apply=%region_20.21 | all-reduce | flops 2048 | bytes 16384 | tf_op jit(solution)/shard_map/psum | solution.py:142
  483.8 0.6 multiply_subtract_fusion.3
  484.5 26.4 %reduce-scatter.23.cloned.1.call-done = f32[32,60]{1,0:T(8,128)} async-done(((f32[256,60]{1,0:T(8,128)}), f32[32,60]{1,0:T(8,128)}) %reduce-scatter.23.cloned.1.call-update) | async-done | bytes 7696 | tf_op jit(solution)/shard_map/reduce_scatter | solution.py:140
  510.8 10.6 %psum.15 = f32[32,60]{1,0:T(8,128)S(1)} all-reduce(f32[32,60]{1,0:T(8,128)} %reduce-scatter.23.cloned.1.call-done), channel_id=1, replica_groups=mesh['rows'=8,'hid'=4] {'hid'}, use_global_device_ids=true, to_apply=%region_23.24 | all-reduce | flops 1920 | bytes 15360 | tf_op jit(solution)/shard_map/psum | solution.py:150
  521.5 0.6 multiply_subtract_fusion.2
  522.1 12.0 %reduce-scatter.19.cloned.1.call-done = f32[64,512]{1,0:T(8,128)} async-done(((f32[256,512]{1,0:T(8,128)}), f32[64,512]{1,0:T(8,128)}) %reduce-scatter.19.cloned.1.call-update) | async-done | bytes 131088
  534.2 1.3 reshape.355
  535.4 0.6 copy.159
  536.0 22.3 %reduce-scatter.21.cloned.1.call-done = f32[64,512]{1,0:T(8,128)} async-done(((f32[256,512]{1,0:T(8,128)}), f32[64,512]{1,0:T(8,128)}) %reduce-scatter.21.cloned.1.call-update) | async-done | bytes 131088
  558.4 1.1 reshape.357
  559.7 1.0 multiply_subtract_fusion.1
  560.7 2.0 multiply_subtract_fusion
  (140 shorter events, 2.6 us)
Async XLA Ops:
  7.2 105.2 %copy-start = (bf16[1024,256]{1,0:T(8,128)(2,1)S(1)}, bf16[1024,256]{1,0:T(8,128)(2,1)}, u32[]{:S(2)}) copy-start(bf16[1024,256]{1,0:T(8,128)(2,1)} %param.14) | copy-start | bytes 1572868
  7.2 115.1 %all-gather.3.cloned.1.call-start = ((), (), s32[]{:S(2)}) async-start(), calls=%async_computation.6 | async-start | bytes 2621440 | tf_op jit(solution)/shard_map/all_gather | solution.py:70
  45.0 110.7 %all-gather.5.cloned.1.call-start = ((), (), s32[]{:S(2)}) async-start(), calls=%async_computation.7 | async-start | bytes 2621440 | tf_op jit(solution)/shard_map/all_gather | solution.py:71
  81.0 265.9 %reduce-scatter.15.cloned.1.call-start = ((), (), s32[]{:S(2)}) async-start(), calls=%async_computation.8 | async-start | bytes 4718592 | tf_op jit(solution)/shard_map/reduce_scatter | solution.py:134
  81.0 56.9 %copy-start.38 = (f32[16]{0:T(128)}, f32[16]{0:T(128)S(1)}, u32[]{:S(2)}) copy-start(f32[16]{0:T(128)S(1)} %get-tuple-element.135) | copy-start | bytes 196
  81.0 56.9 %copy-start.39 = (f32[16]{0:T(128)}, f32[16]{0:T(128)S(1)}, u32[]{:S(2)}) copy-start(f32[16]{0:T(128)S(1)} %get-tuple-element.136) | copy-start | bytes 196
  81.1 56.9 %copy-start.40 = (f32[16]{0:T(128)}, f32[16]{0:T(128)S(1)}, u32[]{:S(2)}) copy-start(f32[16]{0:T(128)S(1)} %get-tuple-element.133) | copy-start | bytes 196
  81.1 56.9 %copy-start.41 = (f32[16]{0:T(128)}, f32[16]{0:T(128)S(1)}, u32[]{:S(2)}) copy-start(f32[16]{0:T(128)S(1)} %get-tuple-element.134) | copy-start | bytes 196
  81.1 56.8 %copy-start.42 = (f32[16]{0:T(128)}, f32[16]{0:T(128)S(1)}, u32[]{:S(2)}) copy-start(f32[16]{0:T(128)S(1)} %get-tuple-element.137) | copy-start | bytes 196
  81.1 56.8 %copy-start.43 = (f32[16]{0:T(128)}, f32[16]{0:T(128)S(1)}, u32[]{:S(2)}) copy-start(f32[16]{0:T(128)S(1)} %get-tuple-element.138) | copy-start | bytes 196
  81.1 56.8 %copy-start.44 = (f32[16]{0:T(128)}, f32[16]{0:T(128)S(1)}, u32[]{:S(2)}) copy-start(f32[16]{0:T(128)S(1)} %get-tuple-element.131) | copy-start | bytes 196
  81.1 56.8 %copy-start.45 = (f32[16]{0:T(128)}, f32[16]{0:T(128)S(1)}, u32[]{:S(2)}) copy-start(f32[16]{0:T(128)S(1)} %get-tuple-element.132) | copy-start | bytes 196
  112.4 1.1 copy-start.15
  112.6 0.9 copy-start.7
  113.6 24.4 %copy-start.5 = (f32[3,4,4,1024]{3,2,1,0:T(4,128)}, f32[3,4,4,1024]{3,2,1,0:T(4,128)S(1)}, u32[]{:S(2)}) copy-start(f32[3,4,4,1024]{3,2,1,0:T(4,128)S(1)} %min.12) | copy-start | bytes 589828
  113.6 24.4 %copy-start.8 = (f32[3,4,1024]{2,1,0:T(4,128)}, f32[3,4,1024]{2,1,0:T(4,128)S(1)}, u32[]{:S(2)}) copy-start(f32[3,4,1024]{2,1,0:T(4,128)S(1)} %reshape.342) | copy-start | bytes 147460
  113.7 7.7 %copy-start.28 = (f32[3,1024]{1,0:T(4,128)}, f32[3,1024]{1,0:T(4,128)S(1)}, u32[]{:S(2)}) copy-start(f32[3,1024]{1,0:T(4,128)S(1)} %reduce_max.9) | copy-start | bytes 36868
  113.7 7.6 %copy-start.31 = (f32[3,1024]{1,0:T(4,128)}, f32[3,1024]{1,0:T(4,128)S(1)}, u32[]{:S(2)}) copy-start(f32[3,1024]{1,0:T(4,128)S(1)} %fusion.29) | copy-start | bytes 36868
  121.3 16.7 %copy-start.27 = (f32[3,4,1024]{2,1,0:T(4,128)}, f32[3,4,1024]{2,1,0:T(4,128)S(1)}, u32[]{:S(2)}) copy-start(f32[3,4,1024]{2,1,0:T(4,128)S(1)} %fusion.28) | copy-start | bytes 147460
  121.6 16.4 %copy-start.17 = (f32[3,4,1024]{2,1,0:T(4,128)}, f32[3,4,1024]{2,1,0:T(4,128)S(1)}, u32[]{:S(2)}) copy-start(f32[3,4,1024]{2,1,0:T(4,128)S(1)} %get-tuple-element.121) | copy-start | bytes 147460
  121.6 16.4 %copy-start.19 = (f32[3,4,1024]{2,1,0:T(4,128)}, f32[3,4,1024]{2,1,0:T(4,128)S(1)}, u32[]{:S(2)}) copy-start(f32[3,4,1024]{2,1,0:T(4,128)S(1)} %get-tuple-element.122) | copy-start | bytes 147460
  121.7 16.4 %copy-start.21 = (f32[3,4,1024]{2,1,0:T(4,128)}, f32[3,4,1024]{2,1,0:T(4,128)S(1)}, u32[]{:S(2)}) copy-start(f32[3,4,1024]{2,1,0:T(4,128)S(1)} %get-tuple-element.123) | copy-start | bytes 147460
  121.7 16.4 %copy-start.22 = (f32[3,4,1024]{2,1,0:T(4,128)}, f32[3,4,1024]{2,1,0:T(4,128)S(1)}, u32[]{:S(2)}) copy-start(f32[3,4,1024]{2,1,0:T(4,128)S(1)} %get-tuple-element.124) | copy-start | bytes 147460
  121.7 16.4 %copy-start.23 = (f32[3,4,1024]{2,1,0:T(4,128)}, f32[3,4,1024]{2,1,0:T(4,128)S(1)}, u32[]{:S(2)}) copy-start(f32[3,4,1024]{2,1,0:T(4,128)S(1)} %get-tuple-element.125) | copy-start | bytes 147460
  121.7 16.4 %copy-start.24 = (f32[3,4,1024]{2,1,0:T(4,128)}, f32[3,4,1024]{2,1,0:T(4,128)S(1)}, u32[]{:S(2)}) copy-start(f32[3,4,1024]{2,1,0:T(4,128)S(1)} %get-tuple-element.126) | copy-start | bytes 147460
  121.7 16.4 %copy-start.25 = (f32[3,4,1024]{2,1,0:T(4,128)}, f32[3,4,1024]{2,1,0:T(4,128)S(1)}, u32[]{:S(2)}) copy-start(f32[3,4,1024]{2,1,0:T(4,128)S(1)} %get-tuple-element.127) | copy-start | bytes 147460
  121.7 16.4 %copy-start.26 = (f32[3,4,1024]{2,1,0:T(4,128)}, f32[3,4,1024]{2,1,0:T(4,128)S(1)}, u32[]{:S(2)}) copy-start(f32[3,4,1024]{2,1,0:T(4,128)S(1)} %get-tuple-element.128) | copy-start | bytes 147460
  124.6 13.5 %copy-start.3 = (bf16[256,16,256]{0,2,1:T(8,128)(2,1)}, bf16[256,16,256]{0,2,1:T(8,128)(2,1)S(1)}, u32[]{:S(2)}) copy-start(bf16[256,16,256]{0,2,1:T(8,128)(2,1)S(1)} %copy.127) | copy-start | bytes 6291460
  138.1 17.6 %copy-start.1 = (bf16[1024,3,256]{2,0,1:T(8,128)(2,1)S(1)}, bf16[1024,3,256]{2,0,1:T(8,128)(2,1)}, u32[]{:S(2)}) copy-start(bf16[1024,3,256]{2,0,1:T(8,128)(2,1)} %param.19) | copy-start | bytes 4718596
  210.5 3.2 copy-start.2
  224.2 199.4 %reduce-scatter.17.cloned.1.call-start = ((), (), s32[]{:S(2)}) async-start(), calls=%async_computation.9 | async-start | bytes 4718592 | tf_op jit(solution)/shard_map/reduce_scatter | solution.py:137
  320.1 13.6 %copy-start.14 = (f32[48,1024]{1,0:T(8,128)S(1)}, f32[48,1024]{1,0:T(8,128)}, u32[]{:S(2)}) copy-start(f32[48,1024]{1,0:T(8,128)} %get-tuple-element.117) | copy-start | bytes 589828
  320.1 13.6 %copy-start.13 = (f32[48,1024]{1,0:T(8,128)S(1)}, f32[48,1024]{1,0:T(8,128)}, u32[]{:S(2)}) copy-start(f32[48,1024]{1,0:T(8,128)} %get-tuple-element.116) | copy-start | bytes 589828
  320.1 15.9 %copy-start.10 = (f32[1,16,256]{1,0,2:T(1,128)S(1)}, f32[1,16,256]{1,0,2:T(1,128)}, u32[]{:S(2)}) copy-start(f32[1,16,256]{1,0,2:T(1,128)} %get-tuple-element.119) | copy-start | bytes 49156
  320.2 17.3 %copy-start.18 = (f32[3,4,1024]{2,1,0:T(4,128)S(1)}, f32[3,4,1024]{2,1,0:T(4,128)}, u32[]{:S(2)}) copy-start(f32[3,4,1024]{2,1,0:T(4,128)} %copy-done.17) | copy-start | bytes 147460
  320.2 17.3 %copy-start.20 = (f32[3,4,1024]{2,1,0:T(4,128)S(1)}, f32[3,4,1024]{2,1,0:T(4,128)}, u32[]{:S(2)}) copy-start(f32[3,4,1024]{2,1,0:T(4,128)} %copy-done.19) | copy-start | bytes 147460
  320.2 20.7 %copy-start.6 = (f32[3,4,4,1024]{3,2,1,0:T(4,128)S(1)}, f32[3,4,4,1024]{3,2,1,0:T(4,128)}, u32[]{:S(2)}) copy-start(f32[3,4,4,1024]{3,2,1,0:T(4,128)} %copy-done.5) | copy-start | bytes 589828
  320.2 21.4 %copy-start.9 = (f32[3,4,1024]{2,1,0:T(4,128)S(1)}, f32[3,4,1024]{2,1,0:T(4,128)}, u32[]{:S(2)}) copy-start(f32[3,4,1024]{2,1,0:T(4,128)} %copy-done.8) | copy-start | bytes 147460
  333.7 112.2 %reduce-scatter.25.cloned.1.call-start = ((), (), s32[]{:S(2)}) async-start(), calls=%async_computation.13 | async-start | bytes 163840
  345.7 165.1 %reduce-scatter.23.cloned.1.call-start = ((), (), s32[]{:S(2)}) async-start(), calls=%async_computation.12 | async-start | bytes 147456 | tf_op jit(solution)/shard_map/reduce_scatter | solution.py:140
  346.8 187.4 %reduce-scatter.19.cloned.1.call-start = ((), (), s32[]{:S(2)}) async-start(), calls=%async_computation.10 | async-start | bytes 655360
  357.3 201.1 %reduce-scatter.21.cloned.1.call-start = ((), (), s32[]{:S(2)}) async-start(), calls=%async_computation.11 | async-start | bytes 655360
  357.5 12.8 %copy-start.4 = (bf16[256,16,256]{0,2,1:T(8,128)(2,1)S(1)}, bf16[256,16,256]{0,2,1:T(8,128)(2,1)}, u32[]{:S(2)}) copy-start(bf16[256,16,256]{0,2,1:T(8,128)(2,1)} %copy-done.3) | copy-start | bytes 6291460
  370.3 59.8 %copy-start.16 = (bf16[256,60]{1,0:T(8,128)(2,1)S(1)}, bf16[256,60]{1,0:T(8,128)(2,1)}, u32[]{:S(2)}) copy-start(bf16[256,60]{1,0:T(8,128)(2,1)} %copy-done.15) | copy-start | bytes 92164
  370.3 113.5 %copy-start.32 = (f32[2,16,64]{2,1,0:T(8,128)S(1)}, f32[2,16,64]{2,1,0:T(8,128)}, u32[]{:S(2)}) copy-start(f32[2,16,64]{2,1,0:T(8,128)} %param.17) | copy-start | bytes 24580
  370.3 113.5 %copy-start.34 = (f32[2,16,64]{2,1,0:T(8,128)S(1)}, f32[2,16,64]{2,1,0:T(8,128)}, u32[]{:S(2)}) copy-start(f32[2,16,64]{2,1,0:T(8,128)} %param.25) | copy-start | bytes 24580
  370.3 113.5 %copy-start.35 = (f32[2,16,64]{2,1,0:T(8,128)S(1)}, f32[2,16,64]{2,1,0:T(8,128)}, u32[]{:S(2)}) copy-start(f32[2,16,64]{2,1,0:T(8,128)} %param.24) | copy-start | bytes 24580
  370.4 151.1 %copy-start.33 = (f32[32,60]{1,0:T(8,128)S(1)}, f32[32,60]{1,0:T(8,128)}, u32[]{:S(2)}) copy-start(f32[32,60]{1,0:T(8,128)} %param.18) | copy-start | bytes 23044
  370.4 151.1 %copy-start.36 = (f32[32,60]{1,0:T(8,128)S(1)}, f32[32,60]{1,0:T(8,128)}, u32[]{:S(2)}) copy-start(f32[32,60]{1,0:T(8,128)} %param.27) | copy-start | bytes 23044
  370.4 151.1 %copy-start.37 = (f32[32,60]{1,0:T(8,128)S(1)}, f32[32,60]{1,0:T(8,128)}, u32[]{:S(2)}) copy-start(f32[32,60]{1,0:T(8,128)} %param.26) | copy-start | bytes 23044
  370.4 189.3 %copy-start.11 = (f32[32,16,64]{2,1,0:T(8,128)S(1)}, f32[32,16,64]{2,1,0:T(8,128)}, u32[]{:S(2)}) copy-start(f32[32,16,64]{2,1,0:T(8,128)} %param.15) | copy-start | bytes 393220
  370.4 189.3 %copy-start.29 = (f32[32,16,64]{2,1,0:T(8,128)S(1)}, f32[32,16,64]{2,1,0:T(8,128)}, u32[]{:S(2)}) copy-start(f32[32,16,64]{2,1,0:T(8,128)} %param.21) | copy-start | bytes 393220
  370.4 189.3 %copy-start.30 = (f32[32,16,64]{2,1,0:T(8,128)S(1)}, f32[32,16,64]{2,1,0:T(8,128)}, u32[]{:S(2)}) copy-start(f32[32,16,64]{2,1,0:T(8,128)} %param.20) | copy-start | bytes 393220
  370.4 190.3 %copy-start.12 = (f32[16,64,32]{1,2,0:T(8,128)S(1)}, f32[16,64,32]{1,2,0:T(8,128)}, u32[]{:S(2)}) copy-start(f32[16,64,32]{1,2,0:T(8,128)} %param.16) | copy-start | bytes 393220
Sparse Core Ops, SparseCore 0:
  45.1 23.4 all-gather.2
  81.1 23.9 all-gather.4
  224.3 89.4 reduce-scatter.14
  333.8 89.7 reduce-scatter.16
  426.5 19.3 reduce-scatter.24
  449.9 60.8 reduce-scatter.22
  513.5 20.6 reduce-scatter.18
  536.7 21.6 reduce-scatter.20
where the time goes:
time: 578 us; the launch traced here: 570 us
  local copies, waits for them, and re-layouts  174 us (30%)
  blocking collectives  152 us (26%)
  waiting for transfers between devices  118 us (20%)
  matrix products  82.8 us (14%)
  other arithmetic  28.2 us (5%)
  between operations  15.2 us (3%)
    unnamed x110, local copies, waits for them, and re-layouts  54.4 us
    reduce_scatter x1, waiting for transfers between devices, per_device(): lax.psum_scatter(grad_reduce.reshape(experts_n, hidden_n, width), 'rows',...  47.2 us
    unnamed x11, waiting for transfers between devices  43.9 us
    psum x1, blocking collectives, per_device(): lax.psum(jnp.stack([grad_hbias.reshape(experts_n, hidden_n), grad_obias])...  37.1 us
    convert_element_type x1, local copies, waits for them, and re-layouts, per_device(): weighted = (hidden.reshape(rows_local, 1, experts_n, hidden_n) * gate_row...  35 us
    all_gather x1, blocking collectives, per_device(): lax.all_gather(w_expand.astype(jnp.bfloat16), 'rows', axis=0, tiled=True)  34.6 us
    all_gather x1, blocking collectives, per_device(): lax.all_gather(w_reduce.astype(jnp.bfloat16), 'rows', axis=2, tiled=True)  33.1 us
    all_gather x1, blocking collectives, per_device(): lax.all_gather(w_select.astype(jnp.bfloat16), 'rows', axis=0, tiled=True)  30.5 us
  transfers between devices with their start and end apart: 8, of which 5 were waited for; matrix products, arithmetic and copies ran while one was open for 37% of the time, Pallas kernels for 0%

commit v1 on v0

v1 whole, which is shorter than its diff:
```python
import functools

import jax
import jax.numpy as jnp
import numpy as np
from jax import lax
from jax.experimental import pallas as pl
from jax.experimental.pallas import tpu as pltpu
from jax.sharding import PartitionSpec as P

TASKS = 3
SELECT = 4
BITS = 4
STEP = 5
GAMMA = 2.0
RATE = 0.05
DECAY = 0.01
EPSILON = 1e-08
BETA_ONE = 0.5
BETA_TWO = 0.5

BF = jnp.bfloat16
F32 = jnp.float32
HIGHEST = lax.Precision.HIGHEST
TPAD = 8
GROUPS = BITS * SELECT + SELECT
GROWS = GROUPS * TPAD
ONES = 16
TILE = 512
MIB = 1 << 20


def dot(a, b, ca, cb, precision=None):
    return lax.dot_general(
        a, b, (((ca,), (cb,)), ((), ())), preferred_element_type=F32, precision=precision
    )


def params(mib):
    return pltpu.CompilerParams(
        vmem_limit_bytes=mib * MIB, dimension_semantics=("arbitrary",)
    )


VMEM = functools.partial(pl.BlockSpec, memory_space=pltpu.VMEM)


def gate_parts(z_of, a_of, high):
    smooth, clipped = {}, {}
    for k in range(SELECT):
        for b in range(BITS):
            v = jnp.clip(z_of(b, k), -0.5 * GAMMA, 0.5 * GAMMA)
            clipped[b, k] = v
            smooth[b, k] = v * (1.5 / GAMMA - 2.0 / GAMMA**3 * v * v) + 0.5
    a = [a_of(k) for k in range(SELECT)]
    top = functools.reduce(jnp.maximum, a)
    ex = [jnp.exp(v - top) for v in a]
    inv = 1.0 / functools.reduce(jnp.add, ex)
    alpha = [v * inv for v in ex]
    last = BITS - 1
    f_high = [
        high * smooth[last, k] + (1.0 - high) * (1.0 - smooth[last, k]) for k in range(SELECT)
    ]
    return alpha, smooth, clipped, f_high


def fac(smooth, b, k, bit):
    return smooth[b, k] if bit else 1.0 - smooth[b, k]


def prep_kernel(core, perm, order, sel, xo, xr, go, gr, xt, gt, cc, gates, logits, selp, gb1):
    i = pl.program_id(0)
    half = pl.num_programs(0) // 2
    own = i < half
    high = core[0].astype(F32)

    @pl.when(i == 0)
    def _():
        selp[...] = dot(order[...], sel[...], 1, 1).astype(BF)
        gb1[...] = jnp.zeros_like(gb1)

    x = jnp.where(own, xo[...], xr[...])
    x_t = dot(perm[...], x, 1, 1).astype(BF)
    width = x_t.shape[0]
    xt[0:width, :] = x_t
    xt[width : width + ONES, :] = jnp.ones((ONES, x_t.shape[1]), BF)
    lg = dot(selp[...], x_t, 1, 0)
    logits[...] = lg

    def z_of(b, k):
        at = (b * SELECT + k) * TPAD
        return lg[at : at + TPAD]

    def a_of(k):
        at = (BITS * SELECT + k) * TPAD
        return lg[at : at + TPAD]

    alpha, smooth, _, f_high = gate_parts(z_of, a_of, high)
    gate = [None] * 8
    for k in range(SELECT):
        base = alpha[k] * f_high[k]
        for e2 in range(2):
            w2 = base * fac(smooth, 2, k, e2)
            for e1 in range(2):
                w1 = w2 * fac(smooth, 1, k, e1)
                for e0 in range(2):
                    e = 4 * e2 + 2 * e1 + e0
                    w0 = w1 * fac(smooth, 0, k, e0)
                    gate[e] = w0 if gate[e] is None else gate[e] + w0
    g_t = []
    for t in range(TASKS):
        g = jnp.where(own, go[t], gr[t])
        g = dot(perm[...], g, 1, 1)
        gt[t] = g.astype(BF)
        g_t.append(g)
    ones = jnp.ones((8, x_t.shape[1]), BF)
    for e in range(8):
        gates[e] = gate[e]
        c = gate[e][0:1] * g_t[0]
        for t in range(1, TASKS):
            c = c + gate[e][t : t + 1] * g_t[t]
        c = c.astype(BF)
        cc[e] = c
        gb1[e] += dot(ones, c, 1, 1)


def prep(core, perm, order, sel, x_own, x_recv, g_own, g_recv):
    rows, width = x_own.shape
    total = 2 * rows
    steps = total // TILE
    half = steps // 2
    lo = lambda i: jnp.minimum(i, half - 1)
    hi = lambda i: jnp.maximum(i - half, 0)
    whole = lambda shape: VMEM(shape, lambda i: (0,) * len(shape))
    return pl.pallas_call(
        prep_kernel,
        grid=(steps,),
        out_shape=(
            jax.ShapeDtypeStruct((width + ONES, total), BF),
            jax.ShapeDtypeStruct((TASKS, width, total), BF),
            jax.ShapeDtypeStruct((8, width, total), BF),
            jax.ShapeDtypeStruct((8, TPAD, total), F32),
            jax.ShapeDtypeStruct((GROWS, total), F32),
            jax.ShapeDtypeStruct((GROWS, width), BF),
            jax.ShapeDtypeStruct((8, 8, width), F32),
        ),
        in_specs=[
            pl.BlockSpec(memory_space=pltpu.SMEM),
            whole(perm.shape),
            whole(order.shape),
            whole(sel.shape),
            VMEM((TILE, width), lambda i: (lo(i), 0)),
            VMEM((TILE, width), lambda i: (hi(i), 0)),
            VMEM((TASKS, TILE, width), lambda i: (0, lo(i), 0)),
            VMEM((TASKS, TILE, width), lambda i: (0, hi(i), 0)),
        ],
        out_specs=(
            VMEM((width + ONES, TILE), lambda i: (0, i)),
            VMEM((TASKS, width, TILE), lambda i: (0, 0, i)),
            VMEM((8, width, TILE), lambda i: (0, 0, i)),
            VMEM((8, TPAD, TILE), lambda i: (0, 0, i)),
            VMEM((GROWS, TILE), lambda i: (0, i)),
            whole((GROWS, width)),
            whole((8, 8, width)),
        ),
        compiler_params=params(48),
        cost_estimate=pl.CostEstimate(
            flops=2 * total * width * width * 5, bytes_accessed=18 * MIB, transcendentals=0
        ),
    )(core, perm, order, sel, x_own, x_recv, g_own, g_recv)


def critical_kernel(
    table, w_lo, w_hi, xt, cc, b0, g_lo, g_hi, hid, gp, wun, gb0, wbuf, gbuf
):
    e = pl.program_id(0)
    last = pl.num_programs(0) - 1
    blocks, _, _, depth, lanes = w_lo.shape
    width = depth * blocks
    total = xt.shape[1]

    @pl.when(e == 0)
    def _():
        wbuf[0:blocks] = w_lo[...]
        wbuf[blocks : 2 * blocks] = w_hi[...]

    for q in range(blocks):
        for side in range(2):
            at = table[2 * q + side]
            for which in range(2):
                wun[0, which, q * depth : (q + 1) * depth, side * lanes : (side + 1) * lanes] = (
                    wbuf[at, which, e]
                )
    e_t = (wun[0, 0] * 0.5).T
    r = (wun[0, 1] * 0.5).T
    bias = jnp.concatenate([b0[0]] * (TILE // b0.shape[2]), axis=1)
    for i in range(total // TILE):
        part = slice(i * TILE, (i + 1) * TILE)
        u = dot(e_t, xt[0:width, part], 1, 0) + bias
        t = jnp.tanh(u)
        plus = 1.0 + t
        h = u * plus
        hid[0, :, part] = h.astype(BF)
        gh = dot(r, cc[0, :, part], 1, 0)
        gp[0, :, part] = (gh * (plus + h * (1.0 - t))).astype(BF)
    g_e = dot(xt[...], gp[0], 1, 1)
    g_r = dot(cc[0], hid[0], 1, 1)
    gb0[0] = g_e[width : width + 8]
    for q in range(blocks):
        for side in range(2):
            at = table[2 * q + side]
            rows, cols = slice(q * depth, (q + 1) * depth), slice(side * lanes, (side + 1) * lanes)
            gbuf[at, 0, e] = g_e[rows, cols].astype(BF)
            gbuf[at, 1, e] = g_r[rows, cols].astype(BF)

    @pl.when(e == last)
    def _():
        g_lo[...] = gbuf[0:blocks]
        g_hi[...] = gbuf[blocks : 2 * blocks]


def critical(table, w_lo, w_hi, xt, cc, b0, first):
    blocks, _, chunk, depth, lanes = w_lo.shape
    width, total = blocks * depth, xt.shape[1]
    hidden = 2 * lanes
    whole = lambda shape: VMEM(shape, lambda e: (0,) * len(shape))
    per = lambda *shape: VMEM((1, *shape), lambda e: (e,) + (0,) * len(shape))
    at = lambda *shape: VMEM((1, *shape), lambda e: (e + first,) + (0,) * len(shape))
    return pl.pallas_call(
        critical_kernel,
        grid=(chunk,),
        out_shape=(
            jax.ShapeDtypeStruct(w_lo.shape, BF),
            jax.ShapeDtypeStruct(w_lo.shape, BF),
            jax.ShapeDtypeStruct((chunk, hidden, total), BF),
            jax.ShapeDtypeStruct((chunk, hidden, total), BF),
            jax.ShapeDtypeStruct((chunk, 2, width, hidden), BF),
            jax.ShapeDtypeStruct((chunk, 8, hidden), F32),
        ),
        in_specs=[
            pl.BlockSpec(memory_space=pltpu.SMEM),
            whole(w_lo.shape),
            whole(w_hi.shape),
            whole(xt.shape),
            at(width, total),
            at(hidden, b0.shape[2]),
        ],
        out_specs=(
            whole(w_lo.shape),
            whole(w_lo.shape),
            per(hidden, total),
            per(hidden, total),
            per(2, width, hidden),
            per(8, hidden),
        ),
        scratch_shapes=[
            pltpu.VMEM((2 * blocks, 2, chunk, depth, lanes), BF),
            pltpu.VMEM((2 * blocks, 2, chunk, depth, lanes), BF),
        ],
        compiler_params=params(48),
        cost_estimate=pl.CostEstimate(
            flops=8 * chunk * total * width * hidden,
            bytes_accessed=chunk * 4 * MIB,
            transcendentals=chunk * total * hidden,
        ),
    )(table, w_lo, w_hi, xt, cc, b0)


def rest_kernel(
    wun, hid, gp, gt, gates, b1, mix_in, gx_in, mix_own, mix_other, gx, gg, mix_acc, gx_acc, *, first
):
    e = pl.program_id(0)
    last = pl.num_programs(0) - 1
    width, total = gx_acc.shape
    rows = total // 2

    @pl.when(e == 0)
    def _():
        if first:
            mix_acc[...] = jnp.zeros_like(mix_acc)
            gx_acc[...] = jnp.zeros_like(gx_acc)
        else:
            mix_acc[...] = mix_in[...]
            gx_acc[...] = gx_in[...]

    gg[...] = jnp.zeros_like(gg)
    bias = jnp.concatenate([b1[0]] * (TILE // b1.shape[2]), axis=1)
    for i in range(total // TILE):
        part = slice(i * TILE, (i + 1) * TILE)
        y = dot(wun[0, 1], hid[0, :, part], 1, 0) + bias
        gx_acc[:, part] += dot(wun[0, 0], gp[0, :, part], 1, 0)
        for t in range(TASKS):
            mix_acc[t, :, part] += gates[0, t : t + 1, part] * y
            gg[0, t : t + 1, part] = jnp.sum(
                gt[t, :, part].astype(F32) * y, axis=0, keepdims=True
            )

    @pl.when(e == last)
    def _():
        mix_own[...] = mix_acc[:, :, 0:rows].astype(mix_own.dtype)
        mix_other[...] = mix_acc[:, :, rows:total].astype(mix_other.dtype)
        gx[...] = gx_acc[...]


def rest(wun, hid, gp, gt, gates, b1):
    count, _, width, hidden = wun.shape
    total = gt.shape[2]
    whole = lambda shape: VMEM(shape, lambda e: (0,) * len(shape))
    per = lambda *shape: VMEM((1, *shape), lambda e: (e,) + (0,) * len(shape))
    none = jnp.zeros((8, 128), F32)
    return pl.pallas_call(
        functools.partial(rest_kernel, first=True),
        grid=(count,),
        out_shape=(
            jax.ShapeDtypeStruct((TASKS, width, total // 2), BF),
            jax.ShapeDtypeStruct((TASKS, width, total // 2), BF),
            jax.ShapeDtypeStruct((width, total), F32),
            jax.ShapeDtypeStruct((count, TPAD, total), F32),
        ),
        in_specs=[
            per(2, width, hidden),
            per(hidden, total),
            per(hidden, total),
            whole(gt.shape),
            per(TPAD, total),
            per(width, b1.shape[2]),
            whole(none.shape),
            whole(none.shape),
        ],
        out_specs=(
            whole((TASKS, width, total // 2)),
            whole((TASKS, width, total // 2)),
            whole((width, total)),
            per(TPAD, total),
        ),
        scratch_shapes=[
            pltpu.VMEM((TASKS, width, total), F32),
            pltpu.VMEM((width, total), F32),
        ],
        compiler_params=params(56),
        cost_estimate=pl.CostEstimate(
            flops=4 * count * total * width * hidden,
            bytes_accessed=count * 3 * MIB,
            transcendentals=0,
        ),
    )(wun, hid, gp, gt, gates, b1, none, none)


def gate_back_kernel(core, order, selp, logits, gg, xo, xr, gx_in, gx, gsel, acc):
    i = pl.program_id(0)
    last = pl.num_programs(0) - 1
    own = i < pl.num_programs(0) // 2
    high = core[0].astype(F32)
    sign = 2.0 * high - 1.0

    def z_of(b, k):
        at = (b * SELECT + k) * TPAD
        return logits[at : at + TPAD]

    def a_of(k):
        at = (BITS * SELECT + k) * TPAD
        return logits[at : at + TPAD]

    alpha, smooth, clipped, f_high = gate_parts(z_of, a_of, high)
    out = [None] * GROUPS
    d_alpha = []
    for k in range(SELECT):
        f = [[fac(smooth, b, k, bit) for bit in range(2)] for b in range(BITS - 1)]
        t0 = d0 = d1 = d2 = None
        low = {}
        dif = {}
        for e2 in range(2):
            for e1 in range(2):
                p, q = gg[4 * e2 + 2 * e1], gg[4 * e2 + 2 * e1 + 1]
                low[e2, e1] = f[0][0] * p + f[0][1] * q
                dif[e2, e1] = q - p
        mid = [f[1][0] * low[e2, 0] + f[1][1] * low[e2, 1] for e2 in range(2)]
        mid1 = [low[e2, 1] - low[e2, 0] for e2 in range(2)]
        mid0 = [f[1][0] * dif[e2, 0] + f[1][1] * dif[e2, 1] for e2 in range(2)]
        t0 = f[2][0] * mid[0] + f[2][1] * mid[1]
        d2 = mid[1] - mid[0]
        d1 = f[2][0] * mid1[0] + f[2][1] * mid1[1]
        d0 = f[2][0] * mid0[0] + f[2][1] * mid0[1]
        d_alpha.append(f_high[k] * t0)
        scale = alpha[k] * f_high[k]
        for b, d in enumerate((scale * d0, scale * d1, scale * d2, alpha[k] * sign * t0)):
            v = clipped[b, k]
            out[b * SELECT + k] = d * (1.5 / GAMMA - 6.0 / GAMMA**3 * v * v)
    total = functools.reduce(jnp.add, [a * d for a, d in zip(alpha, d_alpha)])
    for k in range(SELECT):
        out[BITS * SELECT + k] = alpha[k] * (d_alpha[k] - total)
    gl = jnp.concatenate(out, axis=0).astype(BF)
    gx[...] = (gx_in[...] + dot(selp[...], gl, 0, 0)).astype(gx.dtype)

    @pl.when(i == 0)
    def _():
        acc[...] = jnp.zeros_like(acc)

    acc[...] += dot(gl, jnp.where(own, xo[...], xr[...]), 1, 0)

    @pl.when(i == last)
    def _():
        gsel[...] = dot(order[...].astype(F32), acc[...], 0, 0, HIGHEST)


def gate_back(core, order, selp, logits, gg, x_own, x_recv, gx):
    rows, width = x_own.shape
    total = 2 * rows
    steps = total // TILE
    half = steps // 2
    lo = lambda i: jnp.minimum(i, half - 1)
    hi = lambda i: jnp.maximum(i - half, 0)
    whole = lambda shape: VMEM(shape, lambda i: (0,) * len(shape))
    return pl.pallas_call(
        gate_back_kernel,
        grid=(steps,),
        out_shape=(
            jax.ShapeDtypeStruct((width, total), BF),
            jax.ShapeDtypeStruct((order.shape[1], width), F32),
        ),
        in_specs=[
            pl.BlockSpec(memory_space=pltpu.SMEM),
            whole(order.shape),
            whole(selp.shape),
            VMEM((GROWS, TILE), lambda i: (0, i)),
            VMEM((8, TPAD, TILE), lambda i: (0, 0, i)),
            VMEM((TILE, width), lambda i: (lo(i), 0)),
            VMEM((TILE, width), lambda i: (hi(i), 0)),
            VMEM((width, TILE), lambda i: (0, i)),
        ],
        out_specs=(
            VMEM((width, TILE), lambda i: (0, i)),
            whole((order.shape[1], width)),
        ),
        scratch_shapes=[pltpu.VMEM((GROWS, width), F32)],
        compiler_params=params(32),
        cost_estimate=pl.CostEstimate(
            flops=4 * total * width * GROWS, bytes_accessed=8 * MIB, transcendentals=0
        ),
    )(core, order, selp, logits, gg, x_own, x_recv, gx)


def final_kernel(perm, mo, mr, xo, xr, mixed, gf):
    for t in range(TASKS):
        s = (mo[t].astype(F32) + mr[t].astype(F32)).astype(BF)
        mixed[t] = dot(s, perm[...], 0, 0).astype(BF)
    s = (xo[...].astype(F32) + xr[...].astype(F32)).astype(BF)
    gf[...] = dot(s, perm[...], 0, 0).astype(BF)


def final(perm, mo, mr, xo, xr):
    width, rows = xo.shape
    whole = lambda shape: VMEM(shape, lambda i: (0,) * len(shape))
    tall = VMEM((width, TILE), lambda i: (0, i))
    deep = VMEM((TASKS, width, TILE), lambda i: (0, 0, i))
    return pl.pallas_call(
        final_kernel,
        grid=(rows // TILE,),
        out_shape=(
            jax.ShapeDtypeStruct((TASKS, rows, width), BF),
            jax.ShapeDtypeStruct((rows, width), BF),
        ),
        in_specs=[whole(perm.shape), deep, deep, tall, tall],
        out_specs=(
            VMEM((TASKS, TILE, width), lambda i: (0, i, 0)),
            VMEM((TILE, width), lambda i: (i, 0)),
        ),
        compiler_params=params(32),
        cost_estimate=pl.CostEstimate(
            flops=8 * rows * width * width, bytes_accessed=6 * MIB, transcendentals=0
        ),
    )(perm, mo, mr, xo, xr)


def adamw(weight, grad, first, second):
    first = BETA_ONE * first + (1.0 - BETA_ONE) * grad
    second = BETA_TWO * second + (1.0 - BETA_TWO) * grad * grad
    mhat = first / (1.0 - BETA_ONE**STEP)
    vhat = second / (1.0 - BETA_TWO**STEP)
    weight = weight - RATE * (mhat / (jnp.sqrt(vhat) + EPSILON) + DECAY * weight)
    return (first, second, weight)


def logit_order():
    order = np.zeros((GROWS, 64), np.float32)
    for t in range(TASKS):
        for k in range(SELECT):
            for b in range(BITS):
                order[(b * SELECT + k) * TPAD + t, (t * SELECT + k) * BITS + b] = 1.0
            at = (BITS * SELECT + k) * TPAD + t
            order[at, TASKS * SELECT * BITS + t * SELECT + k] = 1.0
    return order


def per_device(
    n_rows,
    n_hid,
    features,
    w_expand,
    w_reduce,
    biases,
    w_select,
    grad_mix,
    m_expand,
    v_expand,
    m_reduce,
    v_reduce,
    m_biases,
    v_biases,
    m_select,
    v_select,
):
    d_loc, experts, h_loc = w_expand.shape
    width = d_loc * n_rows
    mine_n = experts // 2
    chunk = mine_n // 2
    row = lax.axis_index("rows")
    hid_at = lax.axis_index("hid")
    core = hid_at % 2

    bits = n_rows.bit_length() - 1
    masks = [1, 2, 6] if n_rows == 8 else [1 << b for b in range(bits)]
    side = (0, 2)
    sibling = ((0, 1), (0, 1))
    dims = [side] + [(m, 0) for m in masks]
    if n_rows == 8:
        orders = [((0, 1, 2, 3), (2, 3, 0, 1)), ((1, 0, 3, 2), (3, 2, 1, 0))]
    else:
        orders = [(tuple(range(len(dims))),) * 2] * 2

    def swap(x, hops):
        pairs = []
        for r in range(n_rows):
            for h in range(n_hid):
                mr, mh = hops[h % 2]
                pairs.append((r * n_hid + h, (r ^ mr) * n_hid + (h ^ mh)))
        return lax.ppermute(x, ("rows", "hid"), pairs)

    def hops_of(c, step):
        return tuple(dims[orders[c][k][step]] for k in range(2))

    def table_of(c):
        if n_rows != 8:
            return jnp.arange(16, dtype=jnp.int32)
        both = []
        for k in range(2):
            order = orders[c][k]
            spots = []
            for q in range(8):
                for s in range(2):
                    on = [s] + [(q >> b) & 1 for b in range(3)]
                    spots.append(sum(on[d] << order.index(d) for d in range(4)))
            both.append(spots)
        both = np.asarray(both, np.int32)
        return jnp.where(core == 0, both[0], both[1])

    spot = np.arange(width)
    away = np.zeros(width, np.int32)
    for b, m in enumerate(masks):
        away ^= np.where((spot // d_loc >> b) & 1, m, 0).astype(np.int32)
    d_of = (row ^ jnp.asarray(away)) * d_loc + jnp.asarray(spot % d_loc, jnp.int32)
    perm32 = (d_of[:, None] == jnp.arange(width, dtype=jnp.int32)[None, :]).astype(F32)
    perm = perm32.astype(BF)
    q_of = (hid_at ^ jnp.asarray(spot // h_loc, jnp.int32)) * h_loc + jnp.asarray(
        spot % h_loc, jnp.int32
    )
    order = jnp.asarray(logit_order(), BF)
    core_arr = jnp.reshape(core, (1,)).astype(jnp.int32)

    def split_experts(x, axis):
        mine = lax.dynamic_slice_in_dim(x, core * mine_n, mine_n, axis)
        other = lax.dynamic_slice_in_dim(x, (1 - core) * mine_n, mine_n, axis)
        return mine, other

    w_pack = jnp.stack(
        [jnp.transpose(w_expand, (1, 0, 2)), jnp.transpose(w_reduce, (0, 2, 1))]
    ).astype(BF)
    w_mine, w_other = split_experts(w_pack, 1)
    w_recv = swap(w_other, sibling)
    chip = jnp.concatenate([w_mine, w_recv], axis=3)
    bufs = [chip[None, :, :chunk], chip[None, :, chunk:]]

    x_own = features
    g_own = jnp.transpose(grad_mix, (1, 0, 2))
    x_recv = swap(x_own, sibling)
    g_recv = swap(g_own, sibling)

    sel = w_select.astype(BF)
    for m in masks:
        sel = jnp.concatenate([sel, swap(sel, ((m, 0), (m, 0)))], axis=0)
    sel = jnp.pad(sel, ((0, 0), (0, order.shape[1] - sel.shape[1])))

    b_mine, b_other = split_experts(biases, 1)
    b_pair = jnp.stack([b_mine, swap(b_other, sibling)])
    b_all = jnp.stack([b_pair, swap(b_pair, (side, side))])
    b_all = jnp.transpose(b_all, (2, 3, 0, 1, 4)).reshape(2, mine_n, width)
    b0 = jnp.broadcast_to((0.5 * b_all[0])[:, :, None], (mine_n, width, 128))
    to_d = (d_of[:, None] == q_of[None, :]).astype(F32)
    b1 = dot(b_all[1], to_d, 1, 1, HIGHEST)
    b1 = jnp.broadcast_to(b1[:, :, None], (mine_n, width, 128))

    steps = len(dims)
    ends = []
    for step in range(steps):
        for c in range(2):
            got = swap(bufs[c], hops_of(c, step))
            if step + 1 < steps:
                bufs[c] = jnp.concatenate([bufs[c], got], axis=0)
            else:
                ends.append((bufs[c], got))

    xt, gt, cc, gates, logits, selp, gb1 = prep(
        core_arr, perm, order, sel, x_own, x_recv, g_own, g_recv
    )

    def canonical(lo, hi):
        if n_rows == 8:
            return lo, hi
        part = n_rows // 8
        w = jnp.concatenate([lo, hi], axis=0).reshape(8, part, 2, 2, chunk, d_loc, 2 * h_loc)
        w = jnp.transpose(w, (0, 2, 3, 4, 1, 5, 6)).reshape(16, 2, chunk, part * d_loc, 2 * h_loc)
        return w[:8], w[8:]

    def uncanonical(lo, hi):
        if n_rows == 8:
            return lo, hi
        part = n_rows // 8
        w = jnp.concatenate([lo, hi], axis=0).reshape(8, 2, 2, chunk, part, d_loc, 2 * h_loc)
        w = jnp.transpose(w, (0, 4, 1, 2, 3, 5, 6)).reshape(
            2 * n_rows, 2, chunk, d_loc, 2 * h_loc
        )
        return w[:n_rows], w[n_rows:]

    outs = []
    for c in range(2):
        lo, hi = canonical(*ends[c])
        outs.append(critical(table_of(c), lo, hi, xt, cc, b0, c * chunk))

    grads = [uncanonical(o[0], o[1]) for o in outs]
    for step in reversed(range(steps)):
        for c in range(2):
            lo, hi = grads[c]
            got = swap(hi, hops_of(c, step))
            half = lo.shape[0] // 2
            if step > 0:
                add = lambda a, b: (a.astype(F32) + b.astype(F32)).astype(BF)
                grads[c] = (add(lo[:half], got[:half]), add(lo[half:], got[half:]))
            else:
                grads[c] = lo[0].astype(F32) + got[0].astype(F32)
    g_chip = jnp.concatenate(grads, axis=1)
    g_recv_w = swap(g_chip[..., h_loc:].astype(BF), sibling).astype(F32)
    g_mine = g_chip[..., :h_loc]
    g_w = jnp.where(
        core == 0,
        jnp.concatenate([g_mine, g_recv_w], axis=1),
        jnp.concatenate([g_recv_w, g_mine], axis=1),
    )
    total_expand = jnp.transpose(g_w[0], (1, 0, 2))
    total_reduce = jnp.transpose(g_w[1], (0, 2, 1))

    cat = lambda k: jnp.concatenate([outs[0][k], outs[1][k]], axis=0)
    mix_own, mix_other, gx, gg = rest(cat(4), cat(2), cat(3), gt, gates, b1)
    gx, gsel = gate_back(core_arr, order, selp, logits, gg, x_own, x_recv, gx)
    rows_n = x_own.shape[0]
    mix_recv = swap(mix_other, sibling)
    gx_recv = swap(gx[:, rows_n:], sibling)
    mixed, grad_features = final(perm, mix_own, mix_recv, gx[:, :rows_n], gx_recv)
    mixed = jnp.transpose(mixed, (1, 0, 2))

    to_q = (q_of[:, None] == jnp.arange(width, dtype=jnp.int32)[None, :]).astype(F32)
    gb0_abs = dot(cat(5)[:, 0], to_q, 1, 0, HIGHEST)
    gb1_abs = dot(gb1[:, 0], perm32, 1, 0, HIGHEST)
    small = jnp.concatenate([gsel, gb0_abs, gb1_abs], axis=0)
    for d in dims:
        small = small + swap(small, (d, d))
    small_recv = swap(small, sibling)
    n_sel = gsel.shape[0]
    gsel = small[:n_sel] + small_recv[:n_sel]
    total_select = jnp.transpose(
        lax.dynamic_slice_in_dim(gsel[: w_select.shape[1]], row * d_loc, d_loc, 1)
    )
    both = [
        lax.dynamic_slice_in_dim(s[n_sel:].reshape(2, mine_n, width), hid_at * h_loc, h_loc, 2)
        for s in (small, small_recv)
    ]
    total_biases = jnp.where(
        core == 0, jnp.concatenate(both, axis=1), jnp.concatenate(both[::-1], axis=1)
    )

    mean_e, square_e, new_e = adamw(w_expand, total_expand, m_expand, v_expand)
    mean_r, square_r, new_r = adamw(w_reduce, total_reduce, m_reduce, v_reduce)
    mean_b, square_b, new_b = adamw(biases, total_biases, m_biases, v_biases)
    mean_s, square_s, new_s = adamw(w_select, total_select, m_select, v_select)
    return (
        mixed,
        grad_features,
        mean_e,
        square_e,
        new_e,
        mean_r,
        square_r,
        new_r,
        mean_b,
        square_b,
        new_b,
        mean_s,
        square_s,
        new_s,
    )


def solution(mesh):
    row_split = P(("rows", "hid"), None)
    task_split = P(("rows", "hid"), None, None)
    expand = P("rows", None, "hid")
    reduce = P(None, "hid", "rows")
    bias = P(None, None, "hid")
    select = P("rows", None)
    return jax.shard_map(
        functools.partial(per_device, mesh.shape["rows"], mesh.shape["hid"]),
        mesh=mesh,
        in_specs=(
            row_split, expand, reduce, bias, select, task_split,
            expand, expand, reduce, reduce, bias, bias, select, select,
        ),
        out_specs=(
            task_split, row_split,
            expand, expand, expand,
            reduce, reduce, reduce,
            bias, bias, bias,
            select, select, select,
        ),
        check_vma=False,
    )
```

time: 578 us -> 185 us (0.32)
  local copies, waits for them, and re-layouts: 174 us -> 16.8 us
  blocking collectives: 152 us -> 0 us
  waiting for transfers between devices: 118 us -> 34.3 us
  matrix products: 82.8 us -> 0.68 us
  Pallas kernels: 0 us -> 57.4 us
  starting transfers between devices: 0.5 us -> 46.9 us
  between operations: 15.2 us -> 1.1 us
    all_gather x4 -> x0, blocking collectives: 104 us -> none  [the longest x1 34.6 us: per_device(): lax.all_gather(w_expand.astype(jnp.bfloat16), 'rows', axis=0, tiled=True)]
    dot_general x12 -> x3, matrix products: 82.8 us -> 0.68 us  [dot(): lax.dot_general(a, b, (((ca,), (cb,)), ((), ())), preferred_element_type=...]
    reduce_scatter x3 -> x0, waiting for transfers between devices: 73.6 us -> none  [the longest x1 47.2 us: per_device(): lax.psum_scatter(grad_reduce.reshape(experts_n, hidden_n, width), 'rows',...]
    pallas_call x0 -> x6, Pallas kernels: none -> 57.4 us  [the longest x2 21 us: critical(): pl.pallas_call(critical_kernel, grid=(chunk,), out_shape=(jax.ShapeDtypeS...]
    convert_element_type x2 -> x0, local copies, waits for them, and re-layouts: 52.6 us -> none  [the longest x1 35 us: per_device(): weighted = (hidden.reshape(rows_local, 1, experts_n, hidden_n) * gate_row...]
    psum x2 -> x0, blocking collectives: 47.7 us -> none  [the longest x1 37.1 us: per_device(): lax.psum(jnp.stack([grad_hbias.reshape(experts_n, hidden_n), grad_obias])...]
    ppermute x0 -> x32, starting transfers between devices: none -> 46.9 us  [swap(): return lax.ppermute(x, ('rows', 'hid'), pairs)]
    unnamed x11 -> x0, waiting for transfers between devices: 43.9 us -> none
  transfers between devices with their start and end apart: 8 -> 32, of which waited for: 5 -> 15; matrix products, arithmetic and copies ran while one was open for 37% -> 11% of each run, Pallas kernels for 0% -> 11%
where the time goes in v1:
time: 185 us; the launch traced here: 182 us
  Pallas kernels  57.4 us (31%)
  starting transfers between devices  46.9 us (25%)
  waiting for transfers between devices  34.3 us (19%)
  other arithmetic  25.2 us (14%)
  local copies, waits for them, and re-layouts  16.8 us (9%)
    ppermute x32, starting transfers between devices, swap(): return lax.ppermute(x, ('rows', 'hid'), pairs)  46.9 us
    ppermute x32, waiting for transfers between devices, swap(): return lax.ppermute(x, ('rows', 'hid'), pairs)  34.3 us
    pallas_call x2, Pallas kernels, critical(): pl.pallas_call(critical_kernel, grid=(chunk,), out_shape=(jax.ShapeDtypeS...  21 us
    pallas_call x1, Pallas kernels, rest(): pl.pallas_call(functools.partial(rest_kernel, first=True), grid=(count,),...  20.2 us
    unnamed x50, local copies, waits for them, and re-layouts  12.5 us
    concatenate x3, other arithmetic, per_device(): cat = lambda k: jnp.concatenate([outs[0][k], outs[1][k]], axis=0)  11.1 us
    pallas_call x1, Pallas kernels, prep(): pl.pallas_call(prep_kernel, grid=(steps,), out_shape=(jax.ShapeDtypeStruc...  10.3 us
    convert_element_type x6, other arithmetic, per_device(): add = lambda a, b: (a.astype(F32) + b.astype(F32)).astype(BF)  5.38 us
  transfers between devices with their start and end apart: 32, of which 15 were waited for; matrix products, arithmetic and copies ran while one was open for 11% of the time, Pallas kernels for 11%

profile of v1, /device:TPU:0, one launch (start us, length us, event | category | flops | bytes accessed | tf_op | source)
XLA Modules:
  0.0 182.4 jit_solution(13869096985287816239)
XLA Ops:
  0.7 1.1 copy.111
  1.8 1.0 convert_bitcast_fusion
  3.4 0.7 dynamic-slice_bitcast_fusion
  4.1 0.7 convert_element_type.144
  4.9 3.0 %collective-permute-start.5 = (bf16[32,60]{1,0:T(8,128)(2,1)S(1)}, bf16[32,60]{1,0:T(8,128)(2,1)S(1)}, u32[]{:S(2)}, u32[]{:S(2)}) collective-permute-start(bf16[32,60]{1,0:T(8,128)(2,1)S(1)} %convert_element_type.144), channel_id=1, source_target_pairs={{0,4},{1,5},{2,6},{3,7},{4,0},{5,1},{6,2},{7,3},{8,12},{9,13},{10,... | collective-permute-start | bytes 11528 | tf_op jit(solution)/shard_map/ppermute | solution.py:537
  8.3 0.7 multiply_add_fusion.5
  9.1 0.7 multiply_add_fusion.4
  10.5 1.6 collective-permute-start.6
  12.2 1.6 collective-permute-start.11
  14.5 3.5 %collective-permute-start.7 = (bf16[128,60]{1,0:T(8,128)(2,1)S(1)}, bf16[128,60]{1,0:T(8,128)(2,1)S(1)}, u32[]{:S(2)}, u32[]{:S(2)}) collective-permute-start(bf16[128,60]{1,0:T(8,128)(2,1)S(1)} %pad_maximum_fusion.12), channel_id=1, source_target_pairs={{0,24},{1,25},{2,26},{3,27},{4,28},{5,29},{6,30},{7,31},{8,16},{9,... | collective-permute-start | bytes 46088 | tf_op jit(solution)/shard_map/ppermute | solution.py:537
  18.2 0.9 collective-permute-start.12
  19.2 1.2 collective-permute-start.2
  20.3 2.1 %collective-permute-done.12 = bf16[1,2,4,32,128]{4,3,2,1,0:T(8,128)(2,1)S(1)} collective-permute-done((bf16[1,2,4,32,128]{4,3,2,1,0:T(8,128)(2,1)S(1)}, bf16[1,2,4,32,128]{4,3,2,1,0:T(8,128)(2,1)S(1)}, u32[]{:S(2)}, u32[]{:S(2)}) %collective-permute-start.12) | collective-permute-done | bytes 65568 | tf_op jit(solution)/shard_map/ppermute | solution.py:537
  22.5 1.4 collective-permute-start.13
  24.8 2.7 %collective-permute-done.13 = bf16[2,2,4,32,128]{4,3,2,1,0:T(8,128)(2,1)S(1)} collective-permute-done((bf16[2,2,4,32,128]{4,3,2,1,0:T(8,128)(2,1)S(1)}, bf16[2,2,4,32,128]{4,3,2,1,0:T(8,128)(2,1)S(1)}, u32[]{:S(2)}, u32[]{:S(2)}) %collective-permute-start.13) | collective-permute-done | bytes 131104 | tf_op jit(solution)/shard_map/ppermute | solution.py:537
  27.6 2.9 %collective-permute-start.14 = (bf16[4,2,4,32,128]{4,3,2,1,0:T(8,128)(2,1)S(1)}, bf16[4,2,4,32,128]{4,3,2,1,0:T(8,128)(2,1)S(1)}, u32[]{:S(2)}, u32[]{:S(2)}) collective-permute-start(bf16[4,2,4,32,128]{4,3,2,1,0:T(8,128)(2,1)S(1)} %pad_maximum_fusion.7), channel_id=1, source_target_pairs={{0,24},{1,5},{2,26},{3,7},{4,28},{5,1},{6,30},{7,3},{8,16},{9,13},... | collective-permute-start | bytes 786440 | tf_op jit(solution)/shard_map/ppermute | solution.py:537
  30.8 1.0 pad_maximum_fusion.3.w_lo
  31.8 2.5 %collective-permute-start.4 = (bf16[8,2,4,32,128]{4,3,2,1,0:T(8,128)(2,1)S(1)}, bf16[8,2,4,32,128]{4,3,2,1,0:T(8,128)(2,1)S(1)}, u32[]{:S(2)}, u32[]{:S(2)}) collective-permute-start(bf16[8,2,4,32,128]{4,3,2,1,0:T(8,128)(2,1)S(1)} %pad_maximum_fusion.3.w_lo), channel_id=1, source_target_pairs={{0,24},{1,5},{2,26},{3,7},{4,28},{5,1},{6,30},{7,3},{8,16},{9,13},... | collective-permute-start | bytes 1572872 | tf_op jit(solution)/shard_map/ppermute | solution.py:537
  34.8 1.1 collective-permute-done.14
  36.0 8.3 %collective-permute-start.15 = (bf16[8,2,4,32,128]{4,3,2,1,0:T(8,128)(2,1)S(1)}, bf16[8,2,4,32,128]{4,3,2,1,0:T(8,128)(2,1)S(1)}, u32[]{:S(2)}, u32[]{:S(2)}) collective-permute-start(bf16[8,2,4,32,128]{4,3,2,1,0:T(8,128)(2,1)S(1)} %pad_maximum_fusion.4.w_lo), channel_id=1, source_target_pairs={{0,8},{1,3},{2,10},{3,1},{4,12},{5,7},{6,14},{7,5},{8,0},{9,11},{1... | collective-permute-start | bytes 1572872 | tf_op jit(solution)/shard_map/ppermute | solution.py:537
  44.3 1.4 copy-done.7
  45.7 10.3 %shard_map.326 = (bf16[272,2048]{1,0:T(8,128)(2,1)S(1)}, bf16[3,256,2048]{2,1,0:T(8,128)(2,1)}, bf16[8,256,2048]{2,1,0:T(8,128)(2,1)}, f32[8,8,2048]{2,1,0:T(8,1...) custom-call(s32[1]{0:T(128)} %bitcast.5.core, ...), custom_call_target="tpu_custom_call" | custom-call | flops 1342177280 | bytes 18874368 | tf_op jit(solution)/shard_map/pallas_call | solution.py:135
  56.3 10.4 %shard_map.327 = (bf16[8,2,4,32,128]{4,3,2,1,0:T(8,128)(2,1)S(1)}, bf16[8,2,4,32,128]{4,3,2,1,0:T(8,128)(2,1)}, bf16[4,256,2048]{2,1,0:T(8,128)(2,1)}, bf16[4,25...) custom-call(s32[16]{0:T(128)S(1)} %broadcast_select_fusion.1.table, ...), custom_call_target="tpu_custom_call" | custom-call | flops 4294967296 | bytes 16777216 | tf_op jit(solution)/shard_map/pallas_call | solution.py:229
  66.7 0.8 copy-done.2
  67.5 10.6 %shard_map.328 = (bf16[8,2,4,32,128]{4,3,2,1,0:T(8,128)(2,1)S(1)}, bf16[8,2,4,32,128]{4,3,2,1,0:T(8,128)(2,1)}, bf16[4,256,2048]{2,1,0:T(8,128)(2,1)}, bf16[4,25...) custom-call(s32[16]{0:T(128)S(1)} %broadcast_select_fusion.table, ...), custom_call_target="tpu_custom_call" | custom-call | flops 4294967296 | bytes 16777216 | tf_op jit(solution)/shard_map/pallas_call | solution.py:229
  78.6 1.6 pad_maximum_fusion.2.wun
  80.1 0.9 copy-done.8
  81.0 9.5 %pad_maximum_fusion = (bf16[8,256,2048]{2,1,0:T(8,128)(2,1)}, bf16[8,256,2048]{2,1,0:T(8,128)(2,1)}) fusion(bf16[4,256,2048]{2,1,0:T(8,128)(2,1)} %get-tuple-element.46, bf16[4,256,2048]{2,1,0:T(8,128)(2,1)S(1)} %copy-done.8, bf16[4,256,2048]{2,1,0:T(8,128)(2,1)} %get-tuple-element.48, bf16[4,256,2048]{2,1,0:T(8,128)(2,1)S(1)} %copy-done.9), kind=kLoop, calls=%fused_computation | loop fusion | flops 8388608 | bytes 33554432 | tf_op jit(solution)/shard_map/concatenate | solution.py:661
  90.5 1.4 broadcast_in_dim.13.b1
  92.5 20.2 %shard_map.329 = (bf16[3,256,1024]{2,1,0:T(8,128)(2,1)}, bf16[3,256,1024]{2,1,0:T(8,128)(2,1)}, f32[256,2048]{1,0:T(8,128)}, f32[8,8,2048]{2,1,0:T(8,128)}) custom-call(bf16[8,2,256,256]{3,2,1,0:T(8,128)(2,1)} %pad_maximum_fusion.2.wun, bf16[8,256,2048]{2,1,0:T(8,128)(2,1)} %get-tuple-element.142.hid, bf16[8,256,2048]{2,1,0:T(8,128)(2,1)} %get-tuple-element.143.gp, ...), custom_call_target="tpu_custom_call" | custom-call | flops 4294967296 | bytes 25165824 | tf_op jit(solution)/shard_map/pallas_call | solution.py:311
  112.7 1.6 copy-done
  114.3 1.0 copy-done.5
  115.3 3.5 %shard_map.330 = (bf16[256,2048]{1,0:T(8,128)(2,1)S(1)}, f32[64,256]{1,0:T(8,128)S(1)}) custom-call(s32[1]{0:T(128)} %bitcast.5.core, bf16[160,64]{1,0:T(8,128)(2,1)S(1)} %copy-done.6, bf16[160,256]{1,0:T(8,128)(2,1)S(1)} %get-tuple-element.53.selp, f32[160,2048]{1,0:T(8,128)S(1)} %get-tuple-element.54.logits, f32[8,8,2048]{2,1,0:T(8,128)S(1)} %copy-done.5, ...), custom_call_target="tpu_custom_call" | custom-call | flops 335544320 | bytes 8388608 | tf_op jit(solution)/shard_map/pallas_call | solution.py:414
  119.1 5.3 %collective-permute-done.27 = f32[80,256]{1,0:T(8,128)S(1)} collective-permute-done((f32[80,256]{1,0:T(8,128)S(1)}, f32[80,256]{1,0:T(8,128)S(1)}, u32[]{:S(2)}, u32[]{:S(2)}) %collective-permute-start.27) | collective-permute-done | bytes 81952 | tf_op jit(solution)/shard_map/ppermute | solution.py:537
  124.4 1.3 collective-permute-start.28
  125.7 3.2 %collective-permute-done.28 = f32[80,256]{1,0:T(8,128)S(1)} collective-permute-done((f32[80,256]{1,0:T(8,128)S(1)}, f32[80,256]{1,0:T(8,128)S(1)}, u32[]{:S(2)}, u32[]{:S(2)}) %collective-permute-start.28) | collective-permute-done | bytes 81952 | tf_op jit(solution)/shard_map/ppermute | solution.py:537
  129.3 3.0 %collective-permute-start.18 = (bf16[8,2,4,32,128]{4,3,2,1,0:T(8,128)(2,1)}, bf16[8,2,4,32,128]{4,3,2,1,0:T(8,128)(2,1)S(1)}, u32[]{:S(2)}, u32[]{:S(2)}) collective-permute-start(bf16[8,2,4,32,128]{4,3,2,1,0:T(8,128)(2,1)} %get-tuple-element.61), channel_id=1, source_target_pairs={{0,24},{1,5},{2,26},{3,7},{4,28},{5,1},{6,30},{7,3},{8,16},{9,13},... | collective-permute-start | bytes 1572872 | tf_op jit(solution)/shard_map/ppermute | solution.py:537
  132.2 1.1 collective-permute-start.22
  133.4 3.0 %collective-permute-start.30 = (f32[80,256]{1,0:T(8,128)S(1)}, f32[80,256]{1,0:T(8,128)S(1)}, u32[]{:S(2)}, u32[]{:S(2)}) collective-permute-start(f32[80,256]{1,0:T(8,128)S(1)} %add.183), channel_id=1, source_target_pairs={{0,24},{1,25},{2,26},{3,27},{4,28},{5,29},{6,30},{7,31},{8,16},{9,... | collective-permute-start | bytes 245768 | tf_op jit(solution)/shard_map/ppermute | solution.py:537
  136.4 0.9 fusion.37
  137.8 9.4 %collective-permute-done.30 = f32[80,256]{1,0:T(8,128)S(1)} collective-permute-done((f32[80,256]{1,0:T(8,128)S(1)}, f32[80,256]{1,0:T(8,128)S(1)}, u32[]{:S(2)}, u32[]{:S(2)}) %collective-permute-start.30) | collective-permute-done | bytes 81952 | tf_op jit(solution)/shard_map/ppermute | solution.py:537
  147.4 1.2 collective-permute-done.31
  148.8 2.0 %add_convert_fusion.3 = (bf16[4,2,4,32,128]{4,3,2,1,0:T(8,128)(2,1)}, bf16[4,2,4,32,128]{4,3,2,1,0:T(8,128)(2,1)}) fusion(bf16[8,2,4,32,128]{4,3,2,1,0:T(8,128)(2,1)S(1)} %collective-permute-done.18, bf16[8,2,4,32,128]{4,3,2,1,0:T(8,128)(2,1)} %copy-done.2), kind=kLoop, calls=%fused_computation.9 | loop fusion | flops 1048576 | bytes 1572864 | tf_op jit(solution)/shard_map/convert_element_type | solution.py:646
  150.7 0.9 collective-permute-start.19
  151.6 1.0 add_convert_fusion.1
  152.6 2.9 %collective-permute-start.23 = (bf16[4,2,4,32,128]{4,3,2,1,0:T(8,128)(2,1)}, bf16[4,2,4,32,128]{4,3,2,1,0:T(8,128)(2,1)S(1)}, u32[]{:S(2)}, u32[]{:S(2)}) collective-permute-start(bf16[4,2,4,32,128]{4,3,2,1,0:T(8,128)(2,1)} %get-tuple-element.125), channel_id=1, source_target_pairs={{0,24},{1,5},{2,26},{3,7},{4,28},{5,1},{6,30},{7,3},{8,16},{9,13},... | collective-permute-start | bytes 786440 | tf_op jit(solution)/shard_map/ppermute | solution.py:537
  156.1 0.7 copy.86
  156.8 0.7 copy.87
  158.2 1.2 add_convert_fusion.7
  159.4 1.3 collective-permute-start.20
  160.8 1.2 collective-permute-done.23
  162.0 0.7 copy-done.13
  162.7 1.2 add_convert_fusion.5
  164.5 1.5 collective-permute-start.21
  166.0 2.8 %collective-permute-done.24 = bf16[2,2,4,32,128]{4,3,2,1,0:T(8,128)(2,1)S(1)} collective-permute-done((bf16[2,2,4,32,128]{4,3,2,1,0:T(8,128)(2,1)S(1)}, bf16[2,2,4,32,128]{4,3,2,1,0:T(8,128)(2,1)S(1)}, u32[]{:S(2)}, u32[]{:S(2)}) %collective-permute-start.24) | collective-permute-done | bytes 131104 | tf_op jit(solution)/shard_map/ppermute | solution.py:537
  168.9 1.3 collective-permute-start.25
  170.3 3.0 %collective-permute-done.25 = bf16[1,2,4,32,128]{4,3,2,1,0:T(8,128)(2,1)S(1)} collective-permute-done((bf16[1,2,4,32,128]{4,3,2,1,0:T(8,128)(2,1)S(1)}, bf16[1,2,4,32,128]{4,3,2,1,0:T(8,128)(2,1)S(1)}, u32[]{:S(2)}, u32[]{:S(2)}) %collective-permute-start.25) | collective-permute-done | bytes 65568 | tf_op jit(solution)/shard_map/ppermute | solution.py:537
  173.5 1.3 collective-permute-done.26
  174.9 1.5 multiply_subtract_fusion.1
  176.4 0.9 copy.83
  177.2 0.9 copy.84
  178.1 0.9 copy.85
  178.9 1.0 multiply_subtract_fusion
  180.0 2.4 %shard_map.331 = (bf16[3,1024,256]{2,1,0:T(8,128)(2,1)}, bf16[1024,256]{1,0:T(8,128)(2,1)}) custom-call(bf16[256,256]{1,0:T(8,128)(2,1)S(1)} %convert_convert_fusion.perm, bf16[3,256,1024]{2,1,0:T(8,128)(2,1)S(1)} %copy-done.1, bf16[3,256,1024]{2,1,0:T(8,128)(2,1)S(1)} %collective-permute-done.16.mr, bf16[256,1024]{1,0:T(8,128)(2,1)S(1)} %get-tuple-element.127.xo, ...), custom_call_target="tpu_custom_call" | custom-call | flops 536870912 | bytes 6291456 | tf_op jit(solution)/shard_map/pallas_call | solution.py:456
  (120 shorter events, 10.0 us)
Async XLA Ops:
  0.6 43.6 %copy-start.6 = (bf16[160,64]{1,0:T(8,128)(2,1)S(1)}, bf16[160,64]{1,0:T(8,128)(2,1)}, u32[]{:S(2)}) copy-start(bf16[160,64]{1,0:T(8,128)(2,1)} %constant.96.clone.order) | copy-start | bytes 61444
  0.7 43.6 %copy-start.4 = (bf16[1024,256]{1,0:T(8,128)(2,1)S(1)}, bf16[1024,256]{1,0:T(8,128)(2,1)}, u32[]{:S(2)}) copy-start(bf16[1024,256]{1,0:T(8,128)(2,1)} %xo.3) | copy-start | bytes 1572868
  2.8 10.9 %collective-permute-start = (bf16[2,8,32,64]{3,2,1,0:T(8,128)(2,1)S(1)}, bf16[2,8,32,64]{3,2,1,0:T(8,128)(2,1)S(1)}, u32[]{:S(2)}, u32[]{:S(2)}) collective-permute-start(bf16[2,8,32,64]{3,2,1,0:T(8,128)(2,1)S(1)} %get-tuple-element.135), channel_id=1, source_target_pairs={{0,1},{1,0},{2,3},{3,2},{4,5},{5,4},{6,7},{7,6},{8,9},{9,8},{10,11... | collective-permute-start | bytes 196616 | tf_op jit(solution)/shard_map/ppermute | solution.py:537
  4.1 8.1 %collective-permute-start.10 = (f32[2,8,64]{2,1,0:T(8,128)S(1)}, f32[2,8,64]{2,1,0:T(8,128)S(1)}, u32[]{:S(2)}, u32[]{:S(2)}) collective-permute-start(f32[2,8,64]{2,1,0:T(8,128)S(1)} %get-tuple-element.141), channel_id=1, source_target_pairs={{0,1},{1,0},{2,3},{3,2},{4,5},{5,4},{6,7},{7,6},{8,9},{9,8},{10,11... | collective-permute-start | bytes 12296 | tf_op jit(solution)/shard_map/ppermute | solution.py:537
  4.9 5.7 %collective-permute-start.5 = (bf16[32,60]{1,0:T(8,128)(2,1)S(1)}, bf16[32,60]{1,0:T(8,128)(2,1)S(1)}, u32[]{:S(2)}, u32[]{:S(2)}) collective-permute-start(bf16[32,60]{1,0:T(8,128)(2,1)S(1)} %convert_element_type.144), channel_id=1, source_target_pairs={{0,4},{1,5},{2,6},{3,7},{4,0},{5,1},{6,2},{7,3},{8,12},{9,13},{10,... | collective-permute-start | bytes 11528 | tf_op jit(solution)/shard_map/ppermute | solution.py:537
  7.8 36.4 %collective-permute-start.9 = (bf16[3,1024,256]{2,1,0:T(8,128)(2,1)}, bf16[3,1024,256]{2,1,0:T(8,128)(2,1)}, u32[]{:S(2)}, u32[]{:S(2)}) collective-permute-start(bf16[3,1024,256]{2,1,0:T(8,128)(2,1)} %bitcast.67), channel_id=1, source_target_pairs={{0,1},{1,0},{2,3},{3,2},{4,5},{5,4},{6,7},{7,6},{8,9},{9,8},{10,11... | collective-permute-start | bytes 4718600 | tf_op jit(solution)/shard_map/ppermute | solution.py:537
  7.8 36.4 %collective-permute-start.8 = (bf16[1024,256]{1,0:T(8,128)(2,1)}, bf16[1024,256]{1,0:T(8,128)(2,1)S(1)}, u32[]{:S(2)}, u32[]{:S(2)}) collective-permute-start(bf16[1024,256]{1,0:T(8,128)(2,1)} %xo.3), channel_id=1, source_target_pairs={{0,1},{1,0},{2,3},{3,2},{4,5},{5,4},{6,7},{7,6},{8,9},{9,8},{10,11... | collective-permute-start | bytes 1572872 | tf_op jit(solution)/shard_map/ppermute | solution.py:537
  10.5 3.9 %collective-permute-start.6 = (bf16[64,60]{1,0:T(8,128)(2,1)S(1)}, bf16[64,60]{1,0:T(8,128)(2,1)S(1)}, u32[]{:S(2)}, u32[]{:S(2)}) collective-permute-start(bf16[64,60]{1,0:T(8,128)(2,1)S(1)} %pad_maximum_fusion.13), channel_id=1, source_target_pairs={{0,8},{1,9},{2,10},{3,11},{4,12},{5,13},{6,14},{7,15},{8,0},{9,1},... | collective-permute-start | bytes 23048 | tf_op jit(solution)/shard_map/ppermute | solution.py:537
  12.2 7.0 %collective-permute-start.11 = (f32[2,2,8,64]{3,2,1,0:T(8,128)S(1)}, f32[2,2,8,64]{3,2,1,0:T(8,128)S(1)}, u32[]{:S(2)}, u32[]{:S(2)}) collective-permute-start(f32[2,2,8,64]{3,2,1,0:T(8,128)S(1)} %get-tuple-element.139), channel_id=1, source_target_pairs={{0,2},{1,3},{2,0},{3,1},{4,6},{5,7},{6,4},{7,5},{8,10},{9,11},{10,... | collective-permute-start | bytes 24584 | tf_op jit(solution)/shard_map/ppermute | solution.py:537
  13.9 4.3 %collective-permute-start.1 = (bf16[1,2,4,32,128]{4,3,2,1,0:T(8,128)(2,1)S(1)}, bf16[1,2,4,32,128]{4,3,2,1,0:T(8,128)(2,1)S(1)}, u32[]{:S(2)}, u32[]{:S(2)}) collective-permute-start(bf16[1,2,4,32,128]{4,3,2,1,0:T(8,128)(2,1)S(1)} %get-tuple-element.132), channel_id=1, source_target_pairs={{0,2},{1,9},{2,0},{3,11},{4,6},{5,13},{6,4},{7,15},{8,10},{9,1},{1... | collective-permute-start | bytes 196616 | tf_op jit(solution)/shard_map/ppermute | solution.py:537
  14.5 20.2 %collective-permute-start.7 = (bf16[128,60]{1,0:T(8,128)(2,1)S(1)}, bf16[128,60]{1,0:T(8,128)(2,1)S(1)}, u32[]{:S(2)}, u32[]{:S(2)}) collective-permute-start(bf16[128,60]{1,0:T(8,128)(2,1)S(1)} %pad_maximum_fusion.12), channel_id=1, source_target_pairs={{0,24},{1,25},{2,26},{3,27},{4,28},{5,29},{6,30},{7,31},{8,16},{9,... | collective-permute-start | bytes 46088 | tf_op jit(solution)/shard_map/ppermute | solution.py:537
  18.2 4.3 %collective-permute-start.12 = (bf16[1,2,4,32,128]{4,3,2,1,0:T(8,128)(2,1)S(1)}, bf16[1,2,4,32,128]{4,3,2,1,0:T(8,128)(2,1)S(1)}, u32[]{:S(2)}, u32[]{:S(2)}) collective-permute-start(bf16[1,2,4,32,128]{4,3,2,1,0:T(8,128)(2,1)S(1)} %get-tuple-element.133), channel_id=1, source_target_pairs={{0,4},{1,25},{2,6},{3,27},{4,0},{5,29},{6,2},{7,31},{8,12},{9,17},... | collective-permute-start | bytes 196616 | tf_op jit(solution)/shard_map/ppermute | solution.py:537
  19.2 5.0 %collective-permute-start.2 = (bf16[2,2,4,32,128]{4,3,2,1,0:T(8,128)(2,1)S(1)}, bf16[2,2,4,32,128]{4,3,2,1,0:T(8,128)(2,1)S(1)}, u32[]{:S(2)}, u32[]{:S(2)}) collective-permute-start(bf16[2,2,4,32,128]{4,3,2,1,0:T(8,128)(2,1)S(1)} %pad_maximum_fusion.8), channel_id=1, source_target_pairs={{0,4},{1,25},{2,6},{3,27},{4,0},{5,29},{6,2},{7,31},{8,12},{9,17},... | collective-permute-start | bytes 393224 | tf_op jit(solution)/shard_map/ppermute | solution.py:537
  22.5 5.0 %collective-permute-start.13 = (bf16[2,2,4,32,128]{4,3,2,1,0:T(8,128)(2,1)S(1)}, bf16[2,2,4,32,128]{4,3,2,1,0:T(8,128)(2,1)S(1)}, u32[]{:S(2)}, u32[]{:S(2)}) collective-permute-start(bf16[2,2,4,32,128]{4,3,2,1,0:T(8,128)(2,1)S(1)} %pad_maximum_fusion.9), channel_id=1, source_target_pairs={{0,2},{1,9},{2,0},{3,11},{4,6},{5,13},{6,4},{7,15},{8,10},{9,1},{1... | collective-permute-start | bytes 393224 | tf_op jit(solution)/shard_map/ppermute | solution.py:537
  24.2 6.5 %collective-permute-start.3 = (bf16[4,2,4,32,128]{4,3,2,1,0:T(8,128)(2,1)S(1)}, bf16[4,2,4,32,128]{4,3,2,1,0:T(8,128)(2,1)}, u32[]{:S(2)}, u32[]{:S(2)}) collective-permute-start(bf16[4,2,4,32,128]{4,3,2,1,0:T(8,128)(2,1)S(1)} %pad_maximum_fusion.6), channel_id=1, source_target_pairs={{0,8},{1,3},{2,10},{3,1},{4,12},{5,7},{6,14},{7,5},{8,0},{9,11},{1... | collective-permute-start | bytes 786440 | tf_op jit(solution)/shard_map/ppermute | solution.py:537
  27.6 8.3 %collective-permute-start.14 = (bf16[4,2,4,32,128]{4,3,2,1,0:T(8,128)(2,1)S(1)}, bf16[4,2,4,32,128]{4,3,2,1,0:T(8,128)(2,1)S(1)}, u32[]{:S(2)}, u32[]{:S(2)}) collective-permute-start(bf16[4,2,4,32,128]{4,3,2,1,0:T(8,128)(2,1)S(1)} %pad_maximum_fusion.7), channel_id=1, source_target_pairs={{0,24},{1,5},{2,26},{3,7},{4,28},{5,1},{6,30},{7,3},{8,16},{9,13},... | collective-permute-start | bytes 786440 | tf_op jit(solution)/shard_map/ppermute | solution.py:537
  31.8 24.2 %collective-permute-start.4 = (bf16[8,2,4,32,128]{4,3,2,1,0:T(8,128)(2,1)S(1)}, bf16[8,2,4,32,128]{4,3,2,1,0:T(8,128)(2,1)S(1)}, u32[]{:S(2)}, u32[]{:S(2)}) collective-permute-start(bf16[8,2,4,32,128]{4,3,2,1,0:T(8,128)(2,1)S(1)} %pad_maximum_fusion.3.w_lo), channel_id=1, source_target_pairs={{0,24},{1,5},{2,26},{3,7},{4,28},{5,1},{6,30},{7,3},{8,16},{9,13},... | collective-permute-start | bytes 1572872 | tf_op jit(solution)/shard_map/ppermute | solution.py:537
  36.0 31.5 %collective-permute-start.15 = (bf16[8,2,4,32,128]{4,3,2,1,0:T(8,128)(2,1)S(1)}, bf16[8,2,4,32,128]{4,3,2,1,0:T(8,128)(2,1)S(1)}, u32[]{:S(2)}, u32[]{:S(2)}) collective-permute-start(bf16[8,2,4,32,128]{4,3,2,1,0:T(8,128)(2,1)S(1)} %pad_maximum_fusion.4.w_lo), channel_id=1, source_target_pairs={{0,8},{1,3},{2,10},{3,1},{4,12},{5,7},{6,14},{7,5},{8,0},{9,11},{1... | collective-permute-start | bytes 1572872 | tf_op jit(solution)/shard_map/ppermute | solution.py:537
  44.3 1.4 copy-start.7
  56.0 10.7 %copy-start.3 = (f32[8,8,2048]{2,1,0:T(8,128)}, f32[8,8,2048]{2,1,0:T(8,128)S(1)}, u32[]{:S(2)}) copy-start(f32[8,8,2048]{2,1,0:T(8,128)S(1)} %get-tuple-element.50.gates) | copy-start | bytes 1572868
  66.7 0.8 copy-start.2
  67.5 12.6 %copy-start.9 = (bf16[4,256,2048]{2,1,0:T(8,128)(2,1)S(1)}, bf16[4,256,2048]{2,1,0:T(8,128)(2,1)}, u32[]{:S(2)}) copy-start(bf16[4,256,2048]{2,1,0:T(8,128)(2,1)} %get-tuple-element.47) | copy-start | bytes 12582916
  78.1 2.9 %copy-start.8 = (bf16[4,256,2048]{2,1,0:T(8,128)(2,1)S(1)}, bf16[4,256,2048]{2,1,0:T(8,128)(2,1)}, u32[]{:S(2)}) copy-start(bf16[4,256,2048]{2,1,0:T(8,128)(2,1)} %get-tuple-element.45) | copy-start | bytes 12582916
  92.5 36.5 %copy-start.14 = (f32[32,60]{1,0:T(8,128)S(1)}, f32[32,60]{1,0:T(8,128)}, u32[]{:S(2)}) copy-start(f32[32,60]{1,0:T(8,128)} %param.27) | copy-start | bytes 23044
  92.5 36.6 %copy-start.16 = (f32[32,60]{1,0:T(8,128)S(1)}, f32[32,60]{1,0:T(8,128)}, u32[]{:S(2)}) copy-start(f32[32,60]{1,0:T(8,128)} %param.35) | copy-start | bytes 23044
  92.5 36.7 %copy-start.17 = (f32[32,60]{1,0:T(8,128)S(1)}, f32[32,60]{1,0:T(8,128)}, u32[]{:S(2)}) copy-start(f32[32,60]{1,0:T(8,128)} %param.36) | copy-start | bytes 23044
  112.7 1.6 copy-start
  114.3 1.0 copy-start.5
  118.8 36.6 %copy-start.15 = (f32[2,16,64]{2,1,0:T(8,128)S(1)}, f32[2,16,64]{2,1,0:T(8,128)}, u32[]{:S(2)}) copy-start(f32[2,16,64]{2,1,0:T(8,128)} %param.26) | copy-start | bytes 24580
  118.9 36.6 %copy-start.18 = (f32[2,16,64]{2,1,0:T(8,128)S(1)}, f32[2,16,64]{2,1,0:T(8,128)}, u32[]{:S(2)}) copy-start(f32[2,16,64]{2,1,0:T(8,128)} %param.34) | copy-start | bytes 24580
  118.9 36.6 %copy-start.19 = (f32[2,16,64]{2,1,0:T(8,128)S(1)}, f32[2,16,64]{2,1,0:T(8,128)}, u32[]{:S(2)}) copy-start(f32[2,16,64]{2,1,0:T(8,128)} %param.33) | copy-start | bytes 24580
  118.9 5.5 %collective-permute-start.27 = (f32[80,256]{1,0:T(8,128)S(1)}, f32[80,256]{1,0:T(8,128)S(1)}, u32[]{:S(2)}, u32[]{:S(2)}) collective-permute-start(f32[80,256]{1,0:T(8,128)S(1)} %pad_maximum_fusion.10), channel_id=1, source_target_pairs={{0,2},{1,3},{2,0},{3,1},{4,6},{5,7},{6,4},{7,5},{8,10},{9,11},{10,... | collective-permute-start | bytes 245768 | tf_op jit(solution)/shard_map/ppermute | solution.py:537
  124.4 4.5 %collective-permute-start.28 = (f32[80,256]{1,0:T(8,128)S(1)}, f32[80,256]{1,0:T(8,128)S(1)}, u32[]{:S(2)}, u32[]{:S(2)}) collective-permute-start(f32[80,256]{1,0:T(8,128)S(1)} %fusion.32), channel_id=1, source_target_pairs={{0,4},{1,5},{2,6},{3,7},{4,0},{5,1},{6,2},{7,3},{8,12},{9,13},{10,... | collective-permute-start | bytes 245768 | tf_op jit(solution)/shard_map/ppermute | solution.py:537
  128.9 4.5 %collective-permute-start.29 = (f32[80,256]{1,0:T(8,128)S(1)}, f32[80,256]{1,0:T(8,128)S(1)}, u32[]{:S(2)}, u32[]{:S(2)}) collective-permute-start(f32[80,256]{1,0:T(8,128)S(1)} %add.182), channel_id=1, source_target_pairs={{0,8},{1,9},{2,10},{3,11},{4,12},{5,13},{6,14},{7,15},{8,0},{9,1},... | collective-permute-start | bytes 245768 | tf_op jit(solution)/shard_map/ppermute | solution.py:537
  129.3 19.5 %collective-permute-start.18 = (bf16[8,2,4,32,128]{4,3,2,1,0:T(8,128)(2,1)}, bf16[8,2,4,32,128]{4,3,2,1,0:T(8,128)(2,1)S(1)}, u32[]{:S(2)}, u32[]{:S(2)}) collective-permute-start(bf16[8,2,4,32,128]{4,3,2,1,0:T(8,128)(2,1)} %get-tuple-element.61), channel_id=1, source_target_pairs={{0,24},{1,5},{2,26},{3,7},{4,28},{5,1},{6,30},{7,3},{8,16},{9,13},... | collective-permute-start | bytes 1572872 | tf_op jit(solution)/shard_map/ppermute | solution.py:537
  132.2 19.4 %collective-permute-start.22 = (bf16[8,2,4,32,128]{4,3,2,1,0:T(8,128)(2,1)}, bf16[8,2,4,32,128]{4,3,2,1,0:T(8,128)(2,1)S(1)}, u32[]{:S(2)}, u32[]{:S(2)}) collective-permute-start(bf16[8,2,4,32,128]{4,3,2,1,0:T(8,128)(2,1)} %get-tuple-element.63), channel_id=1, source_target_pairs={{0,8},{1,3},{2,10},{3,1},{4,12},{5,7},{6,14},{7,5},{8,0},{9,11},{1... | collective-permute-start | bytes 1572872 | tf_op jit(solution)/shard_map/ppermute | solution.py:537
  133.4 13.8 %collective-permute-start.30 = (f32[80,256]{1,0:T(8,128)S(1)}, f32[80,256]{1,0:T(8,128)S(1)}, u32[]{:S(2)}, u32[]{:S(2)}) collective-permute-start(f32[80,256]{1,0:T(8,128)S(1)} %add.183), channel_id=1, source_target_pairs={{0,24},{1,25},{2,26},{3,27},{4,28},{5,29},{6,30},{7,31},{8,16},{9,... | collective-permute-start | bytes 245768 | tf_op jit(solution)/shard_map/ppermute | solution.py:537
  137.2 42.7 %collective-permute-start.17 = (bf16[256,1024]{1,0:T(8,128)(2,1)}, bf16[256,1024]{1,0:T(8,128)(2,1)S(1)}, u32[]{:S(2)}, u32[]{:S(2)}) collective-permute-start(bf16[256,1024]{1,0:T(8,128)(2,1)} %get-tuple-element.126), channel_id=1, source_target_pairs={{0,1},{1,0},{2,3},{3,2},{4,5},{5,4},{6,7},{7,6},{8,9},{9,8},{10,11... | collective-permute-start | bytes 1572872 | tf_op jit(solution)/shard_map/ppermute | solution.py:537
  137.2 42.7 %collective-permute-start.16 = (bf16[3,256,1024]{2,1,0:T(8,128)(2,1)}, bf16[3,256,1024]{2,1,0:T(8,128)(2,1)S(1)}, u32[]{:S(2)}, u32[]{:S(2)}) collective-permute-start(bf16[3,256,1024]{2,1,0:T(8,128)(2,1)} %get-tuple-element.52), channel_id=1, source_target_pairs={{0,1},{1,0},{2,3},{3,2},{4,5},{5,4},{6,7},{7,6},{8,9},{9,8},{10,11... | collective-permute-start | bytes 4718600 | tf_op jit(solution)/shard_map/ppermute | solution.py:537
  147.2 1.3 collective-permute-start.31
  150.7 7.4 %collective-permute-start.19 = (bf16[4,2,4,32,128]{4,3,2,1,0:T(8,128)(2,1)}, bf16[4,2,4,32,128]{4,3,2,1,0:T(8,128)(2,1)}, u32[]{:S(2)}, u32[]{:S(2)}) collective-permute-start(bf16[4,2,4,32,128]{4,3,2,1,0:T(8,128)(2,1)} %get-tuple-element.123), channel_id=1, source_target_pairs={{0,8},{1,3},{2,10},{3,1},{4,12},{5,7},{6,14},{7,5},{8,0},{9,11},{1... | collective-permute-start | bytes 786440 | tf_op jit(solution)/shard_map/ppermute | solution.py:537
  152.6 9.4 %collective-permute-start.23 = (bf16[4,2,4,32,128]{4,3,2,1,0:T(8,128)(2,1)}, bf16[4,2,4,32,128]{4,3,2,1,0:T(8,128)(2,1)S(1)}, u32[]{:S(2)}, u32[]{:S(2)}) collective-permute-start(bf16[4,2,4,32,128]{4,3,2,1,0:T(8,128)(2,1)} %get-tuple-element.125), channel_id=1, source_target_pairs={{0,24},{1,5},{2,26},{3,7},{4,28},{5,1},{6,30},{7,3},{8,16},{9,13},... | collective-permute-start | bytes 786440 | tf_op jit(solution)/shard_map/ppermute | solution.py:537
  158.2 20.8 %copy-start.10 = (f32[16,64,32]{1,2,0:T(8,128)S(1)}, f32[16,64,32]{1,2,0:T(8,128)}, u32[]{:S(2)}) copy-start(f32[16,64,32]{1,2,0:T(8,128)} %param.25) | copy-start | bytes 393220
  158.2 20.8 %copy-start.11 = (f32[16,64,32]{1,2,0:T(8,128)S(1)}, f32[16,64,32]{1,2,0:T(8,128)}, u32[]{:S(2)}) copy-start(f32[16,64,32]{1,2,0:T(8,128)} %param.32) | copy-start | bytes 393220
  158.2 20.8 %copy-start.12 = (f32[16,64,32]{1,2,0:T(8,128)S(1)}, f32[16,64,32]{1,2,0:T(8,128)}, u32[]{:S(2)}) copy-start(f32[16,64,32]{1,2,0:T(8,128)} %param.31) | copy-start | bytes 393220
  159.4 5.1 %collective-permute-start.20 = (bf16[2,2,4,32,128]{4,3,2,1,0:T(8,128)(2,1)S(1)}, bf16[2,2,4,32,128]{4,3,2,1,0:T(8,128)(2,1)S(1)}, u32[]{:S(2)}, u32[]{:S(2)}) collective-permute-start(bf16[2,2,4,32,128]{4,3,2,1,0:T(8,128)(2,1)S(1)} %get-tuple-element.129), channel_id=1, source_target_pairs={{0,4},{1,25},{2,6},{3,27},{4,0},{5,29},{6,2},{7,31},{8,12},{9,17},... | collective-permute-start | bytes 393224 | tf_op jit(solution)/shard_map/ppermute | solution.py:537
  162.0 0.7 copy-start.13
  163.9 5.0 %collective-permute-start.24 = (bf16[2,2,4,32,128]{4,3,2,1,0:T(8,128)(2,1)S(1)}, bf16[2,2,4,32,128]{4,3,2,1,0:T(8,128)(2,1)S(1)}, u32[]{:S(2)}, u32[]{:S(2)}) collective-permute-start(bf16[2,2,4,32,128]{4,3,2,1,0:T(8,128)(2,1)S(1)} %get-tuple-element.131), channel_id=1, source_target_pairs={{0,2},{1,9},{2,0},{3,11},{4,6},{5,13},{6,4},{7,15},{8,10},{9,1},{1... | collective-permute-start | bytes 393224 | tf_op jit(solution)/shard_map/ppermute | solution.py:537
  164.5 5.7 %collective-permute-start.21 = (bf16[1,2,4,32,128]{4,3,2,1,0:T(8,128)(2,1)S(1)}, bf16[1,2,4,32,128]{4,3,2,1,0:T(8,128)(2,1)S(1)}, u32[]{:S(2)}, u32[]{:S(2)}) collective-permute-start(bf16[1,2,4,32,128]{4,3,2,1,0:T(8,128)(2,1)S(1)} %add_convert_fusion.10), channel_id=1, source_target_pairs={{0,2},{1,9},{2,0},{3,11},{4,6},{5,13},{6,4},{7,15},{8,10},{9,1},{1... | collective-permute-start | bytes 196616 | tf_op jit(solution)/shard_map/ppermute | solution.py:537
  168.9 11.1 %copy-start.1 = (bf16[3,256,1024]{2,1,0:T(8,128)(2,1)S(1)}, bf16[3,256,1024]{2,1,0:T(8,128)(2,1)}, u32[]{:S(2)}) copy-start(bf16[3,256,1024]{2,1,0:T(8,128)(2,1)} %get-tuple-element.51.mo) | copy-start | bytes 4718596
  168.9 4.3 %collective-permute-start.25 = (bf16[1,2,4,32,128]{4,3,2,1,0:T(8,128)(2,1)S(1)}, bf16[1,2,4,32,128]{4,3,2,1,0:T(8,128)(2,1)S(1)}, u32[]{:S(2)}, u32[]{:S(2)}) collective-permute-start(bf16[1,2,4,32,128]{4,3,2,1,0:T(8,128)(2,1)S(1)} %add_convert_fusion.8), channel_id=1, source_target_pairs={{0,4},{1,25},{2,6},{3,27},{4,0},{5,29},{6,2},{7,31},{8,12},{9,17},... | collective-permute-start | bytes 196616 | tf_op jit(solution)/shard_map/ppermute | solution.py:537
  173.4 1.4 collective-permute-start.26

commit v2 on v0

v2 whole, which is shorter than its diff:
```python
import functools

import jax
import jax.numpy as jnp
import numpy as np
from jax import lax
from jax.experimental import pallas as pl
from jax.experimental.pallas import tpu as pltpu
from jax.sharding import PartitionSpec as P

TASKS = 3
SELECT = 4
BITS = 4
STEP = 5
GAMMA = 2.0
RATE = 0.05
DECAY = 0.01
EPSILON = 1e-08
BETA_ONE = 0.5
BETA_TWO = 0.5

BF = jnp.bfloat16
F32 = jnp.float32
HIGHEST = lax.Precision.HIGHEST
TPAD = 8
GROUPS = BITS * SELECT + SELECT
GROWS = GROUPS * TPAD
ONES = 16
TILE = 512
WIDE = 1024
MIB = 1 << 20
FLOPS_MICRO = 1.2e10


def dot(a, b, ca, cb, precision=None):
    return lax.dot_general(
        a, b, (((ca,), (cb,)), ((), ())), preferred_element_type=F32, precision=precision
    )


def params(mib):
    return pltpu.CompilerParams(vmem_limit_bytes=mib * MIB)


def kernel_call(body, outs, scratch, mib, micros, smem, *args, after=()):
    in_vmem = pl.BlockSpec(memory_space=pltpu.VMEM)
    in_smem = pl.BlockSpec(memory_space=pltpu.SMEM)
    anywhere = pl.BlockSpec(memory_space=pl.ANY)
    n_in, n_after = len(args), len(after)

    def kernel(*refs):
        body(*refs[:n_in], *refs[n_in + n_after :])

    return pl.pallas_call(
        kernel,
        out_shape=tuple(jax.ShapeDtypeStruct(shape, kind) for shape, kind in outs),
        in_specs=[in_smem] * smem + [in_vmem] * (len(args) - smem) + [anywhere] * len(after),
        out_specs=(in_vmem,) * len(outs),
        scratch_shapes=[pltpu.VMEM(shape, kind) for shape, kind in scratch],
        compiler_params=params(mib),
        cost_estimate=pl.CostEstimate(
            flops=int(micros * FLOPS_MICRO), bytes_accessed=0, transcendentals=0
        ),
    )(*args, *after)


def gate_parts(z_of, a_of, high):
    smooth, clipped = {}, {}
    for k in range(SELECT):
        for b in range(BITS):
            v = jnp.clip(z_of(b, k), -0.5 * GAMMA, 0.5 * GAMMA)
            clipped[b, k] = v
            smooth[b, k] = v * (1.5 / GAMMA - 2.0 / GAMMA**3 * v * v) + 0.5
    a = [a_of(k) for k in range(SELECT)]
    top = functools.reduce(jnp.maximum, a)
    ex = [jnp.exp(v - top) for v in a]
    inv = 1.0 / functools.reduce(jnp.add, ex)
    alpha = [v * inv for v in ex]
    last = BITS - 1
    f_high = [
        high * smooth[last, k] + (1.0 - high) * (1.0 - smooth[last, k]) for k in range(SELECT)
    ]
    return alpha, smooth, clipped, f_high


def fac(smooth, b, k, bit):
    return smooth[b, k] if bit else 1.0 - smooth[b, k]


def part_of(i, tile):
    return pl.ds(pl.multiple_of(i * tile, tile), tile)


def prep_kernel(
    masks, at, order, sel, b_own, b_side, xo, xr, go, gr,
    xt, gt, cc_a, cc_b, gates, logits, selp, gb1, perm, to_q, b0, b1, mul,
):
    core, row, hid = at[0], at[1], at[2]
    high = core.astype(F32)
    rows, width = xo.shape
    tile = min(WIDE, rows)
    steps = rows // tile

    depth = width // (1 << len(masks))
    square = (width, width)
    up = lax.broadcasted_iota(jnp.int32, square, 0)
    across = lax.broadcasted_iota(jnp.int32, square, 1)

    def d_of(spot):
        block, out = spot // depth, row
        for b, m in enumerate(masks):
            out = out ^ (((block >> b) & 1) * m)
        return out * depth + spot % depth

    def q_of(spot):
        lanes = width // 4
        return (hid ^ (spot // lanes)) * lanes + spot % lanes

    one = lambda same: same.astype(F32)
    perm[...] = one(d_of(up) == across).astype(BF)
    to_q[...] = one(q_of(up) == across).astype(BF)
    pieces = []
    for ref in (b_own, b_side):
        for k in range(2):
            block = ref[k * 32 : (k + 1) * 32, :].astype(F32)
            block = block[:, :64] + block[:, 64:]
            pieces.append(block)
    take = lambda x, k: jnp.where(core == 0, x[16 * k : 16 * k + 8], x[16 * k + 8 : 16 * k + 16])
    bias = [jnp.concatenate([take(x, k) for x in pieces], axis=1) for k in range(2)]
    b0[...] = dot(one(up == across), 0.5 * bias[0], 1, 1, HIGHEST)
    b1[...] = dot(one(d_of(up) == q_of(across)), bias[1], 1, 1, HIGHEST)

    selp[...] = dot(order[...], sel[...], 1, 1).astype(BF)
    gb1[...] = jnp.zeros_like(gb1)
    xt[width : width + ONES, :] = jnp.ones((ONES, xt.shape[1]), BF)

    def step(i, x_ref, g_ref, first):
        here, out = part_of(i, tile), part_of(i + first, tile)
        x_t = dot(perm[...], x_ref[here, :], 1, 1).astype(BF)
        xt[0:width, out] = x_t
        lg = dot(selp[...], x_t, 1, 0)
        logits[:, out] = lg

        def z_of(b, k):
            at = (b * SELECT + k) * TPAD
            return lg[at : at + TPAD]

        def a_of(k):
            at = (BITS * SELECT + k) * TPAD
            return lg[at : at + TPAD]

        alpha, smooth, _, f_high = gate_parts(z_of, a_of, high)
        gate = [None] * 8
        for k in range(SELECT):
            base = alpha[k] * f_high[k]
            for e2 in range(2):
                w2 = base * fac(smooth, 2, k, e2)
                for e1 in range(2):
                    w1 = w2 * fac(smooth, 1, k, e1)
                    for e0 in range(2):
                        e = 4 * e2 + 2 * e1 + e0
                        w0 = w1 * fac(smooth, 0, k, e0)
                        gate[e] = w0 if gate[e] is None else gate[e] + w0
        g_t = []
        for t in range(TASKS):
            g = dot(perm[...], g_ref[t, here, :], 1, 1)
            gt[t, :, out] = g.astype(BF)
            g_t.append(g)
        ones = jnp.ones((8, tile), BF)
        for e in range(8):
            gates[e, :, out] = gate[e]
            c = gate[e][0:1] * g_t[0]
            for t in range(1, TASKS):
                c = c + gate[e][t : t + 1] * g_t[t]
            c = c.astype(BF)
            cc = cc_a if e < 4 else cc_b
            cc[e % 4, :, out] = c
            gb1[e] += dot(ones, c, 1, 1)

    @pl.loop(0, steps)
    def _(i):
        step(i, xo, go, 0)

    @pl.loop(0, steps)
    def _(i):
        step(i, xr, gr, steps)


def prep(masks, at, order, sel, b_own, b_side, x_own, x_recv, g_own, g_recv, after):
    rows, width = x_own.shape
    total = 2 * rows
    return kernel_call(
        functools.partial(prep_kernel, masks),
        (
            ((width + ONES, total), BF),
            ((TASKS, width, total), BF),
            ((4, width, total), BF),
            ((4, width, total), BF),
            ((8, TPAD, total), F32),
            ((GROWS, total), F32),
            ((GROWS, width), BF),
            ((8, 8, width), F32),
            ((width, width), BF),
            ((width, width), BF),
            ((width, 8), F32),
            ((width, 8), F32),
        ),
        (((8, 128), F32),),
        16,
        7.5,
        1,
        at, order, sel, b_own, b_side, x_own, x_recv, g_own, g_recv,
        after=after,
    )


def lanes_out(x):
    return jnp.concatenate([x[:, :128], x[:, 128:]], axis=0)


def lanes_in(x):
    rows = x.shape[0] // 2
    return jnp.concatenate([x[:rows], x[rows:]], axis=1)


def critical_kernel(second, spots, back, *refs):
    if second:
        (at_core, w_lo, w_hi, xt, cc, b0, gb0_a, gb1, to_q, perm,
         g_lo, g_hi, hid, gp, e_all, r_all, acc_e, acc_r) = refs
    else:
        (at_core, w_lo, w_hi, xt, cc, b0,
         g_lo, g_hi, hid, gp, e_all, r_all, gb0, acc_e, acc_r) = refs
    core = at_core[0]
    chunk, width, total = cc.shape
    lanes = w_lo.shape[1]
    hidden = 2 * lanes
    blocks = 8
    depth = width // blocks
    first = chunk if second else 0

    def each_block(table, lo, hi, visit):
        for q in range(blocks):
            for side in range(2):
                at = jnp.where(core == 0, table[0][2 * q + side], table[1][2 * q + side])
                rows = slice(q * depth, (q + 1) * depth)

                def cols(e, side=side):
                    return slice(e * hidden + side * lanes, e * hidden + (side + 1) * lanes)

                @pl.when(at < blocks)
                def _():
                    visit(lo, at, rows, cols)

                @pl.when(at >= blocks)
                def _():
                    visit(hi, at - blocks, rows, cols)

    def unpack(ref, at, rows, cols):
        for e in range(chunk):
            for which, out in ((0, e_all), (1, r_all)):
                spot = pl.multiple_of(((at * 2 + which) * chunk + e) * depth, depth)
                out[rows, cols(e)] = ref[pl.ds(spot, depth), :]

    each_block(spots, w_lo, w_hi, unpack)

    sums = []
    for e in range(chunk):
        cols = slice(e * hidden, (e + 1) * hidden)
        e_t = (e_all[:, cols] * 0.5).T
        r = (r_all[:, cols] * 0.5).T
        add = b0[:, first + e : first + e + 1]
        for i in range(total // TILE):
            part = slice(i * TILE, (i + 1) * TILE)
            u = dot(e_t, xt[0:width, part], 1, 0) + add
            t = jnp.tanh(u)
            plus = 1.0 + t
            h = u * plus
            hid[e, :, part] = h.astype(BF)
            gh = dot(r, cc[e, :, part], 1, 0)
            gp[e, :, part] = (gh * (plus + h * (1.0 - t))).astype(BF)
        acc_e[:, cols] = dot(xt[...], gp[e], 1, 1)
        acc_r[:, cols] = dot(cc[e], hid[e], 1, 1)
        sums.append(acc_e[width : width + 1, cols])

    def pack(ref, at, rows, cols):
        for e in range(chunk):
            ref[pl.ds(pl.multiple_of((at * 2 * chunk + e) * depth, depth), depth), :] = acc_e[
                rows, cols(e)
            ].astype(BF)
            ref[
                pl.ds(pl.multiple_of(((at * 2 + 1) * chunk + e) * depth, depth), depth), :
            ] = acc_r[rows, cols(e)].astype(BF)

    each_block(back, g_lo, g_hi, pack)
    sums = jnp.concatenate(sums, axis=0)
    if second:
        mine = jnp.concatenate([gb0_a[...], sums], axis=0).astype(BF)
        outer = jnp.concatenate([gb1[e, 0:1] for e in range(2 * chunk)], axis=0).astype(BF)
        both = jnp.concatenate(
            [dot(mine, to_q[...], 1, 0), dot(outer, perm[...], 1, 0)], axis=0
        ).astype(BF)
        g_hi[2 * chunk * width :, :] = lanes_out(both)
    else:
        gb0[...] = sums


def critical(spots, back, at, w_lo, w_hi, xt, cc, b0, after, more=None):
    chunk, width, total = cc.shape
    rows, lanes = w_lo.shape
    hidden = 2 * lanes
    outs = [
        ((rows, lanes), BF),
        ((rows + (8 * chunk if more else 0), lanes), BF),
        ((chunk, hidden, total), BF),
        ((chunk, hidden, total), BF),
        ((width, chunk * hidden), BF),
        ((width, chunk * hidden), BF),
    ]
    if not more:
        outs.append(((chunk, hidden), F32))
    return kernel_call(
        functools.partial(critical_kernel, more is not None, spots, back),
        tuple(outs),
        (((width + ONES, chunk * hidden), F32), ((width, chunk * hidden), F32)),
        16,
        7.6,
        1,
        at, w_lo, w_hi, xt, cc, b0, *(more or ()),
        after=after,
    )


def add_low(a, b):
    return (a.astype(F32) + b.astype(F32)).astype(BF)


def fold_kernel(n_small, *refs):
    lo, sent, got, *more, keep, msg = refs
    rows = lo.shape[0]
    half = rows // 2
    keep[...] = add_low(lo[0:half, :], got[0:half, :])
    msg[0:half, :] = add_low(lo[half:rows, :], got[half:rows, :])
    small = sent.shape[0] - rows
    if small:
        msg[half : half + small, :] = add_low(sent[rows:, :], got[rows:, :])
    if n_small:
        msg[half + small :, :] = add_low(more[0][...], more[1][...])


def fold(lo, sent, got, more=(), after=()):
    rows, lanes = lo.shape
    small = sent.shape[0] - rows + (more[0].shape[0] if more else 0)
    return kernel_call(
        functools.partial(fold_kernel, len(more)),
        (((rows // 2, lanes), BF), ((rows // 2 + small, lanes), BF)),
        (),
        8,
        0.3,
        0,
        lo, sent, got, *more,
        after=after,
    )


def append_kernel(msg, one, two, out):
    rows = msg.shape[0]
    out[0:rows, :] = msg[...]
    out[rows:, :] = add_low(one[...], two[...])


def append(msg, one, two, after):
    rows, lanes = msg.shape
    (out,) = kernel_call(
        append_kernel,
        (((rows + one.shape[0], lanes), BF),),
        (),
        8,
        0.3,
        0,
        msg, one, two,
        after=after,
    )
    return out


def last_fold_kernel(a_lo, a_got, b_lo, b_sent, b_got, own, msg):
    half = a_lo.shape[1] // 2
    rows = a_lo.shape[0] // 2
    for i, (lo, got) in enumerate(((a_lo, a_got), (b_lo, b_got))):
        e = lo[0:rows, :].astype(F32) + got[0:rows, :].astype(F32)
        r = lo[rows : 2 * rows, :].astype(F32) + got[rows : 2 * rows, :].astype(F32)
        here = slice(i * rows, (i + 1) * rows)
        own[here, :] = jnp.concatenate([e[:, :half], r[:, :half]], axis=1)
        msg[here, :] = jnp.concatenate([e[:, half:], r[:, half:]], axis=1).astype(BF)
    msg[2 * rows :, :] = add_low(b_sent[2 * rows :, :], b_got[2 * rows :, :])


def last_fold(a_lo, a_got, b_lo, b_sent, b_got):
    rows, lanes = a_lo.shape
    small = b_sent.shape[0] - rows
    return kernel_call(
        last_fold_kernel,
        (((rows, lanes), F32), ((rows + small, lanes), BF)),
        (),
        8,
        0.3,
        0,
        a_lo, a_got, b_lo, b_sent, b_got,
    )


def outer_kernel(start, *refs):
    if start:
        at_core, order, r_a, hid_a, r_b, hid_b, gt, logits, b1, x, acc_in, ys, gls, gsel, acc = refs
        acc[...] = acc_in[...]
    else:
        at_core, order, r_a, hid_a, r_b, hid_b, gt, logits, b1, x, ys, gls, acc = refs
        acc[...] = jnp.zeros_like(acc)
    high = at_core[0].astype(F32)
    sign = 2.0 * high - 1.0
    rows, width = x.shape
    chunk, hidden, _ = hid_a.shape
    tile = min(WIDE, rows)

    @pl.loop(0, rows // tile)
    def _(i):
        here, part = part_of(i, tile), part_of(i + start // tile, tile)
        gg = []
        wide = [gt[t, :, part].astype(F32) for t in range(TASKS)]
        for e in range(2 * chunk):
            r_all, hid = (r_a, hid_a) if e < chunk else (r_b, hid_b)
            at = e % chunk
            y = dot(r_all[:, at * hidden : (at + 1) * hidden], hid[at, :, part], 1, 0)
            y = y + b1[:, e : e + 1]
            ys[e, :, here] = y.astype(BF)
            sums = [jnp.sum(wide[t] * y, axis=0, keepdims=True) for t in range(TASKS)]
            gg.append(jnp.concatenate(sums + [jnp.zeros((TPAD - TASKS, tile), F32)], axis=0))
        gl = gate_back(
            lambda b, k: logits[(b * SELECT + k) * TPAD : (b * SELECT + k + 1) * TPAD, part],
            lambda k: logits[
                (BITS * SELECT + k) * TPAD : (BITS * SELECT + k + 1) * TPAD, part
            ],
            gg, high, sign,
        ).astype(BF)
        gls[:, here] = gl
        acc[...] += dot(gl, x[here, :], 1, 0)

    if start:
        gsel[...] = lanes_out(dot(order[:, 0:64], acc[...].astype(BF), 0, 0)).astype(BF)


def outer(start, at, order, first, second, gt, logits, b1, x, acc=None, after=()):
    rows, width = x.shape
    (r_a, hid_a), (r_b, hid_b) = first, second
    chunk, hidden, _ = hid_a.shape
    outs = [((2 * chunk, width, rows), BF), ((GROWS, rows), BF)]
    scratch = ()
    if start:
        outs.append(((order.shape[1], 128), BF))
        scratch = (((GROWS, width), F32),)
    else:
        outs.append(((GROWS, width), F32))
    return kernel_call(
        functools.partial(outer_kernel, start),
        tuple(outs),
        scratch,
        16,
        4.3,
        1,
        at, order, r_a, hid_a, r_b, hid_b, gt, logits, b1, x, *((acc,) if start else ()),
        after=after,
    )


def mix_kernel(start, e_a, gp_a, e_b, gp_b, selp, ys, gls, gates, out):
    count, width, rows = ys.shape
    chunk, hidden, _ = gp_a.shape
    tile, depth = 256, 32

    @pl.loop(0, rows // tile)
    def _(i):
        here, part = part_of(i, tile), part_of(i + start // tile, tile)
        v = dot(e_a[...], gp_a[:, :, part].reshape(chunk * hidden, tile), 1, 0)
        v = v + dot(e_b[...], gp_b[:, :, part].reshape(chunk * hidden, tile), 1, 0)
        out[TASKS, :, here] = (v + dot(selp[...], gls[:, here], 0, 0)).astype(BF)
        for d in range(width // depth):
            block = slice(d * depth, (d + 1) * depth)
            sums = [None] * TASKS
            for e in range(count):
                y = ys[e, block, here].astype(F32)
                for t in range(TASKS):
                    m = gates[e, t : t + 1, part] * y
                    sums[t] = m if e == 0 else sums[t] + m
            for t in range(TASKS):
                out[t, block, here] = sums[t].astype(BF)


def mix(start, first, second, selp, ys, gls, gates, after):
    (e_a, gp_a), (e_b, gp_b) = first, second
    count, width, rows = ys.shape
    chunk, hidden, _ = gp_a.shape
    (out,) = kernel_call(
        functools.partial(mix_kernel, start),
        (((TASKS + 1, width, rows), BF),),
        (),
        16,
        4.0,
        0,
        e_a, gp_a, e_b, gp_b, selp, ys, gls, gates,
        after=after,
    )
    return out


def gate_back(z_of, a_of, gg, high, sign):
    alpha, smooth, clipped, f_high = gate_parts(z_of, a_of, high)
    out = [None] * GROUPS
    d_alpha = []
    for k in range(SELECT):
        f = [[fac(smooth, b, k, bit) for bit in range(2)] for b in range(BITS - 1)]
        low, dif = {}, {}
        for e2 in range(2):
            for e1 in range(2):
                p, q = gg[4 * e2 + 2 * e1], gg[4 * e2 + 2 * e1 + 1]
                low[e2, e1] = f[0][0] * p + f[0][1] * q
                dif[e2, e1] = q - p
        mid = [f[1][0] * low[e2, 0] + f[1][1] * low[e2, 1] for e2 in range(2)]
        mid1 = [low[e2, 1] - low[e2, 0] for e2 in range(2)]
        mid0 = [f[1][0] * dif[e2, 0] + f[1][1] * dif[e2, 1] for e2 in range(2)]
        t0 = f[2][0] * mid[0] + f[2][1] * mid[1]
        d2 = mid[1] - mid[0]
        d1 = f[2][0] * mid1[0] + f[2][1] * mid1[1]
        d0 = f[2][0] * mid0[0] + f[2][1] * mid0[1]
        d_alpha.append(f_high[k] * t0)
        scale = alpha[k] * f_high[k]
        for b, d in enumerate((scale * d0, scale * d1, scale * d2, alpha[k] * sign * t0)):
            v = clipped[b, k]
            out[b * SELECT + k] = d * (1.5 / GAMMA - 6.0 / GAMMA**3 * v * v)
    total = functools.reduce(jnp.add, [a * d for a, d in zip(alpha, d_alpha)])
    for k in range(SELECT):
        out[BITS * SELECT + k] = alpha[k] * (d_alpha[k] - total)
    return jnp.concatenate(out, axis=0)


def final_kernel(perm, own, recv, mixed, gf):
    for t in range(TASKS + 1):
        s = (own[t].astype(F32) + recv[t].astype(F32)).astype(BF)
        rows = dot(s, perm[...], 0, 0).astype(BF)
        if t < TASKS:
            mixed[t] = rows
        else:
            gf[...] = rows


def final(perm, own, recv, after):
    _, width, rows = own.shape
    return kernel_call(
        final_kernel,
        (((TASKS, rows, width), BF), ((rows, width), BF)),
        (),
        16,
        2.7,
        0,
        perm, own, recv,
        after=after,
    )


def adamw(weight, grad, first, second):
    first = BETA_ONE * first + (1.0 - BETA_ONE) * grad
    second = BETA_TWO * second + (1.0 - BETA_TWO) * grad * grad
    mhat = first / (1.0 - BETA_ONE**STEP)
    vhat = second / (1.0 - BETA_TWO**STEP)
    weight = weight - RATE * (mhat / (jnp.sqrt(vhat) + EPSILON) + DECAY * weight)
    return (first, second, weight)


def pack_kernel(with_w, core, w_e, w_r, w_b, w_s, sel, bias, *refs):
    first = core[0] == 0
    sel[...] = jnp.zeros_like(sel)
    sel[:, 0 : w_s.shape[1]] = w_s[...].astype(BF)
    experts, lanes = w_b.shape[1:]
    for k in range(2):
        high = w_b[k].astype(BF)
        low = (w_b[k] - high.astype(F32)).astype(BF)
        bias[k * experts : (k + 1) * experts, :] = jnp.concatenate(
            [high.astype(F32), low.astype(F32)], axis=1
        ).astype(BF)
    if with_w:
        mine, other = refs
        count = experts // 2
        for e in range(count):
            for which in range(2):
                lo, hi = (
                    (w_r[e], w_r[e + count]) if which else (w_e[:, e, :], w_e[:, e + count, :])
                )
                mine[which, e] = jnp.where(first, lo, hi).astype(BF)
                other[which, e] = jnp.where(first, hi, lo).astype(BF)


def pack(core, w_e, w_r, w_b, w_s, with_w):
    experts, depth, lanes = w_r.shape
    half = (2, experts // 2, depth, lanes)
    outs = [((depth, 2 * lanes), BF), ((2 * experts, 2 * lanes), BF)]
    if with_w:
        outs += [(half, BF), (half, BF)]
    block = lambda shape: pl.BlockSpec(shape, lambda i: (0,) * len(shape))
    return pl.pallas_call(
        functools.partial(pack_kernel, with_w),
        grid=(1,),
        out_shape=tuple(jax.ShapeDtypeStruct(shape, kind) for shape, kind in outs),
        in_specs=[pl.BlockSpec(memory_space=pltpu.SMEM)]
        + [block(x.shape) for x in (w_e, w_r, w_b, w_s)],
        out_specs=tuple(block(shape) for shape, _ in outs),
        compiler_params=params(8),
    )(core, w_e, w_r, w_b, w_s)


def join_kernel(plan, n_in, *refs):
    ins, outs = refs[:n_in], refs[n_in:]
    for out, pieces in zip(outs, plan):
        to = 0
        for k, start, rows in pieces:
            out[to : to + rows, :] = ins[k][start : start + rows, :]
            to += rows


def join(plan, *ins, after=()):
    lanes = ins[0].shape[1]
    return kernel_call(
        functools.partial(join_kernel, plan, len(ins)),
        tuple(((sum(p[2] for p in pieces), lanes), BF) for pieces in plan),
        (),
        8,
        0.3,
        0,
        *ins,
        after=after,
    )


def chip_kernel(mine, recv, sel, msg):
    _, count, depth, lanes = mine.shape
    for which in range(2):
        for e in range(count):
            to = (which * count + e) * depth
            msg[to : to + depth, :] = jnp.concatenate([mine[which, e], recv[which, e]], axis=1)
    msg[2 * count * depth :, :] = sel[...]


def chip_message(mine, recv, sel):
    _, count, depth, lanes = mine.shape
    rows = 2 * count * depth
    (msg,) = kernel_call(
        chip_kernel, (((rows + sel.shape[0], 2 * lanes), BF),), (), 8, 0.3, 0,
        mine, recv, sel,
    )
    return msg


def update_kernel(
    at, own, sent, got, w_e, m_e, v_e, w_r, m_r, v_r, w_b, m_b, v_b, w_s, m_s, v_s, *refs
):
    outs, (g_e,) = refs[:-1], refs[-1:]
    core, row, hid = at[0], at[1], at[2]
    first = core == 0
    experts, depth, lanes = w_r.shape
    count = experts // 2
    n_own = own.shape[0]
    theirs = got[0:n_own, :].astype(F32)
    halves = (jnp.where(first, own[...], theirs), jnp.where(first, theirs, own[...]))

    def store(k, new):
        for ref, value in zip(outs[3 * k : 3 * k + 3], new):
            ref[...] = value

    parts = []
    for half in halves:
        for e in range(count):
            rows = half[e * depth : (e + 1) * depth]
            g_e[:, len(parts), :] = rows[:, :lanes]
            parts.append(rows[:, lanes:])
    store(0, adamw(w_e[...], g_e[...], m_e[...], v_e[...]))
    store(1, adamw(w_r[...], jnp.stack(parts), m_r[...], v_r[...]))

    n_bias = 8 * count // 2
    small, small_got = sent[n_own:, :], got[n_own:, :]
    bias = [lanes_in(x[0:n_bias]) for x in (small, small_got)]
    width = bias[0].shape[1]
    spot = lax.broadcasted_iota(jnp.int32, (width, lanes), 0)
    lane = lax.broadcasted_iota(jnp.int32, (width, lanes), 1)
    pick = (spot == hid * lanes + lane).astype(F32).astype(BF)
    mine, other = [dot(x, pick, 1, 0) for x in bias]
    lo, hi = jnp.where(first, mine, other), jnp.where(first, other, mine)
    g_b = jnp.stack(
        [jnp.concatenate([x[k * count : (k + 1) * count] for x in (lo, hi)], axis=0) for k in range(2)]
    )
    store(2, adamw(w_b[...], g_b, m_b[...], v_b[...]))

    g_s = lanes_in(add_low(small[n_bias:], small_got[n_bias:]))
    spot = lax.broadcasted_iota(jnp.int32, (depth, width), 0)
    lane = lax.broadcasted_iota(jnp.int32, (depth, width), 1)
    pick = (lane == row * depth + spot).astype(F32).astype(BF)
    g_s = dot(pick, g_s, 1, 1)[:, : w_s.shape[1]]
    store(3, adamw(w_s[...], g_s, m_s[...], v_s[...]))


def update(at, own, sent, got, *params):
    outs = []
    for k in range(4):
        outs += [(params[3 * k].shape, F32)] * 3
    return kernel_call(
        update_kernel,
        tuple(outs),
        ((params[0].shape, F32),),
        16,
        2.4,
        1,
        at, own, sent, got, *params,
    )


def logit_order():
    order = np.zeros((GROWS, 128), np.float32)
    for t in range(TASKS):
        for k in range(SELECT):
            for b in range(BITS):
                order[(b * SELECT + k) * TPAD + t, (t * SELECT + k) * BITS + b] = 1.0
            at = (BITS * SELECT + k) * TPAD + t
            order[at, TASKS * SELECT * BITS + t * SELECT + k] = 1.0
    return order


def per_device(
    n_rows,
    n_hid,
    features,
    w_expand,
    w_reduce,
    biases,
    w_select,
    grad_mix,
    m_expand,
    v_expand,
    m_reduce,
    v_reduce,
    m_biases,
    v_biases,
    m_select,
    v_select,
):
    d_loc, experts, h_loc = w_expand.shape
    width = d_loc * n_rows
    mine_n = experts // 2
    chunk = mine_n // 2
    row = lax.axis_index("rows")
    hid_at = lax.axis_index("hid")
    core = hid_at % 2

    bits = n_rows.bit_length() - 1
    masks = [1 << b for b in range(bits)]
    side = (0, 2)
    sibling = ((0, 1), (0, 1))
    dims = [side] + [(m, 0) for m in masks]
    if n_rows == 8:
        way = ((3, 2, 0, 1), (1, 3, 2, 0))
    else:
        way = (tuple(range(len(dims))),) * 2

    def swap(x, hops):
        pairs = []
        for r in range(n_rows):
            for h in range(n_hid):
                mr, mh = hops[h % 2]
                pairs.append((r * n_hid + h, (r ^ mr) * n_hid + (h ^ mh)))
        return lax.ppermute(x, ("rows", "hid"), pairs)

    def hops(step):
        return tuple(dims[way[k][step]] for k in range(2))

    def table_of(pair):
        if n_rows != 8:
            return (tuple(range(16)),) * 2
        both = []
        for order in pair:
            spots = []
            for q in range(8):
                for s in range(2):
                    on = [s] + [(q >> b) & 1 for b in range(3)]
                    spots.append(sum(on[d] << order.index(d) for d in range(4)))
            both.append(tuple(spots))
        return tuple(both)

    order = jnp.asarray(logit_order(), BF)
    at = jnp.stack([core, row, hid_at]).astype(jnp.int32)

    def split_experts(x, axis):
        mine = lax.dynamic_slice_in_dim(x, core * mine_n, mine_n, axis)
        other = lax.dynamic_slice_in_dim(x, (1 - core) * mine_n, mine_n, axis)
        return mine, other

    def tie(x, *after):
        return lax.optimization_barrier((x, after))[0]

    part = n_rows // 8

    def canonical(lo, hi):
        w = jnp.concatenate([lo, hi], axis=0).reshape(8, part, 2, 2, chunk, d_loc, 2 * h_loc)
        w = jnp.transpose(w, (0, 2, 3, 4, 1, 5, 6)).reshape(2, -1, 2 * h_loc)
        return w[0], w[1]

    def uncanonical(lo, hi):
        if n_rows == 8:
            return lo, hi
        w = jnp.concatenate([lo, hi], axis=0).reshape(8, 2, 2, chunk, part, d_loc, 2 * h_loc)
        w = jnp.transpose(w, (0, 4, 1, 2, 3, 5, 6)).reshape(2, -1, 2 * h_loc)
        return w[0], w[1]

    w_r_view = jnp.transpose(w_reduce, (0, 2, 1))
    packed = pack(at, w_expand, w_r_view, biases, w_select, d_loc % 16 == 0)
    sel, b_own = packed[:2]
    if d_loc % 16 == 0:
        w_mine, w_other = packed[2:]
    else:
        w_mine, w_other = split_experts(
            jnp.stack([jnp.transpose(w_expand, (1, 0, 2)), w_r_view]).astype(BF), 1
        )
    w_recv = swap(w_other, sibling)
    b_own = jnp.concatenate([b_own, swap(b_own, sibling)], axis=0)
    x_own = features
    g_own = jnp.transpose(grad_mix, (1, 0, 2))
    x_recv = swap(x_own, sibling)
    g_recv = swap(g_own, sibling)

    steps = len(dims)
    ride = n_rows == 8
    if ride:
        whole = 2 * mine_n * d_loc
        msg = chip_message(w_mine, w_recv, sel)
        got = swap(msg, hops(0))
        (msg,) = join(
            (((0, 0, whole), (1, 0, whole), (0, whole, d_loc), (1, whole, d_loc)),), msg, got
        )
        got = swap(msg, hops(1))
        half = whole // 2
        group = chunk * d_loc
        pieces = [
            tuple((k, (2 * j + c) * group, group) for k in range(2) for j in range(4))
            for c in range(2)
        ]
        tail = tuple((k, 2 * whole, 2 * d_loc) for k in range(2)) + ((2, 0, 4 * experts),)
        a_msg, b_msg = join((pieces[0] + tail, pieces[1]), msg, got, b_own)
        a_got = swap(a_msg, hops(2))
        n = 8 * group
        a_lo, riders = join(
            (
                ((0, 0, n), (1, 0, n)),
                ((0, n, 4 * d_loc), (1, n, 4 * d_loc), (1, n + 4 * d_loc, 4 * experts)),
            ),
            a_msg, a_got,
        )
        a_hi = swap(a_lo, hops(3))
        turned = swap(riders, sibling)
        b_got = swap(tie(b_msg, a_lo), hops(2))
        last = a_lo
        sel = jnp.where(core == 1, riders[:width], turned[:width])
        sel = jnp.transpose(sel.reshape(2, 2, 2, d_loc, 2 * h_loc), (1, 0, 2, 3, 4))
        sel = sel.reshape(width, 2 * h_loc)
        n_b = 2 * experts
        turned = jnp.concatenate([turned[width + n_b :], turned[width : width + n_b]], axis=0)
        b_side = jnp.where(core == 0, riders[width:], turned)
    else:
        chip = jnp.concatenate([w_mine, w_recv], axis=3)
        bufs = [chip[None, :, :chunk], chip[None, :, chunk:]]
        for step in range(steps):
            gots = [swap(buf, hops(step)) for buf in bufs]
            if step + 1 < steps:
                bufs = [jnp.concatenate(pair, axis=0) for pair in zip(bufs, gots)]
        for m in masks:
            sel = jnp.concatenate([sel, swap(sel, ((m, 0), (m, 0)))], axis=0)
        b_side = swap(b_own, (side, side))
        (a_lo, a_hi), (b_lo, b_hi) = [canonical(*pair) for pair in zip(bufs, gots)]
        last = a_lo

    xt, gt, cc_a, cc_b, gates, logits, selp, gb1, perm, to_q, b0, b1 = prep(
        masks, at, order, sel, b_own, b_side, x_own, x_recv, g_own, g_recv, (last,)
    )

    spots = table_of(way)
    if ride:
        (b_lo,) = join((((0, 0, n), (1, 0, n)),), b_msg, b_got, after=(b0,))
        b_hi = swap(b_lo, hops(3))
    first = critical(spots, spots, at, a_lo, a_hi, xt, cc_a, b0, (b_lo,))
    a_lo, a_msg = uncanonical(first[0], first[1])
    a_got = swap(a_msg, hops(steps - 1))
    second = critical(
        spots, spots, at, b_lo, b_hi, xt, cc_b, b0, (first[0],), (first[6], gb1, to_q, perm)
    )
    b_lo, b_msg = second[:2]
    if not ride:
        n = b_lo.shape[0]
        b_lo, b_msg = uncanonical(b_lo, b_msg[:n])
        b_msg = jnp.concatenate([b_msg, second[1][n:]], axis=0)
    b_got = swap(b_msg, hops(steps - 1))
    inner = ((first[5], first[2]), (second[5], second[2]))
    ends = ((first[4], first[3]), (second[4], second[3]))
    n_own = x_own.shape[0]
    ys_own, gl_own, acc = outer(0, at, order, *inner, gt, logits, b1, x_own)

    def next_a(step, lo, sent, got, after=()):
        keep, msg = fold(lo, sent, got, (), after)
        return keep, msg, swap(msg, hops(step))

    a_lo, a_msg, a_got = next_a(steps - 2, a_lo, a_msg, a_got, (b_lo,))
    ys_other, gl_other, gsel = outer(
        n_own, at, order, *inner, gt, logits, b1, x_recv, acc, (a_lo,)
    )
    gsel_got = swap(gsel, hops(steps - 1))
    b_lo, b_msg = fold(b_lo, b_msg, b_got)
    a_lo, a_msg, a_got = next_a(steps - 3, a_lo, a_msg, a_got)
    mix_other = mix(n_own, *ends, selp, ys_other, gl_other, gates, (a_lo, b_lo))
    mix_recv = swap(mix_other, sibling)
    b_msg = append(b_msg, gsel, gsel_got, (mix_other,))
    b_got = swap(b_msg, hops(steps - 2))
    mix_own = mix(0, *ends, selp, ys_own, gl_own, gates, (b_msg,))
    for step in reversed(range(steps - 3)):
        a_lo, a_msg, a_got = next_a(step, a_lo, a_msg, a_got)
    mixed, grad_features = final(perm, mix_own, mix_recv, (a_lo,))
    for step in reversed(range(steps - 2)):
        b_lo, b_msg = fold(b_lo, b_msg, b_got, (), (grad_features,))
        b_got = swap(b_msg, hops(step))
    own, msg = last_fold(a_lo, a_got, b_lo, b_msg, b_got)
    got = swap(msg, sibling)
    mixed = jnp.transpose(mixed, (1, 0, 2))

    flip = lambda x: jnp.transpose(x, (0, 2, 1))
    new = list(
        update(
            at, own, msg, got,
            w_expand, m_expand, v_expand,
            w_r_view, flip(m_reduce), flip(v_reduce),
            biases, m_biases, v_biases,
            w_select, m_select, v_select,
        )
    )
    new[3:6] = [flip(x) for x in new[3:6]]
    return (mixed, grad_features, *new)


def solution(mesh):
    row_split = P(("rows", "hid"), None)
    task_split = P(("rows", "hid"), None, None)
    expand = P("rows", None, "hid")
    reduce = P(None, "hid", "rows")
    bias = P(None, None, "hid")
    select = P("rows", None)
    return jax.shard_map(
        functools.partial(per_device, mesh.shape["rows"], mesh.shape["hid"]),
        mesh=mesh,
        in_specs=(
            row_split, expand, reduce, bias, select, task_split,
            expand, expand, reduce, reduce, bias, bias, select, select,
        ),
        out_specs=(
            task_split, row_split,
            expand, expand, expand,
            reduce, reduce, reduce,
            bias, bias, bias,
            select, select, select,
        ),
        check_vma=False,
    )
```

time: 578 us -> 116 us (0.20); the launches traced: 570 us -> 115 us
  local copies, waits for them, and re-layouts: 174 us -> 9.97 us
  blocking collectives: 152 us -> 0 us
  waiting for transfers between devices: 118 us -> 31.7 us
  matrix products: 82.8 us -> 0 us
  Pallas kernels: 0 us -> 47.4 us
  other arithmetic: 28.2 us -> 0.94 us
  starting transfers between devices: 0.5 us -> 23.7 us
  between operations: 15.2 us -> 1.2 us
    all_gather x4 -> x0, blocking collectives: 104 us -> none  [the longest x1 34.6 us: per_device(): lax.all_gather(w_expand.astype(jnp.bfloat16), 'rows', axis=0, tiled=True)]
    dot_general x12 -> x0, matrix products: 82.8 us -> none  [the longest x1 23.9 us: per_device(): lax.dot_general(cot_flat, reduce_flat, (((1,), (1,)), ((), ())), preferre...]
    reduce_scatter x3 -> x0, waiting for transfers between devices: 73.6 us -> none  [the longest x1 47.2 us: per_device(): lax.psum_scatter(grad_reduce.reshape(experts_n, hidden_n, width), 'rows',...]
    convert_element_type x2 -> x0, local copies, waits for them, and re-layouts: 52.6 us -> none  [the longest x1 35 us: per_device(): weighted = (hidden.reshape(rows_local, 1, experts_n, hidden_n) * gate_row...]
    psum x2 -> x0, blocking collectives: 47.7 us -> none  [the longest x1 37.1 us: per_device(): lax.psum(jnp.stack([grad_hbias.reshape(experts_n, hidden_n), grad_obias])...]
    pallas_call x0 -> x23, Pallas kernels: none -> 47.4 us  [the longest x22 46.3 us: kernel_call(): pl.pallas_call(kernel, out_shape=tuple((jax.ShapeDtypeStruct(shape, kind)...]
    unnamed x110 -> x57, local copies, waits for them, and re-layouts: 54.4 us -> 9.24 us
    unnamed x11 -> x0, waiting for transfers between devices: 43.9 us -> none
  transfers between devices with their start and end apart: 8 -> 22, of which waited for: 5 -> 9; matrix products, arithmetic and copies ran while one was open for 37% -> 1% of each run, Pallas kernels for 0% -> 38%
where the time goes in v2:
time: 116 us; the launch traced here: 115 us
  Pallas kernels  47.4 us (41%)
  waiting for transfers between devices  31.7 us (27%)
  starting transfers between devices  23.7 us (20%)
  local copies, waits for them, and re-layouts  9.97 us (9%)
  between operations  1.2 us (1%)
    pallas_call x22, Pallas kernels, kernel_call(): pl.pallas_call(kernel, out_shape=tuple((jax.ShapeDtypeStruct(shape, kind)...  46.3 us
    ppermute x22, waiting for transfers between devices, swap(): return lax.ppermute(x, ('rows', 'hid'), pairs)  31.7 us
    ppermute x22, starting transfers between devices, swap(): return lax.ppermute(x, ('rows', 'hid'), pairs)  23.7 us
    unnamed x57, local copies, waits for them, and re-layouts  9.24 us
  transfers between devices with their start and end apart: 22, of which 9 were waited for; matrix products, arithmetic and copies ran while one was open for 1% of the time, Pallas kernels for 38%

profile of v2, /device:TPU:0, one launch (start us, length us, event | category | flops | bytes accessed | tf_op | source)
XLA Modules:
  0.0 114.8 jit_solution(3577144188505195936)
XLA Ops:
  0.7 0.1 pad_add_fusion.core.refs_0_
  0.7 0.9 copy-done
  1.7 0.9 copy-done.2
  2.6 0.7 copy-done.4
  3.4 0.7 copy-done.6
  4.1 1.0 shard_map.254
  5.1 0.5 collective-permute-start
  5.6 1.0 collective-permute-done.refs_1_
  6.6 0.1 shard_map.255.refs_0_
  6.7 4.0 %collective-permute-start.1 = (bf16[544,128]{1,0:T(8,128)(2,1)S(1)}, bf16[544,128]{1,0:T(8,128)(2,1)S(1)}, u32[]{:S(2)}, u32[]{:S(2)}) collective-permute-start(bf16[544,128]{1,0:T(8,128)(2,1)S(1)} %shard_map.255.refs_0_), channel_id=1, source_target_pairs={{0,16},{1,5},{2,18},{3,7},{4,20},{5,1},{6,22},{7,3},{8,24},{9,13},... | collective-permute-start | bytes 417800 | tf_op jit(solution)/shard_map/ppermute | solution.py:776
  10.7 4.5 %collective-permute-done.1.refs_1_ = bf16[544,128]{1,0:T(8,128)(2,1)S(1)} collective-permute-done((bf16[544,128]{1,0:T(8,128)(2,1)S(1)}, bf16[544,128]{1,0:T(8,128)(2,1)S(1)}, u32[]{:S(2)}, u32[]{:S(2)}) %collective-permute-start.1) | collective-permute-done | bytes 139296 | tf_op jit(solution)/shard_map/ppermute | solution.py:776
  15.3 1.1 collective-permute-start.2
  16.4 0.5 collective-permute-start.7
  16.9 0.7 collective-permute-done.3
  17.5 6.2 %collective-permute-done.2.refs_1_ = bf16[1088,128]{1,0:T(8,128)(2,1)S(1)} collective-permute-done((bf16[1088,128]{1,0:T(8,128)(2,1)S(1)}, bf16[1088,128]{1,0:T(8,128)(2,1)S(1)}, u32[]{:S(2)}, u32[]{:S(2)}) %collective-permute-start.2) | collective-permute-done | bytes 278560 | tf_op jit(solution)/shard_map/ppermute | solution.py:776
  23.8 0.0 copy-start.21
  23.8 1.9 %collective-permute-start.4 = (bf16[1216,128]{1,0:T(8,128)(2,1)S(1)}, bf16[1216,128]{1,0:T(8,128)(2,1)S(1)}, u32[]{:S(2)}, u32[]{:S(2)}) collective-permute-start(bf16[1216,128]{1,0:T(8,128)(2,1)S(1)} %get-tuple-element.86.refs_0_), channel_id=1, source_target_pairs={{0,2},{1,9},{2,0},{3,11},{4,6},{5,13},{6,4},{7,15},{8,10},{9,1},{1... | collective-permute-start | bytes 933896 | tf_op jit(solution)/shard_map/ppermute | solution.py:776
  25.7 5.0 %collective-permute-done.4.refs_1_ = bf16[1216,128]{1,0:T(8,128)(2,1)S(1)} collective-permute-done((bf16[1216,128]{1,0:T(8,128)(2,1)S(1)}, bf16[1216,128]{1,0:T(8,128)(2,1)S(1)}, u32[]{:S(2)}, u32[]{:S(2)}) %collective-permute-start.4) | collective-permute-done | bytes 311328 | tf_op jit(solution)/shard_map/ppermute | solution.py:776
  30.8 0.0 copy-start.9
  30.8 0.8 copy-done.9
  31.6 0.5 collective-permute-start.6
  32.1 1.9 %collective-permute-start.8 = (bf16[2048,128]{1,0:T(8,128)(2,1)}, bf16[2048,128]{1,0:T(8,128)(2,1)S(1)}, u32[]{:S(2)}, u32[]{:S(2)}) collective-permute-start(bf16[2048,128]{1,0:T(8,128)(2,1)} %copy-done.9), channel_id=1, source_target_pairs={{0,4},{1,3},{2,6},{3,1},{4,0},{5,7},{6,2},{7,5},{8,12},{9,11},{10,... | collective-permute-start | bytes 1572872 | tf_op jit(solution)/shard_map/ppermute | solution.py:776
  34.0 1.5 %collective-permute-start.9 = (bf16[1024,128]{1,0:T(8,128)(2,1)S(1)}, bf16[1024,128]{1,0:T(8,128)(2,1)S(1)}, u32[]{:S(2)}, u32[]{:S(2)}) collective-permute-start(bf16[1024,128]{1,0:T(8,128)(2,1)S(1)} %get-tuple-element.94.refs_0_), channel_id=1, source_target_pairs={{0,2},{1,9},{2,0},{3,11},{4,6},{5,13},{6,4},{7,15},{8,10},{9,1},{1... | collective-permute-start | bytes 786440 | tf_op jit(solution)/shard_map/ppermute | solution.py:776
  35.5 0.9 slice_select_fusion
  36.3 0.7 fusion
  37.1 0.0 copy-start.10
  37.1 1.0 copy-done.10
  38.1 7.4 %shard_map.259 = (bf16[272,2048]{1,0:T(8,128)(2,1)S(1)}, bf16[3,256,2048]{2,1,0:T(8,128)(2,1)S(1)}, bf16[4,256,2048]{2,1,0:T(8,128)(2,1)S(1)}, bf16[4,256,2048]{...) custom-call(s32[3]{0:T(128)S(1)} %pad_add_fusion.core.refs_0_, ...), custom_call_target="tpu_custom_call" | custom-call | flops 89999998976 | tf_op jit(solution)/shard_map/pallas_call | solution.py:54
  45.6 0.0 copy-start.11
  45.7 0.7 copy-done.24
  46.4 0.5 collective-permute-start.10
  46.9 0.2 copy-done.11
  47.0 7.6 %shard_map.261 = (bf16[2048,128]{1,0:T(8,128)(2,1)S(1)}, bf16[2048,128]{1,0:T(8,128)(2,1)S(1)}, bf16[4,256,2048]{2,1,0:T(8,128)(2,1)S(1)}, bf16[4,256,2048]{2,1,...) custom-call(s32[3]{0:T(128)S(1)} %pad_add_fusion.core.refs_0_, ...), custom_call_target="tpu_custom_call" | custom-call | flops 91199995904 | tf_op jit(solution)/shard_map/pallas_call | solution.py:54
  54.6 1.4 %collective-permute-start.12 = (bf16[2048,128]{1,0:T(8,128)(2,1)S(1)}, bf16[2048,128]{1,0:T(8,128)(2,1)S(1)}, u32[]{:S(2)}, u32[]{:S(2)}) collective-permute-start(bf16[2048,128]{1,0:T(8,128)(2,1)S(1)} %get-tuple-element.119.refs_1_), channel_id=1, source_target_pairs={{0,4},{1,3},{2,6},{3,1},{4,0},{5,7},{6,2},{7,5},{8,12},{9,11},{10,... | collective-permute-start | bytes 1572872 | tf_op jit(solution)/shard_map/ppermute | solution.py:776
  56.1 7.8 %shard_map.262 = (bf16[2048,128]{1,0:T(8,128)(2,1)S(1)}, bf16[2080,128]{1,0:T(8,128)(2,1)S(1)}, bf16[4,256,2048]{2,1,0:T(8,128)(2,1)S(1)}, bf16[4,256,2048]{2,1,...) custom-call(s32[3]{0:T(128)S(1)} %pad_add_fusion.core.refs_0_, ...), custom_call_target="tpu_custom_call" | custom-call | flops 91199995904 | tf_op jit(solution)/shard_map/pallas_call | solution.py:54
  63.8 0.0 collective-permute-done.12.refs_2_
  63.9 0.1 shard_map.265
  64.0 0.6 collective-permute-start.14
  64.6 1.4 %collective-permute-start.11 = (bf16[2080,128]{1,0:T(8,128)(2,1)S(1)}, bf16[2080,128]{1,0:T(8,128)(2,1)S(1)}, u32[]{:S(2)}, u32[]{:S(2)}) collective-permute-start(bf16[2080,128]{1,0:T(8,128)(2,1)S(1)} %get-tuple-element.116.refs_1_), channel_id=1, source_target_pairs={{0,4},{1,3},{2,6},{3,1},{4,0},{5,7},{6,2},{7,5},{8,12},{9,11},{10,... | collective-permute-start | bytes 1597448 | tf_op jit(solution)/shard_map/ppermute | solution.py:776
  66.0 4.8 %shard_map.263 = (bf16[8,256,1024]{2,1,0:T(8,128)(2,1)S(1)}, bf16[160,1024]{1,0:T(8,128)(2,1)S(1)}, f32[160,256]{1,0:T(8,128)S(1)}) custom-call(s32[3]{0:T(128)S(1)} %pad_add_fusion.core.refs_0_, bf16[160,128]{1,0:T(8,128)(2,1)S(1)} %copy-done.21, bf16[256,1024]{1,0:T(8,128)(2,1)S(1)} %get-tuple-element.105.refs_2_, ...), custom_call_target="tpu_custom_call" | custom-call | flops 51599998976 | tf_op jit(solution)/shard_map/pallas_call | solution.py:54
  70.8 2.6 %collective-permute-done.14.refs_2_ = bf16[1024,128]{1,0:T(8,128)(2,1)S(1)} collective-permute-done((bf16[1024,128]{1,0:T(8,128)(2,1)S(1)}, bf16[1024,128]{1,0:T(8,128)(2,1)S(1)}, u32[]{:S(2)}, u32[]{:S(2)}) %collective-permute-start.14) | collective-permute-done | bytes 262176 | tf_op jit(solution)/shard_map/ppermute | solution.py:776
  73.3 0.1 shard_map.267
  73.4 0.1 collective-permute-start.16
  73.5 1.2 %copy-done.23 = f32[160,2048]{1,0:T(8,128)S(1)} copy-done((f32[160,2048]{1,0:T(8,128)S(1)}, f32[160,2048]{1,0:T(8,128)}, u32[]{:S(2)}) %copy-start.23) | copy-done | bytes 1310744
  74.6 4.9 %shard_map.266 = (bf16[8,256,1024]{2,1,0:T(8,128)(2,1)S(1)}, bf16[160,1024]{1,0:T(8,128)(2,1)S(1)}, bf16[128,128]{1,0:T(8,128)(2,1)S(1)}) custom-call(s32[3]{0:T(128)S(1)} %pad_add_fusion.core.refs_0_, bf16[160,128]{1,0:T(8,128)(2,1)S(1)} %copy-done.21, bf16[256,1024]{1,0:T(8,128)(2,1)S(1)} %get-tuple-element.105.refs_2_, ...), custom_call_target="tpu_custom_call" | custom-call | flops 51599998976 | tf_op jit(solution)/shard_map/pallas_call | solution.py:54
  79.6 1.4 %collective-permute-start.13 = (bf16[128,128]{1,0:T(8,128)(2,1)S(1)}, bf16[128,128]{1,0:T(8,128)(2,1)S(1)}, u32[]{:S(2)}, u32[]{:S(2)}) collective-permute-start(bf16[128,128]{1,0:T(8,128)(2,1)S(1)} %get-tuple-element.121.refs_1_), channel_id=1, source_target_pairs={{0,4},{1,3},{2,6},{3,1},{4,0},{5,7},{6,2},{7,5},{8,12},{9,11},{10,... | collective-permute-start | bytes 98312 | tf_op jit(solution)/shard_map/ppermute | solution.py:776
  81.1 0.1 shard_map.264
  81.2 0.9 copy-done.25
  82.1 3.9 %shard_map.268.refs_3_ = bf16[4,256,1024]{2,1,0:T(8,128)(2,1)S(1)} custom-call(bf16[256,1024]{1,0:T(8,128)(2,1)S(1)} %get-tuple-element.95.refs_0_, bf16[4,256,2048]{2,1,0:T(8,128)(2,1)S(1)} %get-tuple-element.96.refs_1_, bf16[256,1024]{1,0:T(8,128)(2,1)S(1)} %get-tuple-element.102.refs_2_, bf16[4,256,2048]{2,1,0:T(8,128)(2,1)S(1)} %get-tuple-element.103.refs_3_, ...), custom_call_target="tpu_custom_call" | custom-call | flops 48000000000 | tf_op jit(solution)/shard_map/pallas_call | solution.py:54
  86.0 0.1 collective-permute-start.15
  86.2 0.6 collective-permute-start.18
  86.7 3.9 %shard_map.270.refs_1_ = bf16[4,256,1024]{2,1,0:T(8,128)(2,1)S(1)} custom-call(bf16[256,1024]{1,0:T(8,128)(2,1)S(1)} %get-tuple-element.95.refs_0_, bf16[4,256,2048]{2,1,0:T(8,128)(2,1)S(1)} %get-tuple-element.96.refs_1_, bf16[256,1024]{1,0:T(8,128)(2,1)S(1)} %get-tuple-element.102.refs_2_, bf16[4,256,2048]{2,1,0:T(8,128)(2,1)S(1)} %get-tuple-element.103.refs_3_, ...), custom_call_target="tpu_custom_call" | custom-call | flops 48000000000 | tf_op jit(solution)/shard_map/pallas_call | solution.py:54
  90.7 2.7 %shard_map.272 = (bf16[3,1024,256]{2,1,0:T(8,128)(2,1)}, bf16[1024,256]{1,0:T(8,128)(2,1)}) custom-call(bf16[256,256]{1,0:T(8,128)(2,1)S(1)} %copy-done.27, bf16[4,256,1024]{2,1,0:T(8,128)(2,1)S(1)} %shard_map.270.refs_1_, bf16[4,256,1024]{2,1,0:T(8,128)(2,1)S(1)} %collective-permute-done.15.refs_2_, bf16[256,128]{1,0:T(8,128)(2,1)S(1)} %get-tuple-element.128.refs_3_.refs_0_), custom_call_target="tpu_custom_call" | custom-call | flops 32399998976 | tf_op jit(solution)/shard_map/pallas_call | solution.py:54
  93.4 1.0 copy-done.20
  94.5 0.1 shard_map.273
  94.5 0.9 collective-permute-start.19
  95.4 4.6 %collective-permute-done.19.refs_2_ = bf16[672,128]{1,0:T(8,128)(2,1)S(1)} collective-permute-done((bf16[672,128]{1,0:T(8,128)(2,1)S(1)}, bf16[672,128]{1,0:T(8,128)(2,1)S(1)}, u32[]{:S(2)}, u32[]{:S(2)}) %collective-permute-start.19) | collective-permute-done | bytes 172064 | tf_op jit(solution)/shard_map/ppermute | solution.py:776
  100.0 4.6 %collective-permute-start.20 = (bf16[416,128]{1,0:T(8,128)(2,1)S(1)}, bf16[416,128]{1,0:T(8,128)(2,1)S(1)}, u32[]{:S(2)}, u32[]{:S(2)}) collective-permute-start(bf16[416,128]{1,0:T(8,128)(2,1)S(1)} %get-tuple-element.135.refs_3_), channel_id=1, source_target_pairs={{0,16},{1,5},{2,18},{3,7},{4,20},{5,1},{6,22},{7,3},{8,24},{9,13},... | collective-permute-start | bytes 319496 | tf_op jit(solution)/shard_map/ppermute | solution.py:776
  104.7 0.1 collective-permute-start.17
  104.8 5.8 %collective-permute-done.17.refs_1_ = bf16[256,128]{1,0:T(8,128)(2,1)S(1)} collective-permute-done((bf16[256,128]{1,0:T(8,128)(2,1)S(1)}, bf16[256,128]{1,0:T(8,128)(2,1)S(1)}, u32[]{:S(2)}, u32[]{:S(2)}) %collective-permute-start.17) | collective-permute-done | bytes 65568 | tf_op jit(solution)/shard_map/ppermute | solution.py:776
  110.7 0.1 shard_map.275
  110.8 0.1 collective-permute-start.21
  110.9 1.3 %collective-permute-done.21.refs_3_ = bf16[416,128]{1,0:T(8,128)(2,1)S(1)} collective-permute-done((bf16[416,128]{1,0:T(8,128)(2,1)S(1)}, bf16[416,128]{1,0:T(8,128)(2,1)S(1)}, u32[]{:S(2)}, u32[]{:S(2)}) %collective-permute-start.21) | collective-permute-done | bytes 106528 | tf_op jit(solution)/shard_map/ppermute | solution.py:776
  112.3 2.4 %shard_map.276 = (f32[32,16,64]{2,1,0:T(8,128)}, f32[32,16,64]{2,1,0:T(8,128)}, f32[32,16,64]{2,1,0:T(8,128)}, f32[16,32,64]{2,1,0:T(8,128)}, f32[16,32,64]{2,1,...) custom-call(s32[3]{0:T(128)S(1)} %pad_add_fusion.core.refs_0_, ...), custom_call_target="tpu_custom_call" | custom-call | flops 28800000000 | tf_op jit(solution)/shard_map/pallas_call | solution.py:54
  (66 shorter events, 0.4 us)
Async XLA Ops:
  0.7 1.0 copy-start
  1.7 0.9 copy-start.2
  2.6 0.7 copy-start.4
  3.4 0.7 copy-start.6
  5.1 1.5 %collective-permute-start = (bf16[2,8,32,64]{3,2,1,0:T(8,128)(2,1)S(1)}, bf16[2,8,32,64]{3,2,1,0:T(8,128)(2,1)S(1)}, u32[]{:S(2)}, u32[]{:S(2)}) collective-permute-start(bf16[2,8,32,64]{3,2,1,0:T(8,128)(2,1)S(1)} %get-tuple-element.83), channel_id=1, source_target_pairs={{0,1},{1,0},{2,3},{3,2},{4,5},{5,4},{6,7},{7,6},{8,9},{9,8},{10,11... | collective-permute-start | bytes 196616 | tf_op jit(solution)/shard_map/ppermute | solution.py:776
  6.7 9.6 %copy-start.8 = (bf16[1024,3,256]{2,0,1:T(8,128)(2,1)S(1)}, bf16[1024,3,256]{2,0,1:T(8,128)(2,1)}, u32[]{:S(2)}) copy-start(bf16[1024,3,256]{2,0,1:T(8,128)(2,1)} %param.20) | copy-start | bytes 4718596
  6.7 8.5 %collective-permute-start.1 = (bf16[544,128]{1,0:T(8,128)(2,1)S(1)}, bf16[544,128]{1,0:T(8,128)(2,1)S(1)}, u32[]{:S(2)}, u32[]{:S(2)}) collective-permute-start(bf16[544,128]{1,0:T(8,128)(2,1)S(1)} %shard_map.255.refs_0_), channel_id=1, source_target_pairs={{0,16},{1,5},{2,18},{3,7},{4,20},{5,1},{6,22},{7,3},{8,24},{9,13},... | collective-permute-start | bytes 417800 | tf_op jit(solution)/shard_map/ppermute | solution.py:776
  15.3 8.4 %collective-permute-start.2 = (bf16[1088,128]{1,0:T(8,128)(2,1)S(1)}, bf16[1088,128]{1,0:T(8,128)(2,1)S(1)}, u32[]{:S(2)}, u32[]{:S(2)}) collective-permute-start(bf16[1088,128]{1,0:T(8,128)(2,1)S(1)} %shard_map.256.refs_0_), channel_id=1, source_target_pairs={{0,8},{1,17},{2,10},{3,19},{4,12},{5,21},{6,14},{7,23},{8,0},{9,25... | collective-permute-start | bytes 835592 | tf_op jit(solution)/shard_map/ppermute | solution.py:776
  16.3 1.2 %collective-permute-start.3 = (bf16[32,128]{1,0:T(8,128)(2,1)S(1)}, bf16[32,128]{1,0:T(8,128)(2,1)S(1)}, u32[]{:S(2)}, u32[]{:S(2)}) collective-permute-start(bf16[32,128]{1,0:T(8,128)(2,1)S(1)} %get-tuple-element.85), channel_id=1, source_target_pairs={{0,1},{1,0},{2,3},{3,2},{4,5},{5,4},{6,7},{7,6},{8,9},{9,8},{10,11... | collective-permute-start | bytes 24584 | tf_op jit(solution)/shard_map/ppermute | solution.py:776
  16.4 20.7 %collective-permute-start.7 = (bf16[3,1024,256]{2,1,0:T(8,128)(2,1)S(1)}, bf16[3,1024,256]{2,1,0:T(8,128)(2,1)S(1)}, u32[]{:S(2)}, u32[]{:S(2)}) collective-permute-start(bf16[3,1024,256]{2,1,0:T(8,128)(2,1)S(1)} %bitcast.18), channel_id=1, source_target_pairs={{0,1},{1,0},{2,3},{3,2},{4,5},{5,4},{6,7},{7,6},{8,9},{9,8},{10,11... | collective-permute-start | bytes 4718600 | tf_op jit(solution)/shard_map/ppermute | solution.py:776
  23.8 13.3 %copy-start.21 = (bf16[160,128]{1,0:T(8,128)(2,1)S(1)}, bf16[160,128]{1,0:T(8,128)(2,1)}, u32[]{:S(2)}) copy-start(bf16[160,128]{1,0:T(8,128)(2,1)} %constant.26.clone.refs_1_) | copy-start | bytes 122884
  23.8 7.0 %collective-permute-start.4 = (bf16[1216,128]{1,0:T(8,128)(2,1)S(1)}, bf16[1216,128]{1,0:T(8,128)(2,1)S(1)}, u32[]{:S(2)}, u32[]{:S(2)}) collective-permute-start(bf16[1216,128]{1,0:T(8,128)(2,1)S(1)} %get-tuple-element.86.refs_0_), channel_id=1, source_target_pairs={{0,2},{1,9},{2,0},{3,11},{4,6},{5,13},{6,4},{7,15},{8,10},{9,1},{1... | collective-permute-start | bytes 933896 | tf_op jit(solution)/shard_map/ppermute | solution.py:776
  30.8 0.8 copy-start.9
  31.6 3.9 %collective-permute-start.5 = (bf16[320,128]{1,0:T(8,128)(2,1)S(1)}, bf16[320,128]{1,0:T(8,128)(2,1)}, u32[]{:S(2)}, u32[]{:S(2)}) collective-permute-start(bf16[320,128]{1,0:T(8,128)(2,1)S(1)} %get-tuple-element.87), channel_id=1, source_target_pairs={{0,1},{1,0},{2,3},{3,2},{4,5},{5,4},{6,7},{7,6},{8,9},{9,8},{10,11... | collective-permute-start | bytes 245768 | tf_op jit(solution)/shard_map/ppermute | solution.py:776
  31.6 5.5 %collective-permute-start.6 = (bf16[1024,256]{1,0:T(8,128)(2,1)}, bf16[1024,256]{1,0:T(8,128)(2,1)}, u32[]{:S(2)}, u32[]{:S(2)}) collective-permute-start(bf16[1024,256]{1,0:T(8,128)(2,1)} %refs_9_.1), channel_id=1, source_target_pairs={{0,1},{1,0},{2,3},{3,2},{4,5},{5,4},{6,7},{7,6},{8,9},{9,8},{10,11... | collective-permute-start | bytes 1572872 | tf_op jit(solution)/shard_map/ppermute | solution.py:776
  32.1 14.8 %collective-permute-start.8 = (bf16[2048,128]{1,0:T(8,128)(2,1)}, bf16[2048,128]{1,0:T(8,128)(2,1)S(1)}, u32[]{:S(2)}, u32[]{:S(2)}) collective-permute-start(bf16[2048,128]{1,0:T(8,128)(2,1)} %copy-done.9), channel_id=1, source_target_pairs={{0,4},{1,3},{2,6},{3,1},{4,0},{5,7},{6,2},{7,5},{8,12},{9,11},{10,... | collective-permute-start | bytes 1572872 | tf_op jit(solution)/shard_map/ppermute | solution.py:776
  34.0 11.6 %collective-permute-start.9 = (bf16[1024,128]{1,0:T(8,128)(2,1)S(1)}, bf16[1024,128]{1,0:T(8,128)(2,1)S(1)}, u32[]{:S(2)}, u32[]{:S(2)}) collective-permute-start(bf16[1024,128]{1,0:T(8,128)(2,1)S(1)} %get-tuple-element.94.refs_0_), channel_id=1, source_target_pairs={{0,2},{1,9},{2,0},{3,11},{4,6},{5,13},{6,4},{7,15},{8,10},{9,1},{1... | collective-permute-start | bytes 786440 | tf_op jit(solution)/shard_map/ppermute | solution.py:776
  37.1 1.0 copy-start.10
  45.6 0.8 copy-start.24
  45.6 10.5 %copy-start.26 = (bf16[256,256]{1,0:T(8,128)(2,1)}, bf16[256,256]{1,0:T(8,128)(2,1)S(1)}, u32[]{:S(2)}) copy-start(bf16[256,256]{1,0:T(8,128)(2,1)S(1)} %get-tuple-element.89.refs_9_.refs_0_) | copy-start | bytes 393220
  45.6 20.4 %copy-start.22 = (f32[160,2048]{1,0:T(8,128)}, f32[160,2048]{1,0:T(8,128)S(1)}, u32[]{:S(2)}) copy-start(f32[160,2048]{1,0:T(8,128)S(1)} %get-tuple-element.110.refs_7_) | copy-start | bytes 3932164
  45.6 1.4 %copy-start.11 = (bf16[2048,128]{1,0:T(8,128)(2,1)S(1)}, bf16[2048,128]{1,0:T(8,128)(2,1)}, u32[]{:S(2)}) copy-start(bf16[2048,128]{1,0:T(8,128)(2,1)} %copy-done.9) | copy-start | bytes 1572868
  46.4 9.7 %collective-permute-start.10 = (bf16[2048,128]{1,0:T(8,128)(2,1)S(1)}, bf16[2048,128]{1,0:T(8,128)(2,1)S(1)}, u32[]{:S(2)}, u32[]{:S(2)}) collective-permute-start(bf16[2048,128]{1,0:T(8,128)(2,1)S(1)} %shard_map.260.refs_6_.refs_1_), channel_id=1, source_target_pairs={{0,4},{1,3},{2,6},{3,1},{4,0},{5,7},{6,2},{7,5},{8,12},{9,11},{10,... | collective-permute-start | bytes 1572872 | tf_op jit(solution)/shard_map/ppermute | solution.py:776
  54.6 9.2 %collective-permute-start.12 = (bf16[2048,128]{1,0:T(8,128)(2,1)S(1)}, bf16[2048,128]{1,0:T(8,128)(2,1)S(1)}, u32[]{:S(2)}, u32[]{:S(2)}) collective-permute-start(bf16[2048,128]{1,0:T(8,128)(2,1)S(1)} %get-tuple-element.119.refs_1_), channel_id=1, source_target_pairs={{0,4},{1,3},{2,6},{3,1},{4,0},{5,7},{6,2},{7,5},{8,12},{9,11},{10,... | collective-permute-start | bytes 1572872 | tf_op jit(solution)/shard_map/ppermute | solution.py:776
  64.0 9.3 %collective-permute-start.14 = (bf16[1024,128]{1,0:T(8,128)(2,1)S(1)}, bf16[1024,128]{1,0:T(8,128)(2,1)S(1)}, u32[]{:S(2)}, u32[]{:S(2)}) collective-permute-start(bf16[1024,128]{1,0:T(8,128)(2,1)S(1)} %get-tuple-element.124.refs_1_), channel_id=1, source_target_pairs={{0,2},{1,9},{2,0},{3,11},{4,6},{5,13},{6,4},{7,15},{8,10},{9,1},{1... | collective-permute-start | bytes 786440 | tf_op jit(solution)/shard_map/ppermute | solution.py:776
  64.6 16.4 %collective-permute-start.11 = (bf16[2080,128]{1,0:T(8,128)(2,1)S(1)}, bf16[2080,128]{1,0:T(8,128)(2,1)S(1)}, u32[]{:S(2)}, u32[]{:S(2)}) collective-permute-start(bf16[2080,128]{1,0:T(8,128)(2,1)S(1)} %get-tuple-element.116.refs_1_), channel_id=1, source_target_pairs={{0,4},{1,3},{2,6},{3,1},{4,0},{5,7},{6,2},{7,5},{8,12},{9,11},{10,... | collective-permute-start | bytes 1597448 | tf_op jit(solution)/shard_map/ppermute | solution.py:776
  73.3 1.3 %copy-start.23 = (f32[160,2048]{1,0:T(8,128)S(1)}, f32[160,2048]{1,0:T(8,128)}, u32[]{:S(2)}) copy-start(f32[160,2048]{1,0:T(8,128)} %copy-done.22) | copy-start | bytes 3932164
  73.4 7.6 %collective-permute-start.16 = (bf16[512,128]{1,0:T(8,128)(2,1)S(1)}, bf16[512,128]{1,0:T(8,128)(2,1)S(1)}, u32[]{:S(2)}, u32[]{:S(2)}) collective-permute-start(bf16[512,128]{1,0:T(8,128)(2,1)S(1)} %get-tuple-element.127.refs_1_), channel_id=1, source_target_pairs={{0,8},{1,17},{2,10},{3,19},{4,12},{5,21},{6,14},{7,23},{8,0},{9,25... | collective-permute-start | bytes 393224 | tf_op jit(solution)/shard_map/ppermute | solution.py:776
  79.6 6.5 %collective-permute-start.13 = (bf16[128,128]{1,0:T(8,128)(2,1)S(1)}, bf16[128,128]{1,0:T(8,128)(2,1)S(1)}, u32[]{:S(2)}, u32[]{:S(2)}) collective-permute-start(bf16[128,128]{1,0:T(8,128)(2,1)S(1)} %get-tuple-element.121.refs_1_), channel_id=1, source_target_pairs={{0,4},{1,3},{2,6},{3,1},{4,0},{5,7},{6,2},{7,5},{8,12},{9,11},{10,... | collective-permute-start | bytes 98312 | tf_op jit(solution)/shard_map/ppermute | solution.py:776
  81.1 1.0 copy-start.25
  86.0 4.6 %collective-permute-start.15 = (bf16[4,256,1024]{2,1,0:T(8,128)(2,1)S(1)}, bf16[4,256,1024]{2,1,0:T(8,128)(2,1)S(1)}, u32[]{:S(2)}, u32[]{:S(2)}) collective-permute-start(bf16[4,256,1024]{2,1,0:T(8,128)(2,1)S(1)} %shard_map.268.refs_3_), channel_id=1, source_target_pairs={{0,1},{1,0},{2,3},{3,2},{4,5},{5,4},{6,7},{7,6},{8,9},{9,8},{10,11... | collective-permute-start | bytes 6291464 | tf_op jit(solution)/shard_map/ppermute | solution.py:776
  86.2 7.3 %collective-permute-start.18 = (bf16[1184,128]{1,0:T(8,128)(2,1)S(1)}, bf16[1184,128]{1,0:T(8,128)(2,1)S(1)}, u32[]{:S(2)}, u32[]{:S(2)}) collective-permute-start(bf16[1184,128]{1,0:T(8,128)(2,1)S(1)} %shard_map.269.refs_8_.refs_1_), channel_id=1, source_target_pairs={{0,2},{1,9},{2,0},{3,11},{4,6},{5,13},{6,4},{7,15},{8,10},{9,1},{1... | collective-permute-start | bytes 909320 | tf_op jit(solution)/shard_map/ppermute | solution.py:776
  86.7 3.9 %copy-start.27 = (bf16[256,256]{1,0:T(8,128)(2,1)S(1)}, bf16[256,256]{1,0:T(8,128)(2,1)}, u32[]{:S(2)}) copy-start(bf16[256,256]{1,0:T(8,128)(2,1)} %copy-done.26) | copy-start | bytes 393220
  93.4 1.0 copy-start.20
  94.5 5.5 %collective-permute-start.19 = (bf16[672,128]{1,0:T(8,128)(2,1)S(1)}, bf16[672,128]{1,0:T(8,128)(2,1)S(1)}, u32[]{:S(2)}, u32[]{:S(2)}) collective-permute-start(bf16[672,128]{1,0:T(8,128)(2,1)S(1)} %get-tuple-element.133.refs_1_), channel_id=1, source_target_pairs={{0,8},{1,17},{2,10},{3,19},{4,12},{5,21},{6,14},{7,23},{8,0},{9,25... | collective-permute-start | bytes 516104 | tf_op jit(solution)/shard_map/ppermute | solution.py:776
  100.0 10.5 %collective-permute-start.20 = (bf16[416,128]{1,0:T(8,128)(2,1)S(1)}, bf16[416,128]{1,0:T(8,128)(2,1)S(1)}, u32[]{:S(2)}, u32[]{:S(2)}) collective-permute-start(bf16[416,128]{1,0:T(8,128)(2,1)S(1)} %get-tuple-element.135.refs_3_), channel_id=1, source_target_pairs={{0,16},{1,5},{2,18},{3,7},{4,20},{5,1},{6,22},{7,3},{8,24},{9,13},... | collective-permute-start | bytes 319496 | tf_op jit(solution)/shard_map/ppermute | solution.py:776
  104.7 5.9 %collective-permute-start.17 = (bf16[256,128]{1,0:T(8,128)(2,1)S(1)}, bf16[256,128]{1,0:T(8,128)(2,1)S(1)}, u32[]{:S(2)}, u32[]{:S(2)}) collective-permute-start(bf16[256,128]{1,0:T(8,128)(2,1)S(1)} %get-tuple-element.131), channel_id=1, source_target_pairs={{0,16},{1,5},{2,18},{3,7},{4,20},{5,1},{6,22},{7,3},{8,24},{9,13},... | collective-permute-start | bytes 196616 | tf_op jit(solution)/shard_map/ppermute | solution.py:776
  110.6 1.6 %copy-start.1 = (f32[32,16,64]{2,1,0:T(8,128)S(1)}, f32[32,16,64]{2,1,0:T(8,128)}, u32[]{:S(2)}) copy-start(f32[32,16,64]{2,1,0:T(8,128)} %refs_4_.1) | copy-start | bytes 393220
  110.6 1.6 %copy-start.3 = (f32[16,64,32]{1,2,0:T(8,128)S(1)}, f32[16,64,32]{1,2,0:T(8,128)}, u32[]{:S(2)}) copy-start(f32[16,64,32]{1,2,0:T(8,128)} %param.17) | copy-start | bytes 393220
  110.6 1.6 %copy-start.5 = (f32[2,16,64]{2,1,0:T(8,128)S(1)}, f32[2,16,64]{2,1,0:T(8,128)}, u32[]{:S(2)}) copy-start(f32[2,16,64]{2,1,0:T(8,128)} %refs_10_.1) | copy-start | bytes 24580
  110.6 1.6 %copy-start.7 = (f32[32,60]{1,0:T(8,128)S(1)}, f32[32,60]{1,0:T(8,128)}, u32[]{:S(2)}) copy-start(f32[32,60]{1,0:T(8,128)} %refs_13_.1) | copy-start | bytes 23044
  110.6 1.6 %copy-start.12 = (f32[32,16,64]{2,1,0:T(8,128)S(1)}, f32[32,16,64]{2,1,0:T(8,128)}, u32[]{:S(2)}) copy-start(f32[32,16,64]{2,1,0:T(8,128)} %refs_5_.3) | copy-start | bytes 393220
  110.6 1.6 %copy-start.13 = (f32[32,16,64]{2,1,0:T(8,128)S(1)}, f32[32,16,64]{2,1,0:T(8,128)}, u32[]{:S(2)}) copy-start(f32[32,16,64]{2,1,0:T(8,128)} %refs_6_.1) | copy-start | bytes 393220
  110.6 1.6 %copy-start.14 = (f32[16,64,32]{1,2,0:T(8,128)S(1)}, f32[16,64,32]{1,2,0:T(8,128)}, u32[]{:S(2)}) copy-start(f32[16,64,32]{1,2,0:T(8,128)} %param.23) | copy-start | bytes 393220
  110.6 1.6 %copy-start.15 = (f32[16,64,32]{1,2,0:T(8,128)S(1)}, f32[16,64,32]{1,2,0:T(8,128)}, u32[]{:S(2)}) copy-start(f32[16,64,32]{1,2,0:T(8,128)} %param.24) | copy-start | bytes 393220
  110.6 1.6 %copy-start.16 = (f32[2,16,64]{2,1,0:T(8,128)S(1)}, f32[2,16,64]{2,1,0:T(8,128)}, u32[]{:S(2)}) copy-start(f32[2,16,64]{2,1,0:T(8,128)} %refs_11_.1) | copy-start | bytes 24580
  110.6 1.6 %copy-start.17 = (f32[2,16,64]{2,1,0:T(8,128)S(1)}, f32[2,16,64]{2,1,0:T(8,128)}, u32[]{:S(2)}) copy-start(f32[2,16,64]{2,1,0:T(8,128)} %refs_12_.1) | copy-start | bytes 24580
  110.7 1.6 %copy-start.18 = (f32[32,60]{1,0:T(8,128)S(1)}, f32[32,60]{1,0:T(8,128)}, u32[]{:S(2)}) copy-start(f32[32,60]{1,0:T(8,128)} %refs_14_.1) | copy-start | bytes 23044
  110.7 1.6 %copy-start.19 = (f32[32,60]{1,0:T(8,128)S(1)}, f32[32,60]{1,0:T(8,128)}, u32[]{:S(2)}) copy-start(f32[32,60]{1,0:T(8,128)} %refs_15_.1) | copy-start | bytes 23044
  110.8 1.4 %collective-permute-start.21 = (bf16[416,128]{1,0:T(8,128)(2,1)S(1)}, bf16[416,128]{1,0:T(8,128)(2,1)S(1)}, u32[]{:S(2)}, u32[]{:S(2)}) collective-permute-start(bf16[416,128]{1,0:T(8,128)(2,1)S(1)} %get-tuple-element.137.refs_2_), channel_id=1, source_target_pairs={{0,1},{1,0},{2,3},{3,2},{4,5},{5,4},{6,7},{7,6},{8,9},{9,8},{10,11... | collective-permute-start | bytes 319496 | tf_op jit(solution)/shard_map/ppermute | solution.py:776

commit v3 on v2

--- a/solution.py
+++ b/solution.py
@@ -26,7 +26,7 @@
 GROUPS = BITS * SELECT + SELECT
 GROWS = GROUPS * TPAD
 ONES = 16
-TILE = 512
+TILE = 256
 WIDE = 1024
 MIB = 1 << 20
 FLOPS_MICRO = 1.2e10
@@ -91,20 +91,9 @@
     return pl.ds(pl.multiple_of(i * tile, tile), tile)
 
 
-def prep_kernel(
-    masks, at, order, sel, b_own, b_side, xo, xr, go, gr,
-    xt, gt, cc_a, cc_b, gates, logits, selp, gb1, perm, to_q, b0, b1, mul,
-):
-    core, row, hid = at[0], at[1], at[2]
-    high = core.astype(F32)
-    rows, width = xo.shape
-    tile = min(WIDE, rows)
-    steps = rows // tile
-
+def places(masks, at, width):
+    row, hid = at[1], at[2]
     depth = width // (1 << len(masks))
-    square = (width, width)
-    up = lax.broadcasted_iota(jnp.int32, square, 0)
-    across = lax.broadcasted_iota(jnp.int32, square, 1)
 
     def d_of(spot):
         block, out = spot // depth, row
@@ -116,30 +105,93 @@
         lanes = width // 4
         return (hid ^ (spot // lanes)) * lanes + spot % lanes
 
+    return d_of, q_of
+
+
+def turn_kernel(masks, at, xo, xr, go, gr, xt, gt, perm, to_q):
+    rows, width = xo.shape
+    d_of, q_of = places(masks, at, width)
+    up = lax.broadcasted_iota(jnp.int32, (width, width), 0)
+    across = lax.broadcasted_iota(jnp.int32, (width, width), 1)
+    perm[...] = (d_of(up) == across).astype(F32).astype(BF)
+    to_q[...] = (q_of(up) == across).astype(F32).astype(BF)
+    xt[width : width + ONES, :] = jnp.ones((ONES, xt.shape[1]), BF)
+    tile = min(WIDE, rows)
+    for x, g, start in ((xo, go, 0), (xr, gr, rows)):
+        for i in range(rows // tile):
+            here = slice(i * tile, (i + 1) * tile)
+            out = slice(start + i * tile, start + (i + 1) * tile)
+            xt[0:width, out] = dot(perm[...], x[here, :], 1, 1).astype(BF)
+            for t in range(TASKS):
+                gt[t, :, out] = dot(perm[...], g[t, here, :], 1, 1).astype(BF)
+
+
+def turn(masks, at, x_own, x_recv, g_own, g_recv, after):
+    rows, width = x_own.shape
+    total = 2 * rows
+    return kernel_call(
+        functools.partial(turn_kernel, masks),
+        (
+            ((width + ONES, total), BF),
+            ((TASKS, width, total), BF),
+            ((width, width), BF),
+            ((width, width), BF),
+        ),
+        (),
+        12,
+        3.5,
+        1,
+        at, x_own, x_recv, g_own, g_recv,
+        after=after,
+    )
+
+
+def prep_kernel(
+    masks, ride, at, order, riders, turned, b_own, xt, gt,
+    cc_a, cc_b, gates, logits, selp, gb1, b0, b1, sel,
+):
+    core = at[0]
+    high = core.astype(F32)
+    _, width, total = gt.shape
+    tile = min(WIDE, total)
+    d_of, q_of = places(masks, at, width)
+    up = lax.broadcasted_iota(jnp.int32, (width, width), 0)
+    across = lax.broadcasted_iota(jnp.int32, (width, width), 1)
     one = lambda same: same.astype(F32)
-    perm[...] = one(d_of(up) == across).astype(BF)
-    to_q[...] = one(q_of(up) == across).astype(BF)
+    n_b = b_own.shape[0] // 2
+    if ride:
+        depth = width // 8
+        for q in range(8):
+            spot = (q & 1) + 2 * (q >> 2) + 4 * (q >> 1 & 1)
+            rows = slice(spot * depth, (spot + 1) * depth)
+            sel[q * depth : (q + 1) * depth, :] = jnp.where(core == 1, riders[rows, :], turned[rows, :])
+        side = [
+            jnp.where(
+                core == 0,
+                riders[width + k * n_b : width + (k + 1) * n_b, :],
+                turned[width + (1 - k) * n_b : width + (2 - k) * n_b, :],
+            )
+            for k in range(2)
+        ]
+    else:
+        sel[...] = riders[0:width, :]
+        side = [riders[width + k * n_b : width + (k + 1) * n_b, :] for k in range(2)]
     pieces = []
-    for ref in (b_own, b_side):
-        for k in range(2):
-            block = ref[k * 32 : (k + 1) * 32, :].astype(F32)
-            block = block[:, :64] + block[:, 64:]
-            pieces.append(block)
+    for block in [b_own[k * n_b : (k + 1) * n_b, :] for k in range(2)] + side:
+        block = block.astype(F32)
+        pieces.append(block[:, : width // 4] + block[:, width // 4 :])
     take = lambda x, k: jnp.where(core == 0, x[16 * k : 16 * k + 8], x[16 * k + 8 : 16 * k + 16])
     bias = [jnp.concatenate([take(x, k) for x in pieces], axis=1) for k in range(2)]
     b0[...] = dot(one(up == across), 0.5 * bias[0], 1, 1, HIGHEST)
     b1[...] = dot(one(d_of(up) == q_of(across)), bias[1], 1, 1, HIGHEST)
-
     selp[...] = dot(order[...], sel[...], 1, 1).astype(BF)
     gb1[...] = jnp.zeros_like(gb1)
-    xt[width : width + ONES, :] = jnp.ones((ONES, xt.shape[1]), BF)
-
-    def step(i, x_ref, g_ref, first):
-        here, out = part_of(i, tile), part_of(i + first, tile)
-        x_t = dot(perm[...], x_ref[here, :], 1, 1).astype(BF)
-        xt[0:width, out] = x_t
-        lg = dot(selp[...], x_t, 1, 0)
-        logits[:, out] = lg
+
+    @pl.loop(0, total // tile)
+    def _(i):
+        part = part_of(i, tile)
+        lg = dot(selp[...], xt[0:width, part], 1, 0)
+        logits[:, part] = lg
 
         def z_of(b, k):
             at = (b * SELECT + k) * TPAD
@@ -161,56 +213,39 @@
                         e = 4 * e2 + 2 * e1 + e0
                         w0 = w1 * fac(smooth, 0, k, e0)
                         gate[e] = w0 if gate[e] is None else gate[e] + w0
-        g_t = []
-        for t in range(TASKS):
-            g = dot(perm[...], g_ref[t, here, :], 1, 1)
-            gt[t, :, out] = g.astype(BF)
-            g_t.append(g)
+        for e in range(8):
+            gates[e, :, part] = gate[e]
         ones = jnp.ones((8, tile), BF)
+        g_t = [gt[t, :, part].astype(F32) for t in range(TASKS)]
         for e in range(8):
-            gates[e, :, out] = gate[e]
             c = gate[e][0:1] * g_t[0]
             for t in range(1, TASKS):
                 c = c + gate[e][t : t + 1] * g_t[t]
             c = c.astype(BF)
             cc = cc_a if e < 4 else cc_b
-            cc[e % 4, :, out] = c
+            cc[e % 4, :, part] = c
             gb1[e] += dot(ones, c, 1, 1)
 
-    @pl.loop(0, steps)
-    def _(i):
-        step(i, xo, go, 0)
-
-    @pl.loop(0, steps)
-    def _(i):
-        step(i, xr, gr, steps)
-
-
-def prep(masks, at, order, sel, b_own, b_side, x_own, x_recv, g_own, g_recv, after):
-    rows, width = x_own.shape
-    total = 2 * rows
+
+def prep(masks, ride, at, order, riders, turned, b_own, xt, gt):
+    _, width, total = gt.shape
     return kernel_call(
-        functools.partial(prep_kernel, masks),
+        functools.partial(prep_kernel, masks, ride),
         (
-            ((width + ONES, total), BF),
-            ((TASKS, width, total), BF),
             ((4, width, total), BF),
             ((4, width, total), BF),
             ((8, TPAD, total), F32),
             ((GROWS, total), F32),
             ((GROWS, width), BF),
             ((8, 8, width), F32),
-            ((width, width), BF),
-            ((width, width), BF),
             ((width, 8), F32),
             ((width, 8), F32),
         ),
-        (((8, 128), F32),),
-        16,
-        7.5,
+        (((width, 128), BF),),
+        14,
+        5.0,
         1,
-        at, order, sel, b_own, b_side, x_own, x_recv, g_own, g_recv,
-        after=after,
+        at, order, riders, turned, b_own, xt, gt,
     )
 
 
@@ -263,24 +298,34 @@
 
     each_block(spots, w_lo, w_hi, unpack)
 
-    sums = []
+    e_t = [(e_all[:, e * hidden : (e + 1) * hidden] * 0.5).T for e in range(chunk)]
+    r = [(r_all[:, e * hidden : (e + 1) * hidden] * 0.5).T for e in range(chunk)]
+    parts = [slice(i, i + TILE) for i in range(0, total, TILE)]
+
+    def products(e, part):
+        return dot(e_t[e], xt[0:width, part], 1, 0), dot(r[e], cc[e, :, part], 1, 0)
+
+    def finish(e, part, u, gh):
+        u = u + b0[:, first + e : first + e + 1]
+        t = jnp.tanh(u)
+        plus = 1.0 + t
+        h = u * plus
+        hid[e, :, part] = h.astype(BF)
+        gp[e, :, part] = (gh * (plus + h * (1.0 - t))).astype(BF)
+        if part is parts[-1]:
+            cols = slice(e * hidden, (e + 1) * hidden)
+            acc_e[:, cols] = dot(xt[...], gp[e], 1, 1)
+            acc_r[:, cols] = dot(cc[e], hid[e], 1, 1)
+
+    held = None
     for e in range(chunk):
-        cols = slice(e * hidden, (e + 1) * hidden)
-        e_t = (e_all[:, cols] * 0.5).T
-        r = (r_all[:, cols] * 0.5).T
-        add = b0[:, first + e : first + e + 1]
-        for i in range(total // TILE):
-            part = slice(i * TILE, (i + 1) * TILE)
-            u = dot(e_t, xt[0:width, part], 1, 0) + add
-            t = jnp.tanh(u)
-            plus = 1.0 + t
-            h = u * plus
-            hid[e, :, part] = h.astype(BF)
-            gh = dot(r, cc[e, :, part], 1, 0)
-            gp[e, :, part] = (gh * (plus + h * (1.0 - t))).astype(BF)
-        acc_e[:, cols] = dot(xt[...], gp[e], 1, 1)
-        acc_r[:, cols] = dot(cc[e], hid[e], 1, 1)
-        sums.append(acc_e[width : width + 1, cols])
+        for part in parts:
+            ready = (e, part, *products(e, part))
+            if held:
+                finish(*held)
+            held = ready
+    finish(*held)
+    sums = [acc_e[width : width + 1, e * hidden : (e + 1) * hidden] for e in range(chunk)]
 
     def pack(ref, at, rows, cols):
         for e in range(chunk):
@@ -334,30 +379,31 @@
     return (a.astype(F32) + b.astype(F32)).astype(BF)
 
 
-def fold_kernel(n_small, *refs):
-    lo, sent, got, *more, keep, msg = refs
+def fold_kernel(lo, sent, got, *refs):
+    *tail, keep, msg = refs
     rows = lo.shape[0]
     half = rows // 2
+    end = sent.shape[0] - half
     keep[...] = add_low(lo[0:half, :], got[0:half, :])
     msg[0:half, :] = add_low(lo[half:rows, :], got[half:rows, :])
-    small = sent.shape[0] - rows
-    if small:
-        msg[half : half + small, :] = add_low(sent[rows:, :], got[rows:, :])
-    if n_small:
-        msg[half + small :, :] = add_low(more[0][...], more[1][...])
-
-
-def fold(lo, sent, got, more=(), after=()):
+    if end > half:
+        msg[half:end, :] = add_low(sent[rows:, :], got[rows:, :])
+    if tail:
+        msg[end:, :] = tail[0][...]
+
+
+def fold(lo, sent, got, after=(), tail=()):
     rows, lanes = lo.shape
-    small = sent.shape[0] - rows + (more[0].shape[0] if more else 0)
+    half = rows // 2
+    end = sent.shape[0] - half + sum(x.shape[0] for x in tail)
     return kernel_call(
-        functools.partial(fold_kernel, len(more)),
-        (((rows // 2, lanes), BF), ((rows // 2 + small, lanes), BF)),
+        fold_kernel,
+        (((half, lanes), BF), ((end, lanes), BF)),
         (),
         8,
         0.3,
         0,
-        lo, sent, got, *more,
+        lo, sent, got, *tail,
         after=after,
     )
 
@@ -383,21 +429,32 @@
     return out
 
 
-def last_fold_kernel(a_lo, a_got, b_lo, b_sent, b_got, own, msg):
+def plus_kernel(one, two, out):
+    out[...] = add_low(one[...], two[...])
+
+
+def plus(one, two, after):
+    (out,) = kernel_call(plus_kernel, ((one.shape, BF),), (), 8, 0.3, 0, one, two, after=after)
+    return out
+
+
+def last_fold_kernel(a_lo, b_lo, sent, got, own, msg):
     half = a_lo.shape[1] // 2
-    rows = a_lo.shape[0] // 2
-    for i, (lo, got) in enumerate(((a_lo, a_got), (b_lo, b_got))):
-        e = lo[0:rows, :].astype(F32) + got[0:rows, :].astype(F32)
-        r = lo[rows : 2 * rows, :].astype(F32) + got[rows : 2 * rows, :].astype(F32)
+    size = a_lo.shape[0]
+    rows = size // 2
+    a_at = sent.shape[0] - size
+    for i, (lo, at) in enumerate(((a_lo, a_at), (b_lo, 0))):
+        e = lo[0:rows, :].astype(F32) + got[at : at + rows, :].astype(F32)
+        r = lo[rows:size, :].astype(F32) + got[at + rows : at + size, :].astype(F32)
         here = slice(i * rows, (i + 1) * rows)
         own[here, :] = jnp.concatenate([e[:, :half], r[:, :half]], axis=1)
         msg[here, :] = jnp.concatenate([e[:, half:], r[:, half:]], axis=1).astype(BF)
-    msg[2 * rows :, :] = add_low(b_sent[2 * rows :, :], b_got[2 * rows :, :])
-
-
-def last_fold(a_lo, a_got, b_lo, b_sent, b_got):
+    msg[size:, :] = add_low(sent[size:a_at, :], got[size:a_at, :])
+
+
+def last_fold(a_lo, b_lo, sent, got):
     rows, lanes = a_lo.shape
-    small = b_sent.shape[0] - rows
+    small = sent.shape[0] - 2 * rows
     return kernel_call(
         last_fold_kernel,
         (((rows, lanes), F32), ((rows + small, lanes), BF)),
@@ -405,20 +462,20 @@
         8,
         0.3,
         0,
-        a_lo, a_got, b_lo, b_sent, b_got,
+        a_lo, b_lo, sent, got,
     )
 
 
 def outer_kernel(start, *refs):
     if start:
-        at_core, order, r_a, hid_a, r_b, hid_b, gt, logits, b1, x, acc_in, ys, gls, gsel, acc = refs
+        at_core, order, r_a, hid_a, r_b, hid_b, gt, logits, b1, xt, perm, acc_in, ys, gls, gsel, acc = refs
         acc[...] = acc_in[...]
     else:
-        at_core, order, r_a, hid_a, r_b, hid_b, gt, logits, b1, x, ys, gls, acc = refs
+        at_core, order, r_a, hid_a, r_b, hid_b, gt, logits, b1, xt, ys, gls, acc = refs
         acc[...] = jnp.zeros_like(acc)
     high = at_core[0].astype(F32)
     sign = 2.0 * high - 1.0
-    rows, width = x.shape
+    _, width, rows = ys.shape
     chunk, hidden, _ = hid_a.shape
     tile = min(WIDE, rows)
 
@@ -443,14 +500,15 @@
             gg, high, sign,
         ).astype(BF)
         gls[:, here] = gl
-        acc[...] += dot(gl, x[here, :], 1, 0)
+        acc[...] += dot(gl, xt[0:width, part], 1, 1)
 
     if start:
-        gsel[...] = lanes_out(dot(order[:, 0:64], acc[...].astype(BF), 0, 0)).astype(BF)
-
-
-def outer(start, at, order, first, second, gt, logits, b1, x, acc=None, after=()):
-    rows, width = x.shape
+        turned = dot(order[:, 0:64], acc[...].astype(BF), 0, 0).astype(BF)
+        gsel[...] = lanes_out(dot(turned, perm[...], 1, 0)).astype(BF)
+
+
+def outer(start, rows, at, order, first, second, gt, logits, b1, xt, more=(), after=()):
+    width = gt.shape[1]
     (r_a, hid_a), (r_b, hid_b) = first, second
     chunk, hidden, _ = hid_a.shape
     outs = [((2 * chunk, width, rows), BF), ((GROWS, rows), BF)]
@@ -467,7 +525,7 @@
         16,
         4.3,
         1,
-        at, order, r_a, hid_a, r_b, hid_b, gt, logits, b1, x, *((acc,) if start else ()),
+        at, order, r_a, hid_a, r_b, hid_b, gt, logits, b1, xt, *more,
         after=after,
     )
 
@@ -475,7 +533,7 @@
 def mix_kernel(start, e_a, gp_a, e_b, gp_b, selp, ys, gls, gates, out):
     count, width, rows = ys.shape
     chunk, hidden, _ = gp_a.shape
-    tile, depth = 256, 32
+    tile, depth = 512, 16
 
     @pl.loop(0, rows // tile)
     def _(i):
@@ -542,26 +600,32 @@
     return jnp.concatenate(out, axis=0)
 
 
-def final_kernel(perm, own, recv, mixed, gf):
+def final_kernel(masks, at, own, recv, mixed, gf, token):
+    token[...] = jnp.zeros_like(token)
+    width = gf.shape[1]
+    d_of, _ = places(masks, at, width)
+    up = lax.broadcasted_iota(jnp.int32, (width, width), 0)
+    across = lax.broadcasted_iota(jnp.int32, (width, width), 1)
+    perm = (d_of(up) == across).astype(F32).astype(BF)
     for t in range(TASKS + 1):
         s = (own[t].astype(F32) + recv[t].astype(F32)).astype(BF)
-        rows = dot(s, perm[...], 0, 0).astype(BF)
+        rows = dot(s, perm, 0, 0).astype(BF)
         if t < TASKS:
             mixed[t] = rows
         else:
             gf[...] = rows
 
 
-def final(perm, own, recv, after):
+def final(masks, at, own, recv, after):
     _, width, rows = own.shape
     return kernel_call(
-        final_kernel,
-        (((TASKS, rows, width), BF), ((rows, width), BF)),
+        functools.partial(final_kernel, masks),
+        (((TASKS, rows, width), BF), ((rows, width), BF), ((8, 128), F32)),
         (),
         16,
         2.7,
-        0,
-        perm, own, recv,
+        1,
+        at, own, recv,
         after=after,
     )
 
@@ -613,7 +677,7 @@
         + [block(x.shape) for x in (w_e, w_r, w_b, w_s)],
         out_specs=tuple(block(shape) for shape, _ in outs),
         compiler_params=params(8),
-    )(core, w_e, w_r, w_b, w_s)
+    )(core, *(pltpu.with_memory_space_constraint(x, pltpu.HBM) for x in (w_e, w_r, w_b, w_s)))
 
 
 def join_kernel(plan, n_in, *refs):
@@ -764,8 +828,9 @@
     dims = [side] + [(m, 0) for m in masks]
     if n_rows == 8:
         way = ((3, 2, 0, 1), (1, 3, 2, 0))
+        back_way = ((2, 3, 0, 1), (1, 2, 3, 0))
     else:
-        way = (tuple(range(len(dims))),) * 2
+        way = back_way = (tuple(range(len(dims))),) * 2
 
     def swap(x, hops):
         pairs = []
@@ -777,6 +842,9 @@
 
     def hops(step):
         return tuple(dims[way[k][step]] for k in range(2))
+
+    def back_hops(step):
+        return tuple(dims[back_way[k][step]] for k in range(2))
 
     def table_of(pair):
         if n_rows != 8:
@@ -829,8 +897,8 @@
     b_own = jnp.concatenate([b_own, swap(b_own, sibling)], axis=0)
     x_own = features
     g_own = jnp.transpose(grad_mix, (1, 0, 2))
-    x_recv = swap(x_own, sibling)
-    g_recv = swap(g_own, sibling)
+    x_recv = swap(tie(x_own, w_recv), sibling)
+    g_recv = swap(tie(g_own, w_recv), sibling)
 
     steps = len(dims)
     ride = n_rows == 8
@@ -842,6 +910,7 @@
             (((0, 0, whole), (1, 0, whole), (0, whole, d_loc), (1, whole, d_loc)),), msg, got
         )
         got = swap(msg, hops(1))
+        xt, gt, perm, to_q = turn(masks, at, x_own, x_recv, g_own, g_recv, (msg,))
         half = whole // 2
         group = chunk * d_loc
         pieces = [
@@ -849,7 +918,7 @@
             for c in range(2)
         ]
         tail = tuple((k, 2 * whole, 2 * d_loc) for k in range(2)) + ((2, 0, 4 * experts),)
-        a_msg, b_msg = join((pieces[0] + tail, pieces[1]), msg, got, b_own)
+        a_msg, b_msg = join((pieces[0] + tail, pieces[1]), msg, got, b_own, after=(perm,))
         a_got = swap(a_msg, hops(2))
         n = 8 * group
         a_lo, riders = join(
@@ -861,15 +930,9 @@
         )
         a_hi = swap(a_lo, hops(3))
         turned = swap(riders, sibling)
-        b_got = swap(tie(b_msg, a_lo), hops(2))
-        last = a_lo
-        sel = jnp.where(core == 1, riders[:width], turned[:width])
-        sel = jnp.transpose(sel.reshape(2, 2, 2, d_loc, 2 * h_loc), (1, 0, 2, 3, 4))
-        sel = sel.reshape(width, 2 * h_loc)
-        n_b = 2 * experts
-        turned = jnp.concatenate([turned[width + n_b :], turned[width : width + n_b]], axis=0)
-        b_side = jnp.where(core == 0, riders[width:], turned)
+        b_got = swap(b_msg, hops(2))
     else:
+        xt, gt, perm, to_q = turn(masks, at, x_own, x_recv, g_own, g_recv, (sel,))
         chip = jnp.concatenate([w_mine, w_recv], axis=3)
         bufs = [chip[None, :, :chunk], chip[None, :, chunk:]]
         for step in range(steps):
@@ -878,58 +941,63 @@
                 bufs = [jnp.concatenate(pair, axis=0) for pair in zip(bufs, gots)]
         for m in masks:
             sel = jnp.concatenate([sel, swap(sel, ((m, 0), (m, 0)))], axis=0)
-        b_side = swap(b_own, (side, side))
+        riders = turned = jnp.concatenate([sel, swap(b_own, (side, side))], axis=0)
         (a_lo, a_hi), (b_lo, b_hi) = [canonical(*pair) for pair in zip(bufs, gots)]
-        last = a_lo
-
-    xt, gt, cc_a, cc_b, gates, logits, selp, gb1, perm, to_q, b0, b1 = prep(
-        masks, at, order, sel, b_own, b_side, x_own, x_recv, g_own, g_recv, (last,)
-    )
-
-    spots = table_of(way)
+
+    cc_a, cc_b, gates, logits, selp, gb1, b0, b1 = prep(
+        masks, ride, at, order, riders, turned, b_own, xt, gt
+    )
+
+    spots, back = table_of(way), table_of(back_way)
     if ride:
         (b_lo,) = join((((0, 0, n), (1, 0, n)),), b_msg, b_got, after=(b0,))
         b_hi = swap(b_lo, hops(3))
-    first = critical(spots, spots, at, a_lo, a_hi, xt, cc_a, b0, (b_lo,))
+    first = critical(spots, back, at, a_lo, a_hi, xt, cc_a, b0, (b_lo,))
     a_lo, a_msg = uncanonical(first[0], first[1])
-    a_got = swap(a_msg, hops(steps - 1))
+    a_got = swap(a_msg, back_hops(steps - 1))
     second = critical(
-        spots, spots, at, b_lo, b_hi, xt, cc_b, b0, (first[0],), (first[6], gb1, to_q, perm)
+        spots, back, at, b_lo, b_hi, xt, cc_b, b0, (first[0],), (first[6], gb1, to_q, perm)
     )
     b_lo, b_msg = second[:2]
     if not ride:
         n = b_lo.shape[0]
         b_lo, b_msg = uncanonical(b_lo, b_msg[:n])
         b_msg = jnp.concatenate([b_msg, second[1][n:]], axis=0)
-    b_got = swap(b_msg, hops(steps - 1))
+    b_got = swap(b_msg, back_hops(steps - 1))
     inner = ((first[5], first[2]), (second[5], second[2]))
     ends = ((first[4], first[3]), (second[4], second[3]))
     n_own = x_own.shape[0]
-    ys_own, gl_own, acc = outer(0, at, order, *inner, gt, logits, b1, x_own)
+    ys_own, gl_own, acc = outer(0, n_own, at, order, *inner, gt, logits, b1, xt)
 
     def next_a(step, lo, sent, got, after=()):
-        keep, msg = fold(lo, sent, got, (), after)
-        return keep, msg, swap(msg, hops(step))
+        keep, msg = fold(lo, sent, got, after)
+        return keep, msg, swap(msg, back_hops(step))
 
     a_lo, a_msg, a_got = next_a(steps - 2, a_lo, a_msg, a_got, (b_lo,))
     ys_other, gl_other, gsel = outer(
-        n_own, at, order, *inner, gt, logits, b1, x_recv, acc, (a_lo,)
-    )
-    gsel_got = swap(gsel, hops(steps - 1))
+        n_own, n_own, at, order, *inner, gt, logits, b1, xt, (perm, acc), (a_lo,)
+    )
+    gsel_got = swap(gsel, back_hops(steps - 1))
     b_lo, b_msg = fold(b_lo, b_msg, b_got)
-    a_lo, a_msg, a_got = next_a(steps - 3, a_lo, a_msg, a_got)
+    b_got = swap(b_msg, back_hops(steps - 2))
+    a_lo, a_msg, a_got = next_a(steps - 3, a_lo, a_msg, a_got, (b_lo,))
     mix_other = mix(n_own, *ends, selp, ys_other, gl_other, gates, (a_lo, b_lo))
     mix_recv = swap(mix_other, sibling)
-    b_msg = append(b_msg, gsel, gsel_got, (mix_other,))
-    b_got = swap(b_msg, hops(steps - 2))
+    gsel = plus(gsel, gsel_got, (mix_other,))
+    gsel_got = swap(gsel, back_hops(steps - 2))
+    b_lo, b_msg = fold(b_lo, b_msg, b_got, (mix_other,))
+    b_msg = append(b_msg, gsel, gsel_got, (b_lo,))
+    b_got = swap(b_msg, back_hops(steps - 3))
     mix_own = mix(0, *ends, selp, ys_own, gl_own, gates, (b_msg,))
+    for step in reversed(range(1, steps - 3)):
+        a_lo, a_msg, a_got = next_a(step, a_lo, a_msg, a_got, (mix_own,))
+    a_lo, a_msg = fold(a_lo, a_msg, a_got, (mix_own,))
+    mixed, grad_features, token = final(masks, at, mix_own, mix_recv, (a_lo, b_msg))
     for step in reversed(range(steps - 3)):
-        a_lo, a_msg, a_got = next_a(step, a_lo, a_msg, a_got)
-    mixed, grad_features = final(perm, mix_own, mix_recv, (a_lo,))
-    for step in reversed(range(steps - 2)):
-        b_lo, b_msg = fold(b_lo, b_msg, b_got, (), (grad_features,))
-        b_got = swap(b_msg, hops(step))
-    own, msg = last_fold(a_lo, a_got, b_lo, b_msg, b_got)
+        tail = () if step else (a_msg,)
+        b_lo, b_msg = fold(b_lo, b_msg, b_got, (token,), tail)
+        b_got = swap(b_msg, back_hops(step))
+    own, msg = last_fold(a_lo, b_lo, b_msg, b_got)
     got = swap(msg, sibling)
     mixed = jnp.transpose(mixed, (1, 0, 2))
 

time: 116 us -> 97.5 us (0.84)
  local copies, waits for them, and re-layouts: 9.97 us -> 0.6 us
  waiting for transfers between devices: 31.7 us -> 22.7 us
  starting transfers between devices: 23.7 us -> 26 us
    ppermute x22, waiting for transfers between devices: 31.7 us -> 22.7 us  [swap(): return lax.ppermute(x, ('rows', 'hid'), pairs)]
    unnamed x57 -> x45, local copies, waits for them, and re-layouts: 9.24 us -> 0.59 us
    ppermute x22, starting transfers between devices: 23.7 us -> 26 us  [swap(): return lax.ppermute(x, ('rows', 'hid'), pairs)]
    pallas_call x22 -> x24, Pallas kernels: 46.3 us -> 45.3 us  [kernel_call(): pl.pallas_call(kernel, out_shape=tuple((jax.ShapeDtypeStruct(shape, kind)...]
  transfers between devices with their start and end apart: 22 -> 22, of which waited for: 9 -> 7; matrix products, arithmetic and copies ran while one was open for 1% -> 0% of each run, Pallas kernels for 38% -> 44%
where the time goes in v3:
time: 97.5 us; the launch traced here: 97.3 us
  Pallas kernels  46.8 us (48%)
  starting transfers between devices  26 us (27%)
  waiting for transfers between devices  22.7 us (23%)
  between operations  1.13 us (1%)
    pallas_call x24, Pallas kernels, kernel_call(): pl.pallas_call(kernel, out_shape=tuple((jax.ShapeDtypeStruct(shape, kind)...  45.3 us
    ppermute x22, starting transfers between devices, swap(): return lax.ppermute(x, ('rows', 'hid'), pairs)  26 us
    ppermute x22, waiting for transfers between devices, swap(): return lax.ppermute(x, ('rows', 'hid'), pairs)  22.7 us
  transfers between devices with their start and end apart: 22, of which 7 were waited for; matrix products, arithmetic and copies ran while one was open for 0% of the time, Pallas kernels for 44%

profile of v3, /device:TPU:0, one launch (start us, length us, event | category | flops | bytes accessed | tf_op | source)
XLA Modules:
  0.0 97.3 jit_solution(2919969424025542909)
XLA Ops:
  0.7 0.1 pad_add_fusion.core.refs_0_
  0.7 1.5 %shard_map.254 = (bf16[32,128]{1,0:T(8,128)(2,1)S(1)}, bf16[32,128]{1,0:T(8,128)(2,1)S(1)}, bf16[2,8,32,64]{3,2,1,0:T(8,128)(2,1)S(1)}, bf16[2,8,32,64]{3,2,1,0:T(8,128)(2,1)S(1)}) custom-call(s32[3]{0:T(128)S(1)} %pad_add_fusion.core.refs_0_, f32[32,16,64]{2,1,0:T(8,128)} %refs_4_.1, f32[16,32,64]{2,1,0:T(8,128)} %bitcast.11, f32[2,16,64]{2,1,0:T(8,128)} %refs_10_.1, ...), custom_call_target="tpu_custom_call" | custom-call | tf_op jit(solution)/shard_map/pallas_call | solution.py:672
  2.3 0.5 collective-permute-start
  2.8 1.0 %collective-permute-done.refs_1_ = bf16[2,8,32,64]{3,2,1,0:T(8,128)(2,1)S(1)} collective-permute-done((bf16[2,8,32,64]{3,2,1,0:T(8,128)(2,1)S(1)}, bf16[2,8,32,64]{3,2,1,0:T(8,128)(2,1)S(1)}, u32[]{:S(2)}, u32[]{:S(2)}) %collective-permute-start) | collective-permute-done | bytes 65568 | tf_op jit(solution)/shard_map/ppermute | solution.py:841
  3.8 0.4 collective-permute-start.5
  4.1 0.1 collective-permute-start.3
  4.3 0.1 shard_map.255.refs_0_
  4.4 4.0 %collective-permute-start.1 = (bf16[544,128]{1,0:T(8,128)(2,1)S(1)}, bf16[544,128]{1,0:T(8,128)(2,1)S(1)}, u32[]{:S(2)}, u32[]{:S(2)}) collective-permute-start(bf16[544,128]{1,0:T(8,128)(2,1)S(1)} %shard_map.255.refs_0_), channel_id=1, source_target_pairs={{0,16},{1,5},{2,18},{3,7},{4,20},{5,1},{6,22},{7,3},{8,24},{9,13},... | collective-permute-start | bytes 417800 | tf_op jit(solution)/shard_map/ppermute | solution.py:841
  8.4 0.0 collective-permute-done.3
  8.4 0.0 copy-start.4
  8.4 4.5 %collective-permute-done.1.refs_1_ = bf16[544,128]{1,0:T(8,128)(2,1)S(1)} collective-permute-done((bf16[544,128]{1,0:T(8,128)(2,1)S(1)}, bf16[544,128]{1,0:T(8,128)(2,1)S(1)}, u32[]{:S(2)}, u32[]{:S(2)}) %collective-permute-start.1) | collective-permute-done | bytes 139296 | tf_op jit(solution)/shard_map/ppermute | solution.py:841
  13.0 1.1 %collective-permute-start.2 = (bf16[1088,128]{1,0:T(8,128)(2,1)S(1)}, bf16[1088,128]{1,0:T(8,128)(2,1)S(1)}, u32[]{:S(2)}, u32[]{:S(2)}) collective-permute-start(bf16[1088,128]{1,0:T(8,128)(2,1)S(1)} %shard_map.256.refs_5_.refs_0_), channel_id=1, source_target_pairs={{0,8},{1,17},{2,10},{3,19},{4,12},{5,21},{6,14},{7,23},{8,0},{9,25... | collective-permute-start | bytes 835592 | tf_op jit(solution)/shard_map/ppermute | solution.py:841
  14.0 1.9 %shard_map.257 = (bf16[272,2048]{1,0:T(8,128)(2,1)S(1)}, bf16[3,256,2048]{2,1,0:T(8,128)(2,1)S(1)}, bf16[256,256]{1,0:T(8,128)(2,1)S(1)}, bf16[256,256]{1,0:T(8,128)(2,1)S(1)}) custom-call(s32[3]{0:T(128)S(1)} %pad_add_fusion.core.refs_0_, bf16[1024,256]{1,0:T(8,128)(2,1)S(1)} %copy-done.5, bf16[1024,256]{1,0:T(8,128)(2,1)S(1)} %collective-permute-done.4.refs_2_, ...), custom_call_target="tpu_custom_call" | custom-call | flops 41999998976 | tf_op jit(solution)/shard_map/pallas_call | solution.py:54
  15.9 0.0 copy-start.16
  15.9 5.5 %collective-permute-done.2.refs_1_ = bf16[1088,128]{1,0:T(8,128)(2,1)S(1)} collective-permute-done((bf16[1088,128]{1,0:T(8,128)(2,1)S(1)}, bf16[1088,128]{1,0:T(8,128)(2,1)S(1)}, u32[]{:S(2)}, u32[]{:S(2)}) %collective-permute-start.2) | collective-permute-done | bytes 278560 | tf_op jit(solution)/shard_map/ppermute | solution.py:841
  21.4 0.0 copy-start.14
  21.5 1.9 %collective-permute-start.6 = (bf16[1216,128]{1,0:T(8,128)(2,1)S(1)}, bf16[1216,128]{1,0:T(8,128)(2,1)S(1)}, u32[]{:S(2)}, u32[]{:S(2)}) collective-permute-start(bf16[1216,128]{1,0:T(8,128)(2,1)S(1)} %get-tuple-element.91.refs_0_), channel_id=1, source_target_pairs={{0,2},{1,9},{2,0},{3,11},{4,6},{5,13},{6,4},{7,15},{8,10},{9,1},{1... | collective-permute-start | bytes 933896 | tf_op jit(solution)/shard_map/ppermute | solution.py:841
  23.4 5.0 %collective-permute-done.6.refs_1_ = bf16[1216,128]{1,0:T(8,128)(2,1)S(1)} collective-permute-done((bf16[1216,128]{1,0:T(8,128)(2,1)S(1)}, bf16[1216,128]{1,0:T(8,128)(2,1)S(1)}, u32[]{:S(2)}, u32[]{:S(2)}) %collective-permute-start.6) | collective-permute-done | bytes 311328 | tf_op jit(solution)/shard_map/ppermute | solution.py:841
  28.5 0.1 collective-permute-start.8
  28.5 1.9 %collective-permute-start.9 = (bf16[1024,128]{1,0:T(8,128)(2,1)S(1)}, bf16[1024,128]{1,0:T(8,128)(2,1)S(1)}, u32[]{:S(2)}, u32[]{:S(2)}) collective-permute-start(bf16[1024,128]{1,0:T(8,128)(2,1)S(1)} %get-tuple-element.98.refs_0_), channel_id=1, source_target_pairs={{0,2},{1,9},{2,0},{3,11},{4,6},{5,13},{6,4},{7,15},{8,10},{9,1},{1... | collective-permute-start | bytes 786440 | tf_op jit(solution)/shard_map/ppermute | solution.py:841
  30.5 1.5 %collective-permute-start.7 = (bf16[2048,128]{1,0:T(8,128)(2,1)S(1)}, bf16[2048,128]{1,0:T(8,128)(2,1)S(1)}, u32[]{:S(2)}, u32[]{:S(2)}) collective-permute-start(bf16[2048,128]{1,0:T(8,128)(2,1)S(1)} %get-tuple-element.92.refs_1_), channel_id=1, source_target_pairs={{0,4},{1,3},{2,6},{3,1},{4,0},{5,7},{6,2},{7,5},{8,12},{9,11},{10,... | collective-permute-start | bytes 1572872 | tf_op jit(solution)/shard_map/ppermute | solution.py:841
  32.0 0.0 collective-permute-done.8.refs_3_
  32.0 6.1 %shard_map.260 = (bf16[4,256,2048]{2,1,0:T(8,128)(2,1)S(1)}, bf16[4,256,2048]{2,1,0:T(8,128)(2,1)S(1)}, f32[8,8,2048]{2,1,0:T(8,128)S(1)}, f32[160,2048]{1,0:T(8...) custom-call(s32[3]{0:T(128)S(1)} %pad_add_fusion.core.refs_0_, ...), custom_call_target="tpu_custom_call" | custom-call | flops 60000002048 | tf_op jit(solution)/shard_map/pallas_call | solution.py:54
  38.1 0.0 collective-permute-done.9.refs_1_
  38.2 1.5 %collective-permute-start.10 = (bf16[2048,128]{1,0:T(8,128)(2,1)S(1)}, bf16[2048,128]{1,0:T(8,128)(2,1)S(1)}, u32[]{:S(2)}, u32[]{:S(2)}) collective-permute-start(bf16[2048,128]{1,0:T(8,128)(2,1)S(1)} %shard_map.261.refs_6_.refs_1_), channel_id=1, source_target_pairs={{0,4},{1,3},{2,6},{3,1},{4,0},{5,7},{6,2},{7,5},{8,12},{9,11},{10,... | collective-permute-start | bytes 1572872 | tf_op jit(solution)/shard_map/ppermute | solution.py:841
  39.7 0.0 collective-permute-done.7.refs_2_
  39.7 7.3 %shard_map.262 = (bf16[2048,128]{1,0:T(8,128)(2,1)S(1)}, bf16[2048,128]{1,0:T(8,128)(2,1)S(1)}, bf16[4,256,2048]{2,1,0:T(8,128)(2,1)S(1)}, bf16[4,256,2048]{2,1,...) custom-call(s32[3]{0:T(128)S(1)} %pad_add_fusion.core.refs_0_, ...), custom_call_target="tpu_custom_call" | custom-call | flops 91199995904 | tf_op jit(solution)/shard_map/pallas_call | solution.py:54
  47.1 1.5 %collective-permute-start.13 = (bf16[2048,128]{1,0:T(8,128)(2,1)S(1)}, bf16[2048,128]{1,0:T(8,128)(2,1)S(1)}, u32[]{:S(2)}, u32[]{:S(2)}) collective-permute-start(bf16[2048,128]{1,0:T(8,128)(2,1)S(1)} %get-tuple-element.123.refs_1_), channel_id=1, source_target_pairs={{0,4},{1,3},{2,6},{3,1},{4,0},{5,7},{6,2},{7,5},{8,12},{9,11},{10,... | collective-permute-start | bytes 1572872 | tf_op jit(solution)/shard_map/ppermute | solution.py:841
  48.6 0.0 collective-permute-done.10.refs_2_
  48.6 7.3 %shard_map.263 = (bf16[2048,128]{1,0:T(8,128)(2,1)S(1)}, bf16[2080,128]{1,0:T(8,128)(2,1)S(1)}, bf16[4,256,2048]{2,1,0:T(8,128)(2,1)S(1)}, bf16[4,256,2048]{2,1,...) custom-call(s32[3]{0:T(128)S(1)} %pad_add_fusion.core.refs_0_, ...), custom_call_target="tpu_custom_call" | custom-call | flops 91199995904 | tf_op jit(solution)/shard_map/pallas_call | solution.py:54
  55.9 0.6 collective-permute-start.11
  56.5 4.3 %shard_map.264 = (bf16[8,256,1024]{2,1,0:T(8,128)(2,1)S(1)}, bf16[160,1024]{1,0:T(8,128)(2,1)S(1)}, f32[160,256]{1,0:T(8,128)S(1)}) custom-call(s32[3]{0:T(128)S(1)} %pad_add_fusion.core.refs_0_, bf16[160,128]{1,0:T(8,128)(2,1)S(1)} %copy-done.15, bf16[256,1024]{1,0:T(8,128)(2,1)S(1)} %get-tuple-element.109.refs_2_, ...), custom_call_target="tpu_custom_call" | custom-call | flops 51599998976 | tf_op jit(solution)/shard_map/pallas_call | solution.py:54
  60.8 0.0 collective-permute-done.13.refs_2_
  60.8 0.1 shard_map.266
  60.9 1.6 %collective-permute-start.14 = (bf16[1024,128]{1,0:T(8,128)(2,1)S(1)}, bf16[1024,128]{1,0:T(8,128)(2,1)S(1)}, u32[]{:S(2)}, u32[]{:S(2)}) collective-permute-start(bf16[1024,128]{1,0:T(8,128)(2,1)S(1)} %get-tuple-element.127.refs_1_), channel_id=1, source_target_pairs={{0,2},{1,17},{2,0},{3,19},{4,6},{5,21},{6,4},{7,23},{8,10},{9,25},... | collective-permute-start | bytes 786440 | tf_op jit(solution)/shard_map/ppermute | solution.py:841
  62.5 0.5 copy-done.21
  63.0 4.7 %shard_map.267 = (bf16[8,256,1024]{2,1,0:T(8,128)(2,1)S(1)}, bf16[160,1024]{1,0:T(8,128)(2,1)S(1)}, bf16[128,128]{1,0:T(8,128)(2,1)S(1)}) custom-call(s32[3]{0:T(128)S(1)} %pad_add_fusion.core.refs_0_, bf16[160,128]{1,0:T(8,128)(2,1)S(1)} %copy-done.15, bf16[256,1024]{1,0:T(8,128)(2,1)S(1)} %get-tuple-element.109.refs_2_, ...), custom_call_target="tpu_custom_call" | custom-call | flops 51599998976 | tf_op jit(solution)/shard_map/pallas_call | solution.py:54
  67.7 1.5 %collective-permute-start.15 = (bf16[128,128]{1,0:T(8,128)(2,1)S(1)}, bf16[128,128]{1,0:T(8,128)(2,1)S(1)}, u32[]{:S(2)}, u32[]{:S(2)}) collective-permute-start(bf16[128,128]{1,0:T(8,128)(2,1)S(1)} %get-tuple-element.130.refs_0_), channel_id=1, source_target_pairs={{0,4},{1,3},{2,6},{3,1},{4,0},{5,7},{6,2},{7,5},{8,12},{9,11},{10,... | collective-permute-start | bytes 98312 | tf_op jit(solution)/shard_map/ppermute | solution.py:841
  69.3 0.1 shard_map.265
  69.4 0.6 collective-permute-start.12
  70.0 0.1 shard_map.268
  70.1 3.7 %shard_map.269.refs_3_.refs_2_ = bf16[4,256,1024]{2,1,0:T(8,128)(2,1)S(1)} custom-call(bf16[256,1024]{1,0:T(8,128)(2,1)S(1)} %get-tuple-element.99.refs_0_, bf16[4,256,2048]{2,1,0:T(8,128)(2,1)S(1)} %get-tuple-element.100.refs_1_, bf16[256,1024]{1,0:T(8,128)(2,1)S(1)} %get-tuple-element.106.refs_2_, bf16[4,256,2048]{2,1,0:T(8,128)(2,1)S(1)} %get-tuple-element.107.refs_3_, ...), custom_call_target="tpu_custom_call" | custom-call | flops 48000000000 | tf_op jit(solution)/shard_map/pallas_call | solution.py:54
  73.8 2.2 %collective-permute-start.17 = (bf16[4,256,1024]{2,1,0:T(8,128)(2,1)S(1)}, bf16[4,256,1024]{2,1,0:T(8,128)(2,1)S(1)}, u32[]{:S(2)}, u32[]{:S(2)}) collective-permute-start(bf16[4,256,1024]{2,1,0:T(8,128)(2,1)S(1)} %shard_map.269.refs_3_.refs_2_), channel_id=1, source_target_pairs={{0,1},{1,0},{2,3},{3,2},{4,5},{5,4},{6,7},{7,6},{8,9},{9,8},{10,11... | collective-permute-start | bytes 6291464 | tf_op jit(solution)/shard_map/ppermute | solution.py:841
  76.0 0.4 collective-permute-start.16
  76.4 1.4 %collective-permute-start.18 = (bf16[512,128]{1,0:T(8,128)(2,1)S(1)}, bf16[512,128]{1,0:T(8,128)(2,1)S(1)}, u32[]{:S(2)}, u32[]{:S(2)}) collective-permute-start(bf16[512,128]{1,0:T(8,128)(2,1)S(1)} %get-tuple-element.132.refs_1_), channel_id=1, source_target_pairs={{0,16},{1,9},{2,18},{3,11},{4,20},{5,13},{6,22},{7,15},{8,24},{9,1... | collective-permute-start | bytes 393224 | tf_op jit(solution)/shard_map/ppermute | solution.py:841
  77.8 0.1 shard_map.270
  77.9 2.1 %collective-permute-done.16.refs_2_ = bf16[128,128]{1,0:T(8,128)(2,1)S(1)} collective-permute-done((bf16[128,128]{1,0:T(8,128)(2,1)S(1)}, bf16[128,128]{1,0:T(8,128)(2,1)S(1)}, u32[]{:S(2)}, u32[]{:S(2)}) %collective-permute-start.16) | collective-permute-done | bytes 32800 | tf_op jit(solution)/shard_map/ppermute | solution.py:841
  80.0 0.7 collective-permute-start.19
  80.7 3.5 %shard_map.273.refs_3_.refs_1_ = bf16[4,256,1024]{2,1,0:T(8,128)(2,1)S(1)} custom-call(bf16[256,1024]{1,0:T(8,128)(2,1)S(1)} %get-tuple-element.99.refs_0_, bf16[4,256,2048]{2,1,0:T(8,128)(2,1)S(1)} %get-tuple-element.100.refs_1_, bf16[256,1024]{1,0:T(8,128)(2,1)S(1)} %get-tuple-element.106.refs_2_, bf16[4,256,2048]{2,1,0:T(8,128)(2,1)S(1)} %get-tuple-element.107.refs_3_, ...), custom_call_target="tpu_custom_call" | custom-call | flops 48000000000 | tf_op jit(solution)/shard_map/pallas_call | solution.py:54
  84.3 3.2 %shard_map.275 = (bf16[3,1024,256]{2,1,0:T(8,128)(2,1)}, bf16[1024,256]{1,0:T(8,128)(2,1)}, f32[8,128]{1,0:T(8,128)S(1)}) custom-call(s32[3]{0:T(128)S(1)} %pad_add_fusion.core.refs_0_, bf16[4,256,1024]{2,1,0:T(8,128)(2,1)S(1)} %shard_map.273.refs_3_.refs_1_, bf16[4,256,1024]{2,1,0:T(8,128)(2,1)S(1)} %collective-permute-done.17.refs_2_, ...), custom_call_target="tpu_custom_call" | custom-call | flops 32399998976 | tf_op jit(solution)/shard_map/pallas_call | solution.py:54
  87.5 2.2 %collective-permute-start.20 = (bf16[672,128]{1,0:T(8,128)(2,1)S(1)}, bf16[672,128]{1,0:T(8,128)(2,1)S(1)}, u32[]{:S(2)}, u32[]{:S(2)}) collective-permute-start(bf16[672,128]{1,0:T(8,128)(2,1)S(1)} %get-tuple-element.139.refs_2_), channel_id=1, source_target_pairs={{0,8},{1,5},{2,10},{3,7},{4,12},{5,1},{6,14},{7,3},{8,0},{9,13},{1... | collective-permute-start | bytes 516104 | tf_op jit(solution)/shard_map/ppermute | solution.py:841
  89.7 3.4 %collective-permute-done.20.refs_3_ = bf16[672,128]{1,0:T(8,128)(2,1)S(1)} collective-permute-done((bf16[672,128]{1,0:T(8,128)(2,1)S(1)}, bf16[672,128]{1,0:T(8,128)(2,1)S(1)}, u32[]{:S(2)}, u32[]{:S(2)}) %collective-permute-start.20) | collective-permute-done | bytes 172064 | tf_op jit(solution)/shard_map/ppermute | solution.py:841
  93.1 0.0 copy-start.6
  93.1 0.0 copy-start.7
  93.1 0.0 copy-start.8
  93.1 0.0 copy-start.9
  93.1 0.0 copy-start.10
  93.1 0.0 copy-start.11
  93.2 0.0 copy-start.12
  93.2 0.0 copy-start.13
  93.2 0.1 shard_map.277
  93.3 0.2 collective-permute-start.21
  93.5 1.2 %collective-permute-done.21.refs_3_ = bf16[416,128]{1,0:T(8,128)(2,1)S(1)} collective-permute-done((bf16[416,128]{1,0:T(8,128)(2,1)S(1)}, bf16[416,128]{1,0:T(8,128)(2,1)S(1)}, u32[]{:S(2)}, u32[]{:S(2)}) %collective-permute-start.21) | collective-permute-done | bytes 106528 | tf_op jit(solution)/shard_map/ppermute | solution.py:841
  94.8 2.4 %shard_map.278 = (f32[32,16,64]{2,1,0:T(8,128)}, f32[32,16,64]{2,1,0:T(8,128)}, f32[32,16,64]{2,1,0:T(8,128)}, f32[16,32,64]{2,1,0:T(8,128)}, f32[16,32,64]{2,1,...) custom-call(s32[3]{0:T(128)S(1)} %pad_add_fusion.core.refs_0_, ...), custom_call_target="tpu_custom_call" | custom-call | flops 28800000000 | tf_op jit(solution)/shard_map/pallas_call | solution.py:54
  (52 shorter events, 0.3 us)
Async XLA Ops:
  2.3 1.5 %collective-permute-start = (bf16[2,8,32,64]{3,2,1,0:T(8,128)(2,1)S(1)}, bf16[2,8,32,64]{3,2,1,0:T(8,128)(2,1)S(1)}, u32[]{:S(2)}, u32[]{:S(2)}) collective-permute-start(bf16[2,8,32,64]{3,2,1,0:T(8,128)(2,1)S(1)} %get-tuple-element.85), channel_id=1, source_target_pairs={{0,1},{1,0},{2,3},{3,2},{4,5},{5,4},{6,7},{7,6},{8,9},{9,8},{10,11... | collective-permute-start | bytes 196616 | tf_op jit(solution)/shard_map/ppermute | solution.py:841
  3.8 10.3 %collective-permute-start.5 = (bf16[3,1024,256]{2,1,0:T(8,128)(2,1)}, bf16[3,1024,256]{2,1,0:T(8,128)(2,1)S(1)}, u32[]{:S(2)}, u32[]{:S(2)}) collective-permute-start(bf16[3,1024,256]{2,1,0:T(8,128)(2,1)} %bitcast.13), channel_id=1, source_target_pairs={{0,1},{1,0},{2,3},{3,2},{4,5},{5,4},{6,7},{7,6},{8,9},{9,8},{10,11... | collective-permute-start | bytes 4718600 | tf_op jit(solution)/shard_map/ppermute | solution.py:841
  4.1 4.3 %collective-permute-start.3 = (bf16[32,128]{1,0:T(8,128)(2,1)S(1)}, bf16[32,128]{1,0:T(8,128)(2,1)S(1)}, u32[]{:S(2)}, u32[]{:S(2)}) collective-permute-start(bf16[32,128]{1,0:T(8,128)(2,1)S(1)} %get-tuple-element.87), channel_id=1, source_target_pairs={{0,1},{1,0},{2,3},{3,2},{4,5},{5,4},{6,7},{7,6},{8,9},{9,8},{10,11... | collective-permute-start | bytes 24584 | tf_op jit(solution)/shard_map/ppermute | solution.py:841
  4.3 4.1 %copy-start.5 = (bf16[1024,256]{1,0:T(8,128)(2,1)S(1)}, bf16[1024,256]{1,0:T(8,128)(2,1)}, u32[]{:S(2)}) copy-start(bf16[1024,256]{1,0:T(8,128)(2,1)} %refs_1_.4) | copy-start | bytes 1572868
  4.4 8.5 %collective-permute-start.1 = (bf16[544,128]{1,0:T(8,128)(2,1)S(1)}, bf16[544,128]{1,0:T(8,128)(2,1)S(1)}, u32[]{:S(2)}, u32[]{:S(2)}) collective-permute-start(bf16[544,128]{1,0:T(8,128)(2,1)S(1)} %shard_map.255.refs_0_), channel_id=1, source_target_pairs={{0,16},{1,5},{2,18},{3,7},{4,20},{5,1},{6,22},{7,3},{8,24},{9,13},... | collective-permute-start | bytes 417800 | tf_op jit(solution)/shard_map/ppermute | solution.py:841
  8.4 5.6 %collective-permute-start.4 = (bf16[1024,256]{1,0:T(8,128)(2,1)S(1)}, bf16[1024,256]{1,0:T(8,128)(2,1)S(1)}, u32[]{:S(2)}, u32[]{:S(2)}) collective-permute-start(bf16[1024,256]{1,0:T(8,128)(2,1)S(1)} %copy-done.5), channel_id=1, source_target_pairs={{0,1},{1,0},{2,3},{3,2},{4,5},{5,4},{6,7},{7,6},{8,9},{9,8},{10,11... | collective-permute-start | bytes 1572872 | tf_op jit(solution)/shard_map/ppermute | solution.py:841
  8.4 5.6 %copy-start.4 = (bf16[1024,3,256]{2,0,1:T(8,128)(2,1)S(1)}, bf16[1024,3,256]{2,0,1:T(8,128)(2,1)}, u32[]{:S(2)}) copy-start(bf16[1024,3,256]{2,0,1:T(8,128)(2,1)} %param.20) | copy-start | bytes 4718596
  13.0 8.4 %collective-permute-start.2 = (bf16[1088,128]{1,0:T(8,128)(2,1)S(1)}, bf16[1088,128]{1,0:T(8,128)(2,1)S(1)}, u32[]{:S(2)}, u32[]{:S(2)}) collective-permute-start(bf16[1088,128]{1,0:T(8,128)(2,1)S(1)} %shard_map.256.refs_5_.refs_0_), channel_id=1, source_target_pairs={{0,8},{1,17},{2,10},{3,19},{4,12},{5,21},{6,14},{7,23},{8,0},{9,25... | collective-permute-start | bytes 835592 | tf_op jit(solution)/shard_map/ppermute | solution.py:841
  15.9 5.5 %copy-start.16 = (bf16[256,256]{1,0:T(8,128)(2,1)}, bf16[256,256]{1,0:T(8,128)(2,1)S(1)}, u32[]{:S(2)}) copy-start(bf16[256,256]{1,0:T(8,128)(2,1)S(1)} %get-tuple-element.90.refs_3_.refs_9_.refs_10_) | copy-start | bytes 393220
  15.9 16.1 %copy-start.18 = (bf16[3,256,2048]{2,1,0:T(8,128)(2,1)}, bf16[3,256,2048]{2,1,0:T(8,128)(2,1)S(1)}, u32[]{:S(2)}) copy-start(bf16[3,256,2048]{2,1,0:T(8,128)(2,1)S(1)} %get-tuple-element.95.refs_6_) | copy-start | bytes 9437188
  21.4 10.6 %copy-start.14 = (bf16[160,128]{1,0:T(8,128)(2,1)S(1)}, bf16[160,128]{1,0:T(8,128)(2,1)}, u32[]{:S(2)}) copy-start(bf16[160,128]{1,0:T(8,128)(2,1)} %constant.24.clone.refs_1_) | copy-start | bytes 122884
  21.5 7.0 %collective-permute-start.6 = (bf16[1216,128]{1,0:T(8,128)(2,1)S(1)}, bf16[1216,128]{1,0:T(8,128)(2,1)S(1)}, u32[]{:S(2)}, u32[]{:S(2)}) collective-permute-start(bf16[1216,128]{1,0:T(8,128)(2,1)S(1)} %get-tuple-element.91.refs_0_), channel_id=1, source_target_pairs={{0,2},{1,9},{2,0},{3,11},{4,6},{5,13},{6,4},{7,15},{8,10},{9,1},{1... | collective-permute-start | bytes 933896 | tf_op jit(solution)/shard_map/ppermute | solution.py:841
  28.5 3.5 %collective-permute-start.8 = (bf16[320,128]{1,0:T(8,128)(2,1)S(1)}, bf16[320,128]{1,0:T(8,128)(2,1)S(1)}, u32[]{:S(2)}, u32[]{:S(2)}) collective-permute-start(bf16[320,128]{1,0:T(8,128)(2,1)S(1)} %get-tuple-element.94.refs_2_), channel_id=1, source_target_pairs={{0,1},{1,0},{2,3},{3,2},{4,5},{5,4},{6,7},{7,6},{8,9},{9,8},{10,11... | collective-permute-start | bytes 245768 | tf_op jit(solution)/shard_map/ppermute | solution.py:841
  28.5 9.6 %collective-permute-start.9 = (bf16[1024,128]{1,0:T(8,128)(2,1)S(1)}, bf16[1024,128]{1,0:T(8,128)(2,1)S(1)}, u32[]{:S(2)}, u32[]{:S(2)}) collective-permute-start(bf16[1024,128]{1,0:T(8,128)(2,1)S(1)} %get-tuple-element.98.refs_0_), channel_id=1, source_target_pairs={{0,2},{1,9},{2,0},{3,11},{4,6},{5,13},{6,4},{7,15},{8,10},{9,1},{1... | collective-permute-start | bytes 786440 | tf_op jit(solution)/shard_map/ppermute | solution.py:841
  30.5 9.2 %collective-permute-start.7 = (bf16[2048,128]{1,0:T(8,128)(2,1)S(1)}, bf16[2048,128]{1,0:T(8,128)(2,1)S(1)}, u32[]{:S(2)}, u32[]{:S(2)}) collective-permute-start(bf16[2048,128]{1,0:T(8,128)(2,1)S(1)} %get-tuple-element.92.refs_1_), channel_id=1, source_target_pairs={{0,4},{1,3},{2,6},{3,1},{4,0},{5,7},{6,2},{7,5},{8,12},{9,11},{10,... | collective-permute-start | bytes 1572872 | tf_op jit(solution)/shard_map/ppermute | solution.py:841
  38.2 10.4 %collective-permute-start.10 = (bf16[2048,128]{1,0:T(8,128)(2,1)S(1)}, bf16[2048,128]{1,0:T(8,128)(2,1)S(1)}, u32[]{:S(2)}, u32[]{:S(2)}) collective-permute-start(bf16[2048,128]{1,0:T(8,128)(2,1)S(1)} %shard_map.261.refs_6_.refs_1_), channel_id=1, source_target_pairs={{0,4},{1,3},{2,6},{3,1},{4,0},{5,7},{6,2},{7,5},{8,12},{9,11},{10,... | collective-permute-start | bytes 1572872 | tf_op jit(solution)/shard_map/ppermute | solution.py:841
  39.7 8.9 %copy-start.17 = (bf16[256,256]{1,0:T(8,128)(2,1)S(1)}, bf16[256,256]{1,0:T(8,128)(2,1)}, u32[]{:S(2)}) copy-start(bf16[256,256]{1,0:T(8,128)(2,1)} %copy-done.16) | copy-start | bytes 393220
  47.1 13.7 %collective-permute-start.13 = (bf16[2048,128]{1,0:T(8,128)(2,1)S(1)}, bf16[2048,128]{1,0:T(8,128)(2,1)S(1)}, u32[]{:S(2)}, u32[]{:S(2)}) collective-permute-start(bf16[2048,128]{1,0:T(8,128)(2,1)S(1)} %get-tuple-element.123.refs_1_), channel_id=1, source_target_pairs={{0,4},{1,3},{2,6},{3,1},{4,0},{5,7},{6,2},{7,5},{8,12},{9,11},{10,... | collective-permute-start | bytes 1572872 | tf_op jit(solution)/shard_map/ppermute | solution.py:841
  48.6 7.9 %copy-start.15 = (bf16[160,128]{1,0:T(8,128)(2,1)S(1)}, bf16[160,128]{1,0:T(8,128)(2,1)}, u32[]{:S(2)}) copy-start(bf16[160,128]{1,0:T(8,128)(2,1)} %constant.24.clone.refs_1_) | copy-start | bytes 122884
  48.6 7.9 %copy-start.19 = (bf16[3,256,2048]{2,1,0:T(8,128)(2,1)S(1)}, bf16[3,256,2048]{2,1,0:T(8,128)(2,1)}, u32[]{:S(2)}) copy-start(bf16[3,256,2048]{2,1,0:T(8,128)(2,1)} %copy-done.18) | copy-start | bytes 9437188
  55.9 4.9 %copy-start.20 = (bf16[4,256,2048]{2,1,0:T(8,128)(2,1)}, bf16[4,256,2048]{2,1,0:T(8,128)(2,1)S(1)}, u32[]{:S(2)}) copy-start(bf16[4,256,2048]{2,1,0:T(8,128)(2,1)S(1)} %get-tuple-element.112.refs_5_) | copy-start | bytes 12582916
  55.9 13.3 %collective-permute-start.11 = (bf16[2080,128]{1,0:T(8,128)(2,1)S(1)}, bf16[2080,128]{1,0:T(8,128)(2,1)S(1)}, u32[]{:S(2)}, u32[]{:S(2)}) collective-permute-start(bf16[2080,128]{1,0:T(8,128)(2,1)S(1)} %get-tuple-element.119.refs_1_), channel_id=1, source_target_pairs={{0,4},{1,3},{2,6},{3,1},{4,0},{5,7},{6,2},{7,5},{8,12},{9,11},{10,... | collective-permute-start | bytes 1597448 | tf_op jit(solution)/shard_map/ppermute | solution.py:841
  60.8 2.2 %copy-start.21 = (bf16[4,256,2048]{2,1,0:T(8,128)(2,1)S(1)}, bf16[4,256,2048]{2,1,0:T(8,128)(2,1)}, u32[]{:S(2)}) copy-start(bf16[4,256,2048]{2,1,0:T(8,128)(2,1)} %copy-done.20) | copy-start | bytes 12582916
  60.9 9.1 %collective-permute-start.14 = (bf16[1024,128]{1,0:T(8,128)(2,1)S(1)}, bf16[1024,128]{1,0:T(8,128)(2,1)S(1)}, u32[]{:S(2)}, u32[]{:S(2)}) collective-permute-start(bf16[1024,128]{1,0:T(8,128)(2,1)S(1)} %get-tuple-element.127.refs_1_), channel_id=1, source_target_pairs={{0,2},{1,17},{2,0},{3,19},{4,6},{5,21},{6,4},{7,23},{8,10},{9,25},... | collective-permute-start | bytes 786440 | tf_op jit(solution)/shard_map/ppermute | solution.py:841
  67.7 8.3 %collective-permute-start.15 = (bf16[128,128]{1,0:T(8,128)(2,1)S(1)}, bf16[128,128]{1,0:T(8,128)(2,1)S(1)}, u32[]{:S(2)}, u32[]{:S(2)}) collective-permute-start(bf16[128,128]{1,0:T(8,128)(2,1)S(1)} %get-tuple-element.130.refs_0_), channel_id=1, source_target_pairs={{0,4},{1,3},{2,6},{3,1},{4,0},{5,7},{6,2},{7,5},{8,12},{9,11},{10,... | collective-permute-start | bytes 98312 | tf_op jit(solution)/shard_map/ppermute | solution.py:841
  69.4 8.4 %collective-permute-start.12 = (bf16[1056,128]{1,0:T(8,128)(2,1)S(1)}, bf16[1056,128]{1,0:T(8,128)(2,1)S(1)}, u32[]{:S(2)}, u32[]{:S(2)}) collective-permute-start(bf16[1056,128]{1,0:T(8,128)(2,1)S(1)} %get-tuple-element.121.refs_1_), channel_id=1, source_target_pairs={{0,2},{1,17},{2,0},{3,19},{4,6},{5,21},{6,4},{7,23},{8,10},{9,25},... | collective-permute-start | bytes 811016 | tf_op jit(solution)/shard_map/ppermute | solution.py:841
  73.8 10.5 %collective-permute-start.17 = (bf16[4,256,1024]{2,1,0:T(8,128)(2,1)S(1)}, bf16[4,256,1024]{2,1,0:T(8,128)(2,1)S(1)}, u32[]{:S(2)}, u32[]{:S(2)}) collective-permute-start(bf16[4,256,1024]{2,1,0:T(8,128)(2,1)S(1)} %shard_map.269.refs_3_.refs_2_), channel_id=1, source_target_pairs={{0,1},{1,0},{2,3},{3,2},{4,5},{5,4},{6,7},{7,6},{8,9},{9,8},{10,11... | collective-permute-start | bytes 6291464 | tf_op jit(solution)/shard_map/ppermute | solution.py:841
  76.0 4.0 %collective-permute-start.16 = (bf16[128,128]{1,0:T(8,128)(2,1)S(1)}, bf16[128,128]{1,0:T(8,128)(2,1)S(1)}, u32[]{:S(2)}, u32[]{:S(2)}) collective-permute-start(bf16[128,128]{1,0:T(8,128)(2,1)S(1)} %shard_map.271.refs_1_), channel_id=1, source_target_pairs={{0,2},{1,17},{2,0},{3,19},{4,6},{5,21},{6,4},{7,23},{8,10},{9,25},... | collective-permute-start | bytes 98312 | tf_op jit(solution)/shard_map/ppermute | solution.py:841
  76.4 7.8 %collective-permute-start.18 = (bf16[512,128]{1,0:T(8,128)(2,1)S(1)}, bf16[512,128]{1,0:T(8,128)(2,1)S(1)}, u32[]{:S(2)}, u32[]{:S(2)}) collective-permute-start(bf16[512,128]{1,0:T(8,128)(2,1)S(1)} %get-tuple-element.132.refs_1_), channel_id=1, source_target_pairs={{0,16},{1,9},{2,18},{3,11},{4,20},{5,13},{6,22},{7,15},{8,24},{9,1... | collective-permute-start | bytes 393224 | tf_op jit(solution)/shard_map/ppermute | solution.py:841
  80.0 7.5 %collective-permute-start.19 = (bf16[672,128]{1,0:T(8,128)(2,1)S(1)}, bf16[672,128]{1,0:T(8,128)(2,1)S(1)}, u32[]{:S(2)}, u32[]{:S(2)}) collective-permute-start(bf16[672,128]{1,0:T(8,128)(2,1)S(1)} %shard_map.272.refs_8_.refs_4_.refs_1_), channel_id=1, source_target_pairs={{0,16},{1,9},{2,18},{3,11},{4,20},{5,13},{6,22},{7,15},{8,24},{9,1... | collective-permute-start | bytes 516104 | tf_op jit(solution)/shard_map/ppermute | solution.py:841
  87.5 5.5 %collective-permute-start.20 = (bf16[672,128]{1,0:T(8,128)(2,1)S(1)}, bf16[672,128]{1,0:T(8,128)(2,1)S(1)}, u32[]{:S(2)}, u32[]{:S(2)}) collective-permute-start(bf16[672,128]{1,0:T(8,128)(2,1)S(1)} %get-tuple-element.139.refs_2_), channel_id=1, source_target_pairs={{0,8},{1,5},{2,10},{3,7},{4,12},{5,1},{6,14},{7,3},{8,0},{9,13},{1... | collective-permute-start | bytes 516104 | tf_op jit(solution)/shard_map/ppermute | solution.py:841
  93.1 1.6 %copy-start = (f32[32,16,64]{2,1,0:T(8,128)S(1)}, f32[32,16,64]{2,1,0:T(8,128)}, u32[]{:S(2)}) copy-start(f32[32,16,64]{2,1,0:T(8,128)} %refs_4_.1) | copy-start | bytes 393220
  93.1 1.6 %copy-start.1 = (f32[16,64,32]{1,2,0:T(8,128)S(1)}, f32[16,64,32]{1,2,0:T(8,128)}, u32[]{:S(2)}) copy-start(f32[16,64,32]{1,2,0:T(8,128)} %param.17) | copy-start | bytes 393220
  93.1 1.6 %copy-start.2 = (f32[2,16,64]{2,1,0:T(8,128)S(1)}, f32[2,16,64]{2,1,0:T(8,128)}, u32[]{:S(2)}) copy-start(f32[2,16,64]{2,1,0:T(8,128)} %refs_10_.1) | copy-start | bytes 24580
  93.1 1.6 %copy-start.3 = (f32[32,60]{1,0:T(8,128)S(1)}, f32[32,60]{1,0:T(8,128)}, u32[]{:S(2)}) copy-start(f32[32,60]{1,0:T(8,128)} %refs_13_.1) | copy-start | bytes 23044
  93.1 1.6 %copy-start.6 = (f32[32,16,64]{2,1,0:T(8,128)S(1)}, f32[32,16,64]{2,1,0:T(8,128)}, u32[]{:S(2)}) copy-start(f32[32,16,64]{2,1,0:T(8,128)} %refs_5_.1) | copy-start | bytes 393220
  93.1 1.6 %copy-start.7 = (f32[32,16,64]{2,1,0:T(8,128)S(1)}, f32[32,16,64]{2,1,0:T(8,128)}, u32[]{:S(2)}) copy-start(f32[32,16,64]{2,1,0:T(8,128)} %refs_6_.1) | copy-start | bytes 393220
  93.1 1.6 %copy-start.8 = (f32[16,64,32]{1,2,0:T(8,128)S(1)}, f32[16,64,32]{1,2,0:T(8,128)}, u32[]{:S(2)}) copy-start(f32[16,64,32]{1,2,0:T(8,128)} %param.23) | copy-start | bytes 393220
  93.1 1.6 %copy-start.9 = (f32[16,64,32]{1,2,0:T(8,128)S(1)}, f32[16,64,32]{1,2,0:T(8,128)}, u32[]{:S(2)}) copy-start(f32[16,64,32]{1,2,0:T(8,128)} %param.24) | copy-start | bytes 393220
  93.1 1.6 %copy-start.10 = (f32[2,16,64]{2,1,0:T(8,128)S(1)}, f32[2,16,64]{2,1,0:T(8,128)}, u32[]{:S(2)}) copy-start(f32[2,16,64]{2,1,0:T(8,128)} %refs_11_.1) | copy-start | bytes 24580
  93.1 1.6 %copy-start.11 = (f32[2,16,64]{2,1,0:T(8,128)S(1)}, f32[2,16,64]{2,1,0:T(8,128)}, u32[]{:S(2)}) copy-start(f32[2,16,64]{2,1,0:T(8,128)} %refs_12_.1) | copy-start | bytes 24580
  93.2 1.6 %copy-start.12 = (f32[32,60]{1,0:T(8,128)S(1)}, f32[32,60]{1,0:T(8,128)}, u32[]{:S(2)}) copy-start(f32[32,60]{1,0:T(8,128)} %refs_14_.1) | copy-start | bytes 23044
  93.2 1.6 %copy-start.13 = (f32[32,60]{1,0:T(8,128)S(1)}, f32[32,60]{1,0:T(8,128)}, u32[]{:S(2)}) copy-start(f32[32,60]{1,0:T(8,128)} %refs_15_.1) | copy-start | bytes 23044
  93.3 1.4 %collective-permute-start.21 = (bf16[416,128]{1,0:T(8,128)(2,1)S(1)}, bf16[416,128]{1,0:T(8,128)(2,1)S(1)}, u32[]{:S(2)}, u32[]{:S(2)}) collective-permute-start(bf16[416,128]{1,0:T(8,128)(2,1)S(1)} %get-tuple-element.141.refs_2_), channel_id=1, source_target_pairs={{0,1},{1,0},{2,3},{3,2},{4,5},{5,4},{6,7},{7,6},{8,9},{9,8},{10,11... | collective-permute-start | bytes 319496 | tf_op jit(solution)/shard_map/ppermute | solution.py:841

commit v4 on v3

--- a/solution.py
+++ b/solution.py
@@ -42,7 +42,7 @@
     return pltpu.CompilerParams(vmem_limit_bytes=mib * MIB)
 
 
-def kernel_call(body, outs, scratch, mib, micros, smem, *args, after=()):
+def kernel_call(body, outs, scratch, mib, micros, smem, *args, after=(), far=0, sems=0):
     in_vmem = pl.BlockSpec(memory_space=pltpu.VMEM)
     in_smem = pl.BlockSpec(memory_space=pltpu.SMEM)
     anywhere = pl.BlockSpec(memory_space=pl.ANY)
@@ -55,8 +55,9 @@
         kernel,
         out_shape=tuple(jax.ShapeDtypeStruct(shape, kind) for shape, kind in outs),
         in_specs=[in_smem] * smem + [in_vmem] * (len(args) - smem) + [anywhere] * len(after),
-        out_specs=(in_vmem,) * len(outs),
-        scratch_shapes=[pltpu.VMEM(shape, kind) for shape, kind in scratch],
+        out_specs=(anywhere,) * far + (in_vmem,) * (len(outs) - far),
+        scratch_shapes=[pltpu.VMEM(shape, kind) for shape, kind in scratch]
+        + ([pltpu.SemaphoreType.DMA((sems or far,))] if far else []),
         compiler_params=params(mib),
         cost_estimate=pl.CostEstimate(
             flops=int(micros * FLOPS_MICRO), bytes_accessed=0, transcendentals=0
@@ -148,7 +149,7 @@
 
 def prep_kernel(
     masks, ride, at, order, riders, turned, b_own, xt, gt,
-    cc_a, cc_b, gates, logits, selp, gb1, b0, b1, sel,
+    cc_a, gates, logits, selp, gb1, b0, b1, sel,
 ):
     core = at[0]
     high = core.astype(F32)
@@ -162,7 +163,7 @@
     if ride:
         depth = width // 8
         for q in range(8):
-            spot = (q & 1) + 2 * (q >> 2) + 4 * (q >> 1 & 1)
+            spot = (q >> 2) + 2 * (q >> 1 & 1) + 4 * (q & 1)
             rows = slice(spot * depth, (spot + 1) * depth)
             sel[q * depth : (q + 1) * depth, :] = jnp.where(core == 1, riders[rows, :], turned[rows, :])
         side = [
@@ -215,16 +216,43 @@
                         gate[e] = w0 if gate[e] is None else gate[e] + w0
         for e in range(8):
             gates[e, :, part] = gate[e]
-        ones = jnp.ones((8, tile), BF)
-        g_t = [gt[t, :, part].astype(F32) for t in range(TASKS)]
-        for e in range(8):
-            c = gate[e][0:1] * g_t[0]
-            for t in range(1, TASKS):
-                c = c + gate[e][t : t + 1] * g_t[t]
-            c = c.astype(BF)
-            cc = cc_a if e < 4 else cc_b
-            cc[e % 4, :, part] = c
-            gb1[e] += dot(ones, c, 1, 1)
+        combine(gate[0:4], gt, part, cc_a, gb1)
+
+
+def combine(gate, gt, part, cc, gb1):
+    ones = jnp.ones((8, part.size), BF)
+    low = [[g[t : t + 1].astype(BF) for t in range(TASKS)] for g in gate]
+    for e in range(4):
+        c = low[e][0] * gt[0, :, part]
+        for t in range(1, TASKS):
+            c = c + low[e][t] * gt[t, :, part]
+        cc[e, :, part] = c
+        gb1[e] += dot(ones, c, 1, 1)
+
+
+def late_kernel(gates, gt, cc, gb1):
+    total = gt.shape[2]
+    tile = min(WIDE, total)
+    gb1[...] = jnp.zeros_like(gb1)
+
+    @pl.loop(0, total // tile)
+    def _(i):
+        part = part_of(i, tile)
+        combine([gates[4 + e, :, part] for e in range(4)], gt, part, cc, gb1)
+
+
+def late(gates, gt, after):
+    _, width, total = gt.shape
+    return kernel_call(
+        late_kernel,
+        (((4, width, total), BF), ((4, 8, width), F32)),
+        (),
+        12,
+        2.0,
+        0,
+        gates, gt,
+        after=after,
+    )
 
 
 def prep(masks, ride, at, order, riders, turned, b_own, xt, gt):
@@ -232,12 +260,11 @@
     return kernel_call(
         functools.partial(prep_kernel, masks, ride),
         (
-            ((4, width, total), BF),
             ((4, width, total), BF),
             ((8, TPAD, total), F32),
             ((GROWS, total), F32),
             ((GROWS, width), BF),
-            ((8, 8, width), F32),
+            ((4, 8, width), F32),
             ((width, 8), F32),
             ((width, 8), F32),
         ),
@@ -260,7 +287,7 @@
 
 def critical_kernel(second, spots, back, *refs):
     if second:
-        (at_core, w_lo, w_hi, xt, cc, b0, gb0_a, gb1, to_q, perm,
+        (at_core, w_lo, w_hi, xt, cc, b0, gb0_a, gb1_a, gb1_b, to_q, perm,
          g_lo, g_hi, hid, gp, e_all, r_all, acc_e, acc_r) = refs
     else:
         (at_core, w_lo, w_hi, xt, cc, b0,
@@ -340,7 +367,9 @@
     sums = jnp.concatenate(sums, axis=0)
     if second:
         mine = jnp.concatenate([gb0_a[...], sums], axis=0).astype(BF)
-        outer = jnp.concatenate([gb1[e, 0:1] for e in range(2 * chunk)], axis=0).astype(BF)
+        outer = jnp.concatenate(
+            [x[e, 0:1] for x in (gb1_a, gb1_b) for e in range(chunk)], axis=0
+        ).astype(BF)
         both = jnp.concatenate(
             [dot(mine, to_q[...], 1, 0), dot(outer, perm[...], 1, 0)], axis=0
         ).astype(BF)
@@ -379,160 +408,160 @@
     return (a.astype(F32) + b.astype(F32)).astype(BF)
 
 
-def fold_kernel(lo, sent, got, *refs):
-    *tail, keep, msg = refs
-    rows = lo.shape[0]
-    half = rows // 2
-    end = sent.shape[0] - half
-    keep[...] = add_low(lo[0:half, :], got[0:half, :])
-    msg[0:half, :] = add_low(lo[half:rows, :], got[half:rows, :])
-    if end > half:
-        msg[half:end, :] = add_low(sent[rows:, :], got[rows:, :])
-    if tail:
-        msg[end:, :] = tail[0][...]
-
-
-def fold(lo, sent, got, after=(), tail=()):
-    rows, lanes = lo.shape
-    half = rows // 2
-    end = sent.shape[0] - half + sum(x.shape[0] for x in tail)
-    return kernel_call(
-        fold_kernel,
-        (((half, lanes), BF), ((end, lanes), BF)),
+def fold_kernel(rows, n_small, n_tail, lo, sent, got, *refs):
+    small, tail, (keep, msg) = refs[:n_small], refs[n_small : n_small + n_tail], refs[-2:]
+    at = to = 0
+    for size in rows:
+        half = size // 2
+        keep[to : to + half, :] = add_low(lo[at : at + half, :], got[at : at + half, :])
+        msg[to : to + half, :] = add_low(lo[at + half : at + size, :], got[at + half : at + size, :])
+        at, to = at + size, to + half
+    more = sent.shape[0] - at
+    if more:
+        msg[to : to + more, :] = add_low(sent[at:, :], got[at:, :])
+        to += more
+    if small:
+        msg[to:, :] = add_low(small[0][...], small[1][...])
+
+
+def fold(rows, lo, sent, got, small=(), after=()):
+    total = sum(rows)
+    end = sent.shape[0] - total // 2 + (small[0].shape[0] if small else 0)
+    return kernel_call(
+        functools.partial(fold_kernel, rows, len(small), 0),
+        (((total // 2, lo.shape[1]), BF), ((end, lo.shape[1]), BF)),
         (),
         8,
         0.3,
         0,
-        lo, sent, got, *tail,
+        lo, sent, got, *small,
         after=after,
     )
 
 
-def append_kernel(msg, one, two, out):
-    rows = msg.shape[0]
-    out[0:rows, :] = msg[...]
-    out[rows:, :] = add_low(one[...], two[...])
-
-
-def append(msg, one, two, after):
-    rows, lanes = msg.shape
-    (out,) = kernel_call(
-        append_kernel,
-        (((rows + one.shape[0], lanes), BF),),
+def pair_fold_kernel(a_lo, a_got, b_lo, b_sent, b_got, a_sent, keep, msg):
+    half_b, half_a = b_lo.shape[0] // 2, a_lo.shape[0] // 2
+    both = ((b_lo, b_got, half_b, 0), (a_lo, a_got, half_a, half_b))
+    for lo, got, half, to in both:
+        keep[to : to + half, :] = add_low(lo[0:half, :], got[0:half, :])
+        msg[to : to + half, :] = add_low(lo[half : 2 * half, :], got[half : 2 * half, :])
+    msg[half_a + half_b :, :] = add_low(b_sent[2 * half_b :, :], b_got[2 * half_b :, :])
+
+
+def pair_fold(a_lo, a_sent, a_got, b_lo, b_sent, b_got, after=()):
+    rows, lanes = a_lo.shape
+    return kernel_call(
+        pair_fold_kernel,
+        (((rows, lanes), BF), ((b_sent.shape[0], lanes), BF)),
         (),
         8,
         0.3,
         0,
-        msg, one, two,
+        a_lo, a_got, b_lo, b_sent, b_got, a_sent,
         after=after,
     )
-    return out
-
-
-def plus_kernel(one, two, out):
-    out[...] = add_low(one[...], two[...])
-
-
-def plus(one, two, after):
-    (out,) = kernel_call(plus_kernel, ((one.shape, BF),), (), 8, 0.3, 0, one, two, after=after)
-    return out
-
-
-def last_fold_kernel(a_lo, b_lo, sent, got, own, msg):
-    half = a_lo.shape[1] // 2
-    size = a_lo.shape[0]
+
+
+def last_fold_kernel(lo, sent, got, own, msg):
+    half = lo.shape[1] // 2
+    size = lo.shape[0] // 2
     rows = size // 2
-    a_at = sent.shape[0] - size
-    for i, (lo, at) in enumerate(((a_lo, a_at), (b_lo, 0))):
-        e = lo[0:rows, :].astype(F32) + got[at : at + rows, :].astype(F32)
-        r = lo[rows:size, :].astype(F32) + got[at + rows : at + size, :].astype(F32)
+    for i, at in enumerate((size, 0)):
+        e, r = [
+            lo[k : k + rows, :].astype(F32) + got[k : k + rows, :].astype(F32)
+            for k in (at, at + rows)
+        ]
         here = slice(i * rows, (i + 1) * rows)
         own[here, :] = jnp.concatenate([e[:, :half], r[:, :half]], axis=1)
         msg[here, :] = jnp.concatenate([e[:, half:], r[:, half:]], axis=1).astype(BF)
-    msg[size:, :] = add_low(sent[size:a_at, :], got[size:a_at, :])
-
-
-def last_fold(a_lo, b_lo, sent, got):
-    rows, lanes = a_lo.shape
-    small = sent.shape[0] - 2 * rows
+    msg[size:, :] = add_low(sent[2 * size :, :], got[2 * size :, :])
+
+
+def last_fold(lo, sent, got):
+    rows, lanes = lo.shape
+    small = sent.shape[0] - rows
     return kernel_call(
         last_fold_kernel,
-        (((rows, lanes), F32), ((rows + small, lanes), BF)),
+        (((rows // 2, lanes), F32), ((rows // 2 + small, lanes), BF)),
         (),
         8,
         0.3,
         0,
-        a_lo, b_lo, sent, got,
-    )
-
-
-def outer_kernel(start, *refs):
-    if start:
-        at_core, order, r_a, hid_a, r_b, hid_b, gt, logits, b1, xt, perm, acc_in, ys, gls, gsel, acc = refs
-        acc[...] = acc_in[...]
+        lo, sent, got,
+    )
+
+
+def outer_kernel(chunk_at, *refs):
+    if chunk_at:
+        at_core, order, r_all, hid, gt, logits, b1, gl_in, xt, perm, ys, gls, gsel, acc = refs
+        acc[...] = jnp.zeros_like(acc)
     else:
-        at_core, order, r_a, hid_a, r_b, hid_b, gt, logits, b1, xt, ys, gls, acc = refs
-        acc[...] = jnp.zeros_like(acc)
+        at_core, r_all, hid, gt, logits, b1, ys, gls = refs
     high = at_core[0].astype(F32)
     sign = 2.0 * high - 1.0
-    _, width, rows = ys.shape
-    chunk, hidden, _ = hid_a.shape
-    tile = min(WIDE, rows)
-
-    @pl.loop(0, rows // tile)
+    count, hidden, total = hid.shape
+    width = gt.shape[1]
+    tile = min(WIDE, total)
+
+    @pl.loop(0, total // tile)
     def _(i):
-        here, part = part_of(i, tile), part_of(i + start // tile, tile)
+        part = part_of(i, tile)
         gg = []
-        wide = [gt[t, :, part].astype(F32) for t in range(TASKS)]
-        for e in range(2 * chunk):
-            r_all, hid = (r_a, hid_a) if e < chunk else (r_b, hid_b)
-            at = e % chunk
-            y = dot(r_all[:, at * hidden : (at + 1) * hidden], hid[at, :, part], 1, 0)
-            y = y + b1[:, e : e + 1]
-            ys[e, :, here] = y.astype(BF)
-            sums = [jnp.sum(wide[t] * y, axis=0, keepdims=True) for t in range(TASKS)]
+        for e in range(count):
+            y = dot(r_all[:, e * hidden : (e + 1) * hidden], hid[e, :, part], 1, 0)
+            at = chunk_at * count + e
+            y = y + b1[:, at : at + 1]
+            low = y.astype(BF)
+            ys[e, :, part] = low
+            sums = []
+            for t in range(TASKS):
+                p = None
+                for d in range(0, width, 32):
+                    q = gt[t, d : d + 32, part] * low[d : d + 32]
+                    p = q if p is None else p + q
+                sums.append(jnp.sum(p.astype(F32), axis=0, keepdims=True))
             gg.append(jnp.concatenate(sums + [jnp.zeros((TPAD - TASKS, tile), F32)], axis=0))
         gl = gate_back(
             lambda b, k: logits[(b * SELECT + k) * TPAD : (b * SELECT + k + 1) * TPAD, part],
             lambda k: logits[
                 (BITS * SELECT + k) * TPAD : (BITS * SELECT + k + 1) * TPAD, part
             ],
-            gg, high, sign,
-        ).astype(BF)
-        gls[:, here] = gl
-        acc[...] += dot(gl, xt[0:width, part], 1, 1)
-
-    if start:
+            gg, chunk_at, high, sign,
+        )
+        if chunk_at:
+            gl = (gl + gl_in[:, part]).astype(BF)
+            acc[...] += dot(gl, xt[0:width, part], 1, 1)
+        gls[:, part] = gl
+
+    if chunk_at:
         turned = dot(order[:, 0:64], acc[...].astype(BF), 0, 0).astype(BF)
         gsel[...] = lanes_out(dot(turned, perm[...], 1, 0)).astype(BF)
 
 
-def outer(start, rows, at, order, first, second, gt, logits, b1, xt, more=(), after=()):
+def outer(chunk_at, at, r_all, hid, gt, logits, b1, order=None, more=(), after=()):
+    count, _, total = hid.shape
     width = gt.shape[1]
-    (r_a, hid_a), (r_b, hid_b) = first, second
-    chunk, hidden, _ = hid_a.shape
-    outs = [((2 * chunk, width, rows), BF), ((GROWS, rows), BF)]
-    scratch = ()
-    if start:
+    outs = [((count, width, total), BF), ((GROWS, total), BF if chunk_at else F32)]
+    if chunk_at:
         outs.append(((order.shape[1], 128), BF))
-        scratch = (((GROWS, width), F32),)
+        args = (at, order, r_all, hid, gt, logits, b1, *more)
     else:
-        outs.append(((GROWS, width), F32))
-    return kernel_call(
-        functools.partial(outer_kernel, start),
+        args = (at, r_all, hid, gt, logits, b1)
+    return kernel_call(
+        functools.partial(outer_kernel, chunk_at),
         tuple(outs),
-        scratch,
+        (((GROWS, width), F32),) if chunk_at else (),
         16,
         4.3,
         1,
-        at, order, r_a, hid_a, r_b, hid_b, gt, logits, b1, xt, *more,
+        *args,
         after=after,
     )
 
 
-def mix_kernel(start, e_a, gp_a, e_b, gp_b, selp, ys, gls, gates, out):
-    count, width, rows = ys.shape
+def mix_kernel(start, e_a, gp_a, y_a, e_b, gp_b, y_b, selp, gls, gates, out):
     chunk, hidden, _ = gp_a.shape
+    _, width, rows = out.shape
     tile, depth = 512, 16
 
     @pl.loop(0, rows // tile)
@@ -540,12 +569,12 @@
         here, part = part_of(i, tile), part_of(i + start // tile, tile)
         v = dot(e_a[...], gp_a[:, :, part].reshape(chunk * hidden, tile), 1, 0)
         v = v + dot(e_b[...], gp_b[:, :, part].reshape(chunk * hidden, tile), 1, 0)
-        out[TASKS, :, here] = (v + dot(selp[...], gls[:, here], 0, 0)).astype(BF)
+        out[TASKS, :, here] = (v + dot(selp[...], gls[:, part], 0, 0)).astype(BF)
         for d in range(width // depth):
             block = slice(d * depth, (d + 1) * depth)
             sums = [None] * TASKS
-            for e in range(count):
-                y = ys[e, block, here].astype(F32)
+            for e in range(2 * chunk):
+                y = (y_a if e < chunk else y_b)[e % chunk, block, part].astype(F32)
                 for t in range(TASKS):
                     m = gates[e, t : t + 1, part] * y
                     sums[t] = m if e == 0 else sums[t] + m
@@ -553,10 +582,8 @@
                 out[t, block, here] = sums[t].astype(BF)
 
 
-def mix(start, first, second, selp, ys, gls, gates, after):
-    (e_a, gp_a), (e_b, gp_b) = first, second
-    count, width, rows = ys.shape
-    chunk, hidden, _ = gp_a.shape
+def mix(start, rows, first, second, selp, gls, gates, after):
+    chunk, width, total = first[2].shape
     (out,) = kernel_call(
         functools.partial(mix_kernel, start),
         (((TASKS + 1, width, rows), BF),),
@@ -564,31 +591,25 @@
         16,
         4.0,
         0,
-        e_a, gp_a, e_b, gp_b, selp, ys, gls, gates,
+        *first, *second, selp, gls, gates,
         after=after,
     )
     return out
 
 
-def gate_back(z_of, a_of, gg, high, sign):
+def gate_back(z_of, a_of, gg, e2, high, sign):
     alpha, smooth, clipped, f_high = gate_parts(z_of, a_of, high)
     out = [None] * GROUPS
     d_alpha = []
     for k in range(SELECT):
         f = [[fac(smooth, b, k, bit) for bit in range(2)] for b in range(BITS - 1)]
-        low, dif = {}, {}
-        for e2 in range(2):
-            for e1 in range(2):
-                p, q = gg[4 * e2 + 2 * e1], gg[4 * e2 + 2 * e1 + 1]
-                low[e2, e1] = f[0][0] * p + f[0][1] * q
-                dif[e2, e1] = q - p
-        mid = [f[1][0] * low[e2, 0] + f[1][1] * low[e2, 1] for e2 in range(2)]
-        mid1 = [low[e2, 1] - low[e2, 0] for e2 in range(2)]
-        mid0 = [f[1][0] * dif[e2, 0] + f[1][1] * dif[e2, 1] for e2 in range(2)]
-        t0 = f[2][0] * mid[0] + f[2][1] * mid[1]
-        d2 = mid[1] - mid[0]
-        d1 = f[2][0] * mid1[0] + f[2][1] * mid1[1]
-        d0 = f[2][0] * mid0[0] + f[2][1] * mid0[1]
+        low = [f[0][0] * gg[2 * e1] + f[0][1] * gg[2 * e1 + 1] for e1 in range(2)]
+        dif = [gg[2 * e1 + 1] - gg[2 * e1] for e1 in range(2)]
+        mid = f[1][0] * low[0] + f[1][1] * low[1]
+        t0 = f[2][e2] * mid
+        d2 = mid if e2 else -mid
+        d1 = f[2][e2] * (low[1] - low[0])
+        d0 = f[2][e2] * (f[1][0] * dif[0] + f[1][1] * dif[1])
         d_alpha.append(f_high[k] * t0)
         scale = alpha[k] * f_high[k]
         for b, d in enumerate((scale * d0, scale * d1, scale * d2, alpha[k] * sign * t0)):
@@ -600,20 +621,22 @@
     return jnp.concatenate(out, axis=0)
 
 
-def final_kernel(masks, at, own, recv, mixed, gf, token):
+def final_kernel(masks, at, own, recv, mixed, gf, token, buf, sems):
     token[...] = jnp.zeros_like(token)
-    width = gf.shape[1]
+    width = buf.shape[2]
     d_of, _ = places(masks, at, width)
     up = lax.broadcasted_iota(jnp.int32, (width, width), 0)
     across = lax.broadcasted_iota(jnp.int32, (width, width), 1)
     perm = (d_of(up) == across).astype(F32).astype(BF)
+    copies = []
     for t in range(TASKS + 1):
         s = (own[t].astype(F32) + recv[t].astype(F32)).astype(BF)
-        rows = dot(s, perm, 0, 0).astype(BF)
-        if t < TASKS:
-            mixed[t] = rows
-        else:
-            gf[...] = rows
+        buf[t] = dot(s, perm, 0, 0).astype(BF)
+        to = mixed.at[t] if t < TASKS else gf
+        copies.append(pltpu.make_async_copy(buf.at[t], to, sems.at[t]))
+        copies[-1].start()
+    for copy in copies:
+        copy.wait()
 
 
 def final(masks, at, own, recv, after):
@@ -621,12 +644,14 @@
     return kernel_call(
         functools.partial(final_kernel, masks),
         (((TASKS, rows, width), BF), ((rows, width), BF), ((8, 128), F32)),
-        (),
+        (((TASKS + 1, rows, width), BF),),
         16,
-        2.7,
+        0.1,
         1,
         at, own, recv,
         after=after,
+        far=2,
+        sems=TASKS + 1,
     )
 
 
@@ -703,23 +728,29 @@
     )
 
 
-def chip_kernel(mine, recv, sel, msg):
+def chip_kernel(mine, recv, sel, a_msg, b_msg):
     _, count, depth, lanes = mine.shape
+    half = count // 2
     for which in range(2):
         for e in range(count):
-            to = (which * count + e) * depth
+            msg = a_msg if e < half else b_msg
+            to = (which * half + e % half) * depth
             msg[to : to + depth, :] = jnp.concatenate([mine[which, e], recv[which, e]], axis=1)
-    msg[2 * count * depth :, :] = sel[...]
-
-
-def chip_message(mine, recv, sel):
+    a_msg[2 * half * depth :, :] = sel[...]
+
+
+def chip_messages(mine, recv, sel):
     _, count, depth, lanes = mine.shape
-    rows = 2 * count * depth
-    (msg,) = kernel_call(
-        chip_kernel, (((rows + sel.shape[0], 2 * lanes), BF),), (), 8, 0.3, 0,
+    rows = count * depth
+    return kernel_call(
+        chip_kernel,
+        (((rows + sel.shape[0], 2 * lanes), BF), ((rows, 2 * lanes), BF)),
+        (),
+        8,
+        0.3,
+        0,
         mine, recv, sel,
     )
-    return msg
 
 
 def update_kernel(
@@ -827,7 +858,7 @@
     sibling = ((0, 1), (0, 1))
     dims = [side] + [(m, 0) for m in masks]
     if n_rows == 8:
-        way = ((3, 2, 0, 1), (1, 3, 2, 0))
+        way = ((3, 2, 0, 1), (3, 2, 1, 0))
         back_way = ((2, 3, 0, 1), (1, 2, 3, 0))
     else:
         way = back_way = (tuple(range(len(dims))),) * 2
@@ -894,7 +925,8 @@
             jnp.stack([jnp.transpose(w_expand, (1, 0, 2)), w_r_view]).astype(BF), 1
         )
     w_recv = swap(w_other, sibling)
-    b_own = jnp.concatenate([b_own, swap(b_own, sibling)], axis=0)
+    n_b = b_own.shape[0]
+    (b_own,) = join((((0, 0, n_b), (1, 0, n_b)),), b_own, swap(b_own, sibling))
     x_own = features
     g_own = jnp.transpose(grad_mix, (1, 0, 2))
     x_recv = swap(tie(x_own, w_recv), sibling)
@@ -903,24 +935,25 @@
     steps = len(dims)
     ride = n_rows == 8
     if ride:
-        whole = 2 * mine_n * d_loc
-        msg = chip_message(w_mine, w_recv, sel)
-        got = swap(msg, hops(0))
-        (msg,) = join(
-            (((0, 0, whole), (1, 0, whole), (0, whole, d_loc), (1, whole, d_loc)),), msg, got
+        n = chunk * d_loc * 2
+        a_msg, b_msg = chip_messages(w_mine, w_recv, sel)
+        a_got = swap(a_msg, hops(0))
+        (a_msg,) = join((((0, 0, n), (1, 0, n), (0, n, d_loc), (1, n, d_loc)),), a_msg, a_got)
+        b_got = swap(tie(b_msg, a_got), hops(0))
+        a_got = swap(a_msg, hops(1))
+        xt, gt, perm, to_q = turn(masks, at, x_own, x_recv, g_own, g_recv, (a_msg,))
+        n *= 2
+        tail = tuple((k, n, 2 * d_loc) for k in range(2)) + ((2, 0, 4 * experts),)
+        (a_msg,) = join(
+            (((0, 0, n), (1, 0, n)) + tail,), a_msg, a_got, b_own, after=(perm,)
         )
-        got = swap(msg, hops(1))
-        xt, gt, perm, to_q = turn(masks, at, x_own, x_recv, g_own, g_recv, (msg,))
-        half = whole // 2
-        group = chunk * d_loc
-        pieces = [
-            tuple((k, (2 * j + c) * group, group) for k in range(2) for j in range(4))
-            for c in range(2)
-        ]
-        tail = tuple((k, 2 * whole, 2 * d_loc) for k in range(2)) + ((2, 0, 4 * experts),)
-        a_msg, b_msg = join((pieces[0] + tail, pieces[1]), msg, got, b_own, after=(perm,))
         a_got = swap(a_msg, hops(2))
-        n = 8 * group
+        both = lambda x, y, after: join(
+            (((0, 0, x.shape[0]), (1, 0, x.shape[0])),), x, y, after=after
+        )[0]
+        b_msg = both(b_msg, b_got, (a_msg,))
+        b_got = swap(b_msg, hops(1))
+        n *= 2
         a_lo, riders = join(
             (
                 ((0, 0, n), (1, 0, n)),
@@ -930,6 +963,7 @@
         )
         a_hi = swap(a_lo, hops(3))
         turned = swap(riders, sibling)
+        b_msg = both(b_msg, b_got, (a_lo,))
         b_got = swap(b_msg, hops(2))
     else:
         xt, gt, perm, to_q = turn(masks, at, x_own, x_recv, g_own, g_recv, (sel,))
@@ -944,19 +978,20 @@
         riders = turned = jnp.concatenate([sel, swap(b_own, (side, side))], axis=0)
         (a_lo, a_hi), (b_lo, b_hi) = [canonical(*pair) for pair in zip(bufs, gots)]
 
-    cc_a, cc_b, gates, logits, selp, gb1, b0, b1 = prep(
+    cc_a, gates, logits, selp, gb1_a, b0, b1 = prep(
         masks, ride, at, order, riders, turned, b_own, xt, gt
     )
 
     spots, back = table_of(way), table_of(back_way)
+    cc_b, gb1_b = late(gates, gt, (b0,))
     if ride:
-        (b_lo,) = join((((0, 0, n), (1, 0, n)),), b_msg, b_got, after=(b0,))
+        b_lo = both(b_msg, b_got, (gb1_b,))
         b_hi = swap(b_lo, hops(3))
     first = critical(spots, back, at, a_lo, a_hi, xt, cc_a, b0, (b_lo,))
     a_lo, a_msg = uncanonical(first[0], first[1])
     a_got = swap(a_msg, back_hops(steps - 1))
     second = critical(
-        spots, back, at, b_lo, b_hi, xt, cc_b, b0, (first[0],), (first[6], gb1, to_q, perm)
+        spots, back, at, b_lo, b_hi, xt, cc_b, b0, (first[0],), (first[6], gb1_a, gb1_b, to_q, perm)
     )
     b_lo, b_msg = second[:2]
     if not ride:
@@ -964,40 +999,32 @@
         b_lo, b_msg = uncanonical(b_lo, b_msg[:n])
         b_msg = jnp.concatenate([b_msg, second[1][n:]], axis=0)
     b_got = swap(b_msg, back_hops(steps - 1))
-    inner = ((first[5], first[2]), (second[5], second[2]))
-    ends = ((first[4], first[3]), (second[4], second[3]))
+    ys_a, gl_a = outer(0, at, first[5], first[2], gt, logits, b1, after=(second[0],))
+    a_lo, a_msg = fold(a_lo.shape[:1], a_lo, a_msg, a_got, after=(gl_a,))
+    a_got = swap(a_msg, back_hops(steps - 2))
+    ys_b, gls, gsel = outer(
+        1, at, second[5], second[2], gt, logits, b1, order, (gl_a, xt, perm), (a_lo,)
+    )
+    gsel_got = swap(gsel, back_hops(steps - 1))
+    b_lo, b_msg = fold(b_lo.shape[:1], b_lo, b_msg, b_got, (gsel, gsel_got), (a_got,))
+    b_got = swap(b_msg, back_hops(steps - 2))
+    a_lo, a_msg = fold(a_lo.shape[:1], a_lo, a_msg, a_got, after=(b_lo,))
+    a_got = swap(a_msg, back_hops(steps - 3))
+    ends = ((first[4], first[3], ys_a), (second[4], second[3], ys_b))
     n_own = x_own.shape[0]
-    ys_own, gl_own, acc = outer(0, n_own, at, order, *inner, gt, logits, b1, xt)
-
-    def next_a(step, lo, sent, got, after=()):
-        keep, msg = fold(lo, sent, got, after)
-        return keep, msg, swap(msg, back_hops(step))
-
-    a_lo, a_msg, a_got = next_a(steps - 2, a_lo, a_msg, a_got, (b_lo,))
-    ys_other, gl_other, gsel = outer(
-        n_own, n_own, at, order, *inner, gt, logits, b1, xt, (perm, acc), (a_lo,)
-    )
-    gsel_got = swap(gsel, back_hops(steps - 1))
-    b_lo, b_msg = fold(b_lo, b_msg, b_got)
-    b_got = swap(b_msg, back_hops(steps - 2))
-    a_lo, a_msg, a_got = next_a(steps - 3, a_lo, a_msg, a_got, (b_lo,))
-    mix_other = mix(n_own, *ends, selp, ys_other, gl_other, gates, (a_lo, b_lo))
+    mix_other = mix(n_own, n_own, *ends, selp, gls, gates, (a_lo, b_lo))
     mix_recv = swap(mix_other, sibling)
-    gsel = plus(gsel, gsel_got, (mix_other,))
-    gsel_got = swap(gsel, back_hops(steps - 2))
-    b_lo, b_msg = fold(b_lo, b_msg, b_got, (mix_other,))
-    b_msg = append(b_msg, gsel, gsel_got, (b_lo,))
+    b_lo, b_msg = fold(b_lo.shape[:1], b_lo, b_msg, b_got, after=(mix_other,))
     b_got = swap(b_msg, back_hops(steps - 3))
-    mix_own = mix(0, *ends, selp, ys_own, gl_own, gates, (b_msg,))
+    mix_own = mix(0, n_own, *ends, selp, gls, gates, (b_lo,))
+    mixed, grad_features, token = final(masks, at, mix_own, mix_recv, (b_lo,))
     for step in reversed(range(1, steps - 3)):
-        a_lo, a_msg, a_got = next_a(step, a_lo, a_msg, a_got, (mix_own,))
-    a_lo, a_msg = fold(a_lo, a_msg, a_got, (mix_own,))
-    mixed, grad_features, token = final(masks, at, mix_own, mix_recv, (a_lo, b_msg))
-    for step in reversed(range(steps - 3)):
-        tail = () if step else (a_msg,)
-        b_lo, b_msg = fold(b_lo, b_msg, b_got, (token,), tail)
-        b_got = swap(b_msg, back_hops(step))
-    own, msg = last_fold(a_lo, b_lo, b_msg, b_got)
+        a_lo, a_msg = fold(a_lo.shape[:1], a_lo, a_msg, a_got)
+        b_lo, b_msg = fold(b_lo.shape[:1], b_lo, b_msg, b_got)
+        a_got, b_got = swap(a_msg, back_hops(step)), swap(b_msg, back_hops(step))
+    lo, msg = pair_fold(a_lo, a_msg, a_got, b_lo, b_msg, b_got, (token,))
+    got = swap(msg, back_hops(0))
+    own, msg = last_fold(lo, msg, got)
     got = swap(msg, sibling)
     mixed = jnp.transpose(mixed, (1, 0, 2))
 

time: 97.5 us -> 95.3 us (0.977)
  starting transfers between devices: 26 us -> 29.2 us
  waiting for transfers between devices: 22.7 us -> 19.6 us
  Pallas kernels: 46.8 us -> 44.9 us
    ppermute x22 -> x23, starting transfers between devices: 26 us -> 29.2 us  [swap(): return lax.ppermute(x, ('rows', 'hid'), pairs)]
    ppermute x22 -> x23, waiting for transfers between devices: 22.7 us -> 19.6 us  [swap(): return lax.ppermute(x, ('rows', 'hid'), pairs)]
    pallas_call x24 -> x25, Pallas kernels: 45.3 us -> 43.4 us  [kernel_call(): pl.pallas_call(kernel, out_shape=tuple((jax.ShapeDtypeStruct(shape, kind)...]
  transfers between devices with their start and end apart: 22 -> 23, of which waited for: 7 -> 10; matrix products, arithmetic and copies ran while one was open for 0% -> 0% of each run, Pallas kernels for 44% -> 43%
where the time goes in v4:
time: 95.3 us; the launch traced here: 95 us
  Pallas kernels  44.9 us (47%)
  starting transfers between devices  29.2 us (31%)
  waiting for transfers between devices  19.6 us (21%)
  between operations  1.11 us (1%)
    pallas_call x25, Pallas kernels, kernel_call(): pl.pallas_call(kernel, out_shape=tuple((jax.ShapeDtypeStruct(shape, kind)...  43.4 us
    ppermute x23, starting transfers between devices, swap(): return lax.ppermute(x, ('rows', 'hid'), pairs)  29.2 us
    ppermute x23, waiting for transfers between devices, swap(): return lax.ppermute(x, ('rows', 'hid'), pairs)  19.6 us
  transfers between devices with their start and end apart: 23, of which 10 were waited for; matrix products, arithmetic and copies ran while one was open for 0% of the time, Pallas kernels for 43%

profile of v4, /device:TPU:0, one launch (start us, length us, event | category | flops | bytes accessed | tf_op | source)
XLA Modules:
  0.0 95.0 jit_solution(17944947704643183438)
XLA Ops:
  0.7 0.1 pad_add_fusion.core.refs_0_
  0.7 1.5 %shard_map.254 = (bf16[32,128]{1,0:T(8,128)(2,1)S(1)}, bf16[32,128]{1,0:T(8,128)(2,1)S(1)}, bf16[2,8,32,64]{3,2,1,0:T(8,128)(2,1)S(1)}, bf16[2,8,32,64]{3,2,1,0:T(8,128)(2,1)S(1)}) custom-call(s32[3]{0:T(128)S(1)} %pad_add_fusion.core.refs_0_, f32[32,16,64]{2,1,0:T(8,128)} %refs_4_.1, f32[16,32,64]{2,1,0:T(8,128)} %bitcast.11, f32[2,16,64]{2,1,0:T(8,128)} %refs_10_.1, ...), custom_call_target="tpu_custom_call" | custom-call | tf_op jit(solution)/shard_map/pallas_call | solution.py:697
  2.3 0.5 collective-permute-start
  2.8 1.0 %collective-permute-done.refs_1_ = bf16[2,8,32,64]{3,2,1,0:T(8,128)(2,1)S(1)} collective-permute-done((bf16[2,8,32,64]{3,2,1,0:T(8,128)(2,1)S(1)}, bf16[2,8,32,64]{3,2,1,0:T(8,128)(2,1)S(1)}, u32[]{:S(2)}, u32[]{:S(2)}) %collective-permute-start) | collective-permute-done | bytes 65568 | tf_op jit(solution)/shard_map/ppermute | solution.py:872
  3.8 0.4 collective-permute-start.5
  4.1 0.1 collective-permute-start.3
  4.3 0.1 shard_map.255
  4.4 4.0 %collective-permute-start.1 = (bf16[288,128]{1,0:T(8,128)(2,1)S(1)}, bf16[288,128]{1,0:T(8,128)(2,1)S(1)}, u32[]{:S(2)}, u32[]{:S(2)}) collective-permute-start(bf16[288,128]{1,0:T(8,128)(2,1)S(1)} %get-tuple-element.86.refs_0_), channel_id=1, source_target_pairs={{0,16},{1,17},{2,18},{3,19},{4,20},{5,21},{6,22},{7,23},{8,24},{9,... | collective-permute-start | bytes 221192 | tf_op jit(solution)/shard_map/ppermute | solution.py:872
  8.4 0.0 copy-start.4
  8.4 4.1 %collective-permute-done.1.refs_1_ = bf16[288,128]{1,0:T(8,128)(2,1)S(1)} collective-permute-done((bf16[288,128]{1,0:T(8,128)(2,1)S(1)}, bf16[288,128]{1,0:T(8,128)(2,1)S(1)}, u32[]{:S(2)}, u32[]{:S(2)}) %collective-permute-start.1) | collective-permute-done | bytes 73760 | tf_op jit(solution)/shard_map/ppermute | solution.py:872
  12.6 0.8 collective-permute-start.2
  13.4 3.4 %collective-permute-start.9 = (bf16[256,128]{1,0:T(8,128)(2,1)S(1)}, bf16[256,128]{1,0:T(8,128)(2,1)S(1)}, u32[]{:S(2)}, u32[]{:S(2)}) collective-permute-start(bf16[256,128]{1,0:T(8,128)(2,1)S(1)} %get-tuple-element.98.refs_0_), channel_id=1, source_target_pairs={{0,16},{1,17},{2,18},{3,19},{4,20},{5,21},{6,22},{7,23},{8,24},{9,... | collective-permute-start | bytes 196616 | tf_op jit(solution)/shard_map/ppermute | solution.py:872
  16.8 1.9 %shard_map.258 = (bf16[272,2048]{1,0:T(8,128)(2,1)S(1)}, bf16[3,256,2048]{2,1,0:T(8,128)(2,1)S(1)}, bf16[256,256]{1,0:T(8,128)(2,1)S(1)}, bf16[256,256]{1,0:T(8,128)(2,1)S(1)}) custom-call(s32[3]{0:T(128)S(1)} %pad_add_fusion.core.refs_0_, bf16[1024,256]{1,0:T(8,128)(2,1)S(1)} %copy-done.5, bf16[1024,256]{1,0:T(8,128)(2,1)S(1)} %collective-permute-done.4.refs_2_, ...), custom_call_target="tpu_custom_call" | custom-call | flops 41999998976 | tf_op jit(solution)/shard_map/pallas_call | solution.py:54
  18.6 0.0 copy-start.16
  18.6 0.6 collective-permute-done.2.refs_1_
  19.2 0.1 copy-done.16
  19.3 1.6 %collective-permute-start.6 = (bf16[1216,128]{1,0:T(8,128)(2,1)S(1)}, bf16[1216,128]{1,0:T(8,128)(2,1)S(1)}, u32[]{:S(2)}, u32[]{:S(2)}) collective-permute-start(bf16[1216,128]{1,0:T(8,128)(2,1)S(1)} %shard_map.259.refs_0_.refs_2_), channel_id=1, source_target_pairs={{0,2},{1,5},{2,0},{3,7},{4,6},{5,1},{6,4},{7,3},{8,10},{9,13},{10,... | collective-permute-start | bytes 933896 | tf_op jit(solution)/shard_map/ppermute | solution.py:872
  20.9 1.4 %collective-permute-start.10 = (bf16[512,128]{1,0:T(8,128)(2,1)S(1)}, bf16[512,128]{1,0:T(8,128)(2,1)S(1)}, u32[]{:S(2)}, u32[]{:S(2)}) collective-permute-start(bf16[512,128]{1,0:T(8,128)(2,1)S(1)} %shard_map.262.refs_0_), channel_id=1, source_target_pairs={{0,8},{1,9},{2,10},{3,11},{4,12},{5,13},{6,14},{7,15},{8,0},{9,1},... | collective-permute-start | bytes 393224 | tf_op jit(solution)/shard_map/ppermute | solution.py:872
  22.3 3.9 %collective-permute-done.6.refs_1_ = bf16[1216,128]{1,0:T(8,128)(2,1)S(1)} collective-permute-done((bf16[1216,128]{1,0:T(8,128)(2,1)S(1)}, bf16[1216,128]{1,0:T(8,128)(2,1)S(1)}, u32[]{:S(2)}, u32[]{:S(2)}) %collective-permute-start.6) | collective-permute-done | bytes 311328 | tf_op jit(solution)/shard_map/ppermute | solution.py:872
  26.2 0.1 collective-permute-start.8
  26.3 0.0 copy-start.14
  26.3 1.7 %collective-permute-start.7 = (bf16[2048,128]{1,0:T(8,128)(2,1)S(1)}, bf16[2048,128]{1,0:T(8,128)(2,1)S(1)}, u32[]{:S(2)}, u32[]{:S(2)}) collective-permute-start(bf16[2048,128]{1,0:T(8,128)(2,1)S(1)} %get-tuple-element.91.refs_2_.refs_1_), channel_id=1, source_target_pairs={{0,4},{1,3},{2,6},{3,1},{4,0},{5,7},{6,2},{7,5},{8,12},{9,11},{10,... | collective-permute-start | bytes 1572872 | tf_op jit(solution)/shard_map/ppermute | solution.py:872
  28.0 1.6 %collective-permute-start.11 = (bf16[1024,128]{1,0:T(8,128)(2,1)S(1)}, bf16[1024,128]{1,0:T(8,128)(2,1)S(1)}, u32[]{:S(2)}, u32[]{:S(2)}) collective-permute-start(bf16[1024,128]{1,0:T(8,128)(2,1)S(1)} %shard_map.263.refs_0_), channel_id=1, source_target_pairs={{0,2},{1,5},{2,0},{3,7},{4,6},{5,1},{6,4},{7,3},{8,10},{9,13},{10,... | collective-permute-start | bytes 786440 | tf_op jit(solution)/shard_map/ppermute | solution.py:872
  29.6 3.8 %shard_map.261 = (bf16[4,256,2048]{2,1,0:T(8,128)(2,1)S(1)}, f32[8,8,2048]{2,1,0:T(8,128)S(1)}, f32[160,2048]{1,0:T(8,128)S(1)}, bf16[160,256]{1,0:T(8,128)(2,1)...) custom-call(s32[3]{0:T(128)S(1)} %pad_add_fusion.core.refs_0_, ...), custom_call_target="tpu_custom_call" | custom-call | flops 60000002048 | tf_op jit(solution)/shard_map/pallas_call | solution.py:54
  33.4 1.6 %shard_map.264 = (bf16[4,256,2048]{2,1,0:T(8,128)(2,1)S(1)}, f32[4,8,256]{2,1,0:T(8,128)S(1)}) custom-call(f32[8,8,2048]{2,1,0:T(8,128)S(1)} %get-tuple-element.99.refs_0_.refs_8_, bf16[3,256,2048]{2,1,0:T(8,128)(2,1)S(1)} %get-tuple-element.94.refs_6_.refs_1_.refs_3_.refs_4_, f32[256,8]{1,0:T(8,128)S(1)} %get-tuple-element.96.refs_2_.refs_5_), custom_call_target="tpu_custom_call" | custom-call | flops 24000000000 | tf_op jit(solution)/shard_map/pallas_call | solution.py:54
  35.0 2.3 %collective-permute-done.11.refs_1_ = bf16[1024,128]{1,0:T(8,128)(2,1)S(1)} collective-permute-done((bf16[1024,128]{1,0:T(8,128)(2,1)S(1)}, bf16[1024,128]{1,0:T(8,128)(2,1)S(1)}, u32[]{:S(2)}, u32[]{:S(2)}) %collective-permute-start.11) | collective-permute-done | bytes 262176 | tf_op jit(solution)/shard_map/ppermute | solution.py:872
  37.4 0.4 collective-permute-start.12
  37.8 0.6 collective-permute-done.7.refs_2_
  38.4 7.1 %shard_map.266 = (bf16[2048,128]{1,0:T(8,128)(2,1)S(1)}, bf16[2048,128]{1,0:T(8,128)(2,1)S(1)}, bf16[4,256,2048]{2,1,0:T(8,128)(2,1)S(1)}, bf16[4,256,2048]{2,1,...) custom-call(s32[3]{0:T(128)S(1)} %pad_add_fusion.core.refs_0_, ...), custom_call_target="tpu_custom_call" | custom-call | flops 91199995904 | tf_op jit(solution)/shard_map/pallas_call | solution.py:54
  45.4 1.6 %collective-permute-start.13 = (bf16[2048,128]{1,0:T(8,128)(2,1)S(1)}, bf16[2048,128]{1,0:T(8,128)(2,1)S(1)}, u32[]{:S(2)}, u32[]{:S(2)}) collective-permute-start(bf16[2048,128]{1,0:T(8,128)(2,1)S(1)} %get-tuple-element.119.refs_1_), channel_id=1, source_target_pairs={{0,4},{1,3},{2,6},{3,1},{4,0},{5,7},{6,2},{7,5},{8,12},{9,11},{10,... | collective-permute-start | bytes 1572872 | tf_op jit(solution)/shard_map/ppermute | solution.py:872
  47.1 7.3 %shard_map.267 = (bf16[2048,128]{1,0:T(8,128)(2,1)S(1)}, bf16[2080,128]{1,0:T(8,128)(2,1)S(1)}, bf16[4,256,2048]{2,1,0:T(8,128)(2,1)S(1)}, bf16[4,256,2048]{2,1,...) custom-call(s32[3]{0:T(128)S(1)} %pad_add_fusion.core.refs_0_, ...), custom_call_target="tpu_custom_call" | custom-call | flops 91199995904 | tf_op jit(solution)/shard_map/pallas_call | solution.py:54
  54.4 0.5 collective-permute-start.14
  54.8 4.0 %shard_map.268 = (bf16[4,256,2048]{2,1,0:T(8,128)(2,1)S(1)}, f32[160,2048]{1,0:T(8,128)S(1)}) custom-call(s32[3]{0:T(128)S(1)} %pad_add_fusion.core.refs_0_, bf16[256,1024]{1,0:T(8,128)(2,1)S(1)} %get-tuple-element.103.refs_1_, bf16[4,256,2048]{2,1,0:T(8,128)(2,1)S(1)} %get-tuple-element.104.refs_2_, bf16[3,256,2048]{2,1,0:T(8,128)(2,1)S(1)} %copy-done.19, ...), custom_call_target="tpu_custom_call" | custom-call | flops 51599998976 | tf_op jit(solution)/shard_map/pallas_call | solution.py:54
  58.8 0.0 copy-start.15
  58.8 0.1 shard_map.269
  59.0 1.4 %collective-permute-start.16 = (bf16[1024,128]{1,0:T(8,128)(2,1)S(1)}, bf16[1024,128]{1,0:T(8,128)(2,1)S(1)}, u32[]{:S(2)}, u32[]{:S(2)}) collective-permute-start(bf16[1024,128]{1,0:T(8,128)(2,1)S(1)} %get-tuple-element.126.refs_1_), channel_id=1, source_target_pairs={{0,2},{1,17},{2,0},{3,19},{4,6},{5,21},{6,4},{7,23},{8,10},{9,25},... | collective-permute-start | bytes 786440 | tf_op jit(solution)/shard_map/ppermute | solution.py:872
  60.3 4.8 %shard_map.270 = (bf16[4,256,2048]{2,1,0:T(8,128)(2,1)S(1)}, bf16[160,2048]{1,0:T(8,128)(2,1)S(1)}, bf16[128,128]{1,0:T(8,128)(2,1)S(1)}) custom-call(s32[3]{0:T(128)S(1)} %pad_add_fusion.core.refs_0_, bf16[160,128]{1,0:T(8,128)(2,1)S(1)} %copy-done.15, bf16[256,1024]{1,0:T(8,128)(2,1)S(1)} %get-tuple-element.116.refs_2_, ...), custom_call_target="tpu_custom_call" | custom-call | flops 51599998976 | tf_op jit(solution)/shard_map/pallas_call | solution.py:54
  65.2 1.7 %collective-permute-start.15 = (bf16[128,128]{1,0:T(8,128)(2,1)S(1)}, bf16[128,128]{1,0:T(8,128)(2,1)S(1)}, u32[]{:S(2)}, u32[]{:S(2)}) collective-permute-start(bf16[128,128]{1,0:T(8,128)(2,1)S(1)} %get-tuple-element.125.refs_3_), channel_id=1, source_target_pairs={{0,4},{1,3},{2,6},{3,1},{4,0},{5,7},{6,2},{7,5},{8,12},{9,11},{10,... | collective-permute-start | bytes 98312 | tf_op jit(solution)/shard_map/ppermute | solution.py:872
  66.8 2.3 %collective-permute-done.15.refs_4_ = bf16[128,128]{1,0:T(8,128)(2,1)S(1)} collective-permute-done((bf16[128,128]{1,0:T(8,128)(2,1)S(1)}, bf16[128,128]{1,0:T(8,128)(2,1)S(1)}, u32[]{:S(2)}, u32[]{:S(2)}) %collective-permute-start.15) | collective-permute-done | bytes 32800 | tf_op jit(solution)/shard_map/ppermute | solution.py:872
  69.1 0.1 shard_map.271
  69.3 0.8 collective-permute-start.17
  70.1 0.1 shard_map.272
  70.1 3.5 %shard_map.273.refs_3_ = bf16[4,256,1024]{2,1,0:T(8,128)(2,1)S(1)} custom-call(bf16[256,1024]{1,0:T(8,128)(2,1)S(1)} %get-tuple-element.101.refs_0_, bf16[4,256,2048]{2,1,0:T(8,128)(2,1)S(1)} %get-tuple-element.102.refs_1_, bf16[4,256,2048]{2,1,0:T(8,128)(2,1)S(1)} %get-tuple-element.113.refs_2_, bf16[256,1024]{1,0:T(8,128)(2,1)S(1)} %get-tuple-element.114.refs_3_, ...), custom_call_target="tpu_custom_call" | custom-call | flops 48000000000 | tf_op jit(solution)/shard_map/pallas_call | solution.py:54
  73.6 0.1 collective-permute-start.18
  73.7 2.3 %collective-permute-start.19 = (bf16[512,128]{1,0:T(8,128)(2,1)S(1)}, bf16[512,128]{1,0:T(8,128)(2,1)S(1)}, u32[]{:S(2)}, u32[]{:S(2)}) collective-permute-start(bf16[512,128]{1,0:T(8,128)(2,1)S(1)} %get-tuple-element.133.refs_5_), channel_id=1, source_target_pairs={{0,16},{1,9},{2,18},{3,11},{4,20},{5,13},{6,22},{7,15},{8,24},{9,1... | collective-permute-start | bytes 393224 | tf_op jit(solution)/shard_map/ppermute | solution.py:872
  76.1 0.1 collective-permute-done.17.refs_2_
  76.2 0.1 shard_map.274
  76.2 2.3 %collective-permute-start.20 = (bf16[672,128]{1,0:T(8,128)(2,1)S(1)}, bf16[672,128]{1,0:T(8,128)(2,1)S(1)}, u32[]{:S(2)}, u32[]{:S(2)}) collective-permute-start(bf16[672,128]{1,0:T(8,128)(2,1)S(1)} %get-tuple-element.134.refs_3_), channel_id=1, source_target_pairs={{0,16},{1,9},{2,18},{3,11},{4,20},{5,13},{6,22},{7,15},{8,24},{9,1... | collective-permute-start | bytes 516104 | tf_op jit(solution)/shard_map/ppermute | solution.py:872
  78.6 3.5 %shard_map.275.refs_1_ = bf16[4,256,1024]{2,1,0:T(8,128)(2,1)S(1)} custom-call(bf16[256,1024]{1,0:T(8,128)(2,1)S(1)} %get-tuple-element.101.refs_0_, bf16[4,256,2048]{2,1,0:T(8,128)(2,1)S(1)} %get-tuple-element.102.refs_1_, bf16[4,256,2048]{2,1,0:T(8,128)(2,1)S(1)} %get-tuple-element.113.refs_2_, bf16[256,1024]{1,0:T(8,128)(2,1)S(1)} %get-tuple-element.114.refs_3_, ...), custom_call_target="tpu_custom_call" | custom-call | flops 48000000000 | tf_op jit(solution)/shard_map/pallas_call | solution.py:54
  82.1 2.8 %shard_map.276 = (bf16[3,1024,256]{2,1,0:T(8,128)(2,1)}, bf16[1024,256]{1,0:T(8,128)(2,1)}, f32[8,128]{1,0:T(8,128)S(1)}) custom-call(s32[3]{0:T(128)S(1)} %pad_add_fusion.core.refs_0_, bf16[4,256,1024]{2,1,0:T(8,128)(2,1)S(1)} %shard_map.275.refs_1_, bf16[4,256,1024]{2,1,0:T(8,128)(2,1)S(1)} %collective-permute-done.18.refs_2_, ...), custom_call_target="tpu_custom_call" | custom-call | flops 1200000000 | tf_op jit(solution)/shard_map/pallas_call | solution.py:54
  84.9 0.1 shard_map.277
  84.9 2.5 %collective-permute-start.21 = (bf16[672,128]{1,0:T(8,128)(2,1)S(1)}, bf16[672,128]{1,0:T(8,128)(2,1)S(1)}, u32[]{:S(2)}, u32[]{:S(2)}) collective-permute-start(bf16[672,128]{1,0:T(8,128)(2,1)S(1)} %get-tuple-element.137.refs_1_), channel_id=1, source_target_pairs={{0,8},{1,5},{2,10},{3,7},{4,12},{5,1},{6,14},{7,3},{8,0},{9,13},{1... | collective-permute-start | bytes 516104 | tf_op jit(solution)/shard_map/ppermute | solution.py:872
  87.5 3.4 %collective-permute-done.21.refs_2_ = bf16[672,128]{1,0:T(8,128)(2,1)S(1)} collective-permute-done((bf16[672,128]{1,0:T(8,128)(2,1)S(1)}, bf16[672,128]{1,0:T(8,128)(2,1)S(1)}, u32[]{:S(2)}, u32[]{:S(2)}) %collective-permute-start.21) | collective-permute-done | bytes 172064 | tf_op jit(solution)/shard_map/ppermute | solution.py:872
  90.9 0.0 copy-start.6
  90.9 0.0 copy-start.7
  90.9 0.0 copy-start.8
  90.9 0.0 copy-start.9
  90.9 0.0 copy-start.10
  90.9 0.0 copy-start.11
  90.9 0.0 copy-start.12
  91.0 0.1 shard_map.278
  91.1 0.1 collective-permute-start.22
  91.2 1.3 %collective-permute-done.22.refs_3_ = bf16[416,128]{1,0:T(8,128)(2,1)S(1)} collective-permute-done((bf16[416,128]{1,0:T(8,128)(2,1)S(1)}, bf16[416,128]{1,0:T(8,128)(2,1)S(1)}, u32[]{:S(2)}, u32[]{:S(2)}) %collective-permute-start.22) | collective-permute-done | bytes 106528 | tf_op jit(solution)/shard_map/ppermute | solution.py:872
  92.6 2.4 %shard_map.279 = (f32[32,16,64]{2,1,0:T(8,128)}, f32[32,16,64]{2,1,0:T(8,128)}, f32[32,16,64]{2,1,0:T(8,128)}, f32[16,32,64]{2,1,0:T(8,128)}, f32[16,32,64]{2,1,...) custom-call(s32[3]{0:T(128)S(1)} %pad_add_fusion.core.refs_0_, ...), custom_call_target="tpu_custom_call" | custom-call | flops 28800000000 | tf_op jit(solution)/shard_map/pallas_call | solution.py:54
  (49 shorter events, 0.2 us)
Async XLA Ops:
  2.3 1.5 %collective-permute-start = (bf16[2,8,32,64]{3,2,1,0:T(8,128)(2,1)S(1)}, bf16[2,8,32,64]{3,2,1,0:T(8,128)(2,1)S(1)}, u32[]{:S(2)}, u32[]{:S(2)}) collective-permute-start(bf16[2,8,32,64]{3,2,1,0:T(8,128)(2,1)S(1)} %get-tuple-element.84), channel_id=1, source_target_pairs={{0,1},{1,0},{2,3},{3,2},{4,5},{5,4},{6,7},{7,6},{8,9},{9,8},{10,11... | collective-permute-start | bytes 196616 | tf_op jit(solution)/shard_map/ppermute | solution.py:872
  3.8 13.0 %collective-permute-start.5 = (bf16[3,1024,256]{2,1,0:T(8,128)(2,1)}, bf16[3,1024,256]{2,1,0:T(8,128)(2,1)S(1)}, u32[]{:S(2)}, u32[]{:S(2)}) collective-permute-start(bf16[3,1024,256]{2,1,0:T(8,128)(2,1)} %bitcast.13), channel_id=1, source_target_pairs={{0,1},{1,0},{2,3},{3,2},{4,5},{5,4},{6,7},{7,6},{8,9},{9,8},{10,11... | collective-permute-start | bytes 4718600 | tf_op jit(solution)/shard_map/ppermute | solution.py:872
  4.1 4.3 %collective-permute-start.3 = (bf16[32,128]{1,0:T(8,128)(2,1)S(1)}, bf16[32,128]{1,0:T(8,128)(2,1)S(1)}, u32[]{:S(2)}, u32[]{:S(2)}) collective-permute-start(bf16[32,128]{1,0:T(8,128)(2,1)S(1)} %get-tuple-element.87.refs_0_), channel_id=1, source_target_pairs={{0,1},{1,0},{2,3},{3,2},{4,5},{5,4},{6,7},{7,6},{8,9},{9,8},{10,11... | collective-permute-start | bytes 24584 | tf_op jit(solution)/shard_map/ppermute | solution.py:872
  4.3 4.1 %copy-start.5 = (bf16[1024,256]{1,0:T(8,128)(2,1)S(1)}, bf16[1024,256]{1,0:T(8,128)(2,1)}, u32[]{:S(2)}) copy-start(bf16[1024,256]{1,0:T(8,128)(2,1)} %refs_1_.3) | copy-start | bytes 1572868
  4.4 8.2 %collective-permute-start.1 = (bf16[288,128]{1,0:T(8,128)(2,1)S(1)}, bf16[288,128]{1,0:T(8,128)(2,1)S(1)}, u32[]{:S(2)}, u32[]{:S(2)}) collective-permute-start(bf16[288,128]{1,0:T(8,128)(2,1)S(1)} %get-tuple-element.86.refs_0_), channel_id=1, source_target_pairs={{0,16},{1,17},{2,18},{3,19},{4,20},{5,21},{6,22},{7,23},{8,24},{9,... | collective-permute-start | bytes 221192 | tf_op jit(solution)/shard_map/ppermute | solution.py:872
  8.4 8.3 %collective-permute-start.4 = (bf16[1024,256]{1,0:T(8,128)(2,1)S(1)}, bf16[1024,256]{1,0:T(8,128)(2,1)S(1)}, u32[]{:S(2)}, u32[]{:S(2)}) collective-permute-start(bf16[1024,256]{1,0:T(8,128)(2,1)S(1)} %copy-done.5), channel_id=1, source_target_pairs={{0,1},{1,0},{2,3},{3,2},{4,5},{5,4},{6,7},{7,6},{8,9},{9,8},{10,11... | collective-permute-start | bytes 1572872 | tf_op jit(solution)/shard_map/ppermute | solution.py:872
  8.4 8.3 %copy-start.4 = (bf16[1024,3,256]{2,0,1:T(8,128)(2,1)S(1)}, bf16[1024,3,256]{2,0,1:T(8,128)(2,1)}, u32[]{:S(2)}) copy-start(bf16[1024,3,256]{2,0,1:T(8,128)(2,1)} %param.20) | copy-start | bytes 4718596
  12.6 6.6 %collective-permute-start.2 = (bf16[576,128]{1,0:T(8,128)(2,1)S(1)}, bf16[576,128]{1,0:T(8,128)(2,1)S(1)}, u32[]{:S(2)}, u32[]{:S(2)}) collective-permute-start(bf16[576,128]{1,0:T(8,128)(2,1)S(1)} %shard_map.256.refs_5_.refs_0_), channel_id=1, source_target_pairs={{0,8},{1,9},{2,10},{3,11},{4,12},{5,13},{6,14},{7,15},{8,0},{9,1},... | collective-permute-start | bytes 442376 | tf_op jit(solution)/shard_map/ppermute | solution.py:872
  13.4 7.5 %collective-permute-start.9 = (bf16[256,128]{1,0:T(8,128)(2,1)S(1)}, bf16[256,128]{1,0:T(8,128)(2,1)S(1)}, u32[]{:S(2)}, u32[]{:S(2)}) collective-permute-start(bf16[256,128]{1,0:T(8,128)(2,1)S(1)} %get-tuple-element.98.refs_0_), channel_id=1, source_target_pairs={{0,16},{1,17},{2,18},{3,19},{4,20},{5,21},{6,22},{7,23},{8,24},{9,... | collective-permute-start | bytes 196616 | tf_op jit(solution)/shard_map/ppermute | solution.py:872
  18.6 0.7 copy-start.16
  18.6 14.8 %copy-start.18 = (bf16[3,256,2048]{2,1,0:T(8,128)(2,1)}, bf16[3,256,2048]{2,1,0:T(8,128)(2,1)S(1)}, u32[]{:S(2)}) copy-start(bf16[3,256,2048]{2,1,0:T(8,128)(2,1)S(1)} %get-tuple-element.94.refs_6_.refs_1_.refs_3_.refs_4_) | copy-start | bytes 9437188
  19.3 6.9 %collective-permute-start.6 = (bf16[1216,128]{1,0:T(8,128)(2,1)S(1)}, bf16[1216,128]{1,0:T(8,128)(2,1)S(1)}, u32[]{:S(2)}, u32[]{:S(2)}) collective-permute-start(bf16[1216,128]{1,0:T(8,128)(2,1)S(1)} %shard_map.259.refs_0_.refs_2_), channel_id=1, source_target_pairs={{0,2},{1,5},{2,0},{3,7},{4,6},{5,1},{6,4},{7,3},{8,10},{9,13},{10,... | collective-permute-start | bytes 933896 | tf_op jit(solution)/shard_map/ppermute | solution.py:872
  20.9 7.1 %collective-permute-start.10 = (bf16[512,128]{1,0:T(8,128)(2,1)S(1)}, bf16[512,128]{1,0:T(8,128)(2,1)S(1)}, u32[]{:S(2)}, u32[]{:S(2)}) collective-permute-start(bf16[512,128]{1,0:T(8,128)(2,1)S(1)} %shard_map.262.refs_0_), channel_id=1, source_target_pairs={{0,8},{1,9},{2,10},{3,11},{4,12},{5,13},{6,14},{7,15},{8,0},{9,1},... | collective-permute-start | bytes 393224 | tf_op jit(solution)/shard_map/ppermute | solution.py:872
  26.2 3.3 %collective-permute-start.8 = (bf16[320,128]{1,0:T(8,128)(2,1)S(1)}, bf16[320,128]{1,0:T(8,128)(2,1)S(1)}, u32[]{:S(2)}, u32[]{:S(2)}) collective-permute-start(bf16[320,128]{1,0:T(8,128)(2,1)S(1)} %get-tuple-element.93.refs_2_), channel_id=1, source_target_pairs={{0,1},{1,0},{2,3},{3,2},{4,5},{5,4},{6,7},{7,6},{8,9},{9,8},{10,11... | collective-permute-start | bytes 245768 | tf_op jit(solution)/shard_map/ppermute | solution.py:872
  26.3 3.3 %copy-start.14 = (bf16[160,128]{1,0:T(8,128)(2,1)S(1)}, bf16[160,128]{1,0:T(8,128)(2,1)}, u32[]{:S(2)}) copy-start(bf16[160,128]{1,0:T(8,128)(2,1)} %constant.24.clone.refs_1_) | copy-start | bytes 122884
  26.3 12.1 %collective-permute-start.7 = (bf16[2048,128]{1,0:T(8,128)(2,1)S(1)}, bf16[2048,128]{1,0:T(8,128)(2,1)S(1)}, u32[]{:S(2)}, u32[]{:S(2)}) collective-permute-start(bf16[2048,128]{1,0:T(8,128)(2,1)S(1)} %get-tuple-element.91.refs_2_.refs_1_), channel_id=1, source_target_pairs={{0,4},{1,3},{2,6},{3,1},{4,0},{5,7},{6,2},{7,5},{8,12},{9,11},{10,... | collective-permute-start | bytes 1572872 | tf_op jit(solution)/shard_map/ppermute | solution.py:872
  28.0 9.3 %collective-permute-start.11 = (bf16[1024,128]{1,0:T(8,128)(2,1)S(1)}, bf16[1024,128]{1,0:T(8,128)(2,1)S(1)}, u32[]{:S(2)}, u32[]{:S(2)}) collective-permute-start(bf16[1024,128]{1,0:T(8,128)(2,1)S(1)} %shard_map.263.refs_0_), channel_id=1, source_target_pairs={{0,2},{1,5},{2,0},{3,7},{4,6},{5,1},{6,4},{7,3},{8,10},{9,13},{10,... | collective-permute-start | bytes 786440 | tf_op jit(solution)/shard_map/ppermute | solution.py:872
  37.4 9.7 %collective-permute-start.12 = (bf16[2048,128]{1,0:T(8,128)(2,1)S(1)}, bf16[2048,128]{1,0:T(8,128)(2,1)S(1)}, u32[]{:S(2)}, u32[]{:S(2)}) collective-permute-start(bf16[2048,128]{1,0:T(8,128)(2,1)S(1)} %shard_map.265.refs_6_.refs_1_), channel_id=1, source_target_pairs={{0,4},{1,3},{2,6},{3,1},{4,0},{5,7},{6,2},{7,5},{8,12},{9,11},{10,... | collective-permute-start | bytes 1572872 | tf_op jit(solution)/shard_map/ppermute | solution.py:872
  38.4 8.7 %copy-start.17 = (bf16[256,256]{1,0:T(8,128)(2,1)S(1)}, bf16[256,256]{1,0:T(8,128)(2,1)}, u32[]{:S(2)}) copy-start(bf16[256,256]{1,0:T(8,128)(2,1)} %copy-done.16) | copy-start | bytes 393220
  45.4 13.4 %collective-permute-start.13 = (bf16[2048,128]{1,0:T(8,128)(2,1)S(1)}, bf16[2048,128]{1,0:T(8,128)(2,1)S(1)}, u32[]{:S(2)}, u32[]{:S(2)}) collective-permute-start(bf16[2048,128]{1,0:T(8,128)(2,1)S(1)} %get-tuple-element.119.refs_1_), channel_id=1, source_target_pairs={{0,4},{1,3},{2,6},{3,1},{4,0},{5,7},{6,2},{7,5},{8,12},{9,11},{10,... | collective-permute-start | bytes 1572872 | tf_op jit(solution)/shard_map/ppermute | solution.py:872
  47.1 7.7 %copy-start.19 = (bf16[3,256,2048]{2,1,0:T(8,128)(2,1)S(1)}, bf16[3,256,2048]{2,1,0:T(8,128)(2,1)}, u32[]{:S(2)}) copy-start(bf16[3,256,2048]{2,1,0:T(8,128)(2,1)} %copy-done.18) | copy-start | bytes 9437188
  54.4 14.8 %collective-permute-start.14 = (bf16[2080,128]{1,0:T(8,128)(2,1)S(1)}, bf16[2080,128]{1,0:T(8,128)(2,1)S(1)}, u32[]{:S(2)}, u32[]{:S(2)}) collective-permute-start(bf16[2080,128]{1,0:T(8,128)(2,1)S(1)} %get-tuple-element.124.refs_1_), channel_id=1, source_target_pairs={{0,4},{1,3},{2,6},{3,1},{4,0},{5,7},{6,2},{7,5},{8,12},{9,11},{10,... | collective-permute-start | bytes 1597448 | tf_op jit(solution)/shard_map/ppermute | solution.py:872
  58.8 1.5 %copy-start.15 = (bf16[160,128]{1,0:T(8,128)(2,1)S(1)}, bf16[160,128]{1,0:T(8,128)(2,1)}, u32[]{:S(2)}) copy-start(bf16[160,128]{1,0:T(8,128)(2,1)} %constant.24.clone.refs_1_) | copy-start | bytes 122884
  59.0 10.2 %collective-permute-start.16 = (bf16[1024,128]{1,0:T(8,128)(2,1)S(1)}, bf16[1024,128]{1,0:T(8,128)(2,1)S(1)}, u32[]{:S(2)}, u32[]{:S(2)}) collective-permute-start(bf16[1024,128]{1,0:T(8,128)(2,1)S(1)} %get-tuple-element.126.refs_1_), channel_id=1, source_target_pairs={{0,2},{1,17},{2,0},{3,19},{4,6},{5,21},{6,4},{7,23},{8,10},{9,25},... | collective-permute-start | bytes 786440 | tf_op jit(solution)/shard_map/ppermute | solution.py:872
  65.2 4.0 %collective-permute-start.15 = (bf16[128,128]{1,0:T(8,128)(2,1)S(1)}, bf16[128,128]{1,0:T(8,128)(2,1)S(1)}, u32[]{:S(2)}, u32[]{:S(2)}) collective-permute-start(bf16[128,128]{1,0:T(8,128)(2,1)S(1)} %get-tuple-element.125.refs_3_), channel_id=1, source_target_pairs={{0,4},{1,3},{2,6},{3,1},{4,0},{5,7},{6,2},{7,5},{8,12},{9,11},{10,... | collective-permute-start | bytes 98312 | tf_op jit(solution)/shard_map/ppermute | solution.py:872
  69.3 6.9 %collective-permute-start.17 = (bf16[1184,128]{1,0:T(8,128)(2,1)S(1)}, bf16[1184,128]{1,0:T(8,128)(2,1)S(1)}, u32[]{:S(2)}, u32[]{:S(2)}) collective-permute-start(bf16[1184,128]{1,0:T(8,128)(2,1)S(1)} %get-tuple-element.128.refs_1_), channel_id=1, source_target_pairs={{0,2},{1,17},{2,0},{3,19},{4,6},{5,21},{6,4},{7,23},{8,10},{9,25},... | collective-permute-start | bytes 909320 | tf_op jit(solution)/shard_map/ppermute | solution.py:872
  73.6 8.4 %collective-permute-start.18 = (bf16[4,256,1024]{2,1,0:T(8,128)(2,1)S(1)}, bf16[4,256,1024]{2,1,0:T(8,128)(2,1)S(1)}, u32[]{:S(2)}, u32[]{:S(2)}) collective-permute-start(bf16[4,256,1024]{2,1,0:T(8,128)(2,1)S(1)} %shard_map.273.refs_3_), channel_id=1, source_target_pairs={{0,1},{1,0},{2,3},{3,2},{4,5},{5,4},{6,7},{7,6},{8,9},{9,8},{10,11... | collective-permute-start | bytes 6291464 | tf_op jit(solution)/shard_map/ppermute | solution.py:872
  73.7 11.1 %collective-permute-start.19 = (bf16[512,128]{1,0:T(8,128)(2,1)S(1)}, bf16[512,128]{1,0:T(8,128)(2,1)S(1)}, u32[]{:S(2)}, u32[]{:S(2)}) collective-permute-start(bf16[512,128]{1,0:T(8,128)(2,1)S(1)} %get-tuple-element.133.refs_5_), channel_id=1, source_target_pairs={{0,16},{1,9},{2,18},{3,11},{4,20},{5,13},{6,22},{7,15},{8,24},{9,1... | collective-permute-start | bytes 393224 | tf_op jit(solution)/shard_map/ppermute | solution.py:872
  76.2 8.6 %collective-permute-start.20 = (bf16[672,128]{1,0:T(8,128)(2,1)S(1)}, bf16[672,128]{1,0:T(8,128)(2,1)S(1)}, u32[]{:S(2)}, u32[]{:S(2)}) collective-permute-start(bf16[672,128]{1,0:T(8,128)(2,1)S(1)} %get-tuple-element.134.refs_3_), channel_id=1, source_target_pairs={{0,16},{1,9},{2,18},{3,11},{4,20},{5,13},{6,22},{7,15},{8,24},{9,1... | collective-permute-start | bytes 516104 | tf_op jit(solution)/shard_map/ppermute | solution.py:872
  84.9 5.9 %collective-permute-start.21 = (bf16[672,128]{1,0:T(8,128)(2,1)S(1)}, bf16[672,128]{1,0:T(8,128)(2,1)S(1)}, u32[]{:S(2)}, u32[]{:S(2)}) collective-permute-start(bf16[672,128]{1,0:T(8,128)(2,1)S(1)} %get-tuple-element.137.refs_1_), channel_id=1, source_target_pairs={{0,8},{1,5},{2,10},{3,7},{4,12},{5,1},{6,14},{7,3},{8,0},{9,13},{1... | collective-permute-start | bytes 516104 | tf_op jit(solution)/shard_map/ppermute | solution.py:872
  90.8 1.6 %copy-start = (f32[32,16,64]{2,1,0:T(8,128)S(1)}, f32[32,16,64]{2,1,0:T(8,128)}, u32[]{:S(2)}) copy-start(f32[32,16,64]{2,1,0:T(8,128)} %refs_4_.1) | copy-start | bytes 393220
  90.8 1.6 %copy-start.1 = (f32[16,64,32]{1,2,0:T(8,128)S(1)}, f32[16,64,32]{1,2,0:T(8,128)}, u32[]{:S(2)}) copy-start(f32[16,64,32]{1,2,0:T(8,128)} %param.17) | copy-start | bytes 393220
  90.8 1.6 %copy-start.2 = (f32[2,16,64]{2,1,0:T(8,128)S(1)}, f32[2,16,64]{2,1,0:T(8,128)}, u32[]{:S(2)}) copy-start(f32[2,16,64]{2,1,0:T(8,128)} %refs_10_.1) | copy-start | bytes 24580
  90.8 1.6 %copy-start.3 = (f32[32,60]{1,0:T(8,128)S(1)}, f32[32,60]{1,0:T(8,128)}, u32[]{:S(2)}) copy-start(f32[32,60]{1,0:T(8,128)} %refs_13_.1) | copy-start | bytes 23044
  90.9 1.6 %copy-start.6 = (f32[32,16,64]{2,1,0:T(8,128)S(1)}, f32[32,16,64]{2,1,0:T(8,128)}, u32[]{:S(2)}) copy-start(f32[32,16,64]{2,1,0:T(8,128)} %refs_5_.1) | copy-start | bytes 393220
  90.9 1.6 %copy-start.7 = (f32[32,16,64]{2,1,0:T(8,128)S(1)}, f32[32,16,64]{2,1,0:T(8,128)}, u32[]{:S(2)}) copy-start(f32[32,16,64]{2,1,0:T(8,128)} %refs_6_.1) | copy-start | bytes 393220
  90.9 1.6 %copy-start.8 = (f32[16,64,32]{1,2,0:T(8,128)S(1)}, f32[16,64,32]{1,2,0:T(8,128)}, u32[]{:S(2)}) copy-start(f32[16,64,32]{1,2,0:T(8,128)} %param.23) | copy-start | bytes 393220
  90.9 1.6 %copy-start.9 = (f32[16,64,32]{1,2,0:T(8,128)S(1)}, f32[16,64,32]{1,2,0:T(8,128)}, u32[]{:S(2)}) copy-start(f32[16,64,32]{1,2,0:T(8,128)} %param.24) | copy-start | bytes 393220
  90.9 1.6 %copy-start.10 = (f32[2,16,64]{2,1,0:T(8,128)S(1)}, f32[2,16,64]{2,1,0:T(8,128)}, u32[]{:S(2)}) copy-start(f32[2,16,64]{2,1,0:T(8,128)} %refs_11_.1) | copy-start | bytes 24580
  90.9 1.6 %copy-start.11 = (f32[2,16,64]{2,1,0:T(8,128)S(1)}, f32[2,16,64]{2,1,0:T(8,128)}, u32[]{:S(2)}) copy-start(f32[2,16,64]{2,1,0:T(8,128)} %refs_12_.1) | copy-start | bytes 24580
  90.9 1.6 %copy-start.12 = (f32[32,60]{1,0:T(8,128)S(1)}, f32[32,60]{1,0:T(8,128)}, u32[]{:S(2)}) copy-start(f32[32,60]{1,0:T(8,128)} %refs_14_.1) | copy-start | bytes 23044
  90.9 1.6 %copy-start.13 = (f32[32,60]{1,0:T(8,128)S(1)}, f32[32,60]{1,0:T(8,128)}, u32[]{:S(2)}) copy-start(f32[32,60]{1,0:T(8,128)} %refs_15_.1) | copy-start | bytes 23044
  91.1 1.4 %collective-permute-start.22 = (bf16[416,128]{1,0:T(8,128)(2,1)S(1)}, bf16[416,128]{1,0:T(8,128)(2,1)S(1)}, u32[]{:S(2)}, u32[]{:S(2)}) collective-permute-start(bf16[416,128]{1,0:T(8,128)(2,1)S(1)} %get-tuple-element.139.refs_2_), channel_id=1, source_target_pairs={{0,1},{1,0},{2,3},{3,2},{4,5},{5,4},{6,7},{7,6},{8,9},{9,8},{10,11... | collective-permute-start | bytes 319496 | tf_op jit(solution)/shard_map/ppermute | solution.py:872

commit v5 on v4

--- a/solution.py
+++ b/solution.py
@@ -859,9 +859,10 @@
     dims = [side] + [(m, 0) for m in masks]
     if n_rows == 8:
         way = ((3, 2, 0, 1), (3, 2, 1, 0))
+        late_way = ((0, 3, 2, 1), (1, 3, 2, 0))
         back_way = ((2, 3, 0, 1), (1, 2, 3, 0))
     else:
-        way = back_way = (tuple(range(len(dims))),) * 2
+        way = late_way = back_way = (tuple(range(len(dims))),) * 2
 
     def swap(x, hops):
         pairs = []
@@ -873,6 +874,9 @@
 
     def hops(step):
         return tuple(dims[way[k][step]] for k in range(2))
+
+    def late_hops(step):
+        return tuple(dims[late_way[k][step]] for k in range(2))
 
     def back_hops(step):
         return tuple(dims[back_way[k][step]] for k in range(2))
@@ -939,7 +943,7 @@
         a_msg, b_msg = chip_messages(w_mine, w_recv, sel)
         a_got = swap(a_msg, hops(0))
         (a_msg,) = join((((0, 0, n), (1, 0, n), (0, n, d_loc), (1, n, d_loc)),), a_msg, a_got)
-        b_got = swap(tie(b_msg, a_got), hops(0))
+        b_got = swap(b_msg, late_hops(0))
         a_got = swap(a_msg, hops(1))
         xt, gt, perm, to_q = turn(masks, at, x_own, x_recv, g_own, g_recv, (a_msg,))
         n *= 2
@@ -952,7 +956,7 @@
             (((0, 0, x.shape[0]), (1, 0, x.shape[0])),), x, y, after=after
         )[0]
         b_msg = both(b_msg, b_got, (a_msg,))
-        b_got = swap(b_msg, hops(1))
+        b_got = swap(b_msg, late_hops(1))
         n *= 2
         a_lo, riders = join(
             (
@@ -964,7 +968,7 @@
         a_hi = swap(a_lo, hops(3))
         turned = swap(riders, sibling)
         b_msg = both(b_msg, b_got, (a_lo,))
-        b_got = swap(b_msg, hops(2))
+        b_got = swap(b_msg, late_hops(2))
     else:
         xt, gt, perm, to_q = turn(masks, at, x_own, x_recv, g_own, g_recv, (sel,))
         chip = jnp.concatenate([w_mine, w_recv], axis=3)
@@ -986,12 +990,12 @@
     cc_b, gb1_b = late(gates, gt, (b0,))
     if ride:
         b_lo = both(b_msg, b_got, (gb1_b,))
-        b_hi = swap(b_lo, hops(3))
+        b_hi = swap(b_lo, late_hops(3))
     first = critical(spots, back, at, a_lo, a_hi, xt, cc_a, b0, (b_lo,))
     a_lo, a_msg = uncanonical(first[0], first[1])
     a_got = swap(a_msg, back_hops(steps - 1))
     second = critical(
-        spots, back, at, b_lo, b_hi, xt, cc_b, b0, (first[0],), (first[6], gb1_a, gb1_b, to_q, perm)
+        table_of(late_way), back, at, b_lo, b_hi, xt, cc_b, b0, (first[0],), (first[6], gb1_a, gb1_b, to_q, perm)
     )
     b_lo, b_msg = second[:2]
     if not ride:
@@ -1006,10 +1010,10 @@
         1, at, second[5], second[2], gt, logits, b1, order, (gl_a, xt, perm), (a_lo,)
     )
     gsel_got = swap(gsel, back_hops(steps - 1))
-    b_lo, b_msg = fold(b_lo.shape[:1], b_lo, b_msg, b_got, (gsel, gsel_got), (a_got,))
+    a_lo, a_msg = fold(a_lo.shape[:1], a_lo, a_msg, a_got, after=(gsel,))
+    a_got = swap(a_msg, back_hops(steps - 3))
+    b_lo, b_msg = fold(b_lo.shape[:1], b_lo, b_msg, b_got, (gsel, gsel_got), (a_lo,))
     b_got = swap(b_msg, back_hops(steps - 2))
-    a_lo, a_msg = fold(a_lo.shape[:1], a_lo, a_msg, a_got, after=(b_lo,))
-    a_got = swap(a_msg, back_hops(steps - 3))
     ends = ((first[4], first[3], ys_a), (second[4], second[3], ys_b))
     n_own = x_own.shape[0]
     mix_other = mix(n_own, n_own, *ends, selp, gls, gates, (a_lo, b_lo))

time: 95.3 us -> 94.5 us (level)
  waiting for transfers between devices: 19.6 us -> 17.8 us
  starting transfers between devices: 29.2 us -> 30.3 us
    ppermute x23, waiting for transfers between devices: 19.6 us -> 17.8 us  [swap(): return lax.ppermute(x, ('rows', 'hid'), pairs)]
    ppermute x23, starting transfers between devices: 29.2 us -> 30.3 us  [swap(): return lax.ppermute(x, ('rows', 'hid'), pairs)]
where the time goes in v5:
time: 94.5 us; the launch traced here: 94.3 us
  Pallas kernels  44.9 us (48%)
  starting transfers between devices  30.3 us (32%)
  waiting for transfers between devices  17.8 us (19%)
  between operations  1.08 us (1%)
    pallas_call x25, Pallas kernels, kernel_call(): pl.pallas_call(kernel, out_shape=tuple((jax.ShapeDtypeStruct(shape, kind)...  43.3 us
    ppermute x23, starting transfers between devices, swap(): return lax.ppermute(x, ('rows', 'hid'), pairs)  30.3 us
    ppermute x23, waiting for transfers between devices, swap(): return lax.ppermute(x, ('rows', 'hid'), pairs)  17.8 us
  transfers between devices with their start and end apart: 23, of which 10 were waited for; matrix products, arithmetic and copies ran while one was open for 0% of the time, Pallas kernels for 43%

profile of v5, /device:TPU:0, one launch (start us, length us, event | category | flops | bytes accessed | tf_op | source)
XLA Modules:
  0.0 94.3 jit_solution(7962803254187069764)
XLA Ops:
  0.7 0.1 pad_add_fusion.core.refs_0_
  0.7 1.5 %shard_map.254 = (bf16[32,128]{1,0:T(8,128)(2,1)S(1)}, bf16[32,128]{1,0:T(8,128)(2,1)S(1)}, bf16[2,8,32,64]{3,2,1,0:T(8,128)(2,1)S(1)}, bf16[2,8,32,64]{3,2,1,0:T(8,128)(2,1)S(1)}) custom-call(s32[3]{0:T(128)S(1)} %pad_add_fusion.core.refs_0_, f32[32,16,64]{2,1,0:T(8,128)} %refs_4_.1, f32[16,32,64]{2,1,0:T(8,128)} %bitcast.11, f32[2,16,64]{2,1,0:T(8,128)} %refs_10_.1, ...), custom_call_target="tpu_custom_call" | custom-call | tf_op jit(solution)/shard_map/pallas_call | solution.py:697
  2.3 0.5 collective-permute-start
  2.8 1.0 %collective-permute-done.refs_1_ = bf16[2,8,32,64]{3,2,1,0:T(8,128)(2,1)S(1)} collective-permute-done((bf16[2,8,32,64]{3,2,1,0:T(8,128)(2,1)S(1)}, bf16[2,8,32,64]{3,2,1,0:T(8,128)(2,1)S(1)}, u32[]{:S(2)}, u32[]{:S(2)}) %collective-permute-start) | collective-permute-done | bytes 65568 | tf_op jit(solution)/shard_map/ppermute | solution.py:873
  3.8 0.4 collective-permute-start.5
  4.1 0.1 collective-permute-start.3
  4.3 0.1 shard_map.255
  4.4 4.0 %collective-permute-start.1 = (bf16[288,128]{1,0:T(8,128)(2,1)S(1)}, bf16[288,128]{1,0:T(8,128)(2,1)S(1)}, u32[]{:S(2)}, u32[]{:S(2)}) collective-permute-start(bf16[288,128]{1,0:T(8,128)(2,1)S(1)} %get-tuple-element.85.refs_0_), channel_id=1, source_target_pairs={{0,16},{1,17},{2,18},{3,19},{4,20},{5,21},{6,22},{7,23},{8,24},{9,... | collective-permute-start | bytes 221192 | tf_op jit(solution)/shard_map/ppermute | solution.py:873
  8.4 0.0 copy-start.4
  8.4 1.6 %collective-permute-start.9 = (bf16[256,128]{1,0:T(8,128)(2,1)S(1)}, bf16[256,128]{1,0:T(8,128)(2,1)S(1)}, u32[]{:S(2)}, u32[]{:S(2)}) collective-permute-start(bf16[256,128]{1,0:T(8,128)(2,1)S(1)} %get-tuple-element.96.refs_0_), channel_id=1, source_target_pairs={{0,2},{1,5},{2,0},{3,7},{4,6},{5,1},{6,4},{7,3},{8,10},{9,13},{10,... | collective-permute-start | bytes 196616 | tf_op jit(solution)/shard_map/ppermute | solution.py:873
  10.0 2.6 %collective-permute-done.1.refs_1_ = bf16[288,128]{1,0:T(8,128)(2,1)S(1)} collective-permute-done((bf16[288,128]{1,0:T(8,128)(2,1)S(1)}, bf16[288,128]{1,0:T(8,128)(2,1)S(1)}, u32[]{:S(2)}, u32[]{:S(2)}) %collective-permute-start.1) | collective-permute-done | bytes 73760 | tf_op jit(solution)/shard_map/ppermute | solution.py:873
  12.6 0.8 collective-permute-start.2
  13.4 1.9 %shard_map.258 = (bf16[272,2048]{1,0:T(8,128)(2,1)S(1)}, bf16[3,256,2048]{2,1,0:T(8,128)(2,1)S(1)}, bf16[256,256]{1,0:T(8,128)(2,1)S(1)}, bf16[256,256]{1,0:T(8,128)(2,1)S(1)}) custom-call(s32[3]{0:T(128)S(1)} %pad_add_fusion.core.refs_0_, bf16[1024,256]{1,0:T(8,128)(2,1)S(1)} %copy-done.5, bf16[1024,256]{1,0:T(8,128)(2,1)S(1)} %collective-permute-done.4.refs_2_, ...), custom_call_target="tpu_custom_call" | custom-call | flops 41999998976 | tf_op jit(solution)/shard_map/pallas_call | solution.py:54
  15.2 0.0 copy-start.16
  15.3 2.5 %collective-permute-done.2.refs_1_ = bf16[576,128]{1,0:T(8,128)(2,1)S(1)} collective-permute-done((bf16[576,128]{1,0:T(8,128)(2,1)S(1)}, bf16[576,128]{1,0:T(8,128)(2,1)S(1)}, u32[]{:S(2)}, u32[]{:S(2)}) %collective-permute-start.2) | collective-permute-done | bytes 147488 | tf_op jit(solution)/shard_map/ppermute | solution.py:873
  17.8 1.6 %collective-permute-start.6 = (bf16[1216,128]{1,0:T(8,128)(2,1)S(1)}, bf16[1216,128]{1,0:T(8,128)(2,1)S(1)}, u32[]{:S(2)}, u32[]{:S(2)}) collective-permute-start(bf16[1216,128]{1,0:T(8,128)(2,1)S(1)} %shard_map.259.refs_0_.refs_2_), channel_id=1, source_target_pairs={{0,2},{1,5},{2,0},{3,7},{4,6},{5,1},{6,4},{7,3},{8,10},{9,13},{10,... | collective-permute-start | bytes 933896 | tf_op jit(solution)/shard_map/ppermute | solution.py:873
  19.5 3.0 %collective-permute-start.10 = (bf16[512,128]{1,0:T(8,128)(2,1)S(1)}, bf16[512,128]{1,0:T(8,128)(2,1)S(1)}, u32[]{:S(2)}, u32[]{:S(2)}) collective-permute-start(bf16[512,128]{1,0:T(8,128)(2,1)S(1)} %shard_map.262.refs_0_), channel_id=1, source_target_pairs={{0,16},{1,17},{2,18},{3,19},{4,20},{5,21},{6,22},{7,23},{8,24},{9,... | collective-permute-start | bytes 393224 | tf_op jit(solution)/shard_map/ppermute | solution.py:873
  22.5 2.3 %collective-permute-done.6.refs_1_ = bf16[1216,128]{1,0:T(8,128)(2,1)S(1)} collective-permute-done((bf16[1216,128]{1,0:T(8,128)(2,1)S(1)}, bf16[1216,128]{1,0:T(8,128)(2,1)S(1)}, u32[]{:S(2)}, u32[]{:S(2)}) %collective-permute-start.6) | collective-permute-done | bytes 311328 | tf_op jit(solution)/shard_map/ppermute | solution.py:873
  24.8 0.1 collective-permute-start.8
  24.9 0.0 copy-start.14
  24.9 1.7 %collective-permute-start.7 = (bf16[2048,128]{1,0:T(8,128)(2,1)S(1)}, bf16[2048,128]{1,0:T(8,128)(2,1)S(1)}, u32[]{:S(2)}, u32[]{:S(2)}) collective-permute-start(bf16[2048,128]{1,0:T(8,128)(2,1)S(1)} %get-tuple-element.90.refs_2_.refs_1_), channel_id=1, source_target_pairs={{0,4},{1,3},{2,6},{3,1},{4,0},{5,7},{6,2},{7,5},{8,12},{9,11},{10,... | collective-permute-start | bytes 1572872 | tf_op jit(solution)/shard_map/ppermute | solution.py:873
  26.6 1.6 %collective-permute-done.10.refs_1_ = bf16[512,128]{1,0:T(8,128)(2,1)S(1)} collective-permute-done((bf16[512,128]{1,0:T(8,128)(2,1)S(1)}, bf16[512,128]{1,0:T(8,128)(2,1)S(1)}, u32[]{:S(2)}, u32[]{:S(2)}) %collective-permute-start.10) | collective-permute-done | bytes 131104 | tf_op jit(solution)/shard_map/ppermute | solution.py:873
  28.2 0.7 collective-permute-start.11
  29.0 3.8 %shard_map.261 = (bf16[4,256,2048]{2,1,0:T(8,128)(2,1)S(1)}, f32[8,8,2048]{2,1,0:T(8,128)S(1)}, f32[160,2048]{1,0:T(8,128)S(1)}, bf16[160,256]{1,0:T(8,128)(2,1)...) custom-call(s32[3]{0:T(128)S(1)} %pad_add_fusion.core.refs_0_, ...), custom_call_target="tpu_custom_call" | custom-call | flops 60000002048 | tf_op jit(solution)/shard_map/pallas_call | solution.py:54
  32.8 1.6 %shard_map.264 = (bf16[4,256,2048]{2,1,0:T(8,128)(2,1)S(1)}, f32[4,8,256]{2,1,0:T(8,128)S(1)}) custom-call(f32[8,8,2048]{2,1,0:T(8,128)S(1)} %get-tuple-element.97.refs_0_.refs_8_, bf16[3,256,2048]{2,1,0:T(8,128)(2,1)S(1)} %get-tuple-element.93.refs_6_.refs_1_.refs_3_.refs_4_, f32[256,8]{1,0:T(8,128)S(1)} %get-tuple-element.95.refs_2_.refs_5_), custom_call_target="tpu_custom_call" | custom-call | flops 24000000000 | tf_op jit(solution)/shard_map/pallas_call | solution.py:54
  34.4 1.2 %collective-permute-done.11.refs_1_ = bf16[1024,128]{1,0:T(8,128)(2,1)S(1)} collective-permute-done((bf16[1024,128]{1,0:T(8,128)(2,1)S(1)}, bf16[1024,128]{1,0:T(8,128)(2,1)S(1)}, u32[]{:S(2)}, u32[]{:S(2)}) %collective-permute-start.11) | collective-permute-done | bytes 262176 | tf_op jit(solution)/shard_map/ppermute | solution.py:873
  35.6 1.0 %collective-permute-start.12 = (bf16[2048,128]{1,0:T(8,128)(2,1)S(1)}, bf16[2048,128]{1,0:T(8,128)(2,1)S(1)}, u32[]{:S(2)}, u32[]{:S(2)}) collective-permute-start(bf16[2048,128]{1,0:T(8,128)(2,1)S(1)} %shard_map.265.refs_6_.refs_1_), channel_id=1, source_target_pairs={{0,4},{1,3},{2,6},{3,1},{4,0},{5,7},{6,2},{7,5},{8,12},{9,11},{10,... | collective-permute-start | bytes 1572872 | tf_op jit(solution)/shard_map/ppermute | solution.py:873
  36.6 7.1 %shard_map.266 = (bf16[2048,128]{1,0:T(8,128)(2,1)S(1)}, bf16[2048,128]{1,0:T(8,128)(2,1)S(1)}, bf16[4,256,2048]{2,1,0:T(8,128)(2,1)S(1)}, bf16[4,256,2048]{2,1,...) custom-call(s32[3]{0:T(128)S(1)} %pad_add_fusion.core.refs_0_, ...), custom_call_target="tpu_custom_call" | custom-call | flops 91199995904 | tf_op jit(solution)/shard_map/pallas_call | solution.py:54
  43.7 1.1 %collective-permute-start.13 = (bf16[2048,128]{1,0:T(8,128)(2,1)S(1)}, bf16[2048,128]{1,0:T(8,128)(2,1)S(1)}, u32[]{:S(2)}, u32[]{:S(2)}) collective-permute-start(bf16[2048,128]{1,0:T(8,128)(2,1)S(1)} %get-tuple-element.117.refs_1_), channel_id=1, source_target_pairs={{0,4},{1,3},{2,6},{3,1},{4,0},{5,7},{6,2},{7,5},{8,12},{9,11},{10,... | collective-permute-start | bytes 1572872 | tf_op jit(solution)/shard_map/ppermute | solution.py:873
  44.8 0.0 collective-permute-done.12.refs_2_
  44.9 7.3 %shard_map.267 = (bf16[2048,128]{1,0:T(8,128)(2,1)S(1)}, bf16[2080,128]{1,0:T(8,128)(2,1)S(1)}, bf16[4,256,2048]{2,1,0:T(8,128)(2,1)S(1)}, bf16[4,256,2048]{2,1,...) custom-call(s32[3]{0:T(128)S(1)} %pad_add_fusion.core.refs_0_, ...), custom_call_target="tpu_custom_call" | custom-call | flops 91199995904 | tf_op jit(solution)/shard_map/pallas_call | solution.py:54
  52.2 0.9 collective-permute-start.14
  53.1 4.0 %shard_map.268 = (bf16[4,256,2048]{2,1,0:T(8,128)(2,1)S(1)}, f32[160,2048]{1,0:T(8,128)S(1)}) custom-call(s32[3]{0:T(128)S(1)} %pad_add_fusion.core.refs_0_, bf16[256,1024]{1,0:T(8,128)(2,1)S(1)} %get-tuple-element.101.refs_1_, bf16[4,256,2048]{2,1,0:T(8,128)(2,1)S(1)} %get-tuple-element.102.refs_2_, bf16[3,256,2048]{2,1,0:T(8,128)(2,1)S(1)} %copy-done.19, ...), custom_call_target="tpu_custom_call" | custom-call | flops 51599998976 | tf_op jit(solution)/shard_map/pallas_call | solution.py:54
  57.1 0.0 copy-start.15
  57.1 0.1 shard_map.269
  57.3 1.3 %collective-permute-start.16 = (bf16[1024,128]{1,0:T(8,128)(2,1)S(1)}, bf16[1024,128]{1,0:T(8,128)(2,1)S(1)}, u32[]{:S(2)}, u32[]{:S(2)}) collective-permute-start(bf16[1024,128]{1,0:T(8,128)(2,1)S(1)} %get-tuple-element.124.refs_1_), channel_id=1, source_target_pairs={{0,2},{1,17},{2,0},{3,19},{4,6},{5,21},{6,4},{7,23},{8,10},{9,25},... | collective-permute-start | bytes 786440 | tf_op jit(solution)/shard_map/ppermute | solution.py:873
  58.5 4.8 %shard_map.270 = (bf16[4,256,2048]{2,1,0:T(8,128)(2,1)S(1)}, bf16[160,2048]{1,0:T(8,128)(2,1)S(1)}, bf16[128,128]{1,0:T(8,128)(2,1)S(1)}) custom-call(s32[3]{0:T(128)S(1)} %pad_add_fusion.core.refs_0_, bf16[160,128]{1,0:T(8,128)(2,1)S(1)} %copy-done.15, bf16[256,1024]{1,0:T(8,128)(2,1)S(1)} %get-tuple-element.114.refs_2_, ...), custom_call_target="tpu_custom_call" | custom-call | flops 51599998976 | tf_op jit(solution)/shard_map/pallas_call | solution.py:54
  63.3 2.1 %collective-permute-start.15 = (bf16[128,128]{1,0:T(8,128)(2,1)S(1)}, bf16[128,128]{1,0:T(8,128)(2,1)S(1)}, u32[]{:S(2)}, u32[]{:S(2)}) collective-permute-start(bf16[128,128]{1,0:T(8,128)(2,1)S(1)} %get-tuple-element.123.refs_3_), channel_id=1, source_target_pairs={{0,4},{1,3},{2,6},{3,1},{4,0},{5,7},{6,2},{7,5},{8,12},{9,11},{10,... | collective-permute-start | bytes 98312 | tf_op jit(solution)/shard_map/ppermute | solution.py:873
  65.4 0.1 shard_map.271
  65.5 2.6 %collective-permute-start.19 = (bf16[512,128]{1,0:T(8,128)(2,1)S(1)}, bf16[512,128]{1,0:T(8,128)(2,1)S(1)}, u32[]{:S(2)}, u32[]{:S(2)}) collective-permute-start(bf16[512,128]{1,0:T(8,128)(2,1)S(1)} %get-tuple-element.131.refs_5_), channel_id=1, source_target_pairs={{0,16},{1,9},{2,18},{3,11},{4,20},{5,13},{6,22},{7,15},{8,24},{9,1... | collective-permute-start | bytes 393224 | tf_op jit(solution)/shard_map/ppermute | solution.py:873
  68.1 0.1 shard_map.272
  68.3 0.6 collective-permute-start.17
  68.9 3.5 %shard_map.273.refs_3_ = bf16[4,256,1024]{2,1,0:T(8,128)(2,1)S(1)} custom-call(bf16[256,1024]{1,0:T(8,128)(2,1)S(1)} %get-tuple-element.99.refs_0_, bf16[4,256,2048]{2,1,0:T(8,128)(2,1)S(1)} %get-tuple-element.100.refs_1_, bf16[4,256,2048]{2,1,0:T(8,128)(2,1)S(1)} %get-tuple-element.111.refs_2_, bf16[256,1024]{1,0:T(8,128)(2,1)S(1)} %get-tuple-element.112.refs_3_, ...), custom_call_target="tpu_custom_call" | custom-call | flops 48000000000 | tf_op jit(solution)/shard_map/pallas_call | solution.py:54
  72.4 1.0 %collective-permute-start.18 = (bf16[4,256,1024]{2,1,0:T(8,128)(2,1)S(1)}, bf16[4,256,1024]{2,1,0:T(8,128)(2,1)S(1)}, u32[]{:S(2)}, u32[]{:S(2)}) collective-permute-start(bf16[4,256,1024]{2,1,0:T(8,128)(2,1)S(1)} %shard_map.273.refs_3_), channel_id=1, source_target_pairs={{0,1},{1,0},{2,3},{3,2},{4,5},{5,4},{6,7},{7,6},{8,9},{9,8},{10,11... | collective-permute-start | bytes 6291464 | tf_op jit(solution)/shard_map/ppermute | solution.py:873
  73.3 1.8 %collective-permute-done.17.refs_2_ = bf16[1184,128]{1,0:T(8,128)(2,1)S(1)} collective-permute-done((bf16[1184,128]{1,0:T(8,128)(2,1)S(1)}, bf16[1184,128]{1,0:T(8,128)(2,1)S(1)}, u32[]{:S(2)}, u32[]{:S(2)}) %collective-permute-start.17) | collective-permute-done | bytes 303136 | tf_op jit(solution)/shard_map/ppermute | solution.py:873
  75.1 0.1 shard_map.274
  75.2 2.0 %collective-permute-start.20 = (bf16[672,128]{1,0:T(8,128)(2,1)S(1)}, bf16[672,128]{1,0:T(8,128)(2,1)S(1)}, u32[]{:S(2)}, u32[]{:S(2)}) collective-permute-start(bf16[672,128]{1,0:T(8,128)(2,1)S(1)} %get-tuple-element.132.refs_3_), channel_id=1, source_target_pairs={{0,16},{1,9},{2,18},{3,11},{4,20},{5,13},{6,22},{7,15},{8,24},{9,1... | collective-permute-start | bytes 516104 | tf_op jit(solution)/shard_map/ppermute | solution.py:873
  77.2 3.5 %shard_map.275.refs_1_ = bf16[4,256,1024]{2,1,0:T(8,128)(2,1)S(1)} custom-call(bf16[256,1024]{1,0:T(8,128)(2,1)S(1)} %get-tuple-element.99.refs_0_, bf16[4,256,2048]{2,1,0:T(8,128)(2,1)S(1)} %get-tuple-element.100.refs_1_, bf16[4,256,2048]{2,1,0:T(8,128)(2,1)S(1)} %get-tuple-element.111.refs_2_, bf16[256,1024]{1,0:T(8,128)(2,1)S(1)} %get-tuple-element.112.refs_3_, ...), custom_call_target="tpu_custom_call" | custom-call | flops 48000000000 | tf_op jit(solution)/shard_map/pallas_call | solution.py:54
  80.7 2.8 %shard_map.276 = (bf16[3,1024,256]{2,1,0:T(8,128)(2,1)}, bf16[1024,256]{1,0:T(8,128)(2,1)}, f32[8,128]{1,0:T(8,128)S(1)}) custom-call(s32[3]{0:T(128)S(1)} %pad_add_fusion.core.refs_0_, bf16[4,256,1024]{2,1,0:T(8,128)(2,1)S(1)} %shard_map.275.refs_1_, bf16[4,256,1024]{2,1,0:T(8,128)(2,1)S(1)} %collective-permute-done.18.refs_2_, ...), custom_call_target="tpu_custom_call" | custom-call | flops 1200000000 | tf_op jit(solution)/shard_map/pallas_call | solution.py:54
  83.5 0.1 collective-permute-done.20.refs_4_
  83.5 0.1 shard_map.277
  83.6 1.8 %collective-permute-start.21 = (bf16[672,128]{1,0:T(8,128)(2,1)S(1)}, bf16[672,128]{1,0:T(8,128)(2,1)S(1)}, u32[]{:S(2)}, u32[]{:S(2)}) collective-permute-start(bf16[672,128]{1,0:T(8,128)(2,1)S(1)} %get-tuple-element.135.refs_1_), channel_id=1, source_target_pairs={{0,8},{1,5},{2,10},{3,7},{4,12},{5,1},{6,14},{7,3},{8,0},{9,13},{1... | collective-permute-start | bytes 516104 | tf_op jit(solution)/shard_map/ppermute | solution.py:873
  85.4 3.7 %collective-permute-done.21.refs_2_ = bf16[672,128]{1,0:T(8,128)(2,1)S(1)} collective-permute-done((bf16[672,128]{1,0:T(8,128)(2,1)S(1)}, bf16[672,128]{1,0:T(8,128)(2,1)S(1)}, u32[]{:S(2)}, u32[]{:S(2)}) %collective-permute-start.21) | collective-permute-done | bytes 172064 | tf_op jit(solution)/shard_map/ppermute | solution.py:873
  89.1 0.0 copy-start.6
  89.1 0.0 copy-start.7
  89.1 0.0 copy-start.8
  89.1 0.0 copy-start.9
  89.2 0.0 copy-start.10
  89.2 0.0 copy-start.12
  89.2 0.0 copy-start.13
  89.2 0.1 shard_map.278
  89.3 1.4 %collective-permute-start.22 = (bf16[416,128]{1,0:T(8,128)(2,1)S(1)}, bf16[416,128]{1,0:T(8,128)(2,1)S(1)}, u32[]{:S(2)}, u32[]{:S(2)}) collective-permute-start(bf16[416,128]{1,0:T(8,128)(2,1)S(1)} %get-tuple-element.137.refs_2_), channel_id=1, source_target_pairs={{0,1},{1,0},{2,3},{3,2},{4,5},{5,4},{6,7},{7,6},{8,9},{9,8},{10,11... | collective-permute-start | bytes 319496 | tf_op jit(solution)/shard_map/ppermute | solution.py:873
  90.8 1.0 %collective-permute-done.22.refs_3_ = bf16[416,128]{1,0:T(8,128)(2,1)S(1)} collective-permute-done((bf16[416,128]{1,0:T(8,128)(2,1)S(1)}, bf16[416,128]{1,0:T(8,128)(2,1)S(1)}, u32[]{:S(2)}, u32[]{:S(2)}) %collective-permute-start.22) | collective-permute-done | bytes 106528 | tf_op jit(solution)/shard_map/ppermute | solution.py:873
  91.8 2.4 %shard_map.279 = (f32[32,16,64]{2,1,0:T(8,128)}, f32[32,16,64]{2,1,0:T(8,128)}, f32[32,16,64]{2,1,0:T(8,128)}, f32[16,32,64]{2,1,0:T(8,128)}, f32[16,32,64]{2,1,...) custom-call(s32[3]{0:T(128)S(1)} %pad_add_fusion.core.refs_0_, ...), custom_call_target="tpu_custom_call" | custom-call | flops 28800000000 | tf_op jit(solution)/shard_map/pallas_call | solution.py:54
  (49 shorter events, 0.2 us)
Async XLA Ops:
  2.3 1.5 %collective-permute-start = (bf16[2,8,32,64]{3,2,1,0:T(8,128)(2,1)S(1)}, bf16[2,8,32,64]{3,2,1,0:T(8,128)(2,1)S(1)}, u32[]{:S(2)}, u32[]{:S(2)}) collective-permute-start(bf16[2,8,32,64]{3,2,1,0:T(8,128)(2,1)S(1)} %get-tuple-element.83), channel_id=1, source_target_pairs={{0,1},{1,0},{2,3},{3,2},{4,5},{5,4},{6,7},{7,6},{8,9},{9,8},{10,11... | collective-permute-start | bytes 196616 | tf_op jit(solution)/shard_map/ppermute | solution.py:873
  3.8 9.6 %collective-permute-start.5 = (bf16[3,1024,256]{2,1,0:T(8,128)(2,1)}, bf16[3,1024,256]{2,1,0:T(8,128)(2,1)S(1)}, u32[]{:S(2)}, u32[]{:S(2)}) collective-permute-start(bf16[3,1024,256]{2,1,0:T(8,128)(2,1)} %bitcast.13), channel_id=1, source_target_pairs={{0,1},{1,0},{2,3},{3,2},{4,5},{5,4},{6,7},{7,6},{8,9},{9,8},{10,11... | collective-permute-start | bytes 4718600 | tf_op jit(solution)/shard_map/ppermute | solution.py:873
  4.1 4.3 %collective-permute-start.3 = (bf16[32,128]{1,0:T(8,128)(2,1)S(1)}, bf16[32,128]{1,0:T(8,128)(2,1)S(1)}, u32[]{:S(2)}, u32[]{:S(2)}) collective-permute-start(bf16[32,128]{1,0:T(8,128)(2,1)S(1)} %get-tuple-element.86.refs_0_), channel_id=1, source_target_pairs={{0,1},{1,0},{2,3},{3,2},{4,5},{5,4},{6,7},{7,6},{8,9},{9,8},{10,11... | collective-permute-start | bytes 24584 | tf_op jit(solution)/shard_map/ppermute | solution.py:873
  4.3 4.1 %copy-start.5 = (bf16[1024,256]{1,0:T(8,128)(2,1)S(1)}, bf16[1024,256]{1,0:T(8,128)(2,1)}, u32[]{:S(2)}) copy-start(bf16[1024,256]{1,0:T(8,128)(2,1)} %refs_1_.3) | copy-start | bytes 1572868
  4.4 8.2 %collective-permute-start.1 = (bf16[288,128]{1,0:T(8,128)(2,1)S(1)}, bf16[288,128]{1,0:T(8,128)(2,1)S(1)}, u32[]{:S(2)}, u32[]{:S(2)}) collective-permute-start(bf16[288,128]{1,0:T(8,128)(2,1)S(1)} %get-tuple-element.85.refs_0_), channel_id=1, source_target_pairs={{0,16},{1,17},{2,18},{3,19},{4,20},{5,21},{6,22},{7,23},{8,24},{9,... | collective-permute-start | bytes 221192 | tf_op jit(solution)/shard_map/ppermute | solution.py:873
  8.4 5.0 %collective-permute-start.4 = (bf16[1024,256]{1,0:T(8,128)(2,1)S(1)}, bf16[1024,256]{1,0:T(8,128)(2,1)S(1)}, u32[]{:S(2)}, u32[]{:S(2)}) collective-permute-start(bf16[1024,256]{1,0:T(8,128)(2,1)S(1)} %copy-done.5), channel_id=1, source_target_pairs={{0,1},{1,0},{2,3},{3,2},{4,5},{5,4},{6,7},{7,6},{8,9},{9,8},{10,11... | collective-permute-start | bytes 1572872 | tf_op jit(solution)/shard_map/ppermute | solution.py:873
  8.4 5.0 %copy-start.4 = (bf16[1024,3,256]{2,0,1:T(8,128)(2,1)S(1)}, bf16[1024,3,256]{2,0,1:T(8,128)(2,1)}, u32[]{:S(2)}) copy-start(bf16[1024,3,256]{2,0,1:T(8,128)(2,1)} %param.20) | copy-start | bytes 4718596
  8.4 11.0 %collective-permute-start.9 = (bf16[256,128]{1,0:T(8,128)(2,1)S(1)}, bf16[256,128]{1,0:T(8,128)(2,1)S(1)}, u32[]{:S(2)}, u32[]{:S(2)}) collective-permute-start(bf16[256,128]{1,0:T(8,128)(2,1)S(1)} %get-tuple-element.96.refs_0_), channel_id=1, source_target_pairs={{0,2},{1,5},{2,0},{3,7},{4,6},{5,1},{6,4},{7,3},{8,10},{9,13},{10,... | collective-permute-start | bytes 196616 | tf_op jit(solution)/shard_map/ppermute | solution.py:873
  12.6 5.2 %collective-permute-start.2 = (bf16[576,128]{1,0:T(8,128)(2,1)S(1)}, bf16[576,128]{1,0:T(8,128)(2,1)S(1)}, u32[]{:S(2)}, u32[]{:S(2)}) collective-permute-start(bf16[576,128]{1,0:T(8,128)(2,1)S(1)} %shard_map.256.refs_5_.refs_0_), channel_id=1, source_target_pairs={{0,8},{1,9},{2,10},{3,11},{4,12},{5,13},{6,14},{7,15},{8,0},{9,1},... | collective-permute-start | bytes 442376 | tf_op jit(solution)/shard_map/ppermute | solution.py:873
  15.2 2.6 %copy-start.16 = (bf16[256,256]{1,0:T(8,128)(2,1)}, bf16[256,256]{1,0:T(8,128)(2,1)S(1)}, u32[]{:S(2)}) copy-start(bf16[256,256]{1,0:T(8,128)(2,1)S(1)} %get-tuple-element.89.refs_3_.refs_10_.refs_9_) | copy-start | bytes 393220
  15.3 17.5 %copy-start.18 = (bf16[3,256,2048]{2,1,0:T(8,128)(2,1)}, bf16[3,256,2048]{2,1,0:T(8,128)(2,1)S(1)}, u32[]{:S(2)}) copy-start(bf16[3,256,2048]{2,1,0:T(8,128)(2,1)S(1)} %get-tuple-element.93.refs_6_.refs_1_.refs_3_.refs_4_) | copy-start | bytes 9437188
  17.8 7.0 %collective-permute-start.6 = (bf16[1216,128]{1,0:T(8,128)(2,1)S(1)}, bf16[1216,128]{1,0:T(8,128)(2,1)S(1)}, u32[]{:S(2)}, u32[]{:S(2)}) collective-permute-start(bf16[1216,128]{1,0:T(8,128)(2,1)S(1)} %shard_map.259.refs_0_.refs_2_), channel_id=1, source_target_pairs={{0,2},{1,5},{2,0},{3,7},{4,6},{5,1},{6,4},{7,3},{8,10},{9,13},{10,... | collective-permute-start | bytes 933896 | tf_op jit(solution)/shard_map/ppermute | solution.py:873
  19.5 8.7 %collective-permute-start.10 = (bf16[512,128]{1,0:T(8,128)(2,1)S(1)}, bf16[512,128]{1,0:T(8,128)(2,1)S(1)}, u32[]{:S(2)}, u32[]{:S(2)}) collective-permute-start(bf16[512,128]{1,0:T(8,128)(2,1)S(1)} %shard_map.262.refs_0_), channel_id=1, source_target_pairs={{0,16},{1,17},{2,18},{3,19},{4,20},{5,21},{6,22},{7,23},{8,24},{9,... | collective-permute-start | bytes 393224 | tf_op jit(solution)/shard_map/ppermute | solution.py:873
  24.8 4.1 %collective-permute-start.8 = (bf16[320,128]{1,0:T(8,128)(2,1)S(1)}, bf16[320,128]{1,0:T(8,128)(2,1)S(1)}, u32[]{:S(2)}, u32[]{:S(2)}) collective-permute-start(bf16[320,128]{1,0:T(8,128)(2,1)S(1)} %get-tuple-element.92.refs_2_), channel_id=1, source_target_pairs={{0,1},{1,0},{2,3},{3,2},{4,5},{5,4},{6,7},{7,6},{8,9},{9,8},{10,11... | collective-permute-start | bytes 245768 | tf_op jit(solution)/shard_map/ppermute | solution.py:873
  24.9 4.1 %copy-start.14 = (bf16[160,128]{1,0:T(8,128)(2,1)S(1)}, bf16[160,128]{1,0:T(8,128)(2,1)}, u32[]{:S(2)}) copy-start(bf16[160,128]{1,0:T(8,128)(2,1)} %constant.24.clone.refs_1_) | copy-start | bytes 122884
  24.9 11.7 %collective-permute-start.7 = (bf16[2048,128]{1,0:T(8,128)(2,1)S(1)}, bf16[2048,128]{1,0:T(8,128)(2,1)S(1)}, u32[]{:S(2)}, u32[]{:S(2)}) collective-permute-start(bf16[2048,128]{1,0:T(8,128)(2,1)S(1)} %get-tuple-element.90.refs_2_.refs_1_), channel_id=1, source_target_pairs={{0,4},{1,3},{2,6},{3,1},{4,0},{5,7},{6,2},{7,5},{8,12},{9,11},{10,... | collective-permute-start | bytes 1572872 | tf_op jit(solution)/shard_map/ppermute | solution.py:873
  28.2 7.4 %collective-permute-start.11 = (bf16[1024,128]{1,0:T(8,128)(2,1)S(1)}, bf16[1024,128]{1,0:T(8,128)(2,1)S(1)}, u32[]{:S(2)}, u32[]{:S(2)}) collective-permute-start(bf16[1024,128]{1,0:T(8,128)(2,1)S(1)} %shard_map.263.refs_0_), channel_id=1, source_target_pairs={{0,8},{1,9},{2,10},{3,11},{4,12},{5,13},{6,14},{7,15},{8,0},{9,1},... | collective-permute-start | bytes 786440 | tf_op jit(solution)/shard_map/ppermute | solution.py:873
  35.6 9.2 %collective-permute-start.12 = (bf16[2048,128]{1,0:T(8,128)(2,1)S(1)}, bf16[2048,128]{1,0:T(8,128)(2,1)S(1)}, u32[]{:S(2)}, u32[]{:S(2)}) collective-permute-start(bf16[2048,128]{1,0:T(8,128)(2,1)S(1)} %shard_map.265.refs_6_.refs_1_), channel_id=1, source_target_pairs={{0,4},{1,3},{2,6},{3,1},{4,0},{5,7},{6,2},{7,5},{8,12},{9,11},{10,... | collective-permute-start | bytes 1572872 | tf_op jit(solution)/shard_map/ppermute | solution.py:873
  36.6 8.3 %copy-start.17 = (bf16[256,256]{1,0:T(8,128)(2,1)S(1)}, bf16[256,256]{1,0:T(8,128)(2,1)}, u32[]{:S(2)}) copy-start(bf16[256,256]{1,0:T(8,128)(2,1)} %copy-done.16) | copy-start | bytes 393220
  43.7 13.4 %collective-permute-start.13 = (bf16[2048,128]{1,0:T(8,128)(2,1)S(1)}, bf16[2048,128]{1,0:T(8,128)(2,1)S(1)}, u32[]{:S(2)}, u32[]{:S(2)}) collective-permute-start(bf16[2048,128]{1,0:T(8,128)(2,1)S(1)} %get-tuple-element.117.refs_1_), channel_id=1, source_target_pairs={{0,4},{1,3},{2,6},{3,1},{4,0},{5,7},{6,2},{7,5},{8,12},{9,11},{10,... | collective-permute-start | bytes 1572872 | tf_op jit(solution)/shard_map/ppermute | solution.py:873
  44.9 8.2 %copy-start.19 = (bf16[3,256,2048]{2,1,0:T(8,128)(2,1)S(1)}, bf16[3,256,2048]{2,1,0:T(8,128)(2,1)}, u32[]{:S(2)}) copy-start(bf16[3,256,2048]{2,1,0:T(8,128)(2,1)} %copy-done.18) | copy-start | bytes 9437188
  52.2 16.0 %collective-permute-start.14 = (bf16[2080,128]{1,0:T(8,128)(2,1)S(1)}, bf16[2080,128]{1,0:T(8,128)(2,1)S(1)}, u32[]{:S(2)}, u32[]{:S(2)}) collective-permute-start(bf16[2080,128]{1,0:T(8,128)(2,1)S(1)} %get-tuple-element.122.refs_1_), channel_id=1, source_target_pairs={{0,4},{1,3},{2,6},{3,1},{4,0},{5,7},{6,2},{7,5},{8,12},{9,11},{10,... | collective-permute-start | bytes 1597448 | tf_op jit(solution)/shard_map/ppermute | solution.py:873
  57.1 1.4 %copy-start.15 = (bf16[160,128]{1,0:T(8,128)(2,1)S(1)}, bf16[160,128]{1,0:T(8,128)(2,1)}, u32[]{:S(2)}) copy-start(bf16[160,128]{1,0:T(8,128)(2,1)} %constant.24.clone.refs_1_) | copy-start | bytes 122884
  57.3 8.2 %collective-permute-start.16 = (bf16[1024,128]{1,0:T(8,128)(2,1)S(1)}, bf16[1024,128]{1,0:T(8,128)(2,1)S(1)}, u32[]{:S(2)}, u32[]{:S(2)}) collective-permute-start(bf16[1024,128]{1,0:T(8,128)(2,1)S(1)} %get-tuple-element.124.refs_1_), channel_id=1, source_target_pairs={{0,2},{1,17},{2,0},{3,19},{4,6},{5,21},{6,4},{7,23},{8,10},{9,25},... | collective-permute-start | bytes 786440 | tf_op jit(solution)/shard_map/ppermute | solution.py:873
  63.3 4.8 %collective-permute-start.15 = (bf16[128,128]{1,0:T(8,128)(2,1)S(1)}, bf16[128,128]{1,0:T(8,128)(2,1)S(1)}, u32[]{:S(2)}, u32[]{:S(2)}) collective-permute-start(bf16[128,128]{1,0:T(8,128)(2,1)S(1)} %get-tuple-element.123.refs_3_), channel_id=1, source_target_pairs={{0,4},{1,3},{2,6},{3,1},{4,0},{5,7},{6,2},{7,5},{8,12},{9,11},{10,... | collective-permute-start | bytes 98312 | tf_op jit(solution)/shard_map/ppermute | solution.py:873
  65.5 18.0 %collective-permute-start.19 = (bf16[512,128]{1,0:T(8,128)(2,1)S(1)}, bf16[512,128]{1,0:T(8,128)(2,1)S(1)}, u32[]{:S(2)}, u32[]{:S(2)}) collective-permute-start(bf16[512,128]{1,0:T(8,128)(2,1)S(1)} %get-tuple-element.131.refs_5_), channel_id=1, source_target_pairs={{0,16},{1,9},{2,18},{3,11},{4,20},{5,13},{6,22},{7,15},{8,24},{9,1... | collective-permute-start | bytes 393224 | tf_op jit(solution)/shard_map/ppermute | solution.py:873
  68.3 6.9 %collective-permute-start.17 = (bf16[1184,128]{1,0:T(8,128)(2,1)S(1)}, bf16[1184,128]{1,0:T(8,128)(2,1)S(1)}, u32[]{:S(2)}, u32[]{:S(2)}) collective-permute-start(bf16[1184,128]{1,0:T(8,128)(2,1)S(1)} %get-tuple-element.127.refs_1_), channel_id=1, source_target_pairs={{0,2},{1,17},{2,0},{3,19},{4,6},{5,21},{6,4},{7,23},{8,10},{9,25},... | collective-permute-start | bytes 909320 | tf_op jit(solution)/shard_map/ppermute | solution.py:873
  72.4 8.3 %collective-permute-start.18 = (bf16[4,256,1024]{2,1,0:T(8,128)(2,1)S(1)}, bf16[4,256,1024]{2,1,0:T(8,128)(2,1)S(1)}, u32[]{:S(2)}, u32[]{:S(2)}) collective-permute-start(bf16[4,256,1024]{2,1,0:T(8,128)(2,1)S(1)} %shard_map.273.refs_3_), channel_id=1, source_target_pairs={{0,1},{1,0},{2,3},{3,2},{4,5},{5,4},{6,7},{7,6},{8,9},{9,8},{10,11... | collective-permute-start | bytes 6291464 | tf_op jit(solution)/shard_map/ppermute | solution.py:873
  75.2 8.3 %collective-permute-start.20 = (bf16[672,128]{1,0:T(8,128)(2,1)S(1)}, bf16[672,128]{1,0:T(8,128)(2,1)S(1)}, u32[]{:S(2)}, u32[]{:S(2)}) collective-permute-start(bf16[672,128]{1,0:T(8,128)(2,1)S(1)} %get-tuple-element.132.refs_3_), channel_id=1, source_target_pairs={{0,16},{1,9},{2,18},{3,11},{4,20},{5,13},{6,22},{7,15},{8,24},{9,1... | collective-permute-start | bytes 516104 | tf_op jit(solution)/shard_map/ppermute | solution.py:873
  83.6 5.5 %collective-permute-start.21 = (bf16[672,128]{1,0:T(8,128)(2,1)S(1)}, bf16[672,128]{1,0:T(8,128)(2,1)S(1)}, u32[]{:S(2)}, u32[]{:S(2)}) collective-permute-start(bf16[672,128]{1,0:T(8,128)(2,1)S(1)} %get-tuple-element.135.refs_1_), channel_id=1, source_target_pairs={{0,8},{1,5},{2,10},{3,7},{4,12},{5,1},{6,14},{7,3},{8,0},{9,13},{1... | collective-permute-start | bytes 516104 | tf_op jit(solution)/shard_map/ppermute | solution.py:873
  89.1 2.6 %copy-start = (f32[32,16,64]{2,1,0:T(8,128)S(1)}, f32[32,16,64]{2,1,0:T(8,128)}, u32[]{:S(2)}) copy-start(f32[32,16,64]{2,1,0:T(8,128)} %refs_4_.1) | copy-start | bytes 393220
  89.1 2.6 %copy-start.1 = (f32[16,64,32]{1,2,0:T(8,128)S(1)}, f32[16,64,32]{1,2,0:T(8,128)}, u32[]{:S(2)}) copy-start(f32[16,64,32]{1,2,0:T(8,128)} %param.17) | copy-start | bytes 393220
  89.1 2.6 %copy-start.2 = (f32[2,16,64]{2,1,0:T(8,128)S(1)}, f32[2,16,64]{2,1,0:T(8,128)}, u32[]{:S(2)}) copy-start(f32[2,16,64]{2,1,0:T(8,128)} %refs_10_.1) | copy-start | bytes 24580
  89.1 2.6 %copy-start.3 = (f32[32,60]{1,0:T(8,128)S(1)}, f32[32,60]{1,0:T(8,128)}, u32[]{:S(2)}) copy-start(f32[32,60]{1,0:T(8,128)} %refs_13_.1) | copy-start | bytes 23044
  89.1 2.6 %copy-start.6 = (f32[32,16,64]{2,1,0:T(8,128)S(1)}, f32[32,16,64]{2,1,0:T(8,128)}, u32[]{:S(2)}) copy-start(f32[32,16,64]{2,1,0:T(8,128)} %refs_5_.1) | copy-start | bytes 393220
  89.1 2.6 %copy-start.7 = (f32[32,16,64]{2,1,0:T(8,128)S(1)}, f32[32,16,64]{2,1,0:T(8,128)}, u32[]{:S(2)}) copy-start(f32[32,16,64]{2,1,0:T(8,128)} %refs_6_.1) | copy-start | bytes 393220
  89.1 2.6 %copy-start.8 = (f32[16,64,32]{1,2,0:T(8,128)S(1)}, f32[16,64,32]{1,2,0:T(8,128)}, u32[]{:S(2)}) copy-start(f32[16,64,32]{1,2,0:T(8,128)} %param.23) | copy-start | bytes 393220
  89.1 2.6 %copy-start.9 = (f32[16,64,32]{1,2,0:T(8,128)S(1)}, f32[16,64,32]{1,2,0:T(8,128)}, u32[]{:S(2)}) copy-start(f32[16,64,32]{1,2,0:T(8,128)} %param.24) | copy-start | bytes 393220
  89.2 2.6 %copy-start.10 = (f32[2,16,64]{2,1,0:T(8,128)S(1)}, f32[2,16,64]{2,1,0:T(8,128)}, u32[]{:S(2)}) copy-start(f32[2,16,64]{2,1,0:T(8,128)} %refs_11_.1) | copy-start | bytes 24580
  89.2 2.6 %copy-start.11 = (f32[2,16,64]{2,1,0:T(8,128)S(1)}, f32[2,16,64]{2,1,0:T(8,128)}, u32[]{:S(2)}) copy-start(f32[2,16,64]{2,1,0:T(8,128)} %refs_12_.1) | copy-start | bytes 24580
  89.2 2.6 %copy-start.12 = (f32[32,60]{1,0:T(8,128)S(1)}, f32[32,60]{1,0:T(8,128)}, u32[]{:S(2)}) copy-start(f32[32,60]{1,0:T(8,128)} %refs_14_.1) | copy-start | bytes 23044
  89.2 2.6 %copy-start.13 = (f32[32,60]{1,0:T(8,128)S(1)}, f32[32,60]{1,0:T(8,128)}, u32[]{:S(2)}) copy-start(f32[32,60]{1,0:T(8,128)} %refs_15_.1) | copy-start | bytes 23044
  89.3 2.4 %collective-permute-start.22 = (bf16[416,128]{1,0:T(8,128)(2,1)S(1)}, bf16[416,128]{1,0:T(8,128)(2,1)S(1)}, u32[]{:S(2)}, u32[]{:S(2)}) collective-permute-start(bf16[416,128]{1,0:T(8,128)(2,1)S(1)} %get-tuple-element.137.refs_2_), channel_id=1, source_target_pairs={{0,1},{1,0},{2,3},{3,2},{4,5},{5,4},{6,7},{7,6},{8,9},{9,8},{10,11... | collective-permute-start | bytes 319496 | tf_op jit(solution)/shard_map/ppermute | solution.py:873

commit v6 on v5

--- a/solution.py
+++ b/solution.py
@@ -574,12 +574,12 @@
             block = slice(d * depth, (d + 1) * depth)
             sums = [None] * TASKS
             for e in range(2 * chunk):
-                y = (y_a if e < chunk else y_b)[e % chunk, block, part].astype(F32)
+                y = (y_a if e < chunk else y_b)[e % chunk, block, part]
                 for t in range(TASKS):
-                    m = gates[e, t : t + 1, part] * y
+                    m = gates[e, t : t + 1, part].astype(BF) * y
                     sums[t] = m if e == 0 else sums[t] + m
             for t in range(TASKS):
-                out[t, block, here] = sums[t].astype(BF)
+                out[t, block, here] = sums[t]
 
 
 def mix(start, rows, first, second, selp, gls, gates, after):

time: 94.5 us -> 94.8 us (level)
  transfers between devices with their start and end apart: 23 -> 23, of which waited for: 10 -> 9; matrix products, arithmetic and copies ran while one was open for 0% -> 0% of each run, Pallas kernels for 43% -> 44%
where the time goes in v6:
time: 94.8 us; the launch traced here: 94.6 us
  Pallas kernels  45.4 us (48%)
  starting transfers between devices  30.4 us (32%)
  waiting for transfers between devices  17.4 us (18%)
  between operations  1.09 us (1%)
    pallas_call x25, Pallas kernels, kernel_call(): pl.pallas_call(kernel, out_shape=tuple((jax.ShapeDtypeStruct(shape, kind)...  43.9 us
    ppermute x23, starting transfers between devices, swap(): return lax.ppermute(x, ('rows', 'hid'), pairs)  30.4 us
    ppermute x23, waiting for transfers between devices, swap(): return lax.ppermute(x, ('rows', 'hid'), pairs)  17.4 us
  transfers between devices with their start and end apart: 23, of which 9 were waited for; matrix products, arithmetic and copies ran while one was open for 0% of the time, Pallas kernels for 44%

profile of v6, /device:TPU:0, one launch (start us, length us, event | category | flops | bytes accessed | tf_op | source)
XLA Modules:
  0.0 94.6 jit_solution(4126450070453796150)
XLA Ops:
  0.7 0.1 pad_add_fusion.core.refs_0_
  0.7 1.5 %shard_map.254 = (bf16[32,128]{1,0:T(8,128)(2,1)S(1)}, bf16[32,128]{1,0:T(8,128)(2,1)S(1)}, bf16[2,8,32,64]{3,2,1,0:T(8,128)(2,1)S(1)}, bf16[2,8,32,64]{3,2,1,0:T(8,128)(2,1)S(1)}) custom-call(s32[3]{0:T(128)S(1)} %pad_add_fusion.core.refs_0_, f32[32,16,64]{2,1,0:T(8,128)} %refs_4_.1, f32[16,32,64]{2,1,0:T(8,128)} %bitcast.11, f32[2,16,64]{2,1,0:T(8,128)} %refs_10_.1, ...), custom_call_target="tpu_custom_call" | custom-call | tf_op jit(solution)/shard_map/pallas_call | solution.py:697
  2.3 0.5 collective-permute-start
  2.8 1.0 %collective-permute-done.refs_1_ = bf16[2,8,32,64]{3,2,1,0:T(8,128)(2,1)S(1)} collective-permute-done((bf16[2,8,32,64]{3,2,1,0:T(8,128)(2,1)S(1)}, bf16[2,8,32,64]{3,2,1,0:T(8,128)(2,1)S(1)}, u32[]{:S(2)}, u32[]{:S(2)}) %collective-permute-start) | collective-permute-done | bytes 65568 | tf_op jit(solution)/shard_map/ppermute | solution.py:873
  3.8 0.4 collective-permute-start.5
  4.1 0.1 collective-permute-start.3
  4.3 0.1 shard_map.255
  4.4 4.0 %collective-permute-start.1 = (bf16[288,128]{1,0:T(8,128)(2,1)S(1)}, bf16[288,128]{1,0:T(8,128)(2,1)S(1)}, u32[]{:S(2)}, u32[]{:S(2)}) collective-permute-start(bf16[288,128]{1,0:T(8,128)(2,1)S(1)} %get-tuple-element.85.refs_0_), channel_id=1, source_target_pairs={{0,16},{1,17},{2,18},{3,19},{4,20},{5,21},{6,22},{7,23},{8,24},{9,... | collective-permute-start | bytes 221192 | tf_op jit(solution)/shard_map/ppermute | solution.py:873
  8.4 0.0 copy-start.4
  8.4 1.6 %collective-permute-start.9 = (bf16[256,128]{1,0:T(8,128)(2,1)S(1)}, bf16[256,128]{1,0:T(8,128)(2,1)S(1)}, u32[]{:S(2)}, u32[]{:S(2)}) collective-permute-start(bf16[256,128]{1,0:T(8,128)(2,1)S(1)} %get-tuple-element.96.refs_0_), channel_id=1, source_target_pairs={{0,2},{1,5},{2,0},{3,7},{4,6},{5,1},{6,4},{7,3},{8,10},{9,13},{10,... | collective-permute-start | bytes 196616 | tf_op jit(solution)/shard_map/ppermute | solution.py:873
  10.0 2.6 %collective-permute-done.1.refs_1_ = bf16[288,128]{1,0:T(8,128)(2,1)S(1)} collective-permute-done((bf16[288,128]{1,0:T(8,128)(2,1)S(1)}, bf16[288,128]{1,0:T(8,128)(2,1)S(1)}, u32[]{:S(2)}, u32[]{:S(2)}) %collective-permute-start.1) | collective-permute-done | bytes 73760 | tf_op jit(solution)/shard_map/ppermute | solution.py:873
  12.6 0.8 collective-permute-start.2
  13.4 1.9 %shard_map.258 = (bf16[272,2048]{1,0:T(8,128)(2,1)S(1)}, bf16[3,256,2048]{2,1,0:T(8,128)(2,1)S(1)}, bf16[256,256]{1,0:T(8,128)(2,1)S(1)}, bf16[256,256]{1,0:T(8,128)(2,1)S(1)}) custom-call(s32[3]{0:T(128)S(1)} %pad_add_fusion.core.refs_0_, bf16[1024,256]{1,0:T(8,128)(2,1)S(1)} %copy-done.5, bf16[1024,256]{1,0:T(8,128)(2,1)S(1)} %collective-permute-done.4.refs_2_, ...), custom_call_target="tpu_custom_call" | custom-call | flops 41999998976 | tf_op jit(solution)/shard_map/pallas_call | solution.py:54
  15.2 0.0 copy-start.16
  15.3 2.5 %collective-permute-done.2.refs_1_ = bf16[576,128]{1,0:T(8,128)(2,1)S(1)} collective-permute-done((bf16[576,128]{1,0:T(8,128)(2,1)S(1)}, bf16[576,128]{1,0:T(8,128)(2,1)S(1)}, u32[]{:S(2)}, u32[]{:S(2)}) %collective-permute-start.2) | collective-permute-done | bytes 147488 | tf_op jit(solution)/shard_map/ppermute | solution.py:873
  17.8 1.6 %collective-permute-start.6 = (bf16[1216,128]{1,0:T(8,128)(2,1)S(1)}, bf16[1216,128]{1,0:T(8,128)(2,1)S(1)}, u32[]{:S(2)}, u32[]{:S(2)}) collective-permute-start(bf16[1216,128]{1,0:T(8,128)(2,1)S(1)} %shard_map.259.refs_0_.refs_2_), channel_id=1, source_target_pairs={{0,2},{1,5},{2,0},{3,7},{4,6},{5,1},{6,4},{7,3},{8,10},{9,13},{10,... | collective-permute-start | bytes 933896 | tf_op jit(solution)/shard_map/ppermute | solution.py:873
  19.5 3.0 %collective-permute-start.10 = (bf16[512,128]{1,0:T(8,128)(2,1)S(1)}, bf16[512,128]{1,0:T(8,128)(2,1)S(1)}, u32[]{:S(2)}, u32[]{:S(2)}) collective-permute-start(bf16[512,128]{1,0:T(8,128)(2,1)S(1)} %shard_map.262.refs_0_), channel_id=1, source_target_pairs={{0,16},{1,17},{2,18},{3,19},{4,20},{5,21},{6,22},{7,23},{8,24},{9,... | collective-permute-start | bytes 393224 | tf_op jit(solution)/shard_map/ppermute | solution.py:873
  22.5 2.3 %collective-permute-done.6.refs_1_ = bf16[1216,128]{1,0:T(8,128)(2,1)S(1)} collective-permute-done((bf16[1216,128]{1,0:T(8,128)(2,1)S(1)}, bf16[1216,128]{1,0:T(8,128)(2,1)S(1)}, u32[]{:S(2)}, u32[]{:S(2)}) %collective-permute-start.6) | collective-permute-done | bytes 311328 | tf_op jit(solution)/shard_map/ppermute | solution.py:873
  24.8 0.1 collective-permute-start.8
  24.9 0.0 copy-start.14
  24.9 1.7 %collective-permute-start.7 = (bf16[2048,128]{1,0:T(8,128)(2,1)S(1)}, bf16[2048,128]{1,0:T(8,128)(2,1)S(1)}, u32[]{:S(2)}, u32[]{:S(2)}) collective-permute-start(bf16[2048,128]{1,0:T(8,128)(2,1)S(1)} %get-tuple-element.90.refs_2_.refs_1_), channel_id=1, source_target_pairs={{0,4},{1,3},{2,6},{3,1},{4,0},{5,7},{6,2},{7,5},{8,12},{9,11},{10,... | collective-permute-start | bytes 1572872 | tf_op jit(solution)/shard_map/ppermute | solution.py:873
  26.6 1.6 %collective-permute-done.10.refs_1_ = bf16[512,128]{1,0:T(8,128)(2,1)S(1)} collective-permute-done((bf16[512,128]{1,0:T(8,128)(2,1)S(1)}, bf16[512,128]{1,0:T(8,128)(2,1)S(1)}, u32[]{:S(2)}, u32[]{:S(2)}) %collective-permute-start.10) | collective-permute-done | bytes 131104 | tf_op jit(solution)/shard_map/ppermute | solution.py:873
  28.2 0.7 collective-permute-start.11
  29.0 3.8 %shard_map.261 = (bf16[4,256,2048]{2,1,0:T(8,128)(2,1)S(1)}, f32[8,8,2048]{2,1,0:T(8,128)S(1)}, f32[160,2048]{1,0:T(8,128)S(1)}, bf16[160,256]{1,0:T(8,128)(2,1)...) custom-call(s32[3]{0:T(128)S(1)} %pad_add_fusion.core.refs_0_, ...), custom_call_target="tpu_custom_call" | custom-call | flops 60000002048 | tf_op jit(solution)/shard_map/pallas_call | solution.py:54
  32.8 1.6 %shard_map.264 = (bf16[4,256,2048]{2,1,0:T(8,128)(2,1)S(1)}, f32[4,8,256]{2,1,0:T(8,128)S(1)}) custom-call(f32[8,8,2048]{2,1,0:T(8,128)S(1)} %get-tuple-element.97.refs_0_.refs_8_, bf16[3,256,2048]{2,1,0:T(8,128)(2,1)S(1)} %get-tuple-element.93.refs_6_.refs_1_.refs_3_.refs_4_, f32[256,8]{1,0:T(8,128)S(1)} %get-tuple-element.95.refs_2_.refs_5_), custom_call_target="tpu_custom_call" | custom-call | flops 24000000000 | tf_op jit(solution)/shard_map/pallas_call | solution.py:54
  34.4 1.2 %collective-permute-done.11.refs_1_ = bf16[1024,128]{1,0:T(8,128)(2,1)S(1)} collective-permute-done((bf16[1024,128]{1,0:T(8,128)(2,1)S(1)}, bf16[1024,128]{1,0:T(8,128)(2,1)S(1)}, u32[]{:S(2)}, u32[]{:S(2)}) %collective-permute-start.11) | collective-permute-done | bytes 262176 | tf_op jit(solution)/shard_map/ppermute | solution.py:873
  35.6 1.0 %collective-permute-start.12 = (bf16[2048,128]{1,0:T(8,128)(2,1)S(1)}, bf16[2048,128]{1,0:T(8,128)(2,1)S(1)}, u32[]{:S(2)}, u32[]{:S(2)}) collective-permute-start(bf16[2048,128]{1,0:T(8,128)(2,1)S(1)} %shard_map.265.refs_6_.refs_1_), channel_id=1, source_target_pairs={{0,4},{1,3},{2,6},{3,1},{4,0},{5,7},{6,2},{7,5},{8,12},{9,11},{10,... | collective-permute-start | bytes 1572872 | tf_op jit(solution)/shard_map/ppermute | solution.py:873
  36.6 7.1 %shard_map.266 = (bf16[2048,128]{1,0:T(8,128)(2,1)S(1)}, bf16[2048,128]{1,0:T(8,128)(2,1)S(1)}, bf16[4,256,2048]{2,1,0:T(8,128)(2,1)S(1)}, bf16[4,256,2048]{2,1,...) custom-call(s32[3]{0:T(128)S(1)} %pad_add_fusion.core.refs_0_, ...), custom_call_target="tpu_custom_call" | custom-call | flops 91199995904 | tf_op jit(solution)/shard_map/pallas_call | solution.py:54
  43.7 1.1 %collective-permute-start.13 = (bf16[2048,128]{1,0:T(8,128)(2,1)S(1)}, bf16[2048,128]{1,0:T(8,128)(2,1)S(1)}, u32[]{:S(2)}, u32[]{:S(2)}) collective-permute-start(bf16[2048,128]{1,0:T(8,128)(2,1)S(1)} %get-tuple-element.117.refs_1_), channel_id=1, source_target_pairs={{0,4},{1,3},{2,6},{3,1},{4,0},{5,7},{6,2},{7,5},{8,12},{9,11},{10,... | collective-permute-start | bytes 1572872 | tf_op jit(solution)/shard_map/ppermute | solution.py:873
  44.8 0.0 collective-permute-done.12.refs_2_
  44.9 7.3 %shard_map.267 = (bf16[2048,128]{1,0:T(8,128)(2,1)S(1)}, bf16[2080,128]{1,0:T(8,128)(2,1)S(1)}, bf16[4,256,2048]{2,1,0:T(8,128)(2,1)S(1)}, bf16[4,256,2048]{2,1,...) custom-call(s32[3]{0:T(128)S(1)} %pad_add_fusion.core.refs_0_, ...), custom_call_target="tpu_custom_call" | custom-call | flops 91199995904 | tf_op jit(solution)/shard_map/pallas_call | solution.py:54
  52.2 0.9 collective-permute-start.14
  53.1 4.0 %shard_map.268 = (bf16[4,256,2048]{2,1,0:T(8,128)(2,1)S(1)}, f32[160,2048]{1,0:T(8,128)S(1)}) custom-call(s32[3]{0:T(128)S(1)} %pad_add_fusion.core.refs_0_, bf16[256,1024]{1,0:T(8,128)(2,1)S(1)} %get-tuple-element.101.refs_1_, bf16[4,256,2048]{2,1,0:T(8,128)(2,1)S(1)} %get-tuple-element.102.refs_2_, bf16[3,256,2048]{2,1,0:T(8,128)(2,1)S(1)} %copy-done.19, ...), custom_call_target="tpu_custom_call" | custom-call | flops 51599998976 | tf_op jit(solution)/shard_map/pallas_call | solution.py:54
  57.1 0.0 copy-start.15
  57.1 0.1 shard_map.269
  57.3 1.3 %collective-permute-start.16 = (bf16[1024,128]{1,0:T(8,128)(2,1)S(1)}, bf16[1024,128]{1,0:T(8,128)(2,1)S(1)}, u32[]{:S(2)}, u32[]{:S(2)}) collective-permute-start(bf16[1024,128]{1,0:T(8,128)(2,1)S(1)} %get-tuple-element.124.refs_1_), channel_id=1, source_target_pairs={{0,2},{1,17},{2,0},{3,19},{4,6},{5,21},{6,4},{7,23},{8,10},{9,25},... | collective-permute-start | bytes 786440 | tf_op jit(solution)/shard_map/ppermute | solution.py:873
  58.5 4.8 %shard_map.270 = (bf16[4,256,2048]{2,1,0:T(8,128)(2,1)S(1)}, bf16[160,2048]{1,0:T(8,128)(2,1)S(1)}, bf16[128,128]{1,0:T(8,128)(2,1)S(1)}) custom-call(s32[3]{0:T(128)S(1)} %pad_add_fusion.core.refs_0_, bf16[160,128]{1,0:T(8,128)(2,1)S(1)} %copy-done.15, bf16[256,1024]{1,0:T(8,128)(2,1)S(1)} %get-tuple-element.114.refs_2_, ...), custom_call_target="tpu_custom_call" | custom-call | flops 51599998976 | tf_op jit(solution)/shard_map/pallas_call | solution.py:54
  63.3 2.1 %collective-permute-start.15 = (bf16[128,128]{1,0:T(8,128)(2,1)S(1)}, bf16[128,128]{1,0:T(8,128)(2,1)S(1)}, u32[]{:S(2)}, u32[]{:S(2)}) collective-permute-start(bf16[128,128]{1,0:T(8,128)(2,1)S(1)} %get-tuple-element.123.refs_3_), channel_id=1, source_target_pairs={{0,4},{1,3},{2,6},{3,1},{4,0},{5,7},{6,2},{7,5},{8,12},{9,11},{10,... | collective-permute-start | bytes 98312 | tf_op jit(solution)/shard_map/ppermute | solution.py:873
  65.4 0.1 shard_map.271
  65.5 2.6 %collective-permute-start.19 = (bf16[512,128]{1,0:T(8,128)(2,1)S(1)}, bf16[512,128]{1,0:T(8,128)(2,1)S(1)}, u32[]{:S(2)}, u32[]{:S(2)}) collective-permute-start(bf16[512,128]{1,0:T(8,128)(2,1)S(1)} %get-tuple-element.131.refs_5_), channel_id=1, source_target_pairs={{0,16},{1,9},{2,18},{3,11},{4,20},{5,13},{6,22},{7,15},{8,24},{9,1... | collective-permute-start | bytes 393224 | tf_op jit(solution)/shard_map/ppermute | solution.py:873
  68.1 0.1 shard_map.272
  68.3 0.6 collective-permute-start.17
  68.9 3.8 %shard_map.273.refs_3_ = bf16[4,256,1024]{2,1,0:T(8,128)(2,1)S(1)} custom-call(bf16[256,1024]{1,0:T(8,128)(2,1)S(1)} %get-tuple-element.99.refs_0_, bf16[4,256,2048]{2,1,0:T(8,128)(2,1)S(1)} %get-tuple-element.100.refs_1_, bf16[4,256,2048]{2,1,0:T(8,128)(2,1)S(1)} %get-tuple-element.111.refs_2_, bf16[256,1024]{1,0:T(8,128)(2,1)S(1)} %get-tuple-element.112.refs_3_, ...), custom_call_target="tpu_custom_call" | custom-call | flops 48000000000 | tf_op jit(solution)/shard_map/pallas_call | solution.py:54
  72.7 1.0 %collective-permute-start.18 = (bf16[4,256,1024]{2,1,0:T(8,128)(2,1)S(1)}, bf16[4,256,1024]{2,1,0:T(8,128)(2,1)S(1)}, u32[]{:S(2)}, u32[]{:S(2)}) collective-permute-start(bf16[4,256,1024]{2,1,0:T(8,128)(2,1)S(1)} %shard_map.273.refs_3_), channel_id=1, source_target_pairs={{0,1},{1,0},{2,3},{3,2},{4,5},{5,4},{6,7},{7,6},{8,9},{9,8},{10,11... | collective-permute-start | bytes 6291464 | tf_op jit(solution)/shard_map/ppermute | solution.py:873
  73.6 1.5 %collective-permute-done.17.refs_2_ = bf16[1184,128]{1,0:T(8,128)(2,1)S(1)} collective-permute-done((bf16[1184,128]{1,0:T(8,128)(2,1)S(1)}, bf16[1184,128]{1,0:T(8,128)(2,1)S(1)}, u32[]{:S(2)}, u32[]{:S(2)}) %collective-permute-start.17) | collective-permute-done | bytes 303136 | tf_op jit(solution)/shard_map/ppermute | solution.py:873
  75.1 0.1 shard_map.274
  75.2 2.0 %collective-permute-start.20 = (bf16[672,128]{1,0:T(8,128)(2,1)S(1)}, bf16[672,128]{1,0:T(8,128)(2,1)S(1)}, u32[]{:S(2)}, u32[]{:S(2)}) collective-permute-start(bf16[672,128]{1,0:T(8,128)(2,1)S(1)} %get-tuple-element.132.refs_3_), channel_id=1, source_target_pairs={{0,16},{1,9},{2,18},{3,11},{4,20},{5,13},{6,22},{7,15},{8,24},{9,1... | collective-permute-start | bytes 516104 | tf_op jit(solution)/shard_map/ppermute | solution.py:873
  77.2 3.8 %shard_map.275.refs_1_ = bf16[4,256,1024]{2,1,0:T(8,128)(2,1)S(1)} custom-call(bf16[256,1024]{1,0:T(8,128)(2,1)S(1)} %get-tuple-element.99.refs_0_, bf16[4,256,2048]{2,1,0:T(8,128)(2,1)S(1)} %get-tuple-element.100.refs_1_, bf16[4,256,2048]{2,1,0:T(8,128)(2,1)S(1)} %get-tuple-element.111.refs_2_, bf16[256,1024]{1,0:T(8,128)(2,1)S(1)} %get-tuple-element.112.refs_3_, ...), custom_call_target="tpu_custom_call" | custom-call | flops 48000000000 | tf_op jit(solution)/shard_map/pallas_call | solution.py:54
  81.0 2.8 %shard_map.276 = (bf16[3,1024,256]{2,1,0:T(8,128)(2,1)}, bf16[1024,256]{1,0:T(8,128)(2,1)}, f32[8,128]{1,0:T(8,128)S(1)}) custom-call(s32[3]{0:T(128)S(1)} %pad_add_fusion.core.refs_0_, bf16[4,256,1024]{2,1,0:T(8,128)(2,1)S(1)} %shard_map.275.refs_1_, bf16[4,256,1024]{2,1,0:T(8,128)(2,1)S(1)} %collective-permute-done.18.refs_2_, ...), custom_call_target="tpu_custom_call" | custom-call | flops 1200000000 | tf_op jit(solution)/shard_map/pallas_call | solution.py:54
  83.8 0.1 shard_map.277
  83.9 1.8 %collective-permute-start.21 = (bf16[672,128]{1,0:T(8,128)(2,1)S(1)}, bf16[672,128]{1,0:T(8,128)(2,1)S(1)}, u32[]{:S(2)}, u32[]{:S(2)}) collective-permute-start(bf16[672,128]{1,0:T(8,128)(2,1)S(1)} %get-tuple-element.135.refs_1_), channel_id=1, source_target_pairs={{0,8},{1,5},{2,10},{3,7},{4,12},{5,1},{6,14},{7,3},{8,0},{9,13},{1... | collective-permute-start | bytes 516104 | tf_op jit(solution)/shard_map/ppermute | solution.py:873
  85.7 3.7 %collective-permute-done.21.refs_2_ = bf16[672,128]{1,0:T(8,128)(2,1)S(1)} collective-permute-done((bf16[672,128]{1,0:T(8,128)(2,1)S(1)}, bf16[672,128]{1,0:T(8,128)(2,1)S(1)}, u32[]{:S(2)}, u32[]{:S(2)}) %collective-permute-start.21) | collective-permute-done | bytes 172064 | tf_op jit(solution)/shard_map/ppermute | solution.py:873
  89.3 0.0 copy-start.6
  89.4 0.0 copy-start.7
  89.4 0.0 copy-start.8
  89.4 0.0 copy-start.9
  89.4 0.0 copy-start.10
  89.4 0.0 copy-start.11
  89.4 0.0 copy-start.12
  89.4 0.0 copy-start.13
  89.4 0.1 shard_map.278
  89.6 1.5 %collective-permute-start.22 = (bf16[416,128]{1,0:T(8,128)(2,1)S(1)}, bf16[416,128]{1,0:T(8,128)(2,1)S(1)}, u32[]{:S(2)}, u32[]{:S(2)}) collective-permute-start(bf16[416,128]{1,0:T(8,128)(2,1)S(1)} %get-tuple-element.137.refs_2_), channel_id=1, source_target_pairs={{0,1},{1,0},{2,3},{3,2},{4,5},{5,4},{6,7},{7,6},{8,9},{9,8},{10,11... | collective-permute-start | bytes 319496 | tf_op jit(solution)/shard_map/ppermute | solution.py:873
  91.0 1.0 %collective-permute-done.22.refs_3_ = bf16[416,128]{1,0:T(8,128)(2,1)S(1)} collective-permute-done((bf16[416,128]{1,0:T(8,128)(2,1)S(1)}, bf16[416,128]{1,0:T(8,128)(2,1)S(1)}, u32[]{:S(2)}, u32[]{:S(2)}) %collective-permute-start.22) | collective-permute-done | bytes 106528 | tf_op jit(solution)/shard_map/ppermute | solution.py:873
  92.1 2.4 %shard_map.279 = (f32[32,16,64]{2,1,0:T(8,128)}, f32[32,16,64]{2,1,0:T(8,128)}, f32[32,16,64]{2,1,0:T(8,128)}, f32[16,32,64]{2,1,0:T(8,128)}, f32[16,32,64]{2,1,...) custom-call(s32[3]{0:T(128)S(1)} %pad_add_fusion.core.refs_0_, ...), custom_call_target="tpu_custom_call" | custom-call | flops 28800000000 | tf_op jit(solution)/shard_map/pallas_call | solution.py:54
  (49 shorter events, 0.2 us)
Async XLA Ops:
  2.3 1.5 %collective-permute-start = (bf16[2,8,32,64]{3,2,1,0:T(8,128)(2,1)S(1)}, bf16[2,8,32,64]{3,2,1,0:T(8,128)(2,1)S(1)}, u32[]{:S(2)}, u32[]{:S(2)}) collective-permute-start(bf16[2,8,32,64]{3,2,1,0:T(8,128)(2,1)S(1)} %get-tuple-element.83), channel_id=1, source_target_pairs={{0,1},{1,0},{2,3},{3,2},{4,5},{5,4},{6,7},{7,6},{8,9},{9,8},{10,11... | collective-permute-start | bytes 196616 | tf_op jit(solution)/shard_map/ppermute | solution.py:873
  3.8 9.6 %collective-permute-start.5 = (bf16[3,1024,256]{2,1,0:T(8,128)(2,1)}, bf16[3,1024,256]{2,1,0:T(8,128)(2,1)S(1)}, u32[]{:S(2)}, u32[]{:S(2)}) collective-permute-start(bf16[3,1024,256]{2,1,0:T(8,128)(2,1)} %bitcast.13), channel_id=1, source_target_pairs={{0,1},{1,0},{2,3},{3,2},{4,5},{5,4},{6,7},{7,6},{8,9},{9,8},{10,11... | collective-permute-start | bytes 4718600 | tf_op jit(solution)/shard_map/ppermute | solution.py:873
  4.1 4.3 %collective-permute-start.3 = (bf16[32,128]{1,0:T(8,128)(2,1)S(1)}, bf16[32,128]{1,0:T(8,128)(2,1)S(1)}, u32[]{:S(2)}, u32[]{:S(2)}) collective-permute-start(bf16[32,128]{1,0:T(8,128)(2,1)S(1)} %get-tuple-element.86.refs_0_), channel_id=1, source_target_pairs={{0,1},{1,0},{2,3},{3,2},{4,5},{5,4},{6,7},{7,6},{8,9},{9,8},{10,11... | collective-permute-start | bytes 24584 | tf_op jit(solution)/shard_map/ppermute | solution.py:873
  4.3 4.1 %copy-start.5 = (bf16[1024,256]{1,0:T(8,128)(2,1)S(1)}, bf16[1024,256]{1,0:T(8,128)(2,1)}, u32[]{:S(2)}) copy-start(bf16[1024,256]{1,0:T(8,128)(2,1)} %refs_1_.3) | copy-start | bytes 1572868
  4.4 8.2 %collective-permute-start.1 = (bf16[288,128]{1,0:T(8,128)(2,1)S(1)}, bf16[288,128]{1,0:T(8,128)(2,1)S(1)}, u32[]{:S(2)}, u32[]{:S(2)}) collective-permute-start(bf16[288,128]{1,0:T(8,128)(2,1)S(1)} %get-tuple-element.85.refs_0_), channel_id=1, source_target_pairs={{0,16},{1,17},{2,18},{3,19},{4,20},{5,21},{6,22},{7,23},{8,24},{9,... | collective-permute-start | bytes 221192 | tf_op jit(solution)/shard_map/ppermute | solution.py:873
  8.4 5.0 %collective-permute-start.4 = (bf16[1024,256]{1,0:T(8,128)(2,1)S(1)}, bf16[1024,256]{1,0:T(8,128)(2,1)S(1)}, u32[]{:S(2)}, u32[]{:S(2)}) collective-permute-start(bf16[1024,256]{1,0:T(8,128)(2,1)S(1)} %copy-done.5), channel_id=1, source_target_pairs={{0,1},{1,0},{2,3},{3,2},{4,5},{5,4},{6,7},{7,6},{8,9},{9,8},{10,11... | collective-permute-start | bytes 1572872 | tf_op jit(solution)/shard_map/ppermute | solution.py:873
  8.4 5.0 %copy-start.4 = (bf16[1024,3,256]{2,0,1:T(8,128)(2,1)S(1)}, bf16[1024,3,256]{2,0,1:T(8,128)(2,1)}, u32[]{:S(2)}) copy-start(bf16[1024,3,256]{2,0,1:T(8,128)(2,1)} %param.20) | copy-start | bytes 4718596
  8.4 11.0 %collective-permute-start.9 = (bf16[256,128]{1,0:T(8,128)(2,1)S(1)}, bf16[256,128]{1,0:T(8,128)(2,1)S(1)}, u32[]{:S(2)}, u32[]{:S(2)}) collective-permute-start(bf16[256,128]{1,0:T(8,128)(2,1)S(1)} %get-tuple-element.96.refs_0_), channel_id=1, source_target_pairs={{0,2},{1,5},{2,0},{3,7},{4,6},{5,1},{6,4},{7,3},{8,10},{9,13},{10,... | collective-permute-start | bytes 196616 | tf_op jit(solution)/shard_map/ppermute | solution.py:873
  12.6 5.2 %collective-permute-start.2 = (bf16[576,128]{1,0:T(8,128)(2,1)S(1)}, bf16[576,128]{1,0:T(8,128)(2,1)S(1)}, u32[]{:S(2)}, u32[]{:S(2)}) collective-permute-start(bf16[576,128]{1,0:T(8,128)(2,1)S(1)} %shard_map.256.refs_5_.refs_0_), channel_id=1, source_target_pairs={{0,8},{1,9},{2,10},{3,11},{4,12},{5,13},{6,14},{7,15},{8,0},{9,1},... | collective-permute-start | bytes 442376 | tf_op jit(solution)/shard_map/ppermute | solution.py:873
  15.2 2.6 %copy-start.16 = (bf16[256,256]{1,0:T(8,128)(2,1)}, bf16[256,256]{1,0:T(8,128)(2,1)S(1)}, u32[]{:S(2)}) copy-start(bf16[256,256]{1,0:T(8,128)(2,1)S(1)} %get-tuple-element.89.refs_3_.refs_10_.refs_9_) | copy-start | bytes 393220
  15.3 17.5 %copy-start.18 = (bf16[3,256,2048]{2,1,0:T(8,128)(2,1)}, bf16[3,256,2048]{2,1,0:T(8,128)(2,1)S(1)}, u32[]{:S(2)}) copy-start(bf16[3,256,2048]{2,1,0:T(8,128)(2,1)S(1)} %get-tuple-element.93.refs_6_.refs_1_.refs_3_.refs_4_) | copy-start | bytes 9437188
  17.8 7.0 %collective-permute-start.6 = (bf16[1216,128]{1,0:T(8,128)(2,1)S(1)}, bf16[1216,128]{1,0:T(8,128)(2,1)S(1)}, u32[]{:S(2)}, u32[]{:S(2)}) collective-permute-start(bf16[1216,128]{1,0:T(8,128)(2,1)S(1)} %shard_map.259.refs_0_.refs_2_), channel_id=1, source_target_pairs={{0,2},{1,5},{2,0},{3,7},{4,6},{5,1},{6,4},{7,3},{8,10},{9,13},{10,... | collective-permute-start | bytes 933896 | tf_op jit(solution)/shard_map/ppermute | solution.py:873
  19.5 8.7 %collective-permute-start.10 = (bf16[512,128]{1,0:T(8,128)(2,1)S(1)}, bf16[512,128]{1,0:T(8,128)(2,1)S(1)}, u32[]{:S(2)}, u32[]{:S(2)}) collective-permute-start(bf16[512,128]{1,0:T(8,128)(2,1)S(1)} %shard_map.262.refs_0_), channel_id=1, source_target_pairs={{0,16},{1,17},{2,18},{3,19},{4,20},{5,21},{6,22},{7,23},{8,24},{9,... | collective-permute-start | bytes 393224 | tf_op jit(solution)/shard_map/ppermute | solution.py:873
  24.8 4.1 %collective-permute-start.8 = (bf16[320,128]{1,0:T(8,128)(2,1)S(1)}, bf16[320,128]{1,0:T(8,128)(2,1)S(1)}, u32[]{:S(2)}, u32[]{:S(2)}) collective-permute-start(bf16[320,128]{1,0:T(8,128)(2,1)S(1)} %get-tuple-element.92.refs_2_), channel_id=1, source_target_pairs={{0,1},{1,0},{2,3},{3,2},{4,5},{5,4},{6,7},{7,6},{8,9},{9,8},{10,11... | collective-permute-start | bytes 245768 | tf_op jit(solution)/shard_map/ppermute | solution.py:873
  24.9 4.1 %copy-start.14 = (bf16[160,128]{1,0:T(8,128)(2,1)S(1)}, bf16[160,128]{1,0:T(8,128)(2,1)}, u32[]{:S(2)}) copy-start(bf16[160,128]{1,0:T(8,128)(2,1)} %constant.24.clone.refs_1_) | copy-start | bytes 122884
  24.9 11.7 %collective-permute-start.7 = (bf16[2048,128]{1,0:T(8,128)(2,1)S(1)}, bf16[2048,128]{1,0:T(8,128)(2,1)S(1)}, u32[]{:S(2)}, u32[]{:S(2)}) collective-permute-start(bf16[2048,128]{1,0:T(8,128)(2,1)S(1)} %get-tuple-element.90.refs_2_.refs_1_), channel_id=1, source_target_pairs={{0,4},{1,3},{2,6},{3,1},{4,0},{5,7},{6,2},{7,5},{8,12},{9,11},{10,... | collective-permute-start | bytes 1572872 | tf_op jit(solution)/shard_map/ppermute | solution.py:873
  28.2 7.4 %collective-permute-start.11 = (bf16[1024,128]{1,0:T(8,128)(2,1)S(1)}, bf16[1024,128]{1,0:T(8,128)(2,1)S(1)}, u32[]{:S(2)}, u32[]{:S(2)}) collective-permute-start(bf16[1024,128]{1,0:T(8,128)(2,1)S(1)} %shard_map.263.refs_0_), channel_id=1, source_target_pairs={{0,8},{1,9},{2,10},{3,11},{4,12},{5,13},{6,14},{7,15},{8,0},{9,1},... | collective-permute-start | bytes 786440 | tf_op jit(solution)/shard_map/ppermute | solution.py:873
  35.6 9.2 %collective-permute-start.12 = (bf16[2048,128]{1,0:T(8,128)(2,1)S(1)}, bf16[2048,128]{1,0:T(8,128)(2,1)S(1)}, u32[]{:S(2)}, u32[]{:S(2)}) collective-permute-start(bf16[2048,128]{1,0:T(8,128)(2,1)S(1)} %shard_map.265.refs_6_.refs_1_), channel_id=1, source_target_pairs={{0,4},{1,3},{2,6},{3,1},{4,0},{5,7},{6,2},{7,5},{8,12},{9,11},{10,... | collective-permute-start | bytes 1572872 | tf_op jit(solution)/shard_map/ppermute | solution.py:873
  36.6 8.3 %copy-start.17 = (bf16[256,256]{1,0:T(8,128)(2,1)S(1)}, bf16[256,256]{1,0:T(8,128)(2,1)}, u32[]{:S(2)}) copy-start(bf16[256,256]{1,0:T(8,128)(2,1)} %copy-done.16) | copy-start | bytes 393220
  43.7 13.4 %collective-permute-start.13 = (bf16[2048,128]{1,0:T(8,128)(2,1)S(1)}, bf16[2048,128]{1,0:T(8,128)(2,1)S(1)}, u32[]{:S(2)}, u32[]{:S(2)}) collective-permute-start(bf16[2048,128]{1,0:T(8,128)(2,1)S(1)} %get-tuple-element.117.refs_1_), channel_id=1, source_target_pairs={{0,4},{1,3},{2,6},{3,1},{4,0},{5,7},{6,2},{7,5},{8,12},{9,11},{10,... | collective-permute-start | bytes 1572872 | tf_op jit(solution)/shard_map/ppermute | solution.py:873
  44.9 8.2 %copy-start.19 = (bf16[3,256,2048]{2,1,0:T(8,128)(2,1)S(1)}, bf16[3,256,2048]{2,1,0:T(8,128)(2,1)}, u32[]{:S(2)}) copy-start(bf16[3,256,2048]{2,1,0:T(8,128)(2,1)} %copy-done.18) | copy-start | bytes 9437188
  52.2 16.0 %collective-permute-start.14 = (bf16[2080,128]{1,0:T(8,128)(2,1)S(1)}, bf16[2080,128]{1,0:T(8,128)(2,1)S(1)}, u32[]{:S(2)}, u32[]{:S(2)}) collective-permute-start(bf16[2080,128]{1,0:T(8,128)(2,1)S(1)} %get-tuple-element.122.refs_1_), channel_id=1, source_target_pairs={{0,4},{1,3},{2,6},{3,1},{4,0},{5,7},{6,2},{7,5},{8,12},{9,11},{10,... | collective-permute-start | bytes 1597448 | tf_op jit(solution)/shard_map/ppermute | solution.py:873
  57.1 1.4 %copy-start.15 = (bf16[160,128]{1,0:T(8,128)(2,1)S(1)}, bf16[160,128]{1,0:T(8,128)(2,1)}, u32[]{:S(2)}) copy-start(bf16[160,128]{1,0:T(8,128)(2,1)} %constant.24.clone.refs_1_) | copy-start | bytes 122884
  57.3 8.2 %collective-permute-start.16 = (bf16[1024,128]{1,0:T(8,128)(2,1)S(1)}, bf16[1024,128]{1,0:T(8,128)(2,1)S(1)}, u32[]{:S(2)}, u32[]{:S(2)}) collective-permute-start(bf16[1024,128]{1,0:T(8,128)(2,1)S(1)} %get-tuple-element.124.refs_1_), channel_id=1, source_target_pairs={{0,2},{1,17},{2,0},{3,19},{4,6},{5,21},{6,4},{7,23},{8,10},{9,25},... | collective-permute-start | bytes 786440 | tf_op jit(solution)/shard_map/ppermute | solution.py:873
  63.3 4.8 %collective-permute-start.15 = (bf16[128,128]{1,0:T(8,128)(2,1)S(1)}, bf16[128,128]{1,0:T(8,128)(2,1)S(1)}, u32[]{:S(2)}, u32[]{:S(2)}) collective-permute-start(bf16[128,128]{1,0:T(8,128)(2,1)S(1)} %get-tuple-element.123.refs_3_), channel_id=1, source_target_pairs={{0,4},{1,3},{2,6},{3,1},{4,0},{5,7},{6,2},{7,5},{8,12},{9,11},{10,... | collective-permute-start | bytes 98312 | tf_op jit(solution)/shard_map/ppermute | solution.py:873
  65.5 18.3 %collective-permute-start.19 = (bf16[512,128]{1,0:T(8,128)(2,1)S(1)}, bf16[512,128]{1,0:T(8,128)(2,1)S(1)}, u32[]{:S(2)}, u32[]{:S(2)}) collective-permute-start(bf16[512,128]{1,0:T(8,128)(2,1)S(1)} %get-tuple-element.131.refs_5_), channel_id=1, source_target_pairs={{0,16},{1,9},{2,18},{3,11},{4,20},{5,13},{6,22},{7,15},{8,24},{9,1... | collective-permute-start | bytes 393224 | tf_op jit(solution)/shard_map/ppermute | solution.py:873
  68.3 6.9 %collective-permute-start.17 = (bf16[1184,128]{1,0:T(8,128)(2,1)S(1)}, bf16[1184,128]{1,0:T(8,128)(2,1)S(1)}, u32[]{:S(2)}, u32[]{:S(2)}) collective-permute-start(bf16[1184,128]{1,0:T(8,128)(2,1)S(1)} %get-tuple-element.127.refs_1_), channel_id=1, source_target_pairs={{0,2},{1,17},{2,0},{3,19},{4,6},{5,21},{6,4},{7,23},{8,10},{9,25},... | collective-permute-start | bytes 909320 | tf_op jit(solution)/shard_map/ppermute | solution.py:873
  72.7 8.3 %collective-permute-start.18 = (bf16[4,256,1024]{2,1,0:T(8,128)(2,1)S(1)}, bf16[4,256,1024]{2,1,0:T(8,128)(2,1)S(1)}, u32[]{:S(2)}, u32[]{:S(2)}) collective-permute-start(bf16[4,256,1024]{2,1,0:T(8,128)(2,1)S(1)} %shard_map.273.refs_3_), channel_id=1, source_target_pairs={{0,1},{1,0},{2,3},{3,2},{4,5},{5,4},{6,7},{7,6},{8,9},{9,8},{10,11... | collective-permute-start | bytes 6291464 | tf_op jit(solution)/shard_map/ppermute | solution.py:873
  75.2 8.5 %collective-permute-start.20 = (bf16[672,128]{1,0:T(8,128)(2,1)S(1)}, bf16[672,128]{1,0:T(8,128)(2,1)S(1)}, u32[]{:S(2)}, u32[]{:S(2)}) collective-permute-start(bf16[672,128]{1,0:T(8,128)(2,1)S(1)} %get-tuple-element.132.refs_3_), channel_id=1, source_target_pairs={{0,16},{1,9},{2,18},{3,11},{4,20},{5,13},{6,22},{7,15},{8,24},{9,1... | collective-permute-start | bytes 516104 | tf_op jit(solution)/shard_map/ppermute | solution.py:873
  83.9 5.5 %collective-permute-start.21 = (bf16[672,128]{1,0:T(8,128)(2,1)S(1)}, bf16[672,128]{1,0:T(8,128)(2,1)S(1)}, u32[]{:S(2)}, u32[]{:S(2)}) collective-permute-start(bf16[672,128]{1,0:T(8,128)(2,1)S(1)} %get-tuple-element.135.refs_1_), channel_id=1, source_target_pairs={{0,8},{1,5},{2,10},{3,7},{4,12},{5,1},{6,14},{7,3},{8,0},{9,13},{1... | collective-permute-start | bytes 516104 | tf_op jit(solution)/shard_map/ppermute | solution.py:873
  89.3 2.7 %copy-start = (f32[32,16,64]{2,1,0:T(8,128)S(1)}, f32[32,16,64]{2,1,0:T(8,128)}, u32[]{:S(2)}) copy-start(f32[32,16,64]{2,1,0:T(8,128)} %refs_4_.1) | copy-start | bytes 393220
  89.3 2.7 %copy-start.1 = (f32[16,64,32]{1,2,0:T(8,128)S(1)}, f32[16,64,32]{1,2,0:T(8,128)}, u32[]{:S(2)}) copy-start(f32[16,64,32]{1,2,0:T(8,128)} %param.17) | copy-start | bytes 393220
  89.3 2.7 %copy-start.2 = (f32[2,16,64]{2,1,0:T(8,128)S(1)}, f32[2,16,64]{2,1,0:T(8,128)}, u32[]{:S(2)}) copy-start(f32[2,16,64]{2,1,0:T(8,128)} %refs_10_.1) | copy-start | bytes 24580
  89.3 2.7 %copy-start.3 = (f32[32,60]{1,0:T(8,128)S(1)}, f32[32,60]{1,0:T(8,128)}, u32[]{:S(2)}) copy-start(f32[32,60]{1,0:T(8,128)} %refs_13_.1) | copy-start | bytes 23044
  89.3 2.7 %copy-start.6 = (f32[32,16,64]{2,1,0:T(8,128)S(1)}, f32[32,16,64]{2,1,0:T(8,128)}, u32[]{:S(2)}) copy-start(f32[32,16,64]{2,1,0:T(8,128)} %refs_5_.1) | copy-start | bytes 393220
  89.4 2.7 %copy-start.7 = (f32[32,16,64]{2,1,0:T(8,128)S(1)}, f32[32,16,64]{2,1,0:T(8,128)}, u32[]{:S(2)}) copy-start(f32[32,16,64]{2,1,0:T(8,128)} %refs_6_.1) | copy-start | bytes 393220
  89.4 2.7 %copy-start.8 = (f32[16,64,32]{1,2,0:T(8,128)S(1)}, f32[16,64,32]{1,2,0:T(8,128)}, u32[]{:S(2)}) copy-start(f32[16,64,32]{1,2,0:T(8,128)} %param.23) | copy-start | bytes 393220
  89.4 2.7 %copy-start.9 = (f32[16,64,32]{1,2,0:T(8,128)S(1)}, f32[16,64,32]{1,2,0:T(8,128)}, u32[]{:S(2)}) copy-start(f32[16,64,32]{1,2,0:T(8,128)} %param.24) | copy-start | bytes 393220
  89.4 2.7 %copy-start.10 = (f32[2,16,64]{2,1,0:T(8,128)S(1)}, f32[2,16,64]{2,1,0:T(8,128)}, u32[]{:S(2)}) copy-start(f32[2,16,64]{2,1,0:T(8,128)} %refs_11_.1) | copy-start | bytes 24580
  89.4 2.7 %copy-start.11 = (f32[2,16,64]{2,1,0:T(8,128)S(1)}, f32[2,16,64]{2,1,0:T(8,128)}, u32[]{:S(2)}) copy-start(f32[2,16,64]{2,1,0:T(8,128)} %refs_12_.1) | copy-start | bytes 24580
  89.4 2.7 %copy-start.12 = (f32[32,60]{1,0:T(8,128)S(1)}, f32[32,60]{1,0:T(8,128)}, u32[]{:S(2)}) copy-start(f32[32,60]{1,0:T(8,128)} %refs_14_.1) | copy-start | bytes 23044
  89.4 2.7 %copy-start.13 = (f32[32,60]{1,0:T(8,128)S(1)}, f32[32,60]{1,0:T(8,128)}, u32[]{:S(2)}) copy-start(f32[32,60]{1,0:T(8,128)} %refs_15_.1) | copy-start | bytes 23044
  89.6 2.4 %collective-permute-start.22 = (bf16[416,128]{1,0:T(8,128)(2,1)S(1)}, bf16[416,128]{1,0:T(8,128)(2,1)S(1)}, u32[]{:S(2)}, u32[]{:S(2)}) collective-permute-start(bf16[416,128]{1,0:T(8,128)(2,1)S(1)} %get-tuple-element.137.refs_2_), channel_id=1, source_target_pairs={{0,1},{1,0},{2,3},{3,2},{4,5},{5,4},{6,7},{7,6},{8,9},{9,8},{10,11... | collective-permute-start | bytes 319496 | tf_op jit(solution)/shard_map/ppermute | solution.py:873
